TPU v7x, 32 devices: a whole 2x2x4 slice. The times are simulated.
32 devices in a mesh: seq: 4 (over y, x), exp: 8 (over z, core).
Axes of the slice: x: 2, y: 2, z: 4, core: 2. Of those that a mesh axis runs over, the one named last changes fastest.
Arguments:
- tokens: bfloat16 [8192, 2048], P(('seq', 'exp')), may hold values from -128 to 128
- slot_embed: bfloat16 [2048, 64], P(None, 'exp'), may hold values from -0.397747564 to 0.397747564
- expert_in: bfloat16 [16, 2048, 4096], P('exp', None, 'seq'), may hold values from -0.125 to 0.125
- expert_out: bfloat16 [16, 4096, 2048], P('exp', 'seq'), may hold values from -0.09375 to 0.09375
- out_grad: bfloat16 [8192, 2048], P(('seq', 'exp')), may hold values from -0.59765625 to 0.59765625
Outputs:
- tok_grad: bfloat16 [8192, 2048], P(('seq', 'exp'))
- slot_grad: float32 [2048, 64], P('seq', 'exp')
All inputs are finite; a program needn't handle non-finite values.
Results may differ from a plain program's by a relative error of at most 0.024.
Values may be sent and summed in bfloat16 or wider, within the bound.
No kernel may reach another device: no remote copies, remote signals or barrier semaphores. Data moves between devices by JAX's collectives and lax.ppermute only.
A program may use at most 64 MiB of HBM per device.

v0:
```python
from functools import partial

import jax
import jax.numpy as jnp
from jax import lax
from jax.sharding import PartitionSpec as P


def merged(x, axis, combine):
    everything = jax.tree.map(lambda part: lax.all_gather(part, axis), x)
    first = jax.tree.map(lambda part: part[0], everything)

    def lap(k, so_far):
        return combine(so_far, jax.tree.map(lambda part: part[k], everything))

    return lax.fori_loop(1, lax.axis_size(axis), lap, first)


def contract_rows(left, right):
    return lax.dot_general(
        left, right, (((0,), (0,)), ((), ())), preferred_element_type=jnp.float32
    )


def contract_cols(left, right):
    return lax.dot_general(
        left, right, (((1,), (1,)), ((), ())), preferred_element_type=jnp.float32
    )


def merge_stats(first_pair, second_pair):
    top_value = jnp.maximum(first_pair[0], second_pair[0])
    summed = first_pair[1] * jnp.exp(first_pair[0] - top_value) + second_pair[1] * jnp.exp(
        second_pair[0] - top_value
    )
    return (top_value, summed)


def owner_sum(partial_rows):
    owned = lax.psum_scatter(partial_rows, "exp", scatter_dimension=0, tiled=True)
    return lax.psum(owned, "seq")


def shards(tokens, slot_embed, expert_in, expert_out, out_grad):
    experts_here = expert_in.shape[0]
    model_width = tokens.shape[1]
    slot_table = lax.all_gather(slot_embed, "exp", axis=1, tiled=True)
    logits = jnp.dot(tokens, slot_table, preferred_element_type=jnp.float32)
    local_top = jnp.max(logits, axis=0)
    local_total = jnp.sum(jnp.exp(logits - local_top), axis=0)
    col_top, col_total = merged((local_top, local_total), ("seq", "exp"), merge_stats)
    dispatch = jnp.exp(logits - col_top) / col_total
    dispatch_b = dispatch.astype(jnp.bfloat16)
    combine_w = jax.nn.softmax(logits, axis=1)
    combine_b = combine_w.astype(jnp.bfloat16)
    slot_sum = owner_sum(contract_rows(dispatch_b, tokens))
    slot_in = slot_sum.astype(jnp.bfloat16).reshape(experts_here, -1, model_width)
    pre_act = jnp.einsum("esd,edh->esh", slot_in, expert_in, preferred_element_type=jnp.float32)
    hidden = jax.nn.gelu(pre_act, approximate=True).astype(jnp.bfloat16)
    out_part = jnp.einsum("esh,ehd->esd", hidden, expert_out, preferred_element_type=jnp.float32)
    slot_out = lax.psum(out_part, "seq").astype(jnp.bfloat16).reshape(-1, model_width)
    slot_all = lax.all_gather(slot_out, "exp", axis=0, tiled=True)
    comb_grad = contract_cols(out_grad, slot_all)
    grad_out = owner_sum(contract_rows(combine_b, out_grad))
    grad_out = grad_out.astype(jnp.bfloat16).reshape(experts_here, -1, model_width)
    hid_grad = jnp.einsum("esd,ehd->esh", grad_out, expert_out, preferred_element_type=jnp.float32)
    _, pullback = jax.vjp(partial(jax.nn.gelu, approximate=True), pre_act)
    act_grad = pullback(hid_grad)[0].astype(jnp.bfloat16)
    in_part = jnp.einsum("esh,edh->esd", act_grad, expert_in, preferred_element_type=jnp.float32)
    grad_own = lax.psum(in_part, "seq").astype(jnp.bfloat16).reshape(-1, model_width)
    grad_all = lax.all_gather(grad_own, "exp", axis=0, tiled=True)
    disp_grad = contract_cols(tokens, grad_all)
    centre_local = jnp.sum(dispatch_b.astype(jnp.float32) * disp_grad, axis=0)
    centre = lax.psum(centre_local, ("seq", "exp"))
    comb_mean = jnp.sum(combine_w * comb_grad, axis=1, keepdims=True)
    logit_grad = dispatch * (disp_grad - centre) + combine_w * (comb_grad - comb_mean)
    logit_b = logit_grad.astype(jnp.bfloat16)
    tok_grad = jnp.dot(dispatch_b, grad_all, preferred_element_type=jnp.float32) + contract_cols(
        logit_b, slot_table
    )
    table_part = contract_rows(tokens, logit_b)
    table_owned = lax.psum_scatter(table_part, "exp", scatter_dimension=1, tiled=True)
    slot_grad = lax.psum_scatter(table_owned, "seq", scatter_dimension=0, tiled=True)
    return (tok_grad.astype(jnp.bfloat16), slot_grad)


def solution(mesh):
    placed = (
        P(("seq", "exp"), None),
        P(None, "exp"),
        P("exp", None, "seq"),
        P("exp", "seq", None),
        P(("seq", "exp"), None),
    )
    return jax.shard_map(
        shards,
        mesh=mesh,
        in_specs=placed,
        out_specs=(P(("seq", "exp"), None), P("seq", "exp")),
        check_vma=False,
    )
```

profile of v0, /device:TPU:0, one launch (start us, length us, event | category | flops | bytes accessed | tf_op | source)
XLA Modules:
  0.0 316.5 jit_solution(1277718125075292840)
XLA Ops:
  7.2 0.0 reduce-scatter.7.cloned.1.call-start
  7.2 16.2 %all_gather.21 = bf16[2048,64]{0,1:T(8,128)(2,1)S(1)} all-gather(bf16[2048,8]{0,1:T(8,128)(2,1)} %param.8), channel_id=1, replica_groups=mesh['seq'=4,'exp'=8] {'exp'}, dimensions={1}, use_global_device_ids=true | all-gather | bytes 294912 | tf_op jit(solution)/shard_map/all_gather | solution.py:47
  23.5 0.5 fusion.43
  24.0 0.3 dynamic-update-slice
  24.3 0.2 fusion.4
  24.5 0.3 dynamic-update-slice.1
  24.8 40.4 %all-reduce.2 = (f32[2048]{0:T(1024)S(1)}, f32[2048]{0:T(1024)S(1)}) all-reduce(f32[2048]{0:T(1024)S(1)} %dynamic-update-slice, f32[2048]{0:T(1024)S(1)} %dynamic-update-slice.1), channel_id=2, replica_groups=mesh['seq'=4,'exp'=8] {'seq','exp'}, use_global_device_ids=true, to_apply=%add | all-reduce | flops 4096 | bytes 32768
  65.1 0.1 reshape.27
  65.2 0.1 reshape.28
  65.3 1.4 while.17
  66.7 1.1 fusion.40
  67.8 0.0 reduce-scatter.5.cloned.1.call-start
  67.9 2.3 fusion.12
  70.2 0.0 reduce-scatter.9.cloned.1.call-start
  70.3 28.7 %reduce-scatter.7.cloned.1.call-done = f32[8,2048]{1,0:T(8,128)} async-done(((f32[64,2048]{1,0:T(8,128)}), f32[8,2048]{1,0:T(8,128)}) %reduce-scatter.7.cloned.1.call-update) | async-done | bytes 65552 | tf_op jit(solution)/shard_map/reduce_scatter | solution.py:40
  98.9 31.5 %reduce-scatter.5.cloned.1.call-done = f32[8,2048]{1,0:T(8,128)} async-done(((f32[64,2048]{1,0:T(8,128)}), f32[8,2048]{1,0:T(8,128)}) %reduce-scatter.5.cloned.1.call-update) | async-done | bytes 65552 | tf_op jit(solution)/shard_map/reduce_scatter | solution.py:40
  130.4 18.8 %all-reduce.7 = (bf16[8,2048]{1,0:T(8,128)(2,1)S(1)}, bf16[8,2048]{1,0:T(8,128)(2,1)S(1)}) all-reduce(f32[8,2048]{1,0:T(8,128)} %reduce-scatter.7.cloned.1.call-done, f32[8,2048]{1,0:T(8,128)} %reduce-scatter.5.cloned.1.call-done), channel_id=1, replica_groups=mesh['seq'=4,'exp'=8] {'seq'}, use_global_device_ids=true, to_apply=%region_9.0 | all-reduce | flops 32768 | bytes 196608 | tf_op jit(solution)/shard_map/psum | solution.py:41
  149.2 4.6 %fusion.46 = f32[2,4,1024]{2,1,0:T(4,128)S(1)} fusion(bf16[2,4,2048]{2,1,0:T(4,128)(2,1)S(1)} %reshape.24, bf16[2,2048,1024]{2,1,0:T(8,128)(2,1)} %param.9), kind=kOutput, calls=%fused_computation.58 | convolution fusion | flops 33554432 | bytes 8454144 | tf_op jit(solution)/shard_map/esd,edh->esh/dot_general | solution.py:58
  153.8 4.6 %fusion.16 = f32[2,4,2048]{2,1,0:T(4,128)S(1)} fusion(bf16[2,1024,2048]{2,1,0:T(8,128)(2,1)} %param.10, f32[2,4,1024]{2,1,0:T(4,128)S(1)} %fusion.46), kind=kOutput, calls=%fused_computation.32 | convolution fusion | flops 33628160 | bytes 8486912 | tf_op jit(solution)/shard_map/esh,ehd->esd/dot_general | solution.py:60
  158.4 10.3 %fusion.14 = f32[2,4,2048]{2,1,0:T(4,128)S(1)} fusion(bf16[2,2048,1024]{2,1,0:T(8,128)(2,1)} %param.9, f32[2,4,1024]{2,1,0:T(4,128)S(1)} %fusion.46, bf16[2,4,2048]{2,1,0:T(4,128)(2,1)S(1)} %reshape.23, bf16[2,1024,2048]{2,1,0:T(8,128)(2,1)} %param.10), kind=kOutput, calls=%fused_computation.31 | convolution fusion | flops 67272704 | bytes 16908288 | tf_op jit(solution)/shard_map/esh,edh->esd/dot_general | solution.py:69
  168.7 16.4 %all-reduce.8 = (bf16[2,4,2048]{2,1,0:T(4,128)(2,1)S(1)}, bf16[2,4,2048]{2,1,0:T(4,128)(2,1)S(1)}) all-reduce(f32[2,4,2048]{2,1,0:T(4,128)S(1)} %fusion.14, f32[2,4,2048]{2,1,0:T(4,128)S(1)} %fusion.16), channel_id=1, replica_groups=mesh['seq'=4,'exp'=8] {'seq'}, use_global_device_ids=true, to_apply=%region_10.0 | all-reduce | flops 32768 | bytes 196608 | tf_op jit(solution)/shard_map/psum | solution.py:70
  185.1 14.2 %all_gather.26 = bf16[64,2048]{1,0:T(8,128)(2,1)S(1)} all-gather(bf16[8,2048]{1,0:T(8,128)(2,1)S(1)} %reshape.25), channel_id=1, replica_groups=mesh['seq'=4,'exp'=8] {'exp'}, dimensions={0}, use_global_device_ids=true | all-gather | bytes 294912 | tf_op jit(solution)/shard_map/all_gather | solution.py:71
  199.3 14.2 %all_gather.27 = bf16[64,2048]{1,0:T(8,128)(2,1)S(1)} all-gather(bf16[8,2048]{1,0:T(8,128)(2,1)S(1)} %reshape.26), channel_id=1, replica_groups=mesh['seq'=4,'exp'=8] {'exp'}, dimensions={0}, use_global_device_ids=true | all-gather | bytes 294912 | tf_op jit(solution)/shard_map/all_gather | solution.py:62
  213.5 0.4 convolution_bitcast_fusion.1
  214.0 0.6 multiply_reduce_fusion.1
  214.5 37.5 %psum.38 = f32[64]{0:T(128)S(1)} all-reduce(f32[64]{0:T(128)S(1)} %get-tuple-element.137), channel_id=1, replica_groups=mesh['seq'=4,'exp'=8] {'seq','exp'}, use_global_device_ids=true, to_apply=%region_12.0 | all-reduce | flops 64 | bytes 512 | tf_op jit(solution)/shard_map/psum | solution.py:74
  252.1 1.1 convolution_bitcast_fusion
  253.3 0.0 reduce-scatter.11.cloned.1.call-start
  253.3 1.5 fusion.38
  254.8 29.9 %reduce-scatter.9.cloned.1.call-done = f32[2048,8]{0,1:T(8,128)} async-done(((f32[2048,64]{0,1:T(8,128)}), f32[2048,8]{0,1:T(8,128)}) %reduce-scatter.9.cloned.1.call-update) | async-done | bytes 65552 | tf_op jit(solution)/shard_map/reduce_scatter | solution.py:82
  284.7 2.4 fusion.2
  287.1 22.9 %reduce-scatter.11.cloned.1.call-done = f32[512,8]{0,1:T(8,128)} async-done(((f32[2048,8]{0,1:T(8,128)}), f32[512,8]{0,1:T(8,128)}) %reduce-scatter.11.cloned.1.call-update) | async-done | bytes 16400 | tf_op jit(solution)/shard_map/reduce_scatter | solution.py:83
  (55 shorter events, 1.0 us)
Async XLA Ops:
  7.2 16.3 %copy-start = (bf16[256,2048]{1,0:T(8,128)(2,1)S(1)}, bf16[256,2048]{1,0:T(8,128)(2,1)}, u32[]{:S(2)}) copy-start(bf16[256,2048]{1,0:T(8,128)(2,1)} %param.7) | copy-start | bytes 3145732
  7.2 91.7 %reduce-scatter.7.cloned.1.call-start = ((), (), s32[]{:S(2)}) async-start(), calls=%async_computation.5 | async-start | bytes 589824 | tf_op jit(solution)/shard_map/reduce_scatter | solution.py:40
  67.8 62.6 %reduce-scatter.5.cloned.1.call-start = ((), (), s32[]{:S(2)}) async-start(), calls=%async_computation.4 | async-start | bytes 589824 | tf_op jit(solution)/shard_map/reduce_scatter | solution.py:40
  70.2 214.5 %reduce-scatter.9.cloned.1.call-start = ((), (), s32[]{:S(2)}) async-start(), calls=%async_computation.6 | async-start | bytes 589824 | tf_op jit(solution)/shard_map/reduce_scatter | solution.py:82
  158.4 55.1 %copy-start.1 = (bf16[256,2048]{1,0:T(8,128)(2,1)S(1)}, bf16[256,2048]{1,0:T(8,128)(2,1)}, u32[]{:S(2)}) copy-start(bf16[256,2048]{1,0:T(8,128)(2,1)} %param.11) | copy-start | bytes 3145732
  199.3 54.0 %copy-start.2 = (bf16[64,2048]{1,0:T(8,128)(2,1)}, bf16[64,2048]{1,0:T(8,128)(2,1)S(1)}, u32[]{:S(2)}) copy-start(bf16[64,2048]{1,0:T(8,128)(2,1)S(1)} %all_gather.26) | copy-start | bytes 786436
  214.5 38.7 %copy-start.3 = (f32[256,64]{0,1:T(8,128)}, f32[256,64]{0,1:T(8,128)S(1)}, u32[]{:S(2)}) copy-start(f32[256,64]{0,1:T(8,128)S(1)} %get-tuple-element.162) | copy-start | bytes 196612
  214.5 38.7 %copy-start.4 = (f32[256]{0:T(256)}, f32[256]{0:T(256)S(1)}, u32[]{:S(2)}) copy-start(f32[256]{0:T(256)S(1)} %get-tuple-element.138) | copy-start | bytes 3076
  252.1 1.2 copy-start.5
  253.3 56.7 %reduce-scatter.11.cloned.1.call-start = ((), (), s32[]{:S(2)}) async-start(), calls=%async_computation.7 | async-start | bytes 81920 | tf_op jit(solution)/shard_map/reduce_scatter | solution.py:83
Sparse Core Ops, SparseCore 0:
  67.9 30.9 reduce-scatter.6
  101.3 29.0 reduce-scatter.4
  253.4 31.3 reduce-scatter.8
  288.1 21.8 reduce-scatter.10
where the time goes:
time: 317 us
  blocking collectives  158 us (50%)
  waiting for transfers between devices  113 us (36%)
  matrix products  29.4 us (9%)
  between operations  13.9 us (4%)
    reduce_scatter x2, waiting for transfers between devices, owner_sum(): lax.psum_scatter(partial_rows, 'exp', scatter_dimension=0, tiled=True)  60.1 us
    unnamed x1, blocking collectives  40.4 us
    psum x1, blocking collectives, shards(): centre = lax.psum(centre_local, ('seq', 'exp'))  37.5 us
    reduce_scatter x1, waiting for transfers between devices, shards(): lax.psum_scatter(table_part, 'exp', scatter_dimension=1, tiled=True)  29.9 us
    reduce_scatter x1, waiting for transfers between devices, shards(): lax.psum_scatter(table_owned, 'seq', scatter_dimension=0, tiled=True)  22.9 us
    psum x1, blocking collectives, owner_sum(): return lax.psum(owned, 'seq')  18.8 us
    psum x1, blocking collectives, shards(): lax.psum(in_part, 'seq').astype(jnp.bfloat16).reshape(-1, model_width)  16.4 us
    all_gather x1, blocking collectives, shards(): slot_table = lax.all_gather(slot_embed, 'exp', axis=1, tiled=True)  16.2 us
  transfers between devices with their start and end apart: 4, of which 4 were waited for; matrix products, arithmetic and copies ran while one was open for 2% of the time, Pallas kernels for 0%

commit v1 on v0

v1 whole, which is shorter than its diff:
```python
from functools import partial

import jax
import jax.numpy as jnp
from jax import lax
from jax.sharding import PartitionSpec as P

LANES = 128


def contract_cols(left, right):
    return lax.dot_general(
        left, right, (((1,), (1,)), ((), ())), preferred_element_type=jnp.float32
    )


def contract_rows(left, right):
    return lax.dot_general(
        left, right, (((0,), (0,)), ((), ())), preferred_element_type=jnp.float32
    )


def swap(x, axis, bit):
    return lax.ppermute(x, axis, [(k, k ^ bit) for k in range(lax.axis_size(axis))])


def gather_bits(n):
    return [1 << k for k in reversed(range(n.bit_length() - 1))]


def scatter_bits(n):
    return [1 << k for k in range(n.bit_length() - 1)]


def gathered(x, axis):
    for bit in gather_bits(lax.axis_size(axis)):
        x = jnp.concatenate([x, swap(x, axis, bit)], axis=0)
    return x


def pieces(x):
    high = lax.reduce_precision(x, 8, 7)
    mid = lax.reduce_precision(x - high, 8, 7)
    low = x - high - mid
    return [p.astype(jnp.bfloat16) for p in (high, mid, low)]


def packed(columns):
    parts = [p for c in columns for p in pieces(c)]
    rows = parts[0].shape[0]
    lane = lax.broadcasted_iota(jnp.int32, (rows, LANES), 1)
    out = jnp.zeros((rows, LANES), jnp.bfloat16)
    for k, part in enumerate(parts):
        out = jnp.where(lane == k, part, out)
    return out


def unpacked(block, count):
    f = block.astype(jnp.float32)
    return [
        f[:, 3 * k : 3 * k + 1] + f[:, 3 * k + 1 : 3 * k + 2] + f[:, 3 * k + 2 : 3 * k + 3]
        for k in range(count)
    ]


def merge(mine, other, width):
    top_a, total_a = unpacked(mine[:, 2 * width :], 2)
    top_b, total_b = unpacked(other[:, 2 * width :], 2)
    top = jnp.maximum(top_a, top_b)
    scale_a, scale_b = jnp.exp(top_a - top), jnp.exp(top_b - top)
    a, b = mine.astype(jnp.float32), other.astype(jnp.float32)
    sums = a[:, :width] * scale_a + b[:, :width] * scale_b
    grads = a[:, width : 2 * width] + b[:, width : 2 * width]
    return sums, grads, top, total_a * scale_a + total_b * scale_b


def message(sums, grads, top, total):
    return jnp.concatenate(
        [sums.astype(jnp.bfloat16), grads.astype(jnp.bfloat16), packed([top, total])], axis=1
    )


def shards(tokens, slot_embed, expert_in, expert_out, out_grad):
    experts_here = expert_in.shape[0]
    width = tokens.shape[1]
    n_exp, n_seq = lax.axis_size("exp"), lax.axis_size("seq")
    own = slot_embed.shape[1]

    table = gathered(slot_embed.T, "exp")
    logits = contract_cols(table, tokens)
    top = jnp.max(logits, axis=1, keepdims=True)
    weight = jnp.exp(logits - top)
    total = jnp.sum(weight, axis=1, keepdims=True)
    combine = jax.nn.softmax(logits, axis=0)
    sums = jnp.dot(weight.astype(jnp.bfloat16), tokens, preferred_element_type=jnp.float32)
    grads = jnp.dot(combine.astype(jnp.bfloat16), out_grad, preferred_element_type=jnp.float32)

    state = (sums, grads, top, total)
    for bit in scatter_bits(n_exp):
        packet = message(*state)
        half = packet.shape[0] // 2
        state = merge(packet[:half], swap(packet[half:], "exp", bit), width)
    for bit in scatter_bits(n_seq):
        packet = message(*state)
        state = merge(packet, swap(packet, "seq", bit), width)
    sums, grads, top, total = state
    slot_sum = sums / total

    slot_in = slot_sum.astype(jnp.bfloat16).reshape(experts_here, -1, width)
    pre_act = jnp.einsum("esd,edh->esh", slot_in, expert_in, preferred_element_type=jnp.float32)
    hidden = jax.nn.gelu(pre_act, approximate=True).astype(jnp.bfloat16)
    out_part = jnp.einsum("esh,ehd->esd", hidden, expert_out, preferred_element_type=jnp.float32)
    grad_out = grads.astype(jnp.bfloat16).reshape(experts_here, -1, width)
    hid_grad = jnp.einsum("esd,ehd->esh", grad_out, expert_out, preferred_element_type=jnp.float32)
    _, pullback = jax.vjp(partial(jax.nn.gelu, approximate=True), pre_act)
    act_grad = pullback(hid_grad)[0].astype(jnp.bfloat16)
    in_part = jnp.einsum("esh,edh->esd", act_grad, expert_in, preferred_element_type=jnp.float32)

    both = jnp.concatenate([out_part.reshape(-1, width), in_part.reshape(-1, width)], axis=1)
    for bit in scatter_bits(n_seq):
        packet = both.astype(jnp.bfloat16)
        both = packet.astype(jnp.float32) + swap(packet, "seq", bit).astype(jnp.float32)
    both = both.astype(jnp.bfloat16)
    centre = jnp.sum(slot_sum * both[:, width:].astype(jnp.float32), axis=1, keepdims=True)
    packet = jnp.concatenate([both, packed([centre, top, total])], axis=1)
    packet = gathered(packet, "exp")
    slot_all, grad_all = packet[:, :width], packet[:, width : 2 * width]
    centre, top, total = unpacked(packet[:, 2 * width :], 3)

    comb_grad = contract_cols(slot_all, out_grad)
    disp_grad = contract_cols(grad_all, tokens)
    dispatch = jnp.exp(logits - top) / total
    comb_mean = jnp.sum(combine * comb_grad, axis=0, keepdims=True)
    logit_grad = dispatch * (disp_grad - centre) + combine * (comb_grad - comb_mean)
    logit_b = logit_grad.astype(jnp.bfloat16)

    part = jnp.dot(logit_b, tokens, preferred_element_type=jnp.float32)
    tok_grad = contract_rows(
        jnp.concatenate([dispatch.astype(jnp.bfloat16), logit_b], axis=0),
        jnp.concatenate([grad_all, table], axis=0),
    ).astype(jnp.bfloat16)

    part = part.astype(jnp.bfloat16)
    for bit in scatter_bits(n_exp):
        half = part.shape[0] // 2
        got = swap(part[half:], "exp", bit).astype(jnp.float32)
        part = (part[:half].astype(jnp.float32) + got).astype(jnp.bfloat16)
    me = lax.axis_index("seq")
    for bit in reversed(scatter_bits(n_seq)):
        half = part.shape[1] // 2
        upper = (me & bit) != 0
        low, high = part[:, :half], part[:, half:]
        got = swap(jnp.where(upper, low, high), "seq", bit).astype(jnp.float32)
        part = jnp.where(upper, high, low).astype(jnp.float32) + got
        if bit != 1:
            part = part.astype(jnp.bfloat16)
    return (tok_grad, part.T)


def solution(mesh):
    placed = (
        P(("seq", "exp"), None),
        P(None, "exp"),
        P("exp", None, "seq"),
        P("exp", "seq", None),
        P(("seq", "exp"), None),
    )
    return jax.shard_map(
        shards,
        mesh=mesh,
        in_specs=placed,
        out_specs=(P(("seq", "exp"), None), P("seq", "exp")),
        check_vma=False,
    )
```

time: 317 us -> 105 us (0.33)
  blocking collectives: 158 us -> 0 us
  waiting for transfers between devices: 113 us -> 42.1 us
  starting transfers between devices: 0.16 us -> 28.7 us
  between operations: 13.9 us -> 1.04 us
  other arithmetic: 1.03 us -> 7.29 us
  matrix products: 29.4 us -> 25.3 us
    reduce_scatter x4 -> x0, waiting for transfers between devices: 113 us -> none  [the longest x2 60.1 us: owner_sum(): lax.psum_scatter(partial_rows, 'exp', scatter_dimension=0, tiled=True)]
    psum x3 -> x0, blocking collectives: 72.7 us -> none  [the longest x1 37.5 us: shards(): centre = lax.psum(centre_local, ('seq', 'exp'))]
    all_gather x3 -> x0, blocking collectives: 44.7 us -> none  [the longest x1 16.2 us: shards(): slot_table = lax.all_gather(slot_embed, 'exp', axis=1, tiled=True)]
    ppermute x0 -> x18, waiting for transfers between devices: none -> 42.1 us  [swap(): lax.ppermute(x, axis, [(k, k ^ bit) for k in range(lax.axis_size(axis))])]
    unnamed x1 -> x0, blocking collectives: 40.4 us -> none
    ppermute x0 -> x18, starting transfers between devices: none -> 28.7 us  [swap(): lax.ppermute(x, axis, [(k, k ^ bit) for k in range(lax.axis_size(axis))])]
  transfers between devices with their start and end apart: 4 -> 18, of which waited for: 4 -> 18; matrix products, arithmetic and copies ran while one was open for 2% -> 2% of each run, Pallas kernels for 0% -> 0%
where the time goes in v1:
time: 105 us
  waiting for transfers between devices  42.1 us (40%)
  starting transfers between devices  28.7 us (27%)
  matrix products  25.3 us (24%)
  other arithmetic  7.29 us (7%)
    ppermute x18, waiting for transfers between devices, swap(): lax.ppermute(x, axis, [(k, k ^ bit) for k in range(lax.axis_size(axis))])  42.1 us
    ppermute x18, starting transfers between devices, swap(): lax.ppermute(x, axis, [(k, k ^ bit) for k in range(lax.axis_size(axis))])  28.7 us
    dot_general x1, matrix products, shards(): jnp.einsum('esh,edh->esd', act_grad, expert_in, preferred_element_type=jn...  10.3 us
    dot_general x1, matrix products, shards(): jnp.einsum('esh,ehd->esd', hidden, expert_out, preferred_element_type=jnp...  4.58 us
    dot_general x1, matrix products, shards(): jnp.einsum('esd,edh->esh', slot_in, expert_in, preferred_element_type=jnp...  4.57 us
    dot_general x3, matrix products, contract_cols(): lax.dot_general(left, right, (((1,), (1,)), ((), ())), preferred_element_...  2.23 us
  transfers between devices with their start and end apart: 18, of which 18 were waited for; matrix products, arithmetic and copies ran while one was open for 2% of the time, Pallas kernels for 0%

profile of v1, /device:TPU:0, one launch (start us, length us, event | category | flops | bytes accessed | tf_op | source)
XLA Modules:
  0.0 104.5 jit_solution(2007439191029203971)
XLA Ops:
  0.6 4.1 %collective-permute-start = (bf16[8,2048]{1,0:T(8,128)(2,1)}, bf16[8,2048]{1,0:T(8,128)(2,1)S(1)}, u32[]{:S(2)}, u32[]{:S(2)}) collective-permute-start(bf16[8,2048]{1,0:T(8,128)(2,1)} %bitcast.18), channel_id=1, source_target_pairs={{0,4},{1,5},{2,6},{3,7},{4,0},{5,1},{6,2},{7,3},{8,12},{9,13},{10,... | collective-permute-start | bytes 98312 | tf_op jit(solution)/shard_map/ppermute | solution.py:24
  4.7 2.5 %collective-permute-done = bf16[8,2048]{1,0:T(8,128)(2,1)S(1)} collective-permute-done((bf16[8,2048]{1,0:T(8,128)(2,1)}, bf16[8,2048]{1,0:T(8,128)(2,1)S(1)}, u32[]{:S(2)}, u32[]{:S(2)}) %collective-permute-start) | collective-permute-done | bytes 32800 | tf_op jit(solution)/shard_map/ppermute | solution.py:24
  8.0 1.6 %collective-permute-start.1 = (bf16[16,2048]{1,0:T(8,128)(2,1)S(1)}, bf16[16,2048]{1,0:T(8,128)(2,1)S(1)}, u32[]{:S(2)}, u32[]{:S(2)}) collective-permute-start(bf16[16,2048]{1,0:T(8,128)(2,1)S(1)} %pad_maximum_fusion.18), channel_id=1, source_target_pairs={{0,2},{1,3},{2,0},{3,1},{4,6},{5,7},{6,4},{7,5},{8,10},{9,11},{10,... | collective-permute-start | bytes 196616 | tf_op jit(solution)/shard_map/ppermute | solution.py:24
  9.5 2.7 %collective-permute-done.1 = bf16[16,2048]{1,0:T(8,128)(2,1)S(1)} collective-permute-done((bf16[16,2048]{1,0:T(8,128)(2,1)S(1)}, bf16[16,2048]{1,0:T(8,128)(2,1)S(1)}, u32[]{:S(2)}, u32[]{:S(2)}) %collective-permute-start.1) | collective-permute-done | bytes 65568 | tf_op jit(solution)/shard_map/ppermute | solution.py:24
  16.3 1.5 %convolution_convert_fusion.2 = bf16[64,2048]{1,0:T(8,128)(2,1)S(1)} fusion(bf16[256,2048]{1,0:T(8,128)(2,1)} %param.9, f32[64,256]{1,0:T(8,128)S(1)} %get-tuple-element.96, f32[256]{0:T(256)S(1)} %get-tuple-element.2, f32[256]{0:T(256)S(1)} %get-tuple-element.4), kind=kOutput, calls=%fused_computation.2 | convolution fusion | flops 67289088 | bytes 1378304 | tf_op jit(solution)/shard_map/dot_general | solution.py:96
  20.6 1.6 %collective-permute-start.4 = (bf16[16,4224]{1,0:T(8,128)(2,1)S(1)}, bf16[16,4224]{1,0:T(8,128)(2,1)S(1)}, u32[]{:S(2)}, u32[]{:S(2)}) collective-permute-start(bf16[16,4224]{1,0:T(8,128)(2,1)S(1)} %get-tuple-element.78), channel_id=1, source_target_pairs={{0,2},{1,3},{2,0},{3,1},{4,6},{5,7},{6,4},{7,5},{8,10},{9,11},{10,... | collective-permute-start | bytes 405512 | tf_op jit(solution)/shard_map/ppermute | solution.py:24
  22.2 4.1 %collective-permute-done.4 = bf16[16,4224]{1,0:T(8,128)(2,1)S(1)} collective-permute-done((bf16[16,4224]{1,0:T(8,128)(2,1)S(1)}, bf16[16,4224]{1,0:T(8,128)(2,1)S(1)}, u32[]{:S(2)}, u32[]{:S(2)}) %collective-permute-start.4) | collective-permute-done | bytes 135200 | tf_op jit(solution)/shard_map/ppermute | solution.py:24
  27.2 2.7 %collective-permute-start.5 = (bf16[8,4224]{1,0:T(8,128)(2,1)S(1)}, bf16[8,4224]{1,0:T(8,128)(2,1)S(1)}, u32[]{:S(2)}, u32[]{:S(2)}) collective-permute-start(bf16[8,4224]{1,0:T(8,128)(2,1)S(1)} %get-tuple-element.80), channel_id=1, source_target_pairs={{0,4},{1,5},{2,6},{3,7},{4,0},{5,1},{6,2},{7,3},{8,12},{9,13},{10,... | collective-permute-start | bytes 202760 | tf_op jit(solution)/shard_map/ppermute | solution.py:24
  29.9 2.8 %collective-permute-done.5 = bf16[8,4224]{1,0:T(8,128)(2,1)S(1)} collective-permute-done((bf16[8,4224]{1,0:T(8,128)(2,1)S(1)}, bf16[8,4224]{1,0:T(8,128)(2,1)S(1)}, u32[]{:S(2)}, u32[]{:S(2)}) %collective-permute-start.5) | collective-permute-done | bytes 67616 | tf_op jit(solution)/shard_map/ppermute | solution.py:24
  33.5 1.6 %collective-permute-start.6 = (bf16[8,4224]{1,0:T(8,128)(2,1)S(1)}, bf16[8,4224]{1,0:T(8,128)(2,1)S(1)}, u32[]{:S(2)}, u32[]{:S(2)}) collective-permute-start(bf16[8,4224]{1,0:T(8,128)(2,1)S(1)} %get-tuple-element.84), channel_id=1, source_target_pairs={{0,8},{8,0},{16,24},{24,16},{1,9},{9,1},{17,25},{25,17},{2,10},{10... | collective-permute-start | bytes 202760 | tf_op jit(solution)/shard_map/ppermute | solution.py:24
  35.0 2.8 %collective-permute-done.6 = bf16[8,4224]{1,0:T(8,128)(2,1)S(1)} collective-permute-done((bf16[8,4224]{1,0:T(8,128)(2,1)S(1)}, bf16[8,4224]{1,0:T(8,128)(2,1)S(1)}, u32[]{:S(2)}, u32[]{:S(2)}) %collective-permute-start.6) | collective-permute-done | bytes 67616 | tf_op jit(solution)/shard_map/ppermute | solution.py:24
  38.6 1.6 %collective-permute-start.7 = (bf16[8,4224]{1,0:T(8,128)(2,1)S(1)}, bf16[8,4224]{1,0:T(8,128)(2,1)S(1)}, u32[]{:S(2)}, u32[]{:S(2)}) collective-permute-start(bf16[8,4224]{1,0:T(8,128)(2,1)S(1)} %get-tuple-element.82), channel_id=1, source_target_pairs={{0,16},{8,24},{16,0},{24,8},{1,17},{9,25},{17,1},{25,9},{2,18},{10... | collective-permute-start | bytes 202760 | tf_op jit(solution)/shard_map/ppermute | solution.py:24
  40.2 2.8 %collective-permute-done.7 = bf16[8,4224]{1,0:T(8,128)(2,1)S(1)} collective-permute-done((bf16[8,4224]{1,0:T(8,128)(2,1)S(1)}, bf16[8,4224]{1,0:T(8,128)(2,1)S(1)}, u32[]{:S(2)}, u32[]{:S(2)}) %collective-permute-start.7) | collective-permute-done | bytes 67616 | tf_op jit(solution)/shard_map/ppermute | solution.py:24
  43.6 4.6 %fusion.143 = f32[2,4,1024]{2,1,0:T(4,128)S(1)} fusion(bf16[2,4,2048]{2,1,0:T(4,128)(2,1)S(1)} %reshape.82, bf16[2,2048,1024]{2,1,0:T(8,128)(2,1)} %param.7), kind=kOutput, calls=%fused_computation.317 | convolution fusion | flops 33554432 | bytes 8454144 | tf_op jit(solution)/shard_map/esd,edh->esh/dot_general | solution.py:110
  48.2 4.6 %convolution_convert_fusion.5 = bf16[2,4,2048]{2,1,0:T(4,128)(2,1)S(1)} fusion(bf16[2,1024,2048]{2,1,0:T(8,128)(2,1)} %param.8, f32[2,4,1024]{2,1,0:T(4,128)S(1)} %fusion.143), kind=kOutput, calls=%fused_computation.5 | convolution fusion | flops 33644544 | bytes 8454144 | tf_op jit(solution)/shard_map/esh,ehd->esd/dot_general | solution.py:112
  52.8 10.3 %convolution_convert_fusion.4 = bf16[2,4,2048]{2,1,0:T(4,128)(2,1)S(1)} fusion(bf16[2,2048,1024]{2,1,0:T(8,128)(2,1)} %param.7, f32[2,4,1024]{2,1,0:T(4,128)S(1)} %fusion.143, bf16[2,4,2048]{2,1,0:T(4,128)(2,1)S(1)} %reshape.84, bf16[2,1024,2048]{2,1,0:T(8,128)(2,1)} %param.8), kind=kOutput, calls=%fused_computation.4 | convolution fusion | flops 67289088 | bytes 16875520 | tf_op jit(solution)/shard_map/esh,edh->esd/dot_general | solution.py:117
  63.2 1.6 %collective-permute-start.8 = (bf16[8,4096]{1,0:T(8,128)(2,1)S(1)}, bf16[8,4096]{1,0:T(8,128)(2,1)S(1)}, u32[]{:S(2)}, u32[]{:S(2)}) collective-permute-start(bf16[8,4096]{1,0:T(8,128)(2,1)S(1)} %constant_dynamic-update-slice_fusion), channel_id=1, source_target_pairs={{0,8},{8,0},{16,24},{24,16},{1,9},{9,1},{17,25},{25,17},{2,10},{10... | collective-permute-start | bytes 196616 | tf_op jit(solution)/shard_map/ppermute | solution.py:24
  64.7 2.8 %collective-permute-done.8 = bf16[8,4096]{1,0:T(8,128)(2,1)S(1)} collective-permute-done((bf16[8,4096]{1,0:T(8,128)(2,1)S(1)}, bf16[8,4096]{1,0:T(8,128)(2,1)S(1)}, u32[]{:S(2)}, u32[]{:S(2)}) %collective-permute-start.8) | collective-permute-done | bytes 65568 | tf_op jit(solution)/shard_map/ppermute | solution.py:24
  67.5 1.6 %collective-permute-start.9 = (bf16[8,4096]{1,0:T(8,128)(2,1)S(1)}, bf16[8,4096]{1,0:T(8,128)(2,1)S(1)}, u32[]{:S(2)}, u32[]{:S(2)}) collective-permute-start(bf16[8,4096]{1,0:T(8,128)(2,1)S(1)} %add_convert_fusion.3), channel_id=1, source_target_pairs={{0,16},{8,24},{16,0},{24,8},{1,17},{9,25},{17,1},{25,9},{2,18},{10... | collective-permute-start | bytes 196616 | tf_op jit(solution)/shard_map/ppermute | solution.py:24
  69.3 2.6 %collective-permute-done.9 = bf16[8,4096]{1,0:T(8,128)(2,1)S(1)} collective-permute-done((bf16[8,4096]{1,0:T(8,128)(2,1)S(1)}, bf16[8,4096]{1,0:T(8,128)(2,1)S(1)}, u32[]{:S(2)}, u32[]{:S(2)}) %collective-permute-start.9) | collective-permute-done | bytes 65568 | tf_op jit(solution)/shard_map/ppermute | solution.py:24
  72.1 2.5 %collective-permute-start.10 = (bf16[8,4224]{1,0:T(8,128)(2,1)S(1)}, bf16[8,4224]{1,0:T(8,128)(2,1)S(1)}, u32[]{:S(2)}, u32[]{:S(2)}) collective-permute-start(bf16[8,4224]{1,0:T(8,128)(2,1)S(1)} %pad_maximum_fusion.17), channel_id=1, source_target_pairs={{0,4},{1,5},{2,6},{3,7},{4,0},{5,1},{6,2},{7,3},{8,12},{9,13},{10,... | collective-permute-start | bytes 202760 | tf_op jit(solution)/shard_map/ppermute | solution.py:24
  74.6 2.8 %collective-permute-done.10 = bf16[8,4224]{1,0:T(8,128)(2,1)S(1)} collective-permute-done((bf16[8,4224]{1,0:T(8,128)(2,1)S(1)}, bf16[8,4224]{1,0:T(8,128)(2,1)S(1)}, u32[]{:S(2)}, u32[]{:S(2)}) %collective-permute-start.10) | collective-permute-done | bytes 67616 | tf_op jit(solution)/shard_map/ppermute | solution.py:24
  77.4 1.7 %collective-permute-start.11 = (bf16[16,4224]{1,0:T(8,128)(2,1)S(1)}, bf16[16,4224]{1,0:T(8,128)(2,1)S(1)}, u32[]{:S(2)}, u32[]{:S(2)}) collective-permute-start(bf16[16,4224]{1,0:T(8,128)(2,1)S(1)} %pad_maximum_fusion.13), channel_id=1, source_target_pairs={{0,2},{1,3},{2,0},{3,1},{4,6},{5,7},{6,4},{7,5},{8,10},{9,11},{10,... | collective-permute-start | bytes 405512 | tf_op jit(solution)/shard_map/ppermute | solution.py:24
  79.1 3.4 %collective-permute-done.11 = bf16[16,4224]{1,0:T(8,128)(2,1)S(1)} collective-permute-done((bf16[16,4224]{1,0:T(8,128)(2,1)S(1)}, bf16[16,4224]{1,0:T(8,128)(2,1)S(1)}, u32[]{:S(2)}, u32[]{:S(2)}) %collective-permute-start.11) | collective-permute-done | bytes 135200 | tf_op jit(solution)/shard_map/ppermute | solution.py:24
  82.6 1.5 %collective-permute-done.12 = bf16[32,4224]{1,0:T(8,128)(2,1)S(1)} collective-permute-done((bf16[32,4224]{1,0:T(8,128)(2,1)S(1)}, bf16[32,4224]{1,0:T(8,128)(2,1)S(1)}, u32[]{:S(2)}, u32[]{:S(2)}) %collective-permute-start.12) | collective-permute-done | bytes 270368 | tf_op jit(solution)/shard_map/ppermute | solution.py:24
  87.1 1.7 %collective-permute-start.14 = (bf16[16,2048]{1,0:T(8,128)(2,1)S(1)}, bf16[16,2048]{1,0:T(8,128)(2,1)S(1)}, u32[]{:S(2)}, u32[]{:S(2)}) collective-permute-start(bf16[16,2048]{1,0:T(8,128)(2,1)S(1)} %slice.545), channel_id=1, source_target_pairs={{0,2},{1,3},{2,0},{3,1},{4,6},{5,7},{6,4},{7,5},{8,10},{9,11},{10,... | collective-permute-start | bytes 196616 | tf_op jit(solution)/shard_map/ppermute | solution.py:24
  88.8 2.6 %collective-permute-done.14 = bf16[16,2048]{1,0:T(8,128)(2,1)S(1)} collective-permute-done((bf16[16,2048]{1,0:T(8,128)(2,1)S(1)}, bf16[16,2048]{1,0:T(8,128)(2,1)S(1)}, u32[]{:S(2)}, u32[]{:S(2)}) %collective-permute-start.14) | collective-permute-done | bytes 65568 | tf_op jit(solution)/shard_map/ppermute | solution.py:24
  91.5 2.8 %collective-permute-start.15 = (bf16[8,2048]{1,0:T(8,128)(2,1)S(1)}, bf16[8,2048]{1,0:T(8,128)(2,1)S(1)}, u32[]{:S(2)}, u32[]{:S(2)}) collective-permute-start(bf16[8,2048]{1,0:T(8,128)(2,1)S(1)} %slice.547), channel_id=1, source_target_pairs={{0,4},{1,5},{2,6},{3,7},{4,0},{5,1},{6,2},{7,3},{8,12},{9,13},{10,... | collective-permute-start | bytes 98312 | tf_op jit(solution)/shard_map/ppermute | solution.py:24
  94.3 2.0 %collective-permute-done.15 = bf16[8,2048]{1,0:T(8,128)(2,1)S(1)} collective-permute-done((bf16[8,2048]{1,0:T(8,128)(2,1)S(1)}, bf16[8,2048]{1,0:T(8,128)(2,1)S(1)}, u32[]{:S(2)}, u32[]{:S(2)}) %collective-permute-start.15) | collective-permute-done | bytes 32800 | tf_op jit(solution)/shard_map/ppermute | solution.py:24
  96.4 1.6 %collective-permute-start.16 = (bf16[8,1024]{1,0:T(8,128)(2,1)S(1)}, bf16[8,1024]{1,0:T(8,128)(2,1)S(1)}, u32[]{:S(2)}, u32[]{:S(2)}) collective-permute-start(bf16[8,1024]{1,0:T(8,128)(2,1)S(1)} %broadcast_select_fusion), channel_id=1, source_target_pairs={{0,16},{8,24},{16,0},{24,8},{1,17},{9,25},{17,1},{25,9},{2,18},{10... | collective-permute-start | bytes 49160 | tf_op jit(solution)/shard_map/ppermute | solution.py:24
  98.0 2.2 %collective-permute-done.16 = bf16[8,1024]{1,0:T(8,128)(2,1)S(1)} collective-permute-done((bf16[8,1024]{1,0:T(8,128)(2,1)S(1)}, bf16[8,1024]{1,0:T(8,128)(2,1)S(1)}, u32[]{:S(2)}, u32[]{:S(2)}) %collective-permute-start.16) | collective-permute-done | bytes 16416 | tf_op jit(solution)/shard_map/ppermute | solution.py:24
  100.2 1.6 %collective-permute-start.17 = (bf16[8,512]{1,0:T(8,128)(2,1)S(1)}, bf16[8,512]{1,0:T(8,128)(2,1)S(1)}, u32[]{:S(2)}, u32[]{:S(2)}) collective-permute-start(bf16[8,512]{1,0:T(8,128)(2,1)S(1)} %broadcast_select_fusion.1), channel_id=1, source_target_pairs={{0,8},{8,0},{16,24},{24,16},{1,9},{9,1},{17,25},{25,17},{2,10},{10... | collective-permute-start | bytes 24584 | tf_op jit(solution)/shard_map/ppermute | solution.py:24
  (107 shorter events, 16.9 us)
Async XLA Ops:
  0.6 13.8 %copy-start = (bf16[256,2048]{1,0:T(8,128)(2,1)S(1)}, bf16[256,2048]{1,0:T(8,128)(2,1)}, u32[]{:S(2)}) copy-start(bf16[256,2048]{1,0:T(8,128)(2,1)} %param.5) | copy-start | bytes 3145732
  0.6 6.6 %collective-permute-start = (bf16[8,2048]{1,0:T(8,128)(2,1)}, bf16[8,2048]{1,0:T(8,128)(2,1)S(1)}, u32[]{:S(2)}, u32[]{:S(2)}) collective-permute-start(bf16[8,2048]{1,0:T(8,128)(2,1)} %bitcast.18), channel_id=1, source_target_pairs={{0,4},{1,5},{2,6},{3,7},{4,0},{5,1},{6,2},{7,3},{8,12},{9,13},{10,... | collective-permute-start | bytes 98312 | tf_op jit(solution)/shard_map/ppermute | solution.py:24
  8.0 4.3 %collective-permute-start.1 = (bf16[16,2048]{1,0:T(8,128)(2,1)S(1)}, bf16[16,2048]{1,0:T(8,128)(2,1)S(1)}, u32[]{:S(2)}, u32[]{:S(2)}) collective-permute-start(bf16[16,2048]{1,0:T(8,128)(2,1)S(1)} %pad_maximum_fusion.18), channel_id=1, source_target_pairs={{0,2},{1,3},{2,0},{3,1},{4,6},{5,7},{6,4},{7,5},{8,10},{9,11},{10,... | collective-permute-start | bytes 196616 | tf_op jit(solution)/shard_map/ppermute | solution.py:24
  13.0 1.4 %collective-permute-start.2 = (bf16[32,2048]{1,0:T(8,128)(2,1)S(1)}, bf16[32,2048]{1,0:T(8,128)(2,1)S(1)}, u32[]{:S(2)}, u32[]{:S(2)}) collective-permute-start(bf16[32,2048]{1,0:T(8,128)(2,1)S(1)} %pad_maximum_fusion.14), channel_id=1, source_target_pairs={{0,1},{1,0},{2,3},{3,2},{4,5},{5,4},{6,7},{7,6},{8,9},{9,8},{10,11... | collective-permute-start | bytes 393224 | tf_op jit(solution)/shard_map/ppermute | solution.py:24
  18.1 1.6 %collective-permute-start.3 = (bf16[32,4224]{1,0:T(8,128)(2,1)S(1)}, bf16[32,4224]{1,0:T(8,128)(2,1)S(1)}, u32[]{:S(2)}, u32[]{:S(2)}) collective-permute-start(bf16[32,4224]{1,0:T(8,128)(2,1)S(1)} %get-tuple-element.71), channel_id=1, source_target_pairs={{0,1},{1,0},{2,3},{3,2},{4,5},{5,4},{6,7},{7,6},{8,9},{9,8},{10,11... | collective-permute-start | bytes 811016 | tf_op jit(solution)/shard_map/ppermute | solution.py:24
  20.6 5.7 %collective-permute-start.4 = (bf16[16,4224]{1,0:T(8,128)(2,1)S(1)}, bf16[16,4224]{1,0:T(8,128)(2,1)S(1)}, u32[]{:S(2)}, u32[]{:S(2)}) collective-permute-start(bf16[16,4224]{1,0:T(8,128)(2,1)S(1)} %get-tuple-element.78), channel_id=1, source_target_pairs={{0,2},{1,3},{2,0},{3,1},{4,6},{5,7},{6,4},{7,5},{8,10},{9,11},{10,... | collective-permute-start | bytes 405512 | tf_op jit(solution)/shard_map/ppermute | solution.py:24
  27.2 5.5 %collective-permute-start.5 = (bf16[8,4224]{1,0:T(8,128)(2,1)S(1)}, bf16[8,4224]{1,0:T(8,128)(2,1)S(1)}, u32[]{:S(2)}, u32[]{:S(2)}) collective-permute-start(bf16[8,4224]{1,0:T(8,128)(2,1)S(1)} %get-tuple-element.80), channel_id=1, source_target_pairs={{0,4},{1,5},{2,6},{3,7},{4,0},{5,1},{6,2},{7,3},{8,12},{9,13},{10,... | collective-permute-start | bytes 202760 | tf_op jit(solution)/shard_map/ppermute | solution.py:24
  33.5 4.4 %collective-permute-start.6 = (bf16[8,4224]{1,0:T(8,128)(2,1)S(1)}, bf16[8,4224]{1,0:T(8,128)(2,1)S(1)}, u32[]{:S(2)}, u32[]{:S(2)}) collective-permute-start(bf16[8,4224]{1,0:T(8,128)(2,1)S(1)} %get-tuple-element.84), channel_id=1, source_target_pairs={{0,8},{8,0},{16,24},{24,16},{1,9},{9,1},{17,25},{25,17},{2,10},{10... | collective-permute-start | bytes 202760 | tf_op jit(solution)/shard_map/ppermute | solution.py:24
  38.6 4.4 %collective-permute-start.7 = (bf16[8,4224]{1,0:T(8,128)(2,1)S(1)}, bf16[8,4224]{1,0:T(8,128)(2,1)S(1)}, u32[]{:S(2)}, u32[]{:S(2)}) collective-permute-start(bf16[8,4224]{1,0:T(8,128)(2,1)S(1)} %get-tuple-element.82), channel_id=1, source_target_pairs={{0,16},{8,24},{16,0},{24,8},{1,17},{9,25},{17,1},{25,9},{2,18},{10... | collective-permute-start | bytes 202760 | tf_op jit(solution)/shard_map/ppermute | solution.py:24
  52.8 31.5 %copy-start.1 = (bf16[256,2048]{1,0:T(8,128)(2,1)S(1)}, bf16[256,2048]{1,0:T(8,128)(2,1)}, u32[]{:S(2)}) copy-start(bf16[256,2048]{1,0:T(8,128)(2,1)} %param.9) | copy-start | bytes 3145732
  63.1 22.7 %copy-start.2 = (bf16[2048,8]{0,1:T(8,128)(2,1)S(1)}, bf16[2048,8]{0,1:T(8,128)(2,1)}, u32[]{:S(2)}) copy-start(bf16[2048,8]{0,1:T(8,128)(2,1)} %param.6) | copy-start | bytes 98308
  63.2 4.3 %collective-permute-start.8 = (bf16[8,4096]{1,0:T(8,128)(2,1)S(1)}, bf16[8,4096]{1,0:T(8,128)(2,1)S(1)}, u32[]{:S(2)}, u32[]{:S(2)}) collective-permute-start(bf16[8,4096]{1,0:T(8,128)(2,1)S(1)} %constant_dynamic-update-slice_fusion), channel_id=1, source_target_pairs={{0,8},{8,0},{16,24},{24,16},{1,9},{9,1},{17,25},{25,17},{2,10},{10... | collective-permute-start | bytes 196616 | tf_op jit(solution)/shard_map/ppermute | solution.py:24
  67.5 4.3 %collective-permute-start.9 = (bf16[8,4096]{1,0:T(8,128)(2,1)S(1)}, bf16[8,4096]{1,0:T(8,128)(2,1)S(1)}, u32[]{:S(2)}, u32[]{:S(2)}) collective-permute-start(bf16[8,4096]{1,0:T(8,128)(2,1)S(1)} %add_convert_fusion.3), channel_id=1, source_target_pairs={{0,16},{8,24},{16,0},{24,8},{1,17},{9,25},{17,1},{25,9},{2,18},{10... | collective-permute-start | bytes 196616 | tf_op jit(solution)/shard_map/ppermute | solution.py:24
  72.1 5.3 %collective-permute-start.10 = (bf16[8,4224]{1,0:T(8,128)(2,1)S(1)}, bf16[8,4224]{1,0:T(8,128)(2,1)S(1)}, u32[]{:S(2)}, u32[]{:S(2)}) collective-permute-start(bf16[8,4224]{1,0:T(8,128)(2,1)S(1)} %pad_maximum_fusion.17), channel_id=1, source_target_pairs={{0,4},{1,5},{2,6},{3,7},{4,0},{5,1},{6,2},{7,3},{8,12},{9,13},{10,... | collective-permute-start | bytes 202760 | tf_op jit(solution)/shard_map/ppermute | solution.py:24
  77.4 5.1 %collective-permute-start.11 = (bf16[16,4224]{1,0:T(8,128)(2,1)S(1)}, bf16[16,4224]{1,0:T(8,128)(2,1)S(1)}, u32[]{:S(2)}, u32[]{:S(2)}) collective-permute-start(bf16[16,4224]{1,0:T(8,128)(2,1)S(1)} %pad_maximum_fusion.13), channel_id=1, source_target_pairs={{0,2},{1,3},{2,0},{3,1},{4,6},{5,7},{6,4},{7,5},{8,10},{9,11},{10,... | collective-permute-start | bytes 405512 | tf_op jit(solution)/shard_map/ppermute | solution.py:24
  82.5 1.6 %collective-permute-start.12 = (bf16[32,4224]{1,0:T(8,128)(2,1)S(1)}, bf16[32,4224]{1,0:T(8,128)(2,1)S(1)}, u32[]{:S(2)}, u32[]{:S(2)}) collective-permute-start(bf16[32,4224]{1,0:T(8,128)(2,1)S(1)} %pad_maximum_fusion.2), channel_id=1, source_target_pairs={{0,1},{1,0},{2,3},{3,2},{4,5},{5,4},{6,7},{7,6},{8,9},{9,8},{10,11... | collective-permute-start | bytes 811016 | tf_op jit(solution)/shard_map/ppermute | solution.py:24
  85.6 1.4 %collective-permute-start.13 = (bf16[32,2048]{1,0:T(8,128)(2,1)S(1)}, bf16[32,2048]{1,0:T(8,128)(2,1)S(1)}, u32[]{:S(2)}, u32[]{:S(2)}) collective-permute-start(bf16[32,2048]{1,0:T(8,128)(2,1)S(1)} %slice.543), channel_id=1, source_target_pairs={{0,1},{1,0},{2,3},{3,2},{4,5},{5,4},{6,7},{7,6},{8,9},{9,8},{10,11... | collective-permute-start | bytes 393224 | tf_op jit(solution)/shard_map/ppermute | solution.py:24
  87.1 4.3 %collective-permute-start.14 = (bf16[16,2048]{1,0:T(8,128)(2,1)S(1)}, bf16[16,2048]{1,0:T(8,128)(2,1)S(1)}, u32[]{:S(2)}, u32[]{:S(2)}) collective-permute-start(bf16[16,2048]{1,0:T(8,128)(2,1)S(1)} %slice.545), channel_id=1, source_target_pairs={{0,2},{1,3},{2,0},{3,1},{4,6},{5,7},{6,4},{7,5},{8,10},{9,11},{10,... | collective-permute-start | bytes 196616 | tf_op jit(solution)/shard_map/ppermute | solution.py:24
  91.5 4.9 %collective-permute-start.15 = (bf16[8,2048]{1,0:T(8,128)(2,1)S(1)}, bf16[8,2048]{1,0:T(8,128)(2,1)S(1)}, u32[]{:S(2)}, u32[]{:S(2)}) collective-permute-start(bf16[8,2048]{1,0:T(8,128)(2,1)S(1)} %slice.547), channel_id=1, source_target_pairs={{0,4},{1,5},{2,6},{3,7},{4,0},{5,1},{6,2},{7,3},{8,12},{9,13},{10,... | collective-permute-start | bytes 98312 | tf_op jit(solution)/shard_map/ppermute | solution.py:24
  96.4 3.8 %collective-permute-start.16 = (bf16[8,1024]{1,0:T(8,128)(2,1)S(1)}, bf16[8,1024]{1,0:T(8,128)(2,1)S(1)}, u32[]{:S(2)}, u32[]{:S(2)}) collective-permute-start(bf16[8,1024]{1,0:T(8,128)(2,1)S(1)} %broadcast_select_fusion), channel_id=1, source_target_pairs={{0,16},{8,24},{16,0},{24,8},{1,17},{9,25},{17,1},{25,9},{2,18},{10... | collective-permute-start | bytes 49160 | tf_op jit(solution)/shard_map/ppermute | solution.py:24
  100.2 3.7 %collective-permute-start.17 = (bf16[8,512]{1,0:T(8,128)(2,1)S(1)}, bf16[8,512]{1,0:T(8,128)(2,1)S(1)}, u32[]{:S(2)}, u32[]{:S(2)}) collective-permute-start(bf16[8,512]{1,0:T(8,128)(2,1)S(1)} %broadcast_select_fusion.1), channel_id=1, source_target_pairs={{0,8},{8,0},{16,24},{24,16},{1,9},{9,1},{17,25},{25,17},{2,10},{10... | collective-permute-start | bytes 24584 | tf_op jit(solution)/shard_map/ppermute | solution.py:24

commit v2 on v0

v2 whole, which is shorter than its diff:
```python
from functools import partial
import math

import jax
import jax.numpy as jnp
from jax import lax
from jax.experimental import pallas as pl
from jax.experimental.pallas import tpu as pltpu
from jax.sharding import PartitionSpec as P

LANES = 128
F32 = jnp.float32
BF16 = jnp.bfloat16
MIB = 1 << 20


def swap(x, axis, mask):
    return lax.ppermute(x, axis, [(k, k ^ mask) for k in range(lax.axis_size(axis))])


def swaps(parts, axis, masks):
    return [swap(x, axis, mask) for x, mask in zip(parts, masks)]


def groups(n, first):
    bits = [1 << k for k in range(n.bit_length() - 1) if 1 << k >= first]
    return [
        [b for b in (pair[0], *pair[1:], sum(pair)) if b]
        if len(pair) == 2
        else [pair[0]]
        for pair in (bits[k : k + 2] for k in range(0, len(bits), 2))
    ]


def in_vmem(x):
    return pltpu.with_memory_space_constraint(x, pltpu.VMEM)


def local_call(body, outs, *operands, limit=8, to_hbm=()):
    return pl.pallas_call(
        body,
        out_shape=tuple(
            jax.ShapeDtypeStruct(s, d) if k in to_hbm else pltpu.VMEM(s, d)
            for k, (s, d) in enumerate(outs)
        ),
        in_specs=[pl.BlockSpec(memory_space=pltpu.VMEM)] * len(operands),
        out_specs=tuple(pl.BlockSpec(memory_space=pltpu.VMEM) for _ in outs),
        compiler_params=pltpu.CompilerParams(vmem_limit_bytes=limit * MIB),
    )(*[in_vmem(x) for x in operands])


def product(left, right, over_left, over_right):
    return lax.dot_general(
        left, right, (((over_left,), (over_right,)), ((), ())), preferred_element_type=F32
    )


def rounded(x):
    return x.astype(BF16).astype(F32)


def packed(columns, rows):
    lane = lax.broadcasted_iota(jnp.int32, (rows, LANES), 1)
    out = jnp.zeros((rows, LANES), F32)
    for k, x in enumerate(columns):
        high = rounded(x)
        mid = rounded(x - high)
        for j, piece in enumerate((high, mid, x - high - mid)):
            out = jnp.where(lane == 3 * k + j, piece, out)
    return out


def unpacked(block, count):
    lane = lax.broadcasted_iota(jnp.int32, block.shape, 1)
    return [
        jnp.sum(
            jnp.where((lane >= 3 * k) & (lane < 3 * k + 3), block, 0.0), axis=1, keepdims=True
        )
        for k in range(count)
    ]


def concat_kernel(*refs):
    out = refs[-1]
    out[...] = jnp.concatenate([r[...].astype(F32) for r in refs[:-1]], axis=0).astype(BF16)


def stack(parts):
    if len(parts) == 1:
        return parts[0]
    rows = sum(p.shape[0] for p in parts)
    return local_call(concat_kernel, [((rows, parts[0].shape[1]), BF16)], *parts)[0]


def softmax_columns(logits):
    weight = jnp.exp(logits - jnp.max(logits, axis=0, keepdims=True))
    return weight / jnp.sum(weight, axis=0, keepdims=True)


def first_kernel(near, far, tokens, out_grad, logits_out, keep, send):
    width = tokens.shape[1]
    half = near.shape[0]
    logits = jnp.concatenate(
        [product(near[...], tokens[...], 1, 1), product(far[...], tokens[...], 1, 1)], axis=0
    )
    logits_out[...] = logits
    top = jnp.max(logits, axis=1, keepdims=True)
    weight = jnp.exp(logits - top)
    stats = packed([top, jnp.sum(weight, axis=1, keepdims=True)], 2 * half).astype(BF16)
    sums = product(weight.astype(BF16), tokens[...], 1, 0).astype(BF16)
    grads = product(softmax_columns(logits).astype(BF16), out_grad[...], 1, 0).astype(BF16)
    for k, out in enumerate((keep, send)):
        rows = slice(k * half, (k + 1) * half)
        out[:, :width] = sums[rows]
        out[:, width : 2 * width] = grads[rows]
        out[:, 2 * width :] = stats[rows]


def merged(refs, width):
    stats = [unpacked(r[:, 2 * width :].astype(F32), 2) for r in refs]
    top = stats[0][0]
    for other, _ in stats[1:]:
        top = jnp.maximum(top, other)
    scales = [jnp.exp(t - top) for t, _ in stats]
    total = sum(s * l for s, (_, l) in zip(scales, stats))
    sums = sum(s * r[:, :width].astype(F32) for s, r in zip(scales, refs))
    grads = sum(r[:, width : 2 * width].astype(F32) for r in refs)
    return sums, grads, top, total


def merge_kernel(count, width, *refs):
    sums, grads, top, total = merged(refs[:count], width)
    outs = refs[count:]
    rows = outs[0].shape[0]
    stats = packed([top, total], sums.shape[0])
    for k, out in enumerate(outs):
        part = slice(k * rows, (k + 1) * rows)
        out[:, :width] = sums[part].astype(BF16)
        out[:, width : 2 * width] = grads[part].astype(BF16)
        out[:, 2 * width :] = stats[part].astype(BF16)


def merge(parts, width, pieces):
    rows, columns = parts[0].shape
    return local_call(
        partial(merge_kernel, len(parts), width),
        [((rows // pieces, columns), BF16)] * pieces,
        *parts,
    )


def gelu_and_slope(v):
    root = math.sqrt(2.0 / math.pi)
    t = jnp.tanh(root * (v + 0.044715 * (v * v * v)))
    slope = 0.5 * (1.0 + t) + 0.5 * v * (1.0 - t * t) * (root * (1.0 + 3 * 0.044715 * (v * v)))
    return 0.5 * v * (1.0 + t), slope


def expert_kernel(count, width, *refs):
    parts = refs[:count]
    weight_in, weight_out, both, slot_sum, stats = refs[count:]
    sums, grads, top, total = merged(parts, width)
    stats[...] = packed([top, total], stats.shape[0])
    sums = sums / total
    slot_sum[...] = sums
    slot_in, grad_out = sums.astype(BF16), grads.astype(BF16)
    experts, _, units = weight_in.shape
    rows = sums.shape[0]
    step = min(units, 512)
    row = lax.broadcasted_iota(jnp.int32, (rows, step), 0)
    out_part = jnp.zeros((rows, width), F32)
    in_part = jnp.zeros((rows, width), F32)
    for e in range(experts):
        own = (row >= e * (rows // experts)) & (row < (e + 1) * (rows // experts))
        for c in range(units // step):
            at = slice(c * step, (c + 1) * step)
            pre_act = product(slot_in, weight_in[e, :, at], 1, 0)
            hid_grad = product(grad_out, weight_out[e, at, :], 1, 1)
            act, slope = gelu_and_slope(pre_act)
            hidden = jnp.where(own, act, 0.0).astype(BF16)
            act_grad = jnp.where(own, hid_grad * slope, 0.0).astype(BF16)
            out_part += product(hidden, weight_out[e, at, :], 1, 0)
            in_part += product(act_grad, weight_in[e, :, at], 1, 1)
    both[:, :width] = out_part.astype(BF16)
    both[:, width:] = in_part.astype(BF16)


def sum_kernel(count, *refs):
    total = sum(r[...].astype(F32) for r in refs[:count])
    outs = refs[count:]
    rows = outs[0].shape[0]
    for k, out in enumerate(outs):
        out[...] = total[k * rows : (k + 1) * rows].astype(out.dtype)


def sum_of(parts, pieces, dtype):
    rows, columns = parts[0].shape
    return local_call(
        partial(sum_kernel, len(parts)), [((rows // pieces, columns), dtype)] * pieces, *parts
    )


def centre_kernel(count, width, *refs):
    parts = refs[:count]
    slot_sum, stats, out = refs[count:]
    total = sum(r[...].astype(F32) for r in parts).astype(BF16)
    grad_in = total[:, width:].astype(F32)
    centre = jnp.sum(slot_sum[...] * grad_in, axis=1, keepdims=True)
    top, denominator = unpacked(stats[...], 2)
    out[:, : 2 * width] = total
    out[:, 2 * width :] = packed([centre, top, denominator], stats.shape[0]).astype(BF16)


def second_kernel(near, far, logits, tokens, out_grad, weights, keep, send):
    width = tokens.shape[1]
    half = near.shape[0]

    def against(columns, rows):
        return jnp.concatenate(
            [product(x[:, columns], rows[...], 1, 1) for x in (near, far)], axis=0
        )

    comb_grad = against(slice(0, width), out_grad)
    disp_grad = against(slice(width, 2 * width), tokens)
    stats = jnp.concatenate([x[:, 2 * width :].astype(F32) for x in (near, far)], axis=0)
    centre, top, total = unpacked(stats, 3)
    scores = logits[...]
    dispatch = jnp.exp(scores - top) / total
    combine = softmax_columns(scores)
    comb_mean = jnp.sum(combine * comb_grad, axis=0, keepdims=True)
    logit_grad = dispatch * (disp_grad - centre) + combine * (comb_grad - comb_mean)
    logit_b = logit_grad.astype(BF16)
    weights[: 2 * half] = dispatch.astype(BF16)
    weights[2 * half :] = logit_b
    part = product(logit_b, tokens[...], 1, 0).astype(BF16)
    keep[...] = part[:half]
    send[...] = part[half:]


def patch_kernel(weights, near, far, table_near, table_far, out):
    width = out.shape[1]
    rows = jnp.concatenate(
        [x[:, width : 2 * width] for x in (near, far)] + [table_near[...], table_far[...]], axis=0
    )
    out[...] = product(weights[...], rows, 0, 0).astype(BF16)


def shards(tokens, slot_embed, expert_in, expert_out, out_grad):
    width = tokens.shape[1]
    patches = tokens.shape[0]
    own = slot_embed.shape[1]
    n_exp, n_seq = lax.axis_size("exp"), lax.axis_size("seq")
    slots = own * n_exp
    half = slots // 2
    columns = 2 * width + LANES
    chip_groups = groups(n_exp, 2)
    seq_groups = groups(n_seq, 1)

    def gathered_over_chips(x):
        for masks in reversed(chip_groups):
            x = stack([x] + swaps([x] * len(masks), "exp", masks))
        return x

    table_near = gathered_over_chips(slot_embed.T)
    table_far = swap(table_near, "exp", 1)

    logits, keep, send = local_call(
        first_kernel,
        [((slots, patches), F32), ((half, columns), BF16), ((half, columns), BF16)],
        table_near,
        table_far,
        tokens,
        out_grad,
        limit=12,
    )
    parts = [keep, swap(send, "exp", 1)]
    for masks in chip_groups:
        pieces = merge(parts, width, len(masks) + 1)
        parts = [pieces[0]] + swaps(pieces[1:], "exp", masks)
    for masks in seq_groups:
        (x,) = merge(parts, width, 1)
        parts = [x] + swaps([x] * len(masks), "seq", masks)

    both, slot_sum, stats = local_call(
        partial(expert_kernel, len(parts), width),
        [((own, 2 * width), BF16), ((own, width), F32), ((own, LANES), F32)],
        *parts,
        expert_in,
        expert_out,
        limit=16,
    )
    parts = [both]
    for k, masks in enumerate(seq_groups):
        if k:
            parts = list(sum_of(parts, 1, BF16))
        parts = parts + swaps(parts * len(masks), "seq", masks)
    (packet,) = local_call(
        partial(centre_kernel, len(parts), width),
        [((own, columns), BF16)],
        *parts,
        slot_sum,
        stats,
    )
    near = gathered_over_chips(packet)
    far = swap(near, "exp", 1)

    weights, keep, send = local_call(
        second_kernel,
        [((2 * slots, patches), BF16), ((half, width), BF16), ((half, width), BF16)],
        near,
        far,
        logits,
        tokens,
        out_grad,
        limit=12,
    )
    (tok_grad,) = local_call(
        patch_kernel,
        [((patches, width), BF16)],
        weights,
        near,
        far,
        table_near,
        table_far,
        limit=12,
        to_hbm=(0,),
    )

    parts = [keep, swap(send, "exp", 1)]
    for masks in chip_groups:
        pieces = sum_of(parts, len(masks) + 1, BF16)
        parts = [pieces[0]] + swaps(pieces[1:], "exp", masks)
    part = sum(p.astype(F32) for p in parts)
    me = lax.axis_index("seq")
    share = width // n_seq
    for masks in reversed(seq_groups):
        base = me & (min(masks) - 1)
        count = len(masks) + 1
        span = part.shape[1] // count
        low = min(masks)
        mine = (me // low) % count

        def block(mask):
            at = mine ^ (mask // low)
            return lax.dynamic_slice_in_dim(part, at * span, span, axis=1)

        part = block(0) + sum(
            swap(block(mask).astype(BF16), "seq", mask).astype(F32) for mask in masks
        )
    return (tok_grad, part.T)


def solution(mesh):
    placed = (
        P(("seq", "exp"), None),
        P(None, "exp"),
        P("exp", None, "seq"),
        P("exp", "seq", None),
        P(("seq", "exp"), None),
    )
    return jax.shard_map(
        shards,
        mesh=mesh,
        in_specs=placed,
        out_specs=(P(("seq", "exp"), None), P("seq", "exp")),
        check_vma=False,
    )
```

time: 317 us -> 84 us (0.26)
  blocking collectives: 158 us -> 0 us
  waiting for transfers between devices: 113 us -> 30.7 us
  starting transfers between devices: 0.16 us -> 30.3 us
  matrix products: 29.4 us -> 0 us
  between operations: 13.9 us -> 0.73 us
  Pallas kernels: 0 us -> 11.4 us
  local copies, waits for them, and re-layouts: 0.8 us -> 9.99 us
    reduce_scatter x4 -> x0, waiting for transfers between devices: 113 us -> none  [the longest x2 60.1 us: owner_sum(): lax.psum_scatter(partial_rows, 'exp', scatter_dimension=0, tiled=True)]
    psum x3 -> x0, blocking collectives: 72.7 us -> none  [the longest x1 37.5 us: shards(): centre = lax.psum(centre_local, ('seq', 'exp'))]
    all_gather x3 -> x0, blocking collectives: 44.7 us -> none  [the longest x1 16.2 us: shards(): slot_table = lax.all_gather(slot_embed, 'exp', axis=1, tiled=True)]
    unnamed x1 -> x0, blocking collectives: 40.4 us -> none
    ppermute x0 -> x25, waiting for transfers between devices: none -> 30.7 us  [swap(): lax.ppermute(x, axis, [(k, k ^ mask) for k in range(lax.axis_size(axis))])]
    ppermute x0 -> x25, starting transfers between devices: none -> 30.3 us  [swap(): lax.ppermute(x, axis, [(k, k ^ mask) for k in range(lax.axis_size(axis))])]
    dot_general x11 -> x0, matrix products: 29.4 us -> none  [the longest x1 10.3 us: shards(): jnp.einsum('esh,edh->esd', act_grad, expert_in, preferred_element_type=jn...]
    pallas_call x0 -> x10, Pallas kernels: none -> 11.4 us  [local_call(): pl.pallas_call(body, out_shape=tuple((jax.ShapeDtypeStruct(s, d) if k in...]
  transfers between devices with their start and end apart: 4 -> 25, of which waited for: 4 -> 20; matrix products, arithmetic and copies ran while one was open for 2% -> 0% of each run, Pallas kernels for 0% -> 2%
where the time goes in v2:
time: 84 us; the launch traced here: 83.7 us
  waiting for transfers between devices  30.7 us (37%)
  starting transfers between devices  30.3 us (36%)
  Pallas kernels  11.4 us (14%)
  local copies, waits for them, and re-layouts  9.99 us (12%)
    ppermute x25, waiting for transfers between devices, swap(): lax.ppermute(x, axis, [(k, k ^ mask) for k in range(lax.axis_size(axis))])  30.7 us
    ppermute x25, starting transfers between devices, swap(): lax.ppermute(x, axis, [(k, k ^ mask) for k in range(lax.axis_size(axis))])  30.3 us
    pallas_call x10, Pallas kernels, local_call(): pl.pallas_call(body, out_shape=tuple((jax.ShapeDtypeStruct(s, d) if k in...  11.4 us
    unnamed x14, local copies, waits for them, and re-layouts  9.98 us
  transfers between devices with their start and end apart: 25, of which 20 were waited for; matrix products, arithmetic and copies ran while one was open for 0% of the time, Pallas kernels for 2%

profile of v2, /device:TPU:0, one launch (start us, length us, event | category | flops | bytes accessed | tf_op | source)
XLA Modules:
  0.0 83.7 jit_solution(540456778113414259)
XLA Ops:
  0.6 5.1 %collective-permute-start.2 = (bf16[8,2048]{1,0:T(8,128)(2,1)}, bf16[8,2048]{1,0:T(8,128)(2,1)S(1)}, u32[]{:S(2)}, u32[]{:S(2)}) collective-permute-start(bf16[8,2048]{1,0:T(8,128)(2,1)} %bitcast.3), channel_id=1, source_target_pairs={{0,6},{1,7},{2,4},{3,5},{4,2},{5,3},{6,0},{7,1},{8,14},{9,15},{10,... | collective-permute-start | bytes 98312 | tf_op jit(solution)/shard_map/ppermute | solution.py:18
  6.4 1.5 %collective-permute-done.2.refs_3_ = bf16[8,2048]{1,0:T(8,128)(2,1)S(1)} collective-permute-done((bf16[8,2048]{1,0:T(8,128)(2,1)}, bf16[8,2048]{1,0:T(8,128)(2,1)S(1)}, u32[]{:S(2)}, u32[]{:S(2)}) %collective-permute-start.2) | collective-permute-done | bytes 32800 | tf_op jit(solution)/shard_map/ppermute | solution.py:18
  7.8 2.9 %collective-permute-done.1.refs_2_ = bf16[8,2048]{1,0:T(8,128)(2,1)S(1)} collective-permute-done((bf16[8,2048]{1,0:T(8,128)(2,1)}, bf16[8,2048]{1,0:T(8,128)(2,1)S(1)}, u32[]{:S(2)}, u32[]{:S(2)}) %collective-permute-start.1) | collective-permute-done | bytes 32800 | tf_op jit(solution)/shard_map/ppermute | solution.py:18
  11.6 1.3 %collective-permute-done.3.far.table_far = bf16[32,2048]{1,0:T(8,128)(2,1)S(1)} collective-permute-done((bf16[32,2048]{1,0:T(8,128)(2,1)S(1)}, bf16[32,2048]{1,0:T(8,128)(2,1)S(1)}, u32[]{:S(2)}, u32[]{:S(2)}) %collective-permute-start.3) | collective-permute-done | bytes 131104 | tf_op jit(solution)/shard_map/ppermute | solution.py:18
  13.0 1.2 %copy-done.2 = bf16[256,2048]{1,0:T(8,128)(2,1)S(1)} copy-done((bf16[256,2048]{1,0:T(8,128)(2,1)S(1)}, bf16[256,2048]{1,0:T(8,128)(2,1)}, u32[]{:S(2)}) %copy-start.2) | copy-done | bytes 1048600
  15.4 1.2 %shard_map.69 = (f32[64,256]{1,0:T(8,128)S(1)}, bf16[32,4224]{1,0:T(8,128)(2,1)S(1)}, bf16[32,4224]{1,0:T(8,128)(2,1)S(1)}) custom-call(bf16[32,2048]{1,0:T(8,128)(2,1)S(1)} %shard_map.68.near.table_near, bf16[32,2048]{1,0:T(8,128)(2,1)S(1)} %collective-permute-done.3.far.table_far, bf16[256,2048]{1,0:T(8,128)(2,1)S(1)} %copy-done.2, ...), custom_call_target="tpu_custom_call" | custom-call | tf_op jit(solution)/shard_map/pallas_call | solution.py:40
  16.9 1.4 %collective-permute-done.4.refs_1_ = bf16[32,4224]{1,0:T(8,128)(2,1)S(1)} collective-permute-done((bf16[32,4224]{1,0:T(8,128)(2,1)S(1)}, bf16[32,4224]{1,0:T(8,128)(2,1)S(1)}, u32[]{:S(2)}, u32[]{:S(2)}) %collective-permute-start.4) | collective-permute-done | bytes 270368 | tf_op jit(solution)/shard_map/ppermute | solution.py:18
  18.5 2.1 %collective-permute-start.6 = (bf16[8,4224]{1,0:T(8,128)(2,1)S(1)}, bf16[8,4224]{1,0:T(8,128)(2,1)S(1)}, u32[]{:S(2)}, u32[]{:S(2)}) collective-permute-start(bf16[8,4224]{1,0:T(8,128)(2,1)S(1)} %get-tuple-element.23), channel_id=1, source_target_pairs={{0,4},{1,5},{2,6},{3,7},{4,0},{5,1},{6,2},{7,3},{8,12},{9,13},{10,... | collective-permute-start | bytes 202760 | tf_op jit(solution)/shard_map/ppermute | solution.py:18
  20.6 2.3 %collective-permute-start.7 = (bf16[8,4224]{1,0:T(8,128)(2,1)S(1)}, bf16[8,4224]{1,0:T(8,128)(2,1)S(1)}, u32[]{:S(2)}, u32[]{:S(2)}) collective-permute-start(bf16[8,4224]{1,0:T(8,128)(2,1)S(1)} %get-tuple-element.24), channel_id=1, source_target_pairs={{0,6},{1,7},{2,4},{3,5},{4,2},{5,3},{6,0},{7,1},{8,14},{9,15},{10,... | collective-permute-start | bytes 202760 | tf_op jit(solution)/shard_map/ppermute | solution.py:18
  22.9 1.3 %collective-permute-done.5.refs_1_ = bf16[8,4224]{1,0:T(8,128)(2,1)S(1)} collective-permute-done((bf16[8,4224]{1,0:T(8,128)(2,1)S(1)}, bf16[8,4224]{1,0:T(8,128)(2,1)S(1)}, u32[]{:S(2)}, u32[]{:S(2)}) %collective-permute-start.5) | collective-permute-done | bytes 67616 | tf_op jit(solution)/shard_map/ppermute | solution.py:18
  24.2 2.9 %collective-permute-done.7.refs_3_ = bf16[8,4224]{1,0:T(8,128)(2,1)S(1)} collective-permute-done((bf16[8,4224]{1,0:T(8,128)(2,1)S(1)}, bf16[8,4224]{1,0:T(8,128)(2,1)S(1)}, u32[]{:S(2)}, u32[]{:S(2)}) %collective-permute-start.7) | collective-permute-done | bytes 67616 | tf_op jit(solution)/shard_map/ppermute | solution.py:18
  27.2 2.5 %collective-permute-start.10 = (bf16[8,4224]{1,0:T(8,128)(2,1)S(1)}, bf16[8,4224]{1,0:T(8,128)(2,1)S(1)}, u32[]{:S(2)}, u32[]{:S(2)}) collective-permute-start(bf16[8,4224]{1,0:T(8,128)(2,1)S(1)} %shard_map.71.refs_0_), channel_id=1, source_target_pairs={{0,24},{8,16},{16,8},{24,0},{1,25},{9,17},{17,9},{25,1},{2,26},{10... | collective-permute-start | bytes 202760 | tf_op jit(solution)/shard_map/ppermute | solution.py:18
  30.8 1.8 %collective-permute-done.10.refs_3_ = bf16[8,4224]{1,0:T(8,128)(2,1)S(1)} collective-permute-done((bf16[8,4224]{1,0:T(8,128)(2,1)S(1)}, bf16[8,4224]{1,0:T(8,128)(2,1)S(1)}, u32[]{:S(2)}, u32[]{:S(2)}) %collective-permute-start.10) | collective-permute-done | bytes 67616 | tf_op jit(solution)/shard_map/ppermute | solution.py:18
  32.6 1.4 %collective-permute-done.9.refs_2_ = bf16[8,4224]{1,0:T(8,128)(2,1)S(1)} collective-permute-done((bf16[8,4224]{1,0:T(8,128)(2,1)S(1)}, bf16[8,4224]{1,0:T(8,128)(2,1)S(1)}, u32[]{:S(2)}, u32[]{:S(2)}) %collective-permute-start.9) | collective-permute-done | bytes 67616 | tf_op jit(solution)/shard_map/ppermute | solution.py:18
  34.5 3.4 %copy-done = bf16[2,2048,1024]{2,1,0:T(8,128)(2,1)S(1)} copy-done((bf16[2,2048,1024]{2,1,0:T(8,128)(2,1)S(1)}, bf16[2,2048,1024]{2,1,0:T(8,128)(2,1)}, u32[]{:S(2)}) %copy-start) | copy-done | bytes 8388632
  37.9 3.4 %copy-done.1 = bf16[2,1024,2048]{2,1,0:T(8,128)(2,1)S(1)} copy-done((bf16[2,1024,2048]{2,1,0:T(8,128)(2,1)S(1)}, bf16[2,1024,2048]{2,1,0:T(8,128)(2,1)}, u32[]{:S(2)}) %copy-start.1) | copy-done | bytes 8388632
  41.3 6.7 %shard_map.72 = (bf16[8,4096]{1,0:T(8,128)(2,1)S(1)}, f32[8,2048]{1,0:T(8,128)S(1)}, f32[8,128]{1,0:T(8,128)S(1)}) custom-call(bf16[8,4224]{1,0:T(8,128)(2,1)S(1)} %shard_map.71.refs_0_, bf16[8,4224]{1,0:T(8,128)(2,1)S(1)} %collective-permute-done.8.refs_1_, bf16[8,4224]{1,0:T(8,128)(2,1)S(1)} %collective-permute-done.9.refs_2_, ...), custom_call_target="tpu_custom_call" | custom-call | tf_op jit(solution)/shard_map/pallas_call | solution.py:40
  48.0 1.5 %collective-permute-start.13 = (bf16[8,4096]{1,0:T(8,128)(2,1)S(1)}, bf16[8,4096]{1,0:T(8,128)(2,1)S(1)}, u32[]{:S(2)}, u32[]{:S(2)}) collective-permute-start(bf16[8,4096]{1,0:T(8,128)(2,1)S(1)} %get-tuple-element.25.refs_0_), channel_id=1, source_target_pairs={{0,24},{8,16},{16,8},{24,0},{1,25},{9,17},{17,9},{25,1},{2,26},{10... | collective-permute-start | bytes 196616 | tf_op jit(solution)/shard_map/ppermute | solution.py:18
  50.0 1.5 %collective-permute-start.11 = (bf16[8,4096]{1,0:T(8,128)(2,1)S(1)}, bf16[8,4096]{1,0:T(8,128)(2,1)S(1)}, u32[]{:S(2)}, u32[]{:S(2)}) collective-permute-start(bf16[8,4096]{1,0:T(8,128)(2,1)S(1)} %get-tuple-element.25.refs_0_), channel_id=1, source_target_pairs={{0,8},{8,0},{16,24},{24,16},{1,9},{9,1},{17,25},{25,17},{2,10},{10... | collective-permute-start | bytes 196616 | tf_op jit(solution)/shard_map/ppermute | solution.py:18
  51.5 1.7 %collective-permute-done.13.refs_3_ = bf16[8,4096]{1,0:T(8,128)(2,1)S(1)} collective-permute-done((bf16[8,4096]{1,0:T(8,128)(2,1)S(1)}, bf16[8,4096]{1,0:T(8,128)(2,1)S(1)}, u32[]{:S(2)}, u32[]{:S(2)}) %collective-permute-start.13) | collective-permute-done | bytes 65568 | tf_op jit(solution)/shard_map/ppermute | solution.py:18
  54.4 2.6 %collective-permute-start.16 = (bf16[8,4224]{1,0:T(8,128)(2,1)S(1)}, bf16[8,4224]{1,0:T(8,128)(2,1)S(1)}, u32[]{:S(2)}, u32[]{:S(2)}) collective-permute-start(bf16[8,4224]{1,0:T(8,128)(2,1)S(1)} %shard_map.73.refs_0_), channel_id=1, source_target_pairs={{0,6},{1,7},{2,4},{3,5},{4,2},{5,3},{6,0},{7,1},{8,14},{9,15},{10,... | collective-permute-start | bytes 202760 | tf_op jit(solution)/shard_map/ppermute | solution.py:18
  58.8 2.4 %collective-permute-done.16.refs_3_ = bf16[8,4224]{1,0:T(8,128)(2,1)S(1)} collective-permute-done((bf16[8,4224]{1,0:T(8,128)(2,1)S(1)}, bf16[8,4224]{1,0:T(8,128)(2,1)S(1)}, u32[]{:S(2)}, u32[]{:S(2)}) %collective-permute-start.16) | collective-permute-done | bytes 67616 | tf_op jit(solution)/shard_map/ppermute | solution.py:18
  61.2 1.7 %collective-permute-done.15.refs_2_ = bf16[8,4224]{1,0:T(8,128)(2,1)S(1)} collective-permute-done((bf16[8,4224]{1,0:T(8,128)(2,1)S(1)}, bf16[8,4224]{1,0:T(8,128)(2,1)S(1)}, u32[]{:S(2)}, u32[]{:S(2)}) %collective-permute-start.15) | collective-permute-done | bytes 67616 | tf_op jit(solution)/shard_map/ppermute | solution.py:18
  63.0 1.5 %collective-permute-done.17.far = bf16[32,4224]{1,0:T(8,128)(2,1)S(1)} collective-permute-done((bf16[32,4224]{1,0:T(8,128)(2,1)S(1)}, bf16[32,4224]{1,0:T(8,128)(2,1)S(1)}, u32[]{:S(2)}, u32[]{:S(2)}) %collective-permute-start.17) | collective-permute-done | bytes 270368 | tf_op jit(solution)/shard_map/ppermute | solution.py:18
  64.6 1.6 %shard_map.75 = (bf16[128,256]{1,0:T(8,128)(2,1)S(1)}, bf16[32,2048]{1,0:T(8,128)(2,1)S(1)}, bf16[32,2048]{1,0:T(8,128)(2,1)S(1)}) custom-call(bf16[32,4224]{1,0:T(8,128)(2,1)S(1)} %shard_map.74.near, bf16[32,4224]{1,0:T(8,128)(2,1)S(1)} %collective-permute-done.17.far, f32[64,256]{1,0:T(8,128)S(1)} %get-tuple-element.28.logits, ...), custom_call_target="tpu_custom_call" | custom-call | tf_op jit(solution)/shard_map/pallas_call | solution.py:40
  68.1 2.6 %collective-permute-start.20 = (bf16[8,2048]{1,0:T(8,128)(2,1)S(1)}, bf16[8,2048]{1,0:T(8,128)(2,1)S(1)}, u32[]{:S(2)}, u32[]{:S(2)}) collective-permute-start(bf16[8,2048]{1,0:T(8,128)(2,1)S(1)} %get-tuple-element.34), channel_id=1, source_target_pairs={{0,4},{1,5},{2,6},{3,7},{4,0},{5,1},{6,2},{7,3},{8,12},{9,13},{10,... | collective-permute-start | bytes 98312 | tf_op jit(solution)/shard_map/ppermute | solution.py:18
  70.8 1.3 %collective-permute-start.21 = (bf16[8,2048]{1,0:T(8,128)(2,1)S(1)}, bf16[8,2048]{1,0:T(8,128)(2,1)S(1)}, u32[]{:S(2)}, u32[]{:S(2)}) collective-permute-start(bf16[8,2048]{1,0:T(8,128)(2,1)S(1)} %get-tuple-element.35), channel_id=1, source_target_pairs={{0,6},{1,7},{2,4},{3,5},{4,2},{5,3},{6,0},{7,1},{8,14},{9,15},{10,... | collective-permute-start | bytes 98312 | tf_op jit(solution)/shard_map/ppermute | solution.py:18
  72.1 1.5 %collective-permute-done.20 = bf16[8,2048]{1,0:T(8,128)(2,1)S(1)} collective-permute-done((bf16[8,2048]{1,0:T(8,128)(2,1)S(1)}, bf16[8,2048]{1,0:T(8,128)(2,1)S(1)}, u32[]{:S(2)}, u32[]{:S(2)}) %collective-permute-start.20) | collective-permute-done | bytes 32800 | tf_op jit(solution)/shard_map/ppermute | solution.py:18
  73.5 3.0 %collective-permute-done.21 = bf16[8,2048]{1,0:T(8,128)(2,1)S(1)} collective-permute-done((bf16[8,2048]{1,0:T(8,128)(2,1)S(1)}, bf16[8,2048]{1,0:T(8,128)(2,1)S(1)}, u32[]{:S(2)}, u32[]{:S(2)}) %collective-permute-start.21) | collective-permute-done | bytes 32800 | tf_op jit(solution)/shard_map/ppermute | solution.py:18
  76.6 1.4 %collective-permute-start.22 = (bf16[8,512]{1,0:T(8,128)(2,1)S(1)}, bf16[8,512]{1,0:T(8,128)(2,1)S(1)}, u32[]{:S(2)}, u32[]{:S(2)}) collective-permute-start(bf16[8,512]{1,0:T(8,128)(2,1)S(1)} %get-tuple-element.36), channel_id=1, source_target_pairs={{0,8},{8,0},{16,24},{24,16},{1,9},{9,1},{17,25},{25,17},{2,10},{10... | collective-permute-start | bytes 24584 | tf_op jit(solution)/shard_map/ppermute | solution.py:18
  77.9 1.5 %collective-permute-start.24 = (bf16[8,512]{1,0:T(8,128)(2,1)S(1)}, bf16[8,512]{1,0:T(8,128)(2,1)S(1)}, u32[]{:S(2)}, u32[]{:S(2)}) collective-permute-start(bf16[8,512]{1,0:T(8,128)(2,1)S(1)} %get-tuple-element.37), channel_id=1, source_target_pairs={{0,24},{8,16},{16,8},{24,0},{1,25},{9,17},{17,9},{25,1},{2,26},{10... | collective-permute-start | bytes 24584 | tf_op jit(solution)/shard_map/ppermute | solution.py:18
  80.1 1.4 %shard_map.76 = bf16[256,2048]{1,0:T(8,128)(2,1)} custom-call(bf16[128,256]{1,0:T(8,128)(2,1)S(1)} %get-tuple-element.29.weights, bf16[32,4224]{1,0:T(8,128)(2,1)S(1)} %shard_map.74.near, bf16[32,4224]{1,0:T(8,128)(2,1)S(1)} %collective-permute-done.17.far, bf16[32,2048]{1,0:T(8,128)(2,1)S(1)} %shard_map.68.near.table_near, ...), custom_call_target="tpu_custom_call" | custom-call | tf_op jit(solution)/shard_map/pallas_call | solution.py:40
  (45 shorter events, 13.3 us)
Async XLA Ops:
  0.6 7.2 %collective-permute-start.2 = (bf16[8,2048]{1,0:T(8,128)(2,1)}, bf16[8,2048]{1,0:T(8,128)(2,1)S(1)}, u32[]{:S(2)}, u32[]{:S(2)}) collective-permute-start(bf16[8,2048]{1,0:T(8,128)(2,1)} %bitcast.3), channel_id=1, source_target_pairs={{0,6},{1,7},{2,4},{3,5},{4,2},{5,3},{6,0},{7,1},{8,14},{9,15},{10,... | collective-permute-start | bytes 98312 | tf_op jit(solution)/shard_map/ppermute | solution.py:18
  5.7 5.0 %collective-permute-start.1 = (bf16[8,2048]{1,0:T(8,128)(2,1)}, bf16[8,2048]{1,0:T(8,128)(2,1)S(1)}, u32[]{:S(2)}, u32[]{:S(2)}) collective-permute-start(bf16[8,2048]{1,0:T(8,128)(2,1)} %bitcast.4), channel_id=1, source_target_pairs={{0,4},{1,5},{2,6},{3,7},{4,0},{5,1},{6,2},{7,3},{8,12},{9,13},{10,... | collective-permute-start | bytes 98312 | tf_op jit(solution)/shard_map/ppermute | solution.py:18
  5.7 5.0 %collective-permute-start = (bf16[8,2048]{1,0:T(8,128)(2,1)}, bf16[8,2048]{1,0:T(8,128)(2,1)S(1)}, u32[]{:S(2)}, u32[]{:S(2)}) collective-permute-start(bf16[8,2048]{1,0:T(8,128)(2,1)} %bitcast.5), channel_id=1, source_target_pairs={{0,2},{1,3},{2,0},{3,1},{4,6},{5,7},{6,4},{7,5},{8,10},{9,11},{10,... | collective-permute-start | bytes 98312 | tf_op jit(solution)/shard_map/ppermute | solution.py:18
  10.8 0.8 copy-start.6
  11.5 1.4 %collective-permute-start.3 = (bf16[32,2048]{1,0:T(8,128)(2,1)S(1)}, bf16[32,2048]{1,0:T(8,128)(2,1)S(1)}, u32[]{:S(2)}, u32[]{:S(2)}) collective-permute-start(bf16[32,2048]{1,0:T(8,128)(2,1)S(1)} %shard_map.68.near.table_near), channel_id=1, source_target_pairs={{0,1},{1,0},{2,3},{3,2},{4,5},{5,4},{6,7},{7,6},{8,9},{9,8},{10,11... | collective-permute-start | bytes 393224 | tf_op jit(solution)/shard_map/ppermute | solution.py:18
  13.0 1.2 %copy-start.2 = (bf16[256,2048]{1,0:T(8,128)(2,1)S(1)}, bf16[256,2048]{1,0:T(8,128)(2,1)}, u32[]{:S(2)}) copy-start(bf16[256,2048]{1,0:T(8,128)(2,1)} %tokens.3) | copy-start | bytes 3145732
  14.2 1.2 %copy-start.4 = (bf16[256,2048]{1,0:T(8,128)(2,1)S(1)}, bf16[256,2048]{1,0:T(8,128)(2,1)}, u32[]{:S(2)}) copy-start(bf16[256,2048]{1,0:T(8,128)(2,1)} %out_grad.3) | copy-start | bytes 3145732
  16.7 1.6 %collective-permute-start.4 = (bf16[32,4224]{1,0:T(8,128)(2,1)S(1)}, bf16[32,4224]{1,0:T(8,128)(2,1)S(1)}, u32[]{:S(2)}, u32[]{:S(2)}) collective-permute-start(bf16[32,4224]{1,0:T(8,128)(2,1)S(1)} %get-tuple-element.20), channel_id=1, source_target_pairs={{0,1},{1,0},{2,3},{3,2},{4,5},{5,4},{6,7},{7,6},{8,9},{9,8},{10,11... | collective-permute-start | bytes 811016 | tf_op jit(solution)/shard_map/ppermute | solution.py:18
  18.4 5.8 %collective-permute-start.5 = (bf16[8,4224]{1,0:T(8,128)(2,1)S(1)}, bf16[8,4224]{1,0:T(8,128)(2,1)S(1)}, u32[]{:S(2)}, u32[]{:S(2)}) collective-permute-start(bf16[8,4224]{1,0:T(8,128)(2,1)S(1)} %get-tuple-element.22), channel_id=1, source_target_pairs={{0,2},{1,3},{2,0},{3,1},{4,6},{5,7},{6,4},{7,5},{8,10},{9,11},{10,... | collective-permute-start | bytes 202760 | tf_op jit(solution)/shard_map/ppermute | solution.py:18
  18.5 5.7 %collective-permute-start.6 = (bf16[8,4224]{1,0:T(8,128)(2,1)S(1)}, bf16[8,4224]{1,0:T(8,128)(2,1)S(1)}, u32[]{:S(2)}, u32[]{:S(2)}) collective-permute-start(bf16[8,4224]{1,0:T(8,128)(2,1)S(1)} %get-tuple-element.23), channel_id=1, source_target_pairs={{0,4},{1,5},{2,6},{3,7},{4,0},{5,1},{6,2},{7,3},{8,12},{9,13},{10,... | collective-permute-start | bytes 202760 | tf_op jit(solution)/shard_map/ppermute | solution.py:18
  20.6 6.5 %collective-permute-start.7 = (bf16[8,4224]{1,0:T(8,128)(2,1)S(1)}, bf16[8,4224]{1,0:T(8,128)(2,1)S(1)}, u32[]{:S(2)}, u32[]{:S(2)}) collective-permute-start(bf16[8,4224]{1,0:T(8,128)(2,1)S(1)} %get-tuple-element.24), channel_id=1, source_target_pairs={{0,6},{1,7},{2,4},{3,5},{4,2},{5,3},{6,0},{7,1},{8,14},{9,15},{10,... | collective-permute-start | bytes 202760 | tf_op jit(solution)/shard_map/ppermute | solution.py:18
  27.2 5.4 %collective-permute-start.10 = (bf16[8,4224]{1,0:T(8,128)(2,1)S(1)}, bf16[8,4224]{1,0:T(8,128)(2,1)S(1)}, u32[]{:S(2)}, u32[]{:S(2)}) collective-permute-start(bf16[8,4224]{1,0:T(8,128)(2,1)S(1)} %shard_map.71.refs_0_), channel_id=1, source_target_pairs={{0,24},{8,16},{16,8},{24,0},{1,25},{9,17},{17,9},{25,1},{2,26},{10... | collective-permute-start | bytes 202760 | tf_op jit(solution)/shard_map/ppermute | solution.py:18
  29.7 4.3 %collective-permute-start.9 = (bf16[8,4224]{1,0:T(8,128)(2,1)S(1)}, bf16[8,4224]{1,0:T(8,128)(2,1)S(1)}, u32[]{:S(2)}, u32[]{:S(2)}) collective-permute-start(bf16[8,4224]{1,0:T(8,128)(2,1)S(1)} %shard_map.71.refs_0_), channel_id=1, source_target_pairs={{0,16},{8,24},{16,0},{24,8},{1,17},{9,25},{17,1},{25,9},{2,18},{10... | collective-permute-start | bytes 202760 | tf_op jit(solution)/shard_map/ppermute | solution.py:18
  30.2 4.3 %collective-permute-start.8 = (bf16[8,4224]{1,0:T(8,128)(2,1)S(1)}, bf16[8,4224]{1,0:T(8,128)(2,1)S(1)}, u32[]{:S(2)}, u32[]{:S(2)}) collective-permute-start(bf16[8,4224]{1,0:T(8,128)(2,1)S(1)} %shard_map.71.refs_0_), channel_id=1, source_target_pairs={{0,8},{8,0},{16,24},{24,16},{1,9},{9,1},{17,25},{25,17},{2,10},{10... | collective-permute-start | bytes 202760 | tf_op jit(solution)/shard_map/ppermute | solution.py:18
  34.5 3.4 %copy-start = (bf16[2,2048,1024]{2,1,0:T(8,128)(2,1)S(1)}, bf16[2,2048,1024]{2,1,0:T(8,128)(2,1)}, u32[]{:S(2)}) copy-start(bf16[2,2048,1024]{2,1,0:T(8,128)(2,1)} %refs_4_.1) | copy-start | bytes 25165828
  37.9 3.4 %copy-start.1 = (bf16[2,1024,2048]{2,1,0:T(8,128)(2,1)S(1)}, bf16[2,1024,2048]{2,1,0:T(8,128)(2,1)}, u32[]{:S(2)}) copy-start(bf16[2,1024,2048]{2,1,0:T(8,128)(2,1)} %refs_5_.1) | copy-start | bytes 25165828
  41.3 23.3 %copy-start.3 = (bf16[256,2048]{1,0:T(8,128)(2,1)S(1)}, bf16[256,2048]{1,0:T(8,128)(2,1)}, u32[]{:S(2)}) copy-start(bf16[256,2048]{1,0:T(8,128)(2,1)} %tokens.3) | copy-start | bytes 3145732
  41.3 23.3 %copy-start.5 = (bf16[256,2048]{1,0:T(8,128)(2,1)S(1)}, bf16[256,2048]{1,0:T(8,128)(2,1)}, u32[]{:S(2)}) copy-start(bf16[256,2048]{1,0:T(8,128)(2,1)} %out_grad.3) | copy-start | bytes 3145732
  48.0 5.2 %collective-permute-start.13 = (bf16[8,4096]{1,0:T(8,128)(2,1)S(1)}, bf16[8,4096]{1,0:T(8,128)(2,1)S(1)}, u32[]{:S(2)}, u32[]{:S(2)}) collective-permute-start(bf16[8,4096]{1,0:T(8,128)(2,1)S(1)} %get-tuple-element.25.refs_0_), channel_id=1, source_target_pairs={{0,24},{8,16},{16,8},{24,0},{1,25},{9,17},{17,9},{25,1},{2,26},{10... | collective-permute-start | bytes 196616 | tf_op jit(solution)/shard_map/ppermute | solution.py:18
  49.5 4.4 %collective-permute-start.12 = (bf16[8,4096]{1,0:T(8,128)(2,1)S(1)}, bf16[8,4096]{1,0:T(8,128)(2,1)S(1)}, u32[]{:S(2)}, u32[]{:S(2)}) collective-permute-start(bf16[8,4096]{1,0:T(8,128)(2,1)S(1)} %get-tuple-element.25.refs_0_), channel_id=1, source_target_pairs={{0,16},{8,24},{16,0},{24,8},{1,17},{9,25},{17,1},{25,9},{2,18},{10... | collective-permute-start | bytes 196616 | tf_op jit(solution)/shard_map/ppermute | solution.py:18
  50.0 4.3 %collective-permute-start.11 = (bf16[8,4096]{1,0:T(8,128)(2,1)S(1)}, bf16[8,4096]{1,0:T(8,128)(2,1)S(1)}, u32[]{:S(2)}, u32[]{:S(2)}) collective-permute-start(bf16[8,4096]{1,0:T(8,128)(2,1)S(1)} %get-tuple-element.25.refs_0_), channel_id=1, source_target_pairs={{0,8},{8,0},{16,24},{24,16},{1,9},{9,1},{17,25},{25,17},{2,10},{10... | collective-permute-start | bytes 196616 | tf_op jit(solution)/shard_map/ppermute | solution.py:18
  54.4 6.8 %collective-permute-start.16 = (bf16[8,4224]{1,0:T(8,128)(2,1)S(1)}, bf16[8,4224]{1,0:T(8,128)(2,1)S(1)}, u32[]{:S(2)}, u32[]{:S(2)}) collective-permute-start(bf16[8,4224]{1,0:T(8,128)(2,1)S(1)} %shard_map.73.refs_0_), channel_id=1, source_target_pairs={{0,6},{1,7},{2,4},{3,5},{4,2},{5,3},{6,0},{7,1},{8,14},{9,15},{10,... | collective-permute-start | bytes 202760 | tf_op jit(solution)/shard_map/ppermute | solution.py:18
  57.0 5.9 %collective-permute-start.15 = (bf16[8,4224]{1,0:T(8,128)(2,1)S(1)}, bf16[8,4224]{1,0:T(8,128)(2,1)S(1)}, u32[]{:S(2)}, u32[]{:S(2)}) collective-permute-start(bf16[8,4224]{1,0:T(8,128)(2,1)S(1)} %shard_map.73.refs_0_), channel_id=1, source_target_pairs={{0,4},{1,5},{2,6},{3,7},{4,0},{5,1},{6,2},{7,3},{8,12},{9,13},{10,... | collective-permute-start | bytes 202760 | tf_op jit(solution)/shard_map/ppermute | solution.py:18
  57.6 5.3 %collective-permute-start.14 = (bf16[8,4224]{1,0:T(8,128)(2,1)S(1)}, bf16[8,4224]{1,0:T(8,128)(2,1)S(1)}, u32[]{:S(2)}, u32[]{:S(2)}) collective-permute-start(bf16[8,4224]{1,0:T(8,128)(2,1)S(1)} %shard_map.73.refs_0_), channel_id=1, source_target_pairs={{0,2},{1,3},{2,0},{3,1},{4,6},{5,7},{6,4},{7,5},{8,10},{9,11},{10,... | collective-permute-start | bytes 202760 | tf_op jit(solution)/shard_map/ppermute | solution.py:18
  62.9 1.6 %collective-permute-start.17 = (bf16[32,4224]{1,0:T(8,128)(2,1)S(1)}, bf16[32,4224]{1,0:T(8,128)(2,1)S(1)}, u32[]{:S(2)}, u32[]{:S(2)}) collective-permute-start(bf16[32,4224]{1,0:T(8,128)(2,1)S(1)} %shard_map.74.near), channel_id=1, source_target_pairs={{0,1},{1,0},{2,3},{3,2},{4,5},{5,4},{6,7},{7,6},{8,9},{9,8},{10,11... | collective-permute-start | bytes 811016 | tf_op jit(solution)/shard_map/ppermute | solution.py:18
  66.1 1.4 %collective-permute-start.18 = (bf16[32,2048]{1,0:T(8,128)(2,1)S(1)}, bf16[32,2048]{1,0:T(8,128)(2,1)S(1)}, u32[]{:S(2)}, u32[]{:S(2)}) collective-permute-start(bf16[32,2048]{1,0:T(8,128)(2,1)S(1)} %get-tuple-element.31), channel_id=1, source_target_pairs={{0,1},{1,0},{2,3},{3,2},{4,5},{5,4},{6,7},{7,6},{8,9},{9,8},{10,11... | collective-permute-start | bytes 393224 | tf_op jit(solution)/shard_map/ppermute | solution.py:18
  67.6 4.5 %collective-permute-start.19 = (bf16[8,2048]{1,0:T(8,128)(2,1)S(1)}, bf16[8,2048]{1,0:T(8,128)(2,1)S(1)}, u32[]{:S(2)}, u32[]{:S(2)}) collective-permute-start(bf16[8,2048]{1,0:T(8,128)(2,1)S(1)} %get-tuple-element.33), channel_id=1, source_target_pairs={{0,2},{1,3},{2,0},{3,1},{4,6},{5,7},{6,4},{7,5},{8,10},{9,11},{10,... | collective-permute-start | bytes 98312 | tf_op jit(solution)/shard_map/ppermute | solution.py:18
  68.1 5.4 %collective-permute-start.20 = (bf16[8,2048]{1,0:T(8,128)(2,1)S(1)}, bf16[8,2048]{1,0:T(8,128)(2,1)S(1)}, u32[]{:S(2)}, u32[]{:S(2)}) collective-permute-start(bf16[8,2048]{1,0:T(8,128)(2,1)S(1)} %get-tuple-element.34), channel_id=1, source_target_pairs={{0,4},{1,5},{2,6},{3,7},{4,0},{5,1},{6,2},{7,3},{8,12},{9,13},{10,... | collective-permute-start | bytes 98312 | tf_op jit(solution)/shard_map/ppermute | solution.py:18
  70.8 5.7 %collective-permute-start.21 = (bf16[8,2048]{1,0:T(8,128)(2,1)S(1)}, bf16[8,2048]{1,0:T(8,128)(2,1)S(1)}, u32[]{:S(2)}, u32[]{:S(2)}) collective-permute-start(bf16[8,2048]{1,0:T(8,128)(2,1)S(1)} %get-tuple-element.35), channel_id=1, source_target_pairs={{0,6},{1,7},{2,4},{3,5},{4,2},{5,3},{6,0},{7,1},{8,14},{9,15},{10,... | collective-permute-start | bytes 98312 | tf_op jit(solution)/shard_map/ppermute | solution.py:18
  76.6 5.0 %collective-permute-start.22 = (bf16[8,512]{1,0:T(8,128)(2,1)S(1)}, bf16[8,512]{1,0:T(8,128)(2,1)S(1)}, u32[]{:S(2)}, u32[]{:S(2)}) collective-permute-start(bf16[8,512]{1,0:T(8,128)(2,1)S(1)} %get-tuple-element.36), channel_id=1, source_target_pairs={{0,8},{8,0},{16,24},{24,16},{1,9},{9,1},{17,25},{25,17},{2,10},{10... | collective-permute-start | bytes 24584 | tf_op jit(solution)/shard_map/ppermute | solution.py:18
  77.9 4.5 %collective-permute-start.24 = (bf16[8,512]{1,0:T(8,128)(2,1)S(1)}, bf16[8,512]{1,0:T(8,128)(2,1)S(1)}, u32[]{:S(2)}, u32[]{:S(2)}) collective-permute-start(bf16[8,512]{1,0:T(8,128)(2,1)S(1)} %get-tuple-element.37), channel_id=1, source_target_pairs={{0,24},{8,16},{16,8},{24,0},{1,25},{9,17},{17,9},{25,1},{2,26},{10... | collective-permute-start | bytes 24584 | tf_op jit(solution)/shard_map/ppermute | solution.py:18
  79.4 3.7 %collective-permute-start.23 = (bf16[8,512]{1,0:T(8,128)(2,1)S(1)}, bf16[8,512]{1,0:T(8,128)(2,1)S(1)}, u32[]{:S(2)}, u32[]{:S(2)}) collective-permute-start(bf16[8,512]{1,0:T(8,128)(2,1)S(1)} %get-tuple-element.38), channel_id=1, source_target_pairs={{0,16},{8,24},{16,0},{24,8},{1,17},{9,25},{17,1},{25,9},{2,18},{10... | collective-permute-start | bytes 24584 | tf_op jit(solution)/shard_map/ppermute | solution.py:18

commit v3 on v2

--- a/solution.py
+++ b/solution.py
@@ -46,6 +46,7 @@
         in_specs=[pl.BlockSpec(memory_space=pltpu.VMEM)] * len(operands),
         out_specs=tuple(pl.BlockSpec(memory_space=pltpu.VMEM) for _ in outs),
         compiler_params=pltpu.CompilerParams(vmem_limit_bytes=limit * MIB),
+        cost_estimate=pl.CostEstimate(flops=10**10, bytes_accessed=4 * MIB, transcendentals=0),
     )(*[in_vmem(x) for x in operands])
 
 
@@ -78,6 +79,24 @@
         )
         for k in range(count)
     ]
+
+
+def load_kernel(source, out, semaphore):
+    copy = pltpu.make_async_copy(source, out, semaphore)
+    copy.start()
+    copy.wait()
+
+
+def loaded(x):
+    return pl.pallas_call(
+        load_kernel,
+        out_shape=pltpu.VMEM(x.shape, x.dtype),
+        in_specs=[pl.BlockSpec(memory_space=pl.ANY)],
+        out_specs=pl.BlockSpec(memory_space=pltpu.VMEM),
+        scratch_shapes=[pltpu.SemaphoreType.DMA],
+        compiler_params=pltpu.CompilerParams(vmem_limit_bytes=2 * MIB),
+        cost_estimate=pl.CostEstimate(flops=10**9, bytes_accessed=2 * x.size, transcendentals=0),
+    )(x)
 
 
 def concat_kernel(*refs):
@@ -256,12 +275,12 @@
     chip_groups = groups(n_exp, 2)
     seq_groups = groups(n_seq, 1)
 
-    def gathered_over_chips(x):
+    def gathered_over_chips(x, here):
         for masks in reversed(chip_groups):
-            x = stack([x] + swaps([x] * len(masks), "exp", masks))
+            x = here = stack([here] + swaps([x] * len(masks), "exp", masks))
         return x
 
-    table_near = gathered_over_chips(slot_embed.T)
+    table_near = gathered_over_chips(slot_embed.T, loaded(slot_embed.T))
     table_far = swap(table_near, "exp", 1)
 
     logits, keep, send = local_call(
@@ -301,7 +320,7 @@
         slot_sum,
         stats,
     )
-    near = gathered_over_chips(packet)
+    near = gathered_over_chips(packet, packet)
     far = swap(near, "exp", 1)
 
     weights, keep, send = local_call(

time: 84 us -> 74 us (0.88)
  local copies, waits for them, and re-layouts: 9.99 us -> 0.84 us
    unnamed x14, local copies, waits for them, and re-layouts: 9.98 us -> 0.83 us
where the time goes in v3:
time: 74 us; the launch traced here: 73.8 us
  starting transfers between devices  30.2 us (41%)
  waiting for transfers between devices  29.9 us (40%)
  Pallas kernels  11.4 us (15%)
  local copies, waits for them, and re-layouts  0.84 us (1%)
  between operations  0.8 us (1%)
    ppermute x25, starting transfers between devices, swap(): lax.ppermute(x, axis, [(k, k ^ mask) for k in range(lax.axis_size(axis))])  30.2 us
    ppermute x25, waiting for transfers between devices, swap(): lax.ppermute(x, axis, [(k, k ^ mask) for k in range(lax.axis_size(axis))])  29.9 us
    pallas_call x10, Pallas kernels, local_call(): pl.pallas_call(body, out_shape=tuple((jax.ShapeDtypeStruct(s, d) if k in...  11.4 us
  transfers between devices with their start and end apart: 25, of which 20 were waited for; matrix products, arithmetic and copies ran while one was open for 0% of the time, Pallas kernels for 2%

profile of v3, /device:TPU:0, one launch (start us, length us, event | category | flops | bytes accessed | tf_op | source)
XLA Modules:
  0.0 73.8 jit_solution(4671858775278009352)
XLA Ops:
  0.6 5.1 %collective-permute-start.2 = (bf16[8,2048]{1,0:T(8,128)(2,1)}, bf16[8,2048]{1,0:T(8,128)(2,1)S(1)}, u32[]{:S(2)}, u32[]{:S(2)}) collective-permute-start(bf16[8,2048]{1,0:T(8,128)(2,1)} %bitcast.7), channel_id=1, source_target_pairs={{0,6},{1,7},{2,4},{3,5},{4,2},{5,3},{6,0},{7,1},{8,14},{9,15},{10,... | collective-permute-start | bytes 98312 | tf_op jit(solution)/shard_map/ppermute | solution.py:18
  6.4 0.8 %copy-done.2 = bf16[2048,8]{0,1:T(8,128)(2,1)S(1)} copy-done((bf16[2048,8]{0,1:T(8,128)(2,1)S(1)}, bf16[2048,8]{0,1:T(8,128)(2,1)}, u32[]{:S(2)}) %copy-start.2) | copy-done | bytes 32792
  7.8 2.9 %collective-permute-done.1.refs_2_ = bf16[8,2048]{1,0:T(8,128)(2,1)S(1)} collective-permute-done((bf16[8,2048]{1,0:T(8,128)(2,1)}, bf16[8,2048]{1,0:T(8,128)(2,1)S(1)}, u32[]{:S(2)}, u32[]{:S(2)}) %collective-permute-start.1) | collective-permute-done | bytes 32800 | tf_op jit(solution)/shard_map/ppermute | solution.py:18
  10.9 1.3 %collective-permute-done.3.far.table_far = bf16[32,2048]{1,0:T(8,128)(2,1)S(1)} collective-permute-done((bf16[32,2048]{1,0:T(8,128)(2,1)S(1)}, bf16[32,2048]{1,0:T(8,128)(2,1)S(1)}, u32[]{:S(2)}, u32[]{:S(2)}) %collective-permute-start.3) | collective-permute-done | bytes 131104 | tf_op jit(solution)/shard_map/ppermute | solution.py:18
  12.2 1.2 %shard_map.70 = (f32[64,256]{1,0:T(8,128)S(1)}, bf16[32,4224]{1,0:T(8,128)(2,1)S(1)}, bf16[32,4224]{1,0:T(8,128)(2,1)S(1)}) custom-call(bf16[32,2048]{1,0:T(8,128)(2,1)S(1)} %shard_map.69.near.table_near, bf16[32,2048]{1,0:T(8,128)(2,1)S(1)} %collective-permute-done.3.far.table_far, bf16[256,2048]{1,0:T(8,128)(2,1)S(1)} %copy-done, ...), custom_call_target="tpu_custom_call" | custom-call | flops 10000000000 | bytes 4194304 | tf_op jit(solution)/shard_map/pallas_call | solution.py:40
  13.7 1.4 %collective-permute-done.4.refs_1_ = bf16[32,4224]{1,0:T(8,128)(2,1)S(1)} collective-permute-done((bf16[32,4224]{1,0:T(8,128)(2,1)S(1)}, bf16[32,4224]{1,0:T(8,128)(2,1)S(1)}, u32[]{:S(2)}, u32[]{:S(2)}) %collective-permute-start.4) | collective-permute-done | bytes 270368 | tf_op jit(solution)/shard_map/ppermute | solution.py:18
  15.3 2.1 %collective-permute-start.6 = (bf16[8,4224]{1,0:T(8,128)(2,1)S(1)}, bf16[8,4224]{1,0:T(8,128)(2,1)S(1)}, u32[]{:S(2)}, u32[]{:S(2)}) collective-permute-start(bf16[8,4224]{1,0:T(8,128)(2,1)S(1)} %get-tuple-element.23), channel_id=1, source_target_pairs={{0,4},{1,5},{2,6},{3,7},{4,0},{5,1},{6,2},{7,3},{8,12},{9,13},{10,... | collective-permute-start | bytes 202760 | tf_op jit(solution)/shard_map/ppermute | solution.py:18
  17.4 2.3 %collective-permute-start.7 = (bf16[8,4224]{1,0:T(8,128)(2,1)S(1)}, bf16[8,4224]{1,0:T(8,128)(2,1)S(1)}, u32[]{:S(2)}, u32[]{:S(2)}) collective-permute-start(bf16[8,4224]{1,0:T(8,128)(2,1)S(1)} %get-tuple-element.24), channel_id=1, source_target_pairs={{0,6},{1,7},{2,4},{3,5},{4,2},{5,3},{6,0},{7,1},{8,14},{9,15},{10,... | collective-permute-start | bytes 202760 | tf_op jit(solution)/shard_map/ppermute | solution.py:18
  19.7 1.3 %collective-permute-done.5.refs_1_ = bf16[8,4224]{1,0:T(8,128)(2,1)S(1)} collective-permute-done((bf16[8,4224]{1,0:T(8,128)(2,1)S(1)}, bf16[8,4224]{1,0:T(8,128)(2,1)S(1)}, u32[]{:S(2)}, u32[]{:S(2)}) %collective-permute-start.5) | collective-permute-done | bytes 67616 | tf_op jit(solution)/shard_map/ppermute | solution.py:18
  21.0 2.9 %collective-permute-done.7.refs_3_ = bf16[8,4224]{1,0:T(8,128)(2,1)S(1)} collective-permute-done((bf16[8,4224]{1,0:T(8,128)(2,1)S(1)}, bf16[8,4224]{1,0:T(8,128)(2,1)S(1)}, u32[]{:S(2)}, u32[]{:S(2)}) %collective-permute-start.7) | collective-permute-done | bytes 67616 | tf_op jit(solution)/shard_map/ppermute | solution.py:18
  24.0 2.5 %collective-permute-start.10 = (bf16[8,4224]{1,0:T(8,128)(2,1)S(1)}, bf16[8,4224]{1,0:T(8,128)(2,1)S(1)}, u32[]{:S(2)}, u32[]{:S(2)}) collective-permute-start(bf16[8,4224]{1,0:T(8,128)(2,1)S(1)} %shard_map.72.refs_0_), channel_id=1, source_target_pairs={{0,24},{8,16},{16,8},{24,0},{1,25},{9,17},{17,9},{25,1},{2,26},{10... | collective-permute-start | bytes 202760 | tf_op jit(solution)/shard_map/ppermute | solution.py:18
  27.6 1.8 %collective-permute-done.10.refs_3_ = bf16[8,4224]{1,0:T(8,128)(2,1)S(1)} collective-permute-done((bf16[8,4224]{1,0:T(8,128)(2,1)S(1)}, bf16[8,4224]{1,0:T(8,128)(2,1)S(1)}, u32[]{:S(2)}, u32[]{:S(2)}) %collective-permute-start.10) | collective-permute-done | bytes 67616 | tf_op jit(solution)/shard_map/ppermute | solution.py:18
  29.4 1.4 %collective-permute-done.9.refs_2_ = bf16[8,4224]{1,0:T(8,128)(2,1)S(1)} collective-permute-done((bf16[8,4224]{1,0:T(8,128)(2,1)S(1)}, bf16[8,4224]{1,0:T(8,128)(2,1)S(1)}, u32[]{:S(2)}, u32[]{:S(2)}) %collective-permute-start.9) | collective-permute-done | bytes 67616 | tf_op jit(solution)/shard_map/ppermute | solution.py:18
  31.4 6.7 %shard_map.73 = (bf16[8,4096]{1,0:T(8,128)(2,1)S(1)}, f32[8,2048]{1,0:T(8,128)S(1)}, f32[8,128]{1,0:T(8,128)S(1)}) custom-call(bf16[8,4224]{1,0:T(8,128)(2,1)S(1)} %shard_map.72.refs_0_, bf16[8,4224]{1,0:T(8,128)(2,1)S(1)} %collective-permute-done.8.refs_1_, bf16[8,4224]{1,0:T(8,128)(2,1)S(1)} %collective-permute-done.9.refs_2_, ...), custom_call_target="tpu_custom_call" | custom-call | flops 10000000000 | bytes 4194304 | tf_op jit(solution)/shard_map/pallas_call | solution.py:40
  38.1 1.5 %collective-permute-start.13 = (bf16[8,4096]{1,0:T(8,128)(2,1)S(1)}, bf16[8,4096]{1,0:T(8,128)(2,1)S(1)}, u32[]{:S(2)}, u32[]{:S(2)}) collective-permute-start(bf16[8,4096]{1,0:T(8,128)(2,1)S(1)} %get-tuple-element.25.refs_0_), channel_id=1, source_target_pairs={{0,24},{8,16},{16,8},{24,0},{1,25},{9,17},{17,9},{25,1},{2,26},{10... | collective-permute-start | bytes 196616 | tf_op jit(solution)/shard_map/ppermute | solution.py:18
  40.1 1.5 %collective-permute-start.11 = (bf16[8,4096]{1,0:T(8,128)(2,1)S(1)}, bf16[8,4096]{1,0:T(8,128)(2,1)S(1)}, u32[]{:S(2)}, u32[]{:S(2)}) collective-permute-start(bf16[8,4096]{1,0:T(8,128)(2,1)S(1)} %get-tuple-element.25.refs_0_), channel_id=1, source_target_pairs={{0,8},{8,0},{16,24},{24,16},{1,9},{9,1},{17,25},{25,17},{2,10},{10... | collective-permute-start | bytes 196616 | tf_op jit(solution)/shard_map/ppermute | solution.py:18
  41.6 1.7 %collective-permute-done.13.refs_3_ = bf16[8,4096]{1,0:T(8,128)(2,1)S(1)} collective-permute-done((bf16[8,4096]{1,0:T(8,128)(2,1)S(1)}, bf16[8,4096]{1,0:T(8,128)(2,1)S(1)}, u32[]{:S(2)}, u32[]{:S(2)}) %collective-permute-start.13) | collective-permute-done | bytes 65568 | tf_op jit(solution)/shard_map/ppermute | solution.py:18
  44.5 2.6 %collective-permute-start.16 = (bf16[8,4224]{1,0:T(8,128)(2,1)S(1)}, bf16[8,4224]{1,0:T(8,128)(2,1)S(1)}, u32[]{:S(2)}, u32[]{:S(2)}) collective-permute-start(bf16[8,4224]{1,0:T(8,128)(2,1)S(1)} %shard_map.74.refs_0_), channel_id=1, source_target_pairs={{0,6},{1,7},{2,4},{3,5},{4,2},{5,3},{6,0},{7,1},{8,14},{9,15},{10,... | collective-permute-start | bytes 202760 | tf_op jit(solution)/shard_map/ppermute | solution.py:18
  47.7 1.2 %collective-permute-start.14 = (bf16[8,4224]{1,0:T(8,128)(2,1)S(1)}, bf16[8,4224]{1,0:T(8,128)(2,1)S(1)}, u32[]{:S(2)}, u32[]{:S(2)}) collective-permute-start(bf16[8,4224]{1,0:T(8,128)(2,1)S(1)} %shard_map.74.refs_0_), channel_id=1, source_target_pairs={{0,2},{1,3},{2,0},{3,1},{4,6},{5,7},{6,4},{7,5},{8,10},{9,11},{10,... | collective-permute-start | bytes 202760 | tf_op jit(solution)/shard_map/ppermute | solution.py:18
  48.9 2.4 %collective-permute-done.16.refs_3_ = bf16[8,4224]{1,0:T(8,128)(2,1)S(1)} collective-permute-done((bf16[8,4224]{1,0:T(8,128)(2,1)S(1)}, bf16[8,4224]{1,0:T(8,128)(2,1)S(1)}, u32[]{:S(2)}, u32[]{:S(2)}) %collective-permute-start.16) | collective-permute-done | bytes 67616 | tf_op jit(solution)/shard_map/ppermute | solution.py:18
  51.3 1.7 %collective-permute-done.15.refs_2_ = bf16[8,4224]{1,0:T(8,128)(2,1)S(1)} collective-permute-done((bf16[8,4224]{1,0:T(8,128)(2,1)S(1)}, bf16[8,4224]{1,0:T(8,128)(2,1)S(1)}, u32[]{:S(2)}, u32[]{:S(2)}) %collective-permute-start.15) | collective-permute-done | bytes 67616 | tf_op jit(solution)/shard_map/ppermute | solution.py:18
  53.1 1.5 %collective-permute-done.17.far = bf16[32,4224]{1,0:T(8,128)(2,1)S(1)} collective-permute-done((bf16[32,4224]{1,0:T(8,128)(2,1)S(1)}, bf16[32,4224]{1,0:T(8,128)(2,1)S(1)}, u32[]{:S(2)}, u32[]{:S(2)}) %collective-permute-start.17) | collective-permute-done | bytes 270368 | tf_op jit(solution)/shard_map/ppermute | solution.py:18
  54.6 1.6 %shard_map.76 = (bf16[128,256]{1,0:T(8,128)(2,1)S(1)}, bf16[32,2048]{1,0:T(8,128)(2,1)S(1)}, bf16[32,2048]{1,0:T(8,128)(2,1)S(1)}) custom-call(bf16[32,4224]{1,0:T(8,128)(2,1)S(1)} %shard_map.75.near, bf16[32,4224]{1,0:T(8,128)(2,1)S(1)} %collective-permute-done.17.far, f32[64,256]{1,0:T(8,128)S(1)} %get-tuple-element.28.logits, ...), custom_call_target="tpu_custom_call" | custom-call | flops 10000000000 | bytes 4194304 | tf_op jit(solution)/shard_map/pallas_call | solution.py:40
  56.4 1.2 %collective-permute-done.18.refs_1_ = bf16[32,2048]{1,0:T(8,128)(2,1)S(1)} collective-permute-done((bf16[32,2048]{1,0:T(8,128)(2,1)S(1)}, bf16[32,2048]{1,0:T(8,128)(2,1)S(1)}, u32[]{:S(2)}, u32[]{:S(2)}) %collective-permute-start.18) | collective-permute-done | bytes 131104 | tf_op jit(solution)/shard_map/ppermute | solution.py:18
  58.3 2.6 %collective-permute-start.20 = (bf16[8,2048]{1,0:T(8,128)(2,1)S(1)}, bf16[8,2048]{1,0:T(8,128)(2,1)S(1)}, u32[]{:S(2)}, u32[]{:S(2)}) collective-permute-start(bf16[8,2048]{1,0:T(8,128)(2,1)S(1)} %get-tuple-element.34), channel_id=1, source_target_pairs={{0,4},{1,5},{2,6},{3,7},{4,0},{5,1},{6,2},{7,3},{8,12},{9,13},{10,... | collective-permute-start | bytes 98312 | tf_op jit(solution)/shard_map/ppermute | solution.py:18
  60.9 1.3 %collective-permute-start.21 = (bf16[8,2048]{1,0:T(8,128)(2,1)S(1)}, bf16[8,2048]{1,0:T(8,128)(2,1)S(1)}, u32[]{:S(2)}, u32[]{:S(2)}) collective-permute-start(bf16[8,2048]{1,0:T(8,128)(2,1)S(1)} %get-tuple-element.35), channel_id=1, source_target_pairs={{0,6},{1,7},{2,4},{3,5},{4,2},{5,3},{6,0},{7,1},{8,14},{9,15},{10,... | collective-permute-start | bytes 98312 | tf_op jit(solution)/shard_map/ppermute | solution.py:18
  62.2 1.5 %collective-permute-done.20 = bf16[8,2048]{1,0:T(8,128)(2,1)S(1)} collective-permute-done((bf16[8,2048]{1,0:T(8,128)(2,1)S(1)}, bf16[8,2048]{1,0:T(8,128)(2,1)S(1)}, u32[]{:S(2)}, u32[]{:S(2)}) %collective-permute-start.20) | collective-permute-done | bytes 32800 | tf_op jit(solution)/shard_map/ppermute | solution.py:18
  63.6 3.0 %collective-permute-done.21 = bf16[8,2048]{1,0:T(8,128)(2,1)S(1)} collective-permute-done((bf16[8,2048]{1,0:T(8,128)(2,1)S(1)}, bf16[8,2048]{1,0:T(8,128)(2,1)S(1)}, u32[]{:S(2)}, u32[]{:S(2)}) %collective-permute-start.21) | collective-permute-done | bytes 32800 | tf_op jit(solution)/shard_map/ppermute | solution.py:18
  66.7 1.4 %collective-permute-start.22 = (bf16[8,512]{1,0:T(8,128)(2,1)S(1)}, bf16[8,512]{1,0:T(8,128)(2,1)S(1)}, u32[]{:S(2)}, u32[]{:S(2)}) collective-permute-start(bf16[8,512]{1,0:T(8,128)(2,1)S(1)} %get-tuple-element.36), channel_id=1, source_target_pairs={{0,8},{8,0},{16,24},{24,16},{1,9},{9,1},{17,25},{25,17},{2,10},{10... | collective-permute-start | bytes 24584 | tf_op jit(solution)/shard_map/ppermute | solution.py:18
  68.0 1.5 %collective-permute-start.24 = (bf16[8,512]{1,0:T(8,128)(2,1)S(1)}, bf16[8,512]{1,0:T(8,128)(2,1)S(1)}, u32[]{:S(2)}, u32[]{:S(2)}) collective-permute-start(bf16[8,512]{1,0:T(8,128)(2,1)S(1)} %get-tuple-element.37), channel_id=1, source_target_pairs={{0,24},{8,16},{16,8},{24,0},{1,25},{9,17},{17,9},{25,1},{2,26},{10... | collective-permute-start | bytes 24584 | tf_op jit(solution)/shard_map/ppermute | solution.py:18
  70.2 1.4 %shard_map.77 = bf16[256,2048]{1,0:T(8,128)(2,1)} custom-call(bf16[128,256]{1,0:T(8,128)(2,1)S(1)} %get-tuple-element.29.weights, bf16[32,4224]{1,0:T(8,128)(2,1)S(1)} %shard_map.75.near, bf16[32,4224]{1,0:T(8,128)(2,1)S(1)} %collective-permute-done.17.far, bf16[32,2048]{1,0:T(8,128)(2,1)S(1)} %shard_map.69.near.table_near, ...), custom_call_target="tpu_custom_call" | custom-call | flops 10000000000 | bytes 4194304 | tf_op jit(solution)/shard_map/pallas_call | solution.py:40
  71.6 0.9 %collective-permute-done.24 = bf16[8,512]{1,0:T(8,128)(2,1)S(1)} collective-permute-done((bf16[8,512]{1,0:T(8,128)(2,1)S(1)}, bf16[8,512]{1,0:T(8,128)(2,1)S(1)}, u32[]{:S(2)}, u32[]{:S(2)}) %collective-permute-start.24) | collective-permute-done | bytes 8224 | tf_op jit(solution)/shard_map/ppermute | solution.py:18
  (48 shorter events, 8.7 us)
Async XLA Ops:
  0.6 7.2 %collective-permute-start.2 = (bf16[8,2048]{1,0:T(8,128)(2,1)}, bf16[8,2048]{1,0:T(8,128)(2,1)S(1)}, u32[]{:S(2)}, u32[]{:S(2)}) collective-permute-start(bf16[8,2048]{1,0:T(8,128)(2,1)} %bitcast.7), channel_id=1, source_target_pairs={{0,6},{1,7},{2,4},{3,5},{4,2},{5,3},{6,0},{7,1},{8,14},{9,15},{10,... | collective-permute-start | bytes 98312 | tf_op jit(solution)/shard_map/ppermute | solution.py:18
  5.7 5.0 %collective-permute-start.1 = (bf16[8,2048]{1,0:T(8,128)(2,1)}, bf16[8,2048]{1,0:T(8,128)(2,1)S(1)}, u32[]{:S(2)}, u32[]{:S(2)}) collective-permute-start(bf16[8,2048]{1,0:T(8,128)(2,1)} %bitcast.8), channel_id=1, source_target_pairs={{0,4},{1,5},{2,6},{3,7},{4,0},{5,1},{6,2},{7,3},{8,12},{9,13},{10,... | collective-permute-start | bytes 98312 | tf_op jit(solution)/shard_map/ppermute | solution.py:18
  5.7 5.0 %collective-permute-start = (bf16[8,2048]{1,0:T(8,128)(2,1)}, bf16[8,2048]{1,0:T(8,128)(2,1)S(1)}, u32[]{:S(2)}, u32[]{:S(2)}) collective-permute-start(bf16[8,2048]{1,0:T(8,128)(2,1)} %bitcast.9), channel_id=1, source_target_pairs={{0,2},{1,3},{2,0},{3,1},{4,6},{5,7},{6,4},{7,5},{8,10},{9,11},{10,... | collective-permute-start | bytes 98312 | tf_op jit(solution)/shard_map/ppermute | solution.py:18
  6.4 0.8 %copy-start.2 = (bf16[2048,8]{0,1:T(8,128)(2,1)S(1)}, bf16[2048,8]{0,1:T(8,128)(2,1)}, u32[]{:S(2)}) copy-start(bf16[2048,8]{0,1:T(8,128)(2,1)} %param.6) | copy-start | bytes 98308
  7.2 5.0 %copy-start = (bf16[256,2048]{1,0:T(8,128)(2,1)S(1)}, bf16[256,2048]{1,0:T(8,128)(2,1)}, u32[]{:S(2)}) copy-start(bf16[256,2048]{1,0:T(8,128)(2,1)} %tokens.3) | copy-start | bytes 3145732
  7.2 5.0 %copy-start.1 = (bf16[256,2048]{1,0:T(8,128)(2,1)S(1)}, bf16[256,2048]{1,0:T(8,128)(2,1)}, u32[]{:S(2)}) copy-start(bf16[256,2048]{1,0:T(8,128)(2,1)} %out_grad.3) | copy-start | bytes 3145732
  10.8 1.4 %collective-permute-start.3 = (bf16[32,2048]{1,0:T(8,128)(2,1)S(1)}, bf16[32,2048]{1,0:T(8,128)(2,1)S(1)}, u32[]{:S(2)}, u32[]{:S(2)}) collective-permute-start(bf16[32,2048]{1,0:T(8,128)(2,1)S(1)} %shard_map.69.near.table_near), channel_id=1, source_target_pairs={{0,1},{1,0},{2,3},{3,2},{4,5},{5,4},{6,7},{7,6},{8,9},{9,8},{10,11... | collective-permute-start | bytes 393224 | tf_op jit(solution)/shard_map/ppermute | solution.py:18
  13.5 1.6 %collective-permute-start.4 = (bf16[32,4224]{1,0:T(8,128)(2,1)S(1)}, bf16[32,4224]{1,0:T(8,128)(2,1)S(1)}, u32[]{:S(2)}, u32[]{:S(2)}) collective-permute-start(bf16[32,4224]{1,0:T(8,128)(2,1)S(1)} %get-tuple-element.20), channel_id=1, source_target_pairs={{0,1},{1,0},{2,3},{3,2},{4,5},{5,4},{6,7},{7,6},{8,9},{9,8},{10,11... | collective-permute-start | bytes 811016 | tf_op jit(solution)/shard_map/ppermute | solution.py:18
  15.1 16.3 %slice-start = ((s8[8388608]{0:T(1024)(128)(4,1)}), s8[4194304]{0:T(1024)(128)(4,1)S(1)}, s32[]{:S(2)}) async-start(s8[8388608]{0:T(1024)(128)(4,1)} %bitcast.3), calls=%async_computation | async-start | bytes 8388608
  15.1 16.3 %slice-start.2 = ((s8[8388608]{0:T(1024)(128)(4,1)}), s8[4194304]{0:T(1024)(128)(4,1)S(1)}, s32[]{:S(2)}) async-start(s8[8388608]{0:T(1024)(128)(4,1)} %bitcast.5), calls=%async_computation.2 | async-start | bytes 8388608
  15.2 5.8 %collective-permute-start.5 = (bf16[8,4224]{1,0:T(8,128)(2,1)S(1)}, bf16[8,4224]{1,0:T(8,128)(2,1)S(1)}, u32[]{:S(2)}, u32[]{:S(2)}) collective-permute-start(bf16[8,4224]{1,0:T(8,128)(2,1)S(1)} %get-tuple-element.22), channel_id=1, source_target_pairs={{0,2},{1,3},{2,0},{3,1},{4,6},{5,7},{6,4},{7,5},{8,10},{9,11},{10,... | collective-permute-start | bytes 202760 | tf_op jit(solution)/shard_map/ppermute | solution.py:18
  15.3 16.0 %slice-start.1 = ((s8[8388608]{0:T(1024)(128)(4,1)}), s8[4194304]{0:T(1024)(128)(4,1)S(1)}, s32[]{:S(2)}) async-start(s8[8388608]{0:T(1024)(128)(4,1)} %bitcast.3), calls=%async_computation.1 | async-start | bytes 8388608
  15.3 16.0 %slice-start.3 = ((s8[8388608]{0:T(1024)(128)(4,1)}), s8[4194304]{0:T(1024)(128)(4,1)S(1)}, s32[]{:S(2)}) async-start(s8[8388608]{0:T(1024)(128)(4,1)} %bitcast.5), calls=%async_computation.3 | async-start | bytes 8388608
  15.3 5.7 %collective-permute-start.6 = (bf16[8,4224]{1,0:T(8,128)(2,1)S(1)}, bf16[8,4224]{1,0:T(8,128)(2,1)S(1)}, u32[]{:S(2)}, u32[]{:S(2)}) collective-permute-start(bf16[8,4224]{1,0:T(8,128)(2,1)S(1)} %get-tuple-element.23), channel_id=1, source_target_pairs={{0,4},{1,5},{2,6},{3,7},{4,0},{5,1},{6,2},{7,3},{8,12},{9,13},{10,... | collective-permute-start | bytes 202760 | tf_op jit(solution)/shard_map/ppermute | solution.py:18
  17.4 6.5 %collective-permute-start.7 = (bf16[8,4224]{1,0:T(8,128)(2,1)S(1)}, bf16[8,4224]{1,0:T(8,128)(2,1)S(1)}, u32[]{:S(2)}, u32[]{:S(2)}) collective-permute-start(bf16[8,4224]{1,0:T(8,128)(2,1)S(1)} %get-tuple-element.24), channel_id=1, source_target_pairs={{0,6},{1,7},{2,4},{3,5},{4,2},{5,3},{6,0},{7,1},{8,14},{9,15},{10,... | collective-permute-start | bytes 202760 | tf_op jit(solution)/shard_map/ppermute | solution.py:18
  24.0 5.4 %collective-permute-start.10 = (bf16[8,4224]{1,0:T(8,128)(2,1)S(1)}, bf16[8,4224]{1,0:T(8,128)(2,1)S(1)}, u32[]{:S(2)}, u32[]{:S(2)}) collective-permute-start(bf16[8,4224]{1,0:T(8,128)(2,1)S(1)} %shard_map.72.refs_0_), channel_id=1, source_target_pairs={{0,24},{8,16},{16,8},{24,0},{1,25},{9,17},{17,9},{25,1},{2,26},{10... | collective-permute-start | bytes 202760 | tf_op jit(solution)/shard_map/ppermute | solution.py:18
  26.5 4.3 %collective-permute-start.9 = (bf16[8,4224]{1,0:T(8,128)(2,1)S(1)}, bf16[8,4224]{1,0:T(8,128)(2,1)S(1)}, u32[]{:S(2)}, u32[]{:S(2)}) collective-permute-start(bf16[8,4224]{1,0:T(8,128)(2,1)S(1)} %shard_map.72.refs_0_), channel_id=1, source_target_pairs={{0,16},{8,24},{16,0},{24,8},{1,17},{9,25},{17,1},{25,9},{2,18},{10... | collective-permute-start | bytes 202760 | tf_op jit(solution)/shard_map/ppermute | solution.py:18
  27.0 4.3 %collective-permute-start.8 = (bf16[8,4224]{1,0:T(8,128)(2,1)S(1)}, bf16[8,4224]{1,0:T(8,128)(2,1)S(1)}, u32[]{:S(2)}, u32[]{:S(2)}) collective-permute-start(bf16[8,4224]{1,0:T(8,128)(2,1)S(1)} %shard_map.72.refs_0_), channel_id=1, source_target_pairs={{0,8},{8,0},{16,24},{24,16},{1,9},{9,1},{17,25},{25,17},{2,10},{10... | collective-permute-start | bytes 202760 | tf_op jit(solution)/shard_map/ppermute | solution.py:18
  38.1 5.2 %collective-permute-start.13 = (bf16[8,4096]{1,0:T(8,128)(2,1)S(1)}, bf16[8,4096]{1,0:T(8,128)(2,1)S(1)}, u32[]{:S(2)}, u32[]{:S(2)}) collective-permute-start(bf16[8,4096]{1,0:T(8,128)(2,1)S(1)} %get-tuple-element.25.refs_0_), channel_id=1, source_target_pairs={{0,24},{8,16},{16,8},{24,0},{1,25},{9,17},{17,9},{25,1},{2,26},{10... | collective-permute-start | bytes 196616 | tf_op jit(solution)/shard_map/ppermute | solution.py:18
  39.6 4.4 %collective-permute-start.12 = (bf16[8,4096]{1,0:T(8,128)(2,1)S(1)}, bf16[8,4096]{1,0:T(8,128)(2,1)S(1)}, u32[]{:S(2)}, u32[]{:S(2)}) collective-permute-start(bf16[8,4096]{1,0:T(8,128)(2,1)S(1)} %get-tuple-element.25.refs_0_), channel_id=1, source_target_pairs={{0,16},{8,24},{16,0},{24,8},{1,17},{9,25},{17,1},{25,9},{2,18},{10... | collective-permute-start | bytes 196616 | tf_op jit(solution)/shard_map/ppermute | solution.py:18
  40.1 4.3 %collective-permute-start.11 = (bf16[8,4096]{1,0:T(8,128)(2,1)S(1)}, bf16[8,4096]{1,0:T(8,128)(2,1)S(1)}, u32[]{:S(2)}, u32[]{:S(2)}) collective-permute-start(bf16[8,4096]{1,0:T(8,128)(2,1)S(1)} %get-tuple-element.25.refs_0_), channel_id=1, source_target_pairs={{0,8},{8,0},{16,24},{24,16},{1,9},{9,1},{17,25},{25,17},{2,10},{10... | collective-permute-start | bytes 196616 | tf_op jit(solution)/shard_map/ppermute | solution.py:18
  44.5 6.8 %collective-permute-start.16 = (bf16[8,4224]{1,0:T(8,128)(2,1)S(1)}, bf16[8,4224]{1,0:T(8,128)(2,1)S(1)}, u32[]{:S(2)}, u32[]{:S(2)}) collective-permute-start(bf16[8,4224]{1,0:T(8,128)(2,1)S(1)} %shard_map.74.refs_0_), channel_id=1, source_target_pairs={{0,6},{1,7},{2,4},{3,5},{4,2},{5,3},{6,0},{7,1},{8,14},{9,15},{10,... | collective-permute-start | bytes 202760 | tf_op jit(solution)/shard_map/ppermute | solution.py:18
  47.1 5.9 %collective-permute-start.15 = (bf16[8,4224]{1,0:T(8,128)(2,1)S(1)}, bf16[8,4224]{1,0:T(8,128)(2,1)S(1)}, u32[]{:S(2)}, u32[]{:S(2)}) collective-permute-start(bf16[8,4224]{1,0:T(8,128)(2,1)S(1)} %shard_map.74.refs_0_), channel_id=1, source_target_pairs={{0,4},{1,5},{2,6},{3,7},{4,0},{5,1},{6,2},{7,3},{8,12},{9,13},{10,... | collective-permute-start | bytes 202760 | tf_op jit(solution)/shard_map/ppermute | solution.py:18
  47.7 5.3 %collective-permute-start.14 = (bf16[8,4224]{1,0:T(8,128)(2,1)S(1)}, bf16[8,4224]{1,0:T(8,128)(2,1)S(1)}, u32[]{:S(2)}, u32[]{:S(2)}) collective-permute-start(bf16[8,4224]{1,0:T(8,128)(2,1)S(1)} %shard_map.74.refs_0_), channel_id=1, source_target_pairs={{0,2},{1,3},{2,0},{3,1},{4,6},{5,7},{6,4},{7,5},{8,10},{9,11},{10,... | collective-permute-start | bytes 202760 | tf_op jit(solution)/shard_map/ppermute | solution.py:18
  53.0 1.6 %collective-permute-start.17 = (bf16[32,4224]{1,0:T(8,128)(2,1)S(1)}, bf16[32,4224]{1,0:T(8,128)(2,1)S(1)}, u32[]{:S(2)}, u32[]{:S(2)}) collective-permute-start(bf16[32,4224]{1,0:T(8,128)(2,1)S(1)} %shard_map.75.near), channel_id=1, source_target_pairs={{0,1},{1,0},{2,3},{3,2},{4,5},{5,4},{6,7},{7,6},{8,9},{9,8},{10,11... | collective-permute-start | bytes 811016 | tf_op jit(solution)/shard_map/ppermute | solution.py:18
  56.2 1.4 %collective-permute-start.18 = (bf16[32,2048]{1,0:T(8,128)(2,1)S(1)}, bf16[32,2048]{1,0:T(8,128)(2,1)S(1)}, u32[]{:S(2)}, u32[]{:S(2)}) collective-permute-start(bf16[32,2048]{1,0:T(8,128)(2,1)S(1)} %get-tuple-element.31), channel_id=1, source_target_pairs={{0,1},{1,0},{2,3},{3,2},{4,5},{5,4},{6,7},{7,6},{8,9},{9,8},{10,11... | collective-permute-start | bytes 393224 | tf_op jit(solution)/shard_map/ppermute | solution.py:18
  57.7 4.5 %collective-permute-start.19 = (bf16[8,2048]{1,0:T(8,128)(2,1)S(1)}, bf16[8,2048]{1,0:T(8,128)(2,1)S(1)}, u32[]{:S(2)}, u32[]{:S(2)}) collective-permute-start(bf16[8,2048]{1,0:T(8,128)(2,1)S(1)} %get-tuple-element.33), channel_id=1, source_target_pairs={{0,2},{1,3},{2,0},{3,1},{4,6},{5,7},{6,4},{7,5},{8,10},{9,11},{10,... | collective-permute-start | bytes 98312 | tf_op jit(solution)/shard_map/ppermute | solution.py:18
  58.3 5.4 %collective-permute-start.20 = (bf16[8,2048]{1,0:T(8,128)(2,1)S(1)}, bf16[8,2048]{1,0:T(8,128)(2,1)S(1)}, u32[]{:S(2)}, u32[]{:S(2)}) collective-permute-start(bf16[8,2048]{1,0:T(8,128)(2,1)S(1)} %get-tuple-element.34), channel_id=1, source_target_pairs={{0,4},{1,5},{2,6},{3,7},{4,0},{5,1},{6,2},{7,3},{8,12},{9,13},{10,... | collective-permute-start | bytes 98312 | tf_op jit(solution)/shard_map/ppermute | solution.py:18
  60.9 5.7 %collective-permute-start.21 = (bf16[8,2048]{1,0:T(8,128)(2,1)S(1)}, bf16[8,2048]{1,0:T(8,128)(2,1)S(1)}, u32[]{:S(2)}, u32[]{:S(2)}) collective-permute-start(bf16[8,2048]{1,0:T(8,128)(2,1)S(1)} %get-tuple-element.35), channel_id=1, source_target_pairs={{0,6},{1,7},{2,4},{3,5},{4,2},{5,3},{6,0},{7,1},{8,14},{9,15},{10,... | collective-permute-start | bytes 98312 | tf_op jit(solution)/shard_map/ppermute | solution.py:18
  66.7 5.0 %collective-permute-start.22 = (bf16[8,512]{1,0:T(8,128)(2,1)S(1)}, bf16[8,512]{1,0:T(8,128)(2,1)S(1)}, u32[]{:S(2)}, u32[]{:S(2)}) collective-permute-start(bf16[8,512]{1,0:T(8,128)(2,1)S(1)} %get-tuple-element.36), channel_id=1, source_target_pairs={{0,8},{8,0},{16,24},{24,16},{1,9},{9,1},{17,25},{25,17},{2,10},{10... | collective-permute-start | bytes 24584 | tf_op jit(solution)/shard_map/ppermute | solution.py:18
  68.0 4.5 %collective-permute-start.24 = (bf16[8,512]{1,0:T(8,128)(2,1)S(1)}, bf16[8,512]{1,0:T(8,128)(2,1)S(1)}, u32[]{:S(2)}, u32[]{:S(2)}) collective-permute-start(bf16[8,512]{1,0:T(8,128)(2,1)S(1)} %get-tuple-element.37), channel_id=1, source_target_pairs={{0,24},{8,16},{16,8},{24,0},{1,25},{9,17},{17,9},{25,1},{2,26},{10... | collective-permute-start | bytes 24584 | tf_op jit(solution)/shard_map/ppermute | solution.py:18
  69.5 3.7 %collective-permute-start.23 = (bf16[8,512]{1,0:T(8,128)(2,1)S(1)}, bf16[8,512]{1,0:T(8,128)(2,1)S(1)}, u32[]{:S(2)}, u32[]{:S(2)}) collective-permute-start(bf16[8,512]{1,0:T(8,128)(2,1)S(1)} %get-tuple-element.38), channel_id=1, source_target_pairs={{0,16},{8,24},{16,0},{24,8},{1,17},{9,25},{17,1},{25,9},{2,18},{10... | collective-permute-start | bytes 24584 | tf_op jit(solution)/shard_map/ppermute | solution.py:18

commit v4 on v3

--- a/solution.py
+++ b/solution.py
@@ -230,7 +230,7 @@
     out[:, 2 * width :] = packed([centre, top, denominator], stats.shape[0]).astype(BF16)
 
 
-def second_kernel(near, far, logits, tokens, out_grad, weights, keep, send):
+def second_kernel(order, near, far, logits, tokens, out_grad, weights, blocks):
     width = tokens.shape[1]
     half = near.shape[0]
 
@@ -252,8 +252,14 @@
     weights[: 2 * half] = dispatch.astype(BF16)
     weights[2 * half :] = logit_b
     part = product(logit_b, tokens[...], 1, 0).astype(BF16)
-    keep[...] = part[:half]
-    send[...] = part[half:]
+    me = lax.axis_index("exp")
+    n_seq, n_exp = lax.axis_size("seq"), lax.axis_size("exp")
+    _, rows, share = blocks.shape
+    for k, mask in enumerate(order):
+        for s in range(n_seq):
+            blocks[s * n_exp + (me ^ mask)] = part[
+                k * rows : (k + 1) * rows, s * share : (s + 1) * share
+            ]
 
 
 def patch_kernel(weights, near, far, table_near, table_far, out):
@@ -323,9 +329,13 @@
     near = gathered_over_chips(packet, packet)
     far = swap(near, "exp", 1)
 
-    weights, keep, send = local_call(
-        second_kernel,
-        [((2 * slots, patches), BF16), ((half, width), BF16), ((half, width), BF16)],
+    order = [0]
+    for masks in reversed(chip_groups):
+        order = [r ^ mask for mask in (0, *masks) for r in order]
+    order = order + [r ^ 1 for r in order]
+    weights, blocks = local_call(
+        partial(second_kernel, order),
+        [((2 * slots, patches), BF16), ((n_seq * n_exp, own, width // n_seq), BF16)],
         near,
         far,
         logits,
@@ -345,27 +355,8 @@
         to_hbm=(0,),
     )
 
-    parts = [keep, swap(send, "exp", 1)]
-    for masks in chip_groups:
-        pieces = sum_of(parts, len(masks) + 1, BF16)
-        parts = [pieces[0]] + swaps(pieces[1:], "exp", masks)
-    part = sum(p.astype(F32) for p in parts)
-    me = lax.axis_index("seq")
-    share = width // n_seq
-    for masks in reversed(seq_groups):
-        base = me & (min(masks) - 1)
-        count = len(masks) + 1
-        span = part.shape[1] // count
-        low = min(masks)
-        mine = (me // low) % count
-
-        def block(mask):
-            at = mine ^ (mask // low)
-            return lax.dynamic_slice_in_dim(part, at * span, span, axis=1)
-
-        part = block(0) + sum(
-            swap(block(mask).astype(BF16), "seq", mask).astype(F32) for mask in masks
-        )
+    part = lax.all_to_all(blocks, ("seq", "exp"), 0, 0, tiled=True)
+    part = jnp.sum(part.astype(F32), axis=0)
     return (tok_grad, part.T)
 
 

time: 74 us -> 72.9 us (0.985)
  starting transfers between devices: 30.2 us -> 26.7 us
  waiting for transfers between devices: 29.9 us -> 31.6 us
    all_to_all x0 -> x1, waiting for transfers between devices: none -> 8.95 us  [shards(): part = lax.all_to_all(blocks, ('seq', 'exp'), 0, 0, tiled=True)]
    ppermute x25 -> x18, starting transfers between devices: 30.2 us -> 22 us  [swap(): lax.ppermute(x, axis, [(k, k ^ mask) for k in range(lax.axis_size(axis))])]
    ppermute x25 -> x18, waiting for transfers between devices: 29.9 us -> 22.7 us  [swap(): lax.ppermute(x, axis, [(k, k ^ mask) for k in range(lax.axis_size(axis))])]
    all_to_all x0 -> x1, starting transfers between devices: none -> 4.64 us  [shards(): part = lax.all_to_all(blocks, ('seq', 'exp'), 0, 0, tiled=True)]
    pallas_call x10 -> x9, Pallas kernels: 11.4 us -> 12.1 us  [local_call(): pl.pallas_call(body, out_shape=tuple((jax.ShapeDtypeStruct(s, d) if k in...]
  transfers between devices with their start and end apart: 25 -> 19, of which waited for: 20 -> 16; matrix products, arithmetic and copies ran while one was open for 0% -> 0% of each run, Pallas kernels for 2% -> 2%
where the time goes in v4:
time: 72.9 us; the launch traced here: 72.6 us
  waiting for transfers between devices  31.6 us (43%)
  starting transfers between devices  26.7 us (37%)
  Pallas kernels  12.1 us (17%)
  local copies, waits for them, and re-layouts  0.83 us (1%)
  between operations  0.78 us (1%)
    ppermute x18, waiting for transfers between devices, swap(): lax.ppermute(x, axis, [(k, k ^ mask) for k in range(lax.axis_size(axis))])  22.7 us
    ppermute x18, starting transfers between devices, swap(): lax.ppermute(x, axis, [(k, k ^ mask) for k in range(lax.axis_size(axis))])  22 us
    pallas_call x9, Pallas kernels, local_call(): pl.pallas_call(body, out_shape=tuple((jax.ShapeDtypeStruct(s, d) if k in...  12.1 us
    all_to_all x1, waiting for transfers between devices, shards(): part = lax.all_to_all(blocks, ('seq', 'exp'), 0, 0, tiled=True)  8.95 us
    all_to_all x1, starting transfers between devices, shards(): part = lax.all_to_all(blocks, ('seq', 'exp'), 0, 0, tiled=True)  4.64 us
  transfers between devices with their start and end apart: 19, of which 16 were waited for; matrix products, arithmetic and copies ran while one was open for 0% of the time, Pallas kernels for 2%

profile of v4, /device:TPU:0, one launch (start us, length us, event | category | flops | bytes accessed | tf_op | source)
XLA Modules:
  0.0 72.6 jit_solution(14504368207042591052)
XLA Ops:
  0.6 5.1 %collective-permute-start.2 = (bf16[8,2048]{1,0:T(8,128)(2,1)}, bf16[8,2048]{1,0:T(8,128)(2,1)S(1)}, u32[]{:S(2)}, u32[]{:S(2)}) collective-permute-start(bf16[8,2048]{1,0:T(8,128)(2,1)} %bitcast.6), channel_id=1, source_target_pairs={{0,6},{1,7},{2,4},{3,5},{4,2},{5,3},{6,0},{7,1},{8,14},{9,15},{10,... | collective-permute-start | bytes 98312 | tf_op jit(solution)/shard_map/ppermute | solution.py:18
  5.7 0.6 collective-permute-start
  6.4 0.8 %copy-done.2 = bf16[2048,8]{0,1:T(8,128)(2,1)S(1)} copy-done((bf16[2048,8]{0,1:T(8,128)(2,1)S(1)}, bf16[2048,8]{0,1:T(8,128)(2,1)}, u32[]{:S(2)}) %copy-start.2) | copy-done | bytes 32792
  7.2 0.6 collective-permute-done.2.refs_3_
  7.8 2.9 %collective-permute-done.1.refs_2_ = bf16[8,2048]{1,0:T(8,128)(2,1)S(1)} collective-permute-done((bf16[8,2048]{1,0:T(8,128)(2,1)}, bf16[8,2048]{1,0:T(8,128)(2,1)S(1)}, u32[]{:S(2)}, u32[]{:S(2)}) %collective-permute-start.1) | collective-permute-done | bytes 32800 | tf_op jit(solution)/shard_map/ppermute | solution.py:18
  10.9 1.3 %collective-permute-done.3.far.table_far = bf16[32,2048]{1,0:T(8,128)(2,1)S(1)} collective-permute-done((bf16[32,2048]{1,0:T(8,128)(2,1)S(1)}, bf16[32,2048]{1,0:T(8,128)(2,1)S(1)}, u32[]{:S(2)}, u32[]{:S(2)}) %collective-permute-start.3) | collective-permute-done | bytes 131104 | tf_op jit(solution)/shard_map/ppermute | solution.py:18
  12.2 1.2 %shard_map.70 = (f32[64,256]{1,0:T(8,128)S(1)}, bf16[32,4224]{1,0:T(8,128)(2,1)S(1)}, bf16[32,4224]{1,0:T(8,128)(2,1)S(1)}) custom-call(bf16[32,2048]{1,0:T(8,128)(2,1)S(1)} %shard_map.69.near.table_near, bf16[32,2048]{1,0:T(8,128)(2,1)S(1)} %collective-permute-done.3.far.table_far, bf16[256,2048]{1,0:T(8,128)(2,1)S(1)} %copy-done, ...), custom_call_target="tpu_custom_call" | custom-call | flops 10000000000 | bytes 4194304 | tf_op jit(solution)/shard_map/pallas_call | solution.py:40
  13.7 1.4 %collective-permute-done.4.refs_1_ = bf16[32,4224]{1,0:T(8,128)(2,1)S(1)} collective-permute-done((bf16[32,4224]{1,0:T(8,128)(2,1)S(1)}, bf16[32,4224]{1,0:T(8,128)(2,1)S(1)}, u32[]{:S(2)}, u32[]{:S(2)}) %collective-permute-start.4) | collective-permute-done | bytes 270368 | tf_op jit(solution)/shard_map/ppermute | solution.py:18
  15.3 2.1 %collective-permute-start.6 = (bf16[8,4224]{1,0:T(8,128)(2,1)S(1)}, bf16[8,4224]{1,0:T(8,128)(2,1)S(1)}, u32[]{:S(2)}, u32[]{:S(2)}) collective-permute-start(bf16[8,4224]{1,0:T(8,128)(2,1)S(1)} %get-tuple-element.18), channel_id=1, source_target_pairs={{0,4},{1,5},{2,6},{3,7},{4,0},{5,1},{6,2},{7,3},{8,12},{9,13},{10,... | collective-permute-start | bytes 202760 | tf_op jit(solution)/shard_map/ppermute | solution.py:18
  17.4 2.3 %collective-permute-start.7 = (bf16[8,4224]{1,0:T(8,128)(2,1)S(1)}, bf16[8,4224]{1,0:T(8,128)(2,1)S(1)}, u32[]{:S(2)}, u32[]{:S(2)}) collective-permute-start(bf16[8,4224]{1,0:T(8,128)(2,1)S(1)} %get-tuple-element.19), channel_id=1, source_target_pairs={{0,6},{1,7},{2,4},{3,5},{4,2},{5,3},{6,0},{7,1},{8,14},{9,15},{10,... | collective-permute-start | bytes 202760 | tf_op jit(solution)/shard_map/ppermute | solution.py:18
  19.7 1.3 %collective-permute-done.5.refs_1_ = bf16[8,4224]{1,0:T(8,128)(2,1)S(1)} collective-permute-done((bf16[8,4224]{1,0:T(8,128)(2,1)S(1)}, bf16[8,4224]{1,0:T(8,128)(2,1)S(1)}, u32[]{:S(2)}, u32[]{:S(2)}) %collective-permute-start.5) | collective-permute-done | bytes 67616 | tf_op jit(solution)/shard_map/ppermute | solution.py:18
  21.0 2.9 %collective-permute-done.7.refs_3_ = bf16[8,4224]{1,0:T(8,128)(2,1)S(1)} collective-permute-done((bf16[8,4224]{1,0:T(8,128)(2,1)S(1)}, bf16[8,4224]{1,0:T(8,128)(2,1)S(1)}, u32[]{:S(2)}, u32[]{:S(2)}) %collective-permute-start.7) | collective-permute-done | bytes 67616 | tf_op jit(solution)/shard_map/ppermute | solution.py:18
  24.0 2.5 %collective-permute-start.10 = (bf16[8,4224]{1,0:T(8,128)(2,1)S(1)}, bf16[8,4224]{1,0:T(8,128)(2,1)S(1)}, u32[]{:S(2)}, u32[]{:S(2)}) collective-permute-start(bf16[8,4224]{1,0:T(8,128)(2,1)S(1)} %shard_map.72.refs_0_), channel_id=1, source_target_pairs={{0,24},{8,16},{16,8},{24,0},{1,25},{9,17},{17,9},{25,1},{2,26},{10... | collective-permute-start | bytes 202760 | tf_op jit(solution)/shard_map/ppermute | solution.py:18
  27.0 0.5 collective-permute-start.8
  27.6 1.8 %collective-permute-done.10.refs_3_ = bf16[8,4224]{1,0:T(8,128)(2,1)S(1)} collective-permute-done((bf16[8,4224]{1,0:T(8,128)(2,1)S(1)}, bf16[8,4224]{1,0:T(8,128)(2,1)S(1)}, u32[]{:S(2)}, u32[]{:S(2)}) %collective-permute-start.10) | collective-permute-done | bytes 67616 | tf_op jit(solution)/shard_map/ppermute | solution.py:18
  29.4 1.4 %collective-permute-done.9.refs_2_ = bf16[8,4224]{1,0:T(8,128)(2,1)S(1)} collective-permute-done((bf16[8,4224]{1,0:T(8,128)(2,1)S(1)}, bf16[8,4224]{1,0:T(8,128)(2,1)S(1)}, u32[]{:S(2)}, u32[]{:S(2)}) %collective-permute-start.9) | collective-permute-done | bytes 67616 | tf_op jit(solution)/shard_map/ppermute | solution.py:18
  31.4 6.7 %shard_map.73 = (bf16[8,4096]{1,0:T(8,128)(2,1)S(1)}, f32[8,2048]{1,0:T(8,128)S(1)}, f32[8,128]{1,0:T(8,128)S(1)}) custom-call(bf16[8,4224]{1,0:T(8,128)(2,1)S(1)} %shard_map.72.refs_0_, bf16[8,4224]{1,0:T(8,128)(2,1)S(1)} %collective-permute-done.8.refs_1_, bf16[8,4224]{1,0:T(8,128)(2,1)S(1)} %collective-permute-done.9.refs_2_, ...), custom_call_target="tpu_custom_call" | custom-call | flops 10000000000 | bytes 4194304 | tf_op jit(solution)/shard_map/pallas_call | solution.py:40
  38.1 1.5 %collective-permute-start.13 = (bf16[8,4096]{1,0:T(8,128)(2,1)S(1)}, bf16[8,4096]{1,0:T(8,128)(2,1)S(1)}, u32[]{:S(2)}, u32[]{:S(2)}) collective-permute-start(bf16[8,4096]{1,0:T(8,128)(2,1)S(1)} %get-tuple-element.20.refs_0_), channel_id=1, source_target_pairs={{0,24},{8,16},{16,8},{24,0},{1,25},{9,17},{17,9},{25,1},{2,26},{10... | collective-permute-start | bytes 196616 | tf_op jit(solution)/shard_map/ppermute | solution.py:18
  40.1 1.5 %collective-permute-start.11 = (bf16[8,4096]{1,0:T(8,128)(2,1)S(1)}, bf16[8,4096]{1,0:T(8,128)(2,1)S(1)}, u32[]{:S(2)}, u32[]{:S(2)}) collective-permute-start(bf16[8,4096]{1,0:T(8,128)(2,1)S(1)} %get-tuple-element.20.refs_0_), channel_id=1, source_target_pairs={{0,8},{8,0},{16,24},{24,16},{1,9},{9,1},{17,25},{25,17},{2,10},{10... | collective-permute-start | bytes 196616 | tf_op jit(solution)/shard_map/ppermute | solution.py:18
  41.6 1.7 %collective-permute-done.13.refs_3_ = bf16[8,4096]{1,0:T(8,128)(2,1)S(1)} collective-permute-done((bf16[8,4096]{1,0:T(8,128)(2,1)S(1)}, bf16[8,4096]{1,0:T(8,128)(2,1)S(1)}, u32[]{:S(2)}, u32[]{:S(2)}) %collective-permute-start.13) | collective-permute-done | bytes 65568 | tf_op jit(solution)/shard_map/ppermute | solution.py:18
  43.2 0.7 collective-permute-done.12.refs_2_
  44.5 2.6 %collective-permute-start.16 = (bf16[8,4224]{1,0:T(8,128)(2,1)S(1)}, bf16[8,4224]{1,0:T(8,128)(2,1)S(1)}, u32[]{:S(2)}, u32[]{:S(2)}) collective-permute-start(bf16[8,4224]{1,0:T(8,128)(2,1)S(1)} %shard_map.74.refs_0_), channel_id=1, source_target_pairs={{0,6},{1,7},{2,4},{3,5},{4,2},{5,3},{6,0},{7,1},{8,14},{9,15},{10,... | collective-permute-start | bytes 202760 | tf_op jit(solution)/shard_map/ppermute | solution.py:18
  47.1 0.6 collective-permute-start.15
  47.7 1.2 %collective-permute-start.14 = (bf16[8,4224]{1,0:T(8,128)(2,1)S(1)}, bf16[8,4224]{1,0:T(8,128)(2,1)S(1)}, u32[]{:S(2)}, u32[]{:S(2)}) collective-permute-start(bf16[8,4224]{1,0:T(8,128)(2,1)S(1)} %shard_map.74.refs_0_), channel_id=1, source_target_pairs={{0,2},{1,3},{2,0},{3,1},{4,6},{5,7},{6,4},{7,5},{8,10},{9,11},{10,... | collective-permute-start | bytes 202760 | tf_op jit(solution)/shard_map/ppermute | solution.py:18
  48.9 2.4 %collective-permute-done.16.refs_3_ = bf16[8,4224]{1,0:T(8,128)(2,1)S(1)} collective-permute-done((bf16[8,4224]{1,0:T(8,128)(2,1)S(1)}, bf16[8,4224]{1,0:T(8,128)(2,1)S(1)}, u32[]{:S(2)}, u32[]{:S(2)}) %collective-permute-start.16) | collective-permute-done | bytes 67616 | tf_op jit(solution)/shard_map/ppermute | solution.py:18
  51.3 1.7 %collective-permute-done.15.refs_2_ = bf16[8,4224]{1,0:T(8,128)(2,1)S(1)} collective-permute-done((bf16[8,4224]{1,0:T(8,128)(2,1)S(1)}, bf16[8,4224]{1,0:T(8,128)(2,1)S(1)}, u32[]{:S(2)}, u32[]{:S(2)}) %collective-permute-start.15) | collective-permute-done | bytes 67616 | tf_op jit(solution)/shard_map/ppermute | solution.py:18
  53.1 1.5 %collective-permute-done.17.far = bf16[32,4224]{1,0:T(8,128)(2,1)S(1)} collective-permute-done((bf16[32,4224]{1,0:T(8,128)(2,1)S(1)}, bf16[32,4224]{1,0:T(8,128)(2,1)S(1)}, u32[]{:S(2)}, u32[]{:S(2)}) %collective-permute-start.17) | collective-permute-done | bytes 270368 | tf_op jit(solution)/shard_map/ppermute | solution.py:18
  54.6 2.3 %shard_map.76 = (bf16[128,256]{1,0:T(8,128)(2,1)S(1)}, bf16[32,8,512]{2,1,0:T(8,128)(2,1)}) custom-call(bf16[32,4224]{1,0:T(8,128)(2,1)S(1)} %shard_map.75.near, bf16[32,4224]{1,0:T(8,128)(2,1)S(1)} %collective-permute-done.17.far, f32[64,256]{1,0:T(8,128)S(1)} %get-tuple-element.23.logits, bf16[256,2048]{1,0:T(8,128)(2,1)S(1)} %copy-done, ...), custom_call_target="tpu_custom_call" | custom-call | flops 10000000000 | bytes 4194304 | tf_op jit(solution)/shard_map/pallas_call | solution.py:40
  56.9 4.6 %all-to-all-start = ((bf16[32,8,512]{2,1,0:T(8,128)(2,1)}), bf16[32,8,512]{2,1,0:T(8,128)(2,1)S(1)}, u32[]{:S(2)}, u32[]{:S(2)}) async-start(bf16[32,8,512]{2,1,0:T(8,128)(2,1)} %get-tuple-element.25), calls=%async_computation | async-start | bytes 524288 | tf_op jit(solution)/shard_map/all_to_all | solution.py:358
  61.6 1.4 %shard_map.77 = bf16[256,2048]{1,0:T(8,128)(2,1)} custom-call(bf16[128,256]{1,0:T(8,128)(2,1)S(1)} %get-tuple-element.24.weights, bf16[32,4224]{1,0:T(8,128)(2,1)S(1)} %shard_map.75.near, bf16[32,4224]{1,0:T(8,128)(2,1)S(1)} %collective-permute-done.17.far, bf16[32,2048]{1,0:T(8,128)(2,1)S(1)} %shard_map.69.near.table_near, ...), custom_call_target="tpu_custom_call" | custom-call | flops 10000000000 | bytes 4194304 | tf_op jit(solution)/shard_map/pallas_call | solution.py:40
  63.0 8.9 %all-to-all-done = bf16[32,8,512]{2,1,0:T(8,128)(2,1)S(1)} async-done(((bf16[32,8,512]{2,1,0:T(8,128)(2,1)}), bf16[32,8,512]{2,1,0:T(8,128)(2,1)S(1)}, u32[]{:S(2)}, u32[]{:S(2)}) %all-to-all-start) | async-done | bytes 262176 | tf_op jit(solution)/shard_map/all_to_all | solution.py:358
  72.0 0.7 convert_reduce_fusion
  (33 shorter events, 2.8 us)
Async XLA Ops:
  0.6 7.2 %collective-permute-start.2 = (bf16[8,2048]{1,0:T(8,128)(2,1)}, bf16[8,2048]{1,0:T(8,128)(2,1)S(1)}, u32[]{:S(2)}, u32[]{:S(2)}) collective-permute-start(bf16[8,2048]{1,0:T(8,128)(2,1)} %bitcast.6), channel_id=1, source_target_pairs={{0,6},{1,7},{2,4},{3,5},{4,2},{5,3},{6,0},{7,1},{8,14},{9,15},{10,... | collective-permute-start | bytes 98312 | tf_op jit(solution)/shard_map/ppermute | solution.py:18
  5.7 5.0 %collective-permute-start.1 = (bf16[8,2048]{1,0:T(8,128)(2,1)}, bf16[8,2048]{1,0:T(8,128)(2,1)S(1)}, u32[]{:S(2)}, u32[]{:S(2)}) collective-permute-start(bf16[8,2048]{1,0:T(8,128)(2,1)} %bitcast.7), channel_id=1, source_target_pairs={{0,4},{1,5},{2,6},{3,7},{4,0},{5,1},{6,2},{7,3},{8,12},{9,13},{10,... | collective-permute-start | bytes 98312 | tf_op jit(solution)/shard_map/ppermute | solution.py:18
  5.7 5.0 %collective-permute-start = (bf16[8,2048]{1,0:T(8,128)(2,1)}, bf16[8,2048]{1,0:T(8,128)(2,1)S(1)}, u32[]{:S(2)}, u32[]{:S(2)}) collective-permute-start(bf16[8,2048]{1,0:T(8,128)(2,1)} %bitcast.8), channel_id=1, source_target_pairs={{0,2},{1,3},{2,0},{3,1},{4,6},{5,7},{6,4},{7,5},{8,10},{9,11},{10,... | collective-permute-start | bytes 98312 | tf_op jit(solution)/shard_map/ppermute | solution.py:18
  6.4 0.8 %copy-start.2 = (bf16[2048,8]{0,1:T(8,128)(2,1)S(1)}, bf16[2048,8]{0,1:T(8,128)(2,1)}, u32[]{:S(2)}) copy-start(bf16[2048,8]{0,1:T(8,128)(2,1)} %param.6) | copy-start | bytes 98308
  7.2 5.0 %copy-start = (bf16[256,2048]{1,0:T(8,128)(2,1)S(1)}, bf16[256,2048]{1,0:T(8,128)(2,1)}, u32[]{:S(2)}) copy-start(bf16[256,2048]{1,0:T(8,128)(2,1)} %tokens.3) | copy-start | bytes 3145732
  7.2 5.0 %copy-start.1 = (bf16[256,2048]{1,0:T(8,128)(2,1)S(1)}, bf16[256,2048]{1,0:T(8,128)(2,1)}, u32[]{:S(2)}) copy-start(bf16[256,2048]{1,0:T(8,128)(2,1)} %out_grad.3) | copy-start | bytes 3145732
  10.8 1.4 %collective-permute-start.3 = (bf16[32,2048]{1,0:T(8,128)(2,1)S(1)}, bf16[32,2048]{1,0:T(8,128)(2,1)S(1)}, u32[]{:S(2)}, u32[]{:S(2)}) collective-permute-start(bf16[32,2048]{1,0:T(8,128)(2,1)S(1)} %shard_map.69.near.table_near), channel_id=1, source_target_pairs={{0,1},{1,0},{2,3},{3,2},{4,5},{5,4},{6,7},{7,6},{8,9},{9,8},{10,11... | collective-permute-start | bytes 393224 | tf_op jit(solution)/shard_map/ppermute | solution.py:18
  13.5 1.6 %collective-permute-start.4 = (bf16[32,4224]{1,0:T(8,128)(2,1)S(1)}, bf16[32,4224]{1,0:T(8,128)(2,1)S(1)}, u32[]{:S(2)}, u32[]{:S(2)}) collective-permute-start(bf16[32,4224]{1,0:T(8,128)(2,1)S(1)} %get-tuple-element.15), channel_id=1, source_target_pairs={{0,1},{1,0},{2,3},{3,2},{4,5},{5,4},{6,7},{7,6},{8,9},{9,8},{10,11... | collective-permute-start | bytes 811016 | tf_op jit(solution)/shard_map/ppermute | solution.py:18
  15.1 16.3 %slice-start = ((s8[8388608]{0:T(1024)(128)(4,1)}), s8[4194304]{0:T(1024)(128)(4,1)S(1)}, s32[]{:S(2)}) async-start(s8[8388608]{0:T(1024)(128)(4,1)} %bitcast.2), calls=%async_computation.1 | async-start | bytes 8388608
  15.1 16.3 %slice-start.2 = ((s8[8388608]{0:T(1024)(128)(4,1)}), s8[4194304]{0:T(1024)(128)(4,1)S(1)}, s32[]{:S(2)}) async-start(s8[8388608]{0:T(1024)(128)(4,1)} %bitcast.4), calls=%async_computation.3 | async-start | bytes 8388608
  15.2 5.8 %collective-permute-start.5 = (bf16[8,4224]{1,0:T(8,128)(2,1)S(1)}, bf16[8,4224]{1,0:T(8,128)(2,1)S(1)}, u32[]{:S(2)}, u32[]{:S(2)}) collective-permute-start(bf16[8,4224]{1,0:T(8,128)(2,1)S(1)} %get-tuple-element.17), channel_id=1, source_target_pairs={{0,2},{1,3},{2,0},{3,1},{4,6},{5,7},{6,4},{7,5},{8,10},{9,11},{10,... | collective-permute-start | bytes 202760 | tf_op jit(solution)/shard_map/ppermute | solution.py:18
  15.3 16.0 %slice-start.1 = ((s8[8388608]{0:T(1024)(128)(4,1)}), s8[4194304]{0:T(1024)(128)(4,1)S(1)}, s32[]{:S(2)}) async-start(s8[8388608]{0:T(1024)(128)(4,1)} %bitcast.2), calls=%async_computation.2 | async-start | bytes 8388608
  15.3 16.0 %slice-start.3 = ((s8[8388608]{0:T(1024)(128)(4,1)}), s8[4194304]{0:T(1024)(128)(4,1)S(1)}, s32[]{:S(2)}) async-start(s8[8388608]{0:T(1024)(128)(4,1)} %bitcast.4), calls=%async_computation.4 | async-start | bytes 8388608
  15.3 5.7 %collective-permute-start.6 = (bf16[8,4224]{1,0:T(8,128)(2,1)S(1)}, bf16[8,4224]{1,0:T(8,128)(2,1)S(1)}, u32[]{:S(2)}, u32[]{:S(2)}) collective-permute-start(bf16[8,4224]{1,0:T(8,128)(2,1)S(1)} %get-tuple-element.18), channel_id=1, source_target_pairs={{0,4},{1,5},{2,6},{3,7},{4,0},{5,1},{6,2},{7,3},{8,12},{9,13},{10,... | collective-permute-start | bytes 202760 | tf_op jit(solution)/shard_map/ppermute | solution.py:18
  17.4 6.5 %collective-permute-start.7 = (bf16[8,4224]{1,0:T(8,128)(2,1)S(1)}, bf16[8,4224]{1,0:T(8,128)(2,1)S(1)}, u32[]{:S(2)}, u32[]{:S(2)}) collective-permute-start(bf16[8,4224]{1,0:T(8,128)(2,1)S(1)} %get-tuple-element.19), channel_id=1, source_target_pairs={{0,6},{1,7},{2,4},{3,5},{4,2},{5,3},{6,0},{7,1},{8,14},{9,15},{10,... | collective-permute-start | bytes 202760 | tf_op jit(solution)/shard_map/ppermute | solution.py:18
  24.0 5.4 %collective-permute-start.10 = (bf16[8,4224]{1,0:T(8,128)(2,1)S(1)}, bf16[8,4224]{1,0:T(8,128)(2,1)S(1)}, u32[]{:S(2)}, u32[]{:S(2)}) collective-permute-start(bf16[8,4224]{1,0:T(8,128)(2,1)S(1)} %shard_map.72.refs_0_), channel_id=1, source_target_pairs={{0,24},{8,16},{16,8},{24,0},{1,25},{9,17},{17,9},{25,1},{2,26},{10... | collective-permute-start | bytes 202760 | tf_op jit(solution)/shard_map/ppermute | solution.py:18
  26.5 4.3 %collective-permute-start.9 = (bf16[8,4224]{1,0:T(8,128)(2,1)S(1)}, bf16[8,4224]{1,0:T(8,128)(2,1)S(1)}, u32[]{:S(2)}, u32[]{:S(2)}) collective-permute-start(bf16[8,4224]{1,0:T(8,128)(2,1)S(1)} %shard_map.72.refs_0_), channel_id=1, source_target_pairs={{0,16},{8,24},{16,0},{24,8},{1,17},{9,25},{17,1},{25,9},{2,18},{10... | collective-permute-start | bytes 202760 | tf_op jit(solution)/shard_map/ppermute | solution.py:18
  27.0 4.3 %collective-permute-start.8 = (bf16[8,4224]{1,0:T(8,128)(2,1)S(1)}, bf16[8,4224]{1,0:T(8,128)(2,1)S(1)}, u32[]{:S(2)}, u32[]{:S(2)}) collective-permute-start(bf16[8,4224]{1,0:T(8,128)(2,1)S(1)} %shard_map.72.refs_0_), channel_id=1, source_target_pairs={{0,8},{8,0},{16,24},{24,16},{1,9},{9,1},{17,25},{25,17},{2,10},{10... | collective-permute-start | bytes 202760 | tf_op jit(solution)/shard_map/ppermute | solution.py:18
  38.1 5.2 %collective-permute-start.13 = (bf16[8,4096]{1,0:T(8,128)(2,1)S(1)}, bf16[8,4096]{1,0:T(8,128)(2,1)S(1)}, u32[]{:S(2)}, u32[]{:S(2)}) collective-permute-start(bf16[8,4096]{1,0:T(8,128)(2,1)S(1)} %get-tuple-element.20.refs_0_), channel_id=1, source_target_pairs={{0,24},{8,16},{16,8},{24,0},{1,25},{9,17},{17,9},{25,1},{2,26},{10... | collective-permute-start | bytes 196616 | tf_op jit(solution)/shard_map/ppermute | solution.py:18
  39.6 4.4 %collective-permute-start.12 = (bf16[8,4096]{1,0:T(8,128)(2,1)S(1)}, bf16[8,4096]{1,0:T(8,128)(2,1)S(1)}, u32[]{:S(2)}, u32[]{:S(2)}) collective-permute-start(bf16[8,4096]{1,0:T(8,128)(2,1)S(1)} %get-tuple-element.20.refs_0_), channel_id=1, source_target_pairs={{0,16},{8,24},{16,0},{24,8},{1,17},{9,25},{17,1},{25,9},{2,18},{10... | collective-permute-start | bytes 196616 | tf_op jit(solution)/shard_map/ppermute | solution.py:18
  40.1 4.3 %collective-permute-start.11 = (bf16[8,4096]{1,0:T(8,128)(2,1)S(1)}, bf16[8,4096]{1,0:T(8,128)(2,1)S(1)}, u32[]{:S(2)}, u32[]{:S(2)}) collective-permute-start(bf16[8,4096]{1,0:T(8,128)(2,1)S(1)} %get-tuple-element.20.refs_0_), channel_id=1, source_target_pairs={{0,8},{8,0},{16,24},{24,16},{1,9},{9,1},{17,25},{25,17},{2,10},{10... | collective-permute-start | bytes 196616 | tf_op jit(solution)/shard_map/ppermute | solution.py:18
  44.5 6.8 %collective-permute-start.16 = (bf16[8,4224]{1,0:T(8,128)(2,1)S(1)}, bf16[8,4224]{1,0:T(8,128)(2,1)S(1)}, u32[]{:S(2)}, u32[]{:S(2)}) collective-permute-start(bf16[8,4224]{1,0:T(8,128)(2,1)S(1)} %shard_map.74.refs_0_), channel_id=1, source_target_pairs={{0,6},{1,7},{2,4},{3,5},{4,2},{5,3},{6,0},{7,1},{8,14},{9,15},{10,... | collective-permute-start | bytes 202760 | tf_op jit(solution)/shard_map/ppermute | solution.py:18
  47.1 5.9 %collective-permute-start.15 = (bf16[8,4224]{1,0:T(8,128)(2,1)S(1)}, bf16[8,4224]{1,0:T(8,128)(2,1)S(1)}, u32[]{:S(2)}, u32[]{:S(2)}) collective-permute-start(bf16[8,4224]{1,0:T(8,128)(2,1)S(1)} %shard_map.74.refs_0_), channel_id=1, source_target_pairs={{0,4},{1,5},{2,6},{3,7},{4,0},{5,1},{6,2},{7,3},{8,12},{9,13},{10,... | collective-permute-start | bytes 202760 | tf_op jit(solution)/shard_map/ppermute | solution.py:18
  47.7 5.3 %collective-permute-start.14 = (bf16[8,4224]{1,0:T(8,128)(2,1)S(1)}, bf16[8,4224]{1,0:T(8,128)(2,1)S(1)}, u32[]{:S(2)}, u32[]{:S(2)}) collective-permute-start(bf16[8,4224]{1,0:T(8,128)(2,1)S(1)} %shard_map.74.refs_0_), channel_id=1, source_target_pairs={{0,2},{1,3},{2,0},{3,1},{4,6},{5,7},{6,4},{7,5},{8,10},{9,11},{10,... | collective-permute-start | bytes 202760 | tf_op jit(solution)/shard_map/ppermute | solution.py:18
  53.0 1.6 %collective-permute-start.17 = (bf16[32,4224]{1,0:T(8,128)(2,1)S(1)}, bf16[32,4224]{1,0:T(8,128)(2,1)S(1)}, u32[]{:S(2)}, u32[]{:S(2)}) collective-permute-start(bf16[32,4224]{1,0:T(8,128)(2,1)S(1)} %shard_map.75.near), channel_id=1, source_target_pairs={{0,1},{1,0},{2,3},{3,2},{4,5},{5,4},{6,7},{7,6},{8,9},{9,8},{10,11... | collective-permute-start | bytes 811016 | tf_op jit(solution)/shard_map/ppermute | solution.py:18
  56.9 15.0 %all-to-all-start = ((bf16[32,8,512]{2,1,0:T(8,128)(2,1)}), bf16[32,8,512]{2,1,0:T(8,128)(2,1)S(1)}, u32[]{:S(2)}, u32[]{:S(2)}) async-start(bf16[32,8,512]{2,1,0:T(8,128)(2,1)} %get-tuple-element.25), calls=%async_computation | async-start | bytes 524288 | tf_op jit(solution)/shard_map/all_to_all | solution.py:358

commit v5 on v4

--- a/solution.py
+++ b/solution.py
@@ -152,7 +152,8 @@
     outs = refs[count:]
     rows = outs[0].shape[0]
     stats = packed([top, total], sums.shape[0])
-    for k, out in enumerate(outs):
+    places = [0, *reversed(range(1, len(outs)))]
+    for k, out in zip(places, outs):
         part = slice(k * rows, (k + 1) * rows)
         out[:, :width] = sums[part].astype(BF16)
         out[:, width : 2 * width] = grads[part].astype(BF16)
@@ -301,7 +302,7 @@
     parts = [keep, swap(send, "exp", 1)]
     for masks in chip_groups:
         pieces = merge(parts, width, len(masks) + 1)
-        parts = [pieces[0]] + swaps(pieces[1:], "exp", masks)
+        parts = [pieces[0]] + swaps(pieces[1:], "exp", masks[::-1])
     for masks in seq_groups:
         (x,) = merge(parts, width, 1)
         parts = [x] + swaps([x] * len(masks), "seq", masks)

time: 72.9 us -> 72.4 us (level)
  no operation moved by 1% of the time
where the time goes in v5:
time: 72.4 us; the launch traced here: 72.1 us
  waiting for transfers between devices  31.3 us (43%)
  starting transfers between devices  26.5 us (37%)
  Pallas kernels  12.1 us (17%)
  local copies, waits for them, and re-layouts  0.82 us (1%)
  between operations  0.76 us (1%)
    ppermute x18, waiting for transfers between devices, swap(): lax.ppermute(x, axis, [(k, k ^ mask) for k in range(lax.axis_size(axis))])  22.4 us
    ppermute x18, starting transfers between devices, swap(): lax.ppermute(x, axis, [(k, k ^ mask) for k in range(lax.axis_size(axis))])  22.1 us
    pallas_call x9, Pallas kernels, local_call(): pl.pallas_call(body, out_shape=tuple((jax.ShapeDtypeStruct(s, d) if k in...  12.1 us
    all_to_all x1, waiting for transfers between devices, shards(): part = lax.all_to_all(blocks, ('seq', 'exp'), 0, 0, tiled=True)  8.95 us
    all_to_all x1, starting transfers between devices, shards(): part = lax.all_to_all(blocks, ('seq', 'exp'), 0, 0, tiled=True)  4.42 us
  transfers between devices with their start and end apart: 19, of which 16 were waited for; matrix products, arithmetic and copies ran while one was open for 0% of the time, Pallas kernels for 2%

profile of v5, /device:TPU:0, one launch (start us, length us, event | category | flops | bytes accessed | tf_op | source)
XLA Modules:
  0.0 72.1 jit_solution(9548532140561859788)
XLA Ops:
  0.6 5.1 %collective-permute-start.2 = (bf16[8,2048]{1,0:T(8,128)(2,1)}, bf16[8,2048]{1,0:T(8,128)(2,1)S(1)}, u32[]{:S(2)}, u32[]{:S(2)}) collective-permute-start(bf16[8,2048]{1,0:T(8,128)(2,1)} %bitcast.6), channel_id=1, source_target_pairs={{0,6},{1,7},{2,4},{3,5},{4,2},{5,3},{6,0},{7,1},{8,14},{9,15},{10,... | collective-permute-start | bytes 98312 | tf_op jit(solution)/shard_map/ppermute | solution.py:18
  5.7 0.6 collective-permute-start
  6.4 0.8 %copy-done.2 = bf16[2048,8]{0,1:T(8,128)(2,1)S(1)} copy-done((bf16[2048,8]{0,1:T(8,128)(2,1)S(1)}, bf16[2048,8]{0,1:T(8,128)(2,1)}, u32[]{:S(2)}) %copy-start.2) | copy-done | bytes 32792
  7.2 0.6 collective-permute-done.2.refs_3_
  7.8 2.9 %collective-permute-done.1.refs_2_ = bf16[8,2048]{1,0:T(8,128)(2,1)S(1)} collective-permute-done((bf16[8,2048]{1,0:T(8,128)(2,1)}, bf16[8,2048]{1,0:T(8,128)(2,1)S(1)}, u32[]{:S(2)}, u32[]{:S(2)}) %collective-permute-start.1) | collective-permute-done | bytes 32800 | tf_op jit(solution)/shard_map/ppermute | solution.py:18
  10.9 1.3 %collective-permute-done.3.far.table_far = bf16[32,2048]{1,0:T(8,128)(2,1)S(1)} collective-permute-done((bf16[32,2048]{1,0:T(8,128)(2,1)S(1)}, bf16[32,2048]{1,0:T(8,128)(2,1)S(1)}, u32[]{:S(2)}, u32[]{:S(2)}) %collective-permute-start.3) | collective-permute-done | bytes 131104 | tf_op jit(solution)/shard_map/ppermute | solution.py:18
  12.2 1.2 %shard_map.70 = (f32[64,256]{1,0:T(8,128)S(1)}, bf16[32,4224]{1,0:T(8,128)(2,1)S(1)}, bf16[32,4224]{1,0:T(8,128)(2,1)S(1)}) custom-call(bf16[32,2048]{1,0:T(8,128)(2,1)S(1)} %shard_map.69.near.table_near, bf16[32,2048]{1,0:T(8,128)(2,1)S(1)} %collective-permute-done.3.far.table_far, bf16[256,2048]{1,0:T(8,128)(2,1)S(1)} %copy-done, ...), custom_call_target="tpu_custom_call" | custom-call | flops 10000000000 | bytes 4194304 | tf_op jit(solution)/shard_map/pallas_call | solution.py:40
  13.7 1.4 %collective-permute-done.4.refs_1_ = bf16[32,4224]{1,0:T(8,128)(2,1)S(1)} collective-permute-done((bf16[32,4224]{1,0:T(8,128)(2,1)S(1)}, bf16[32,4224]{1,0:T(8,128)(2,1)S(1)}, u32[]{:S(2)}, u32[]{:S(2)}) %collective-permute-start.4) | collective-permute-done | bytes 270368 | tf_op jit(solution)/shard_map/ppermute | solution.py:18
  15.2 1.6 %collective-permute-start.5 = (bf16[8,4224]{1,0:T(8,128)(2,1)S(1)}, bf16[8,4224]{1,0:T(8,128)(2,1)S(1)}, u32[]{:S(2)}, u32[]{:S(2)}) collective-permute-start(bf16[8,4224]{1,0:T(8,128)(2,1)S(1)} %get-tuple-element.17), channel_id=1, source_target_pairs={{0,6},{1,7},{2,4},{3,5},{4,2},{5,3},{6,0},{7,1},{8,14},{9,15},{10,... | collective-permute-start | bytes 202760 | tf_op jit(solution)/shard_map/ppermute | solution.py:18
  16.8 0.6 collective-permute-start.6
  17.4 2.3 %collective-permute-start.7 = (bf16[8,4224]{1,0:T(8,128)(2,1)S(1)}, bf16[8,4224]{1,0:T(8,128)(2,1)S(1)}, u32[]{:S(2)}, u32[]{:S(2)}) collective-permute-start(bf16[8,4224]{1,0:T(8,128)(2,1)S(1)} %get-tuple-element.19), channel_id=1, source_target_pairs={{0,2},{1,3},{2,0},{3,1},{4,6},{5,7},{6,4},{7,5},{8,10},{9,11},{10,... | collective-permute-start | bytes 202760 | tf_op jit(solution)/shard_map/ppermute | solution.py:18
  19.7 2.4 %collective-permute-done.5.refs_1_ = bf16[8,4224]{1,0:T(8,128)(2,1)S(1)} collective-permute-done((bf16[8,4224]{1,0:T(8,128)(2,1)S(1)}, bf16[8,4224]{1,0:T(8,128)(2,1)S(1)}, u32[]{:S(2)}, u32[]{:S(2)}) %collective-permute-start.5) | collective-permute-done | bytes 67616 | tf_op jit(solution)/shard_map/ppermute | solution.py:18
  22.1 2.1 %collective-permute-done.6.refs_2_ = bf16[8,4224]{1,0:T(8,128)(2,1)S(1)} collective-permute-done((bf16[8,4224]{1,0:T(8,128)(2,1)S(1)}, bf16[8,4224]{1,0:T(8,128)(2,1)S(1)}, u32[]{:S(2)}, u32[]{:S(2)}) %collective-permute-start.6) | collective-permute-done | bytes 67616 | tf_op jit(solution)/shard_map/ppermute | solution.py:18
  24.3 2.5 %collective-permute-start.10 = (bf16[8,4224]{1,0:T(8,128)(2,1)S(1)}, bf16[8,4224]{1,0:T(8,128)(2,1)S(1)}, u32[]{:S(2)}, u32[]{:S(2)}) collective-permute-start(bf16[8,4224]{1,0:T(8,128)(2,1)S(1)} %shard_map.72.refs_0_), channel_id=1, source_target_pairs={{0,24},{8,16},{16,8},{24,0},{1,25},{9,17},{17,9},{25,1},{2,26},{10... | collective-permute-start | bytes 202760 | tf_op jit(solution)/shard_map/ppermute | solution.py:18
  27.9 1.7 %collective-permute-done.10.refs_3_ = bf16[8,4224]{1,0:T(8,128)(2,1)S(1)} collective-permute-done((bf16[8,4224]{1,0:T(8,128)(2,1)S(1)}, bf16[8,4224]{1,0:T(8,128)(2,1)S(1)}, u32[]{:S(2)}, u32[]{:S(2)}) %collective-permute-start.10) | collective-permute-done | bytes 67616 | tf_op jit(solution)/shard_map/ppermute | solution.py:18
  29.6 1.5 %collective-permute-done.9.refs_2_ = bf16[8,4224]{1,0:T(8,128)(2,1)S(1)} collective-permute-done((bf16[8,4224]{1,0:T(8,128)(2,1)S(1)}, bf16[8,4224]{1,0:T(8,128)(2,1)S(1)}, u32[]{:S(2)}, u32[]{:S(2)}) %collective-permute-start.9) | collective-permute-done | bytes 67616 | tf_op jit(solution)/shard_map/ppermute | solution.py:18
  31.7 6.7 %shard_map.73 = (bf16[8,4096]{1,0:T(8,128)(2,1)S(1)}, f32[8,2048]{1,0:T(8,128)S(1)}, f32[8,128]{1,0:T(8,128)S(1)}) custom-call(bf16[8,4224]{1,0:T(8,128)(2,1)S(1)} %shard_map.72.refs_0_, bf16[8,4224]{1,0:T(8,128)(2,1)S(1)} %collective-permute-done.8.refs_1_, bf16[8,4224]{1,0:T(8,128)(2,1)S(1)} %collective-permute-done.9.refs_2_, ...), custom_call_target="tpu_custom_call" | custom-call | flops 10000000000 | bytes 4194304 | tf_op jit(solution)/shard_map/pallas_call | solution.py:40
  38.3 1.5 %collective-permute-start.13 = (bf16[8,4096]{1,0:T(8,128)(2,1)S(1)}, bf16[8,4096]{1,0:T(8,128)(2,1)S(1)}, u32[]{:S(2)}, u32[]{:S(2)}) collective-permute-start(bf16[8,4096]{1,0:T(8,128)(2,1)S(1)} %get-tuple-element.20.refs_0_), channel_id=1, source_target_pairs={{0,24},{8,16},{16,8},{24,0},{1,25},{9,17},{17,9},{25,1},{2,26},{10... | collective-permute-start | bytes 196616 | tf_op jit(solution)/shard_map/ppermute | solution.py:18
  39.8 0.7 collective-permute-start.12
  40.5 1.3 %collective-permute-start.11 = (bf16[8,4096]{1,0:T(8,128)(2,1)S(1)}, bf16[8,4096]{1,0:T(8,128)(2,1)S(1)}, u32[]{:S(2)}, u32[]{:S(2)}) collective-permute-start(bf16[8,4096]{1,0:T(8,128)(2,1)S(1)} %get-tuple-element.20.refs_0_), channel_id=1, source_target_pairs={{0,8},{8,0},{16,24},{24,16},{1,9},{9,1},{17,25},{25,17},{2,10},{10... | collective-permute-start | bytes 196616 | tf_op jit(solution)/shard_map/ppermute | solution.py:18
  41.8 1.7 %collective-permute-done.13.refs_3_ = bf16[8,4096]{1,0:T(8,128)(2,1)S(1)} collective-permute-done((bf16[8,4096]{1,0:T(8,128)(2,1)S(1)}, bf16[8,4096]{1,0:T(8,128)(2,1)S(1)}, u32[]{:S(2)}, u32[]{:S(2)}) %collective-permute-start.13) | collective-permute-done | bytes 65568 | tf_op jit(solution)/shard_map/ppermute | solution.py:18
  43.5 0.7 collective-permute-done.12.refs_2_
  44.9 2.4 %collective-permute-start.16 = (bf16[8,4224]{1,0:T(8,128)(2,1)S(1)}, bf16[8,4224]{1,0:T(8,128)(2,1)S(1)}, u32[]{:S(2)}, u32[]{:S(2)}) collective-permute-start(bf16[8,4224]{1,0:T(8,128)(2,1)S(1)} %shard_map.74.refs_0_), channel_id=1, source_target_pairs={{0,6},{1,7},{2,4},{3,5},{4,2},{5,3},{6,0},{7,1},{8,14},{9,15},{10,... | collective-permute-start | bytes 202760 | tf_op jit(solution)/shard_map/ppermute | solution.py:18
  47.4 2.0 %collective-permute-start.14 = (bf16[8,4224]{1,0:T(8,128)(2,1)S(1)}, bf16[8,4224]{1,0:T(8,128)(2,1)S(1)}, u32[]{:S(2)}, u32[]{:S(2)}) collective-permute-start(bf16[8,4224]{1,0:T(8,128)(2,1)S(1)} %shard_map.74.refs_0_), channel_id=1, source_target_pairs={{0,2},{1,3},{2,0},{3,1},{4,6},{5,7},{6,4},{7,5},{8,10},{9,11},{10,... | collective-permute-start | bytes 202760 | tf_op jit(solution)/shard_map/ppermute | solution.py:18
  49.4 1.8 %collective-permute-done.16.refs_3_ = bf16[8,4224]{1,0:T(8,128)(2,1)S(1)} collective-permute-done((bf16[8,4224]{1,0:T(8,128)(2,1)S(1)}, bf16[8,4224]{1,0:T(8,128)(2,1)S(1)}, u32[]{:S(2)}, u32[]{:S(2)}) %collective-permute-start.16) | collective-permute-done | bytes 67616 | tf_op jit(solution)/shard_map/ppermute | solution.py:18
  51.2 1.6 %collective-permute-done.15.refs_2_ = bf16[8,4224]{1,0:T(8,128)(2,1)S(1)} collective-permute-done((bf16[8,4224]{1,0:T(8,128)(2,1)S(1)}, bf16[8,4224]{1,0:T(8,128)(2,1)S(1)}, u32[]{:S(2)}, u32[]{:S(2)}) %collective-permute-start.15) | collective-permute-done | bytes 67616 | tf_op jit(solution)/shard_map/ppermute | solution.py:18
  52.8 1.5 %collective-permute-done.17.far = bf16[32,4224]{1,0:T(8,128)(2,1)S(1)} collective-permute-done((bf16[32,4224]{1,0:T(8,128)(2,1)S(1)}, bf16[32,4224]{1,0:T(8,128)(2,1)S(1)}, u32[]{:S(2)}, u32[]{:S(2)}) %collective-permute-start.17) | collective-permute-done | bytes 270368 | tf_op jit(solution)/shard_map/ppermute | solution.py:18
  54.4 2.3 %shard_map.76 = (bf16[128,256]{1,0:T(8,128)(2,1)S(1)}, bf16[32,8,512]{2,1,0:T(8,128)(2,1)}) custom-call(bf16[32,4224]{1,0:T(8,128)(2,1)S(1)} %shard_map.75.near, bf16[32,4224]{1,0:T(8,128)(2,1)S(1)} %collective-permute-done.17.far, f32[64,256]{1,0:T(8,128)S(1)} %get-tuple-element.23.logits, bf16[256,2048]{1,0:T(8,128)(2,1)S(1)} %copy-done, ...), custom_call_target="tpu_custom_call" | custom-call | flops 10000000000 | bytes 4194304 | tf_op jit(solution)/shard_map/pallas_call | solution.py:40
  56.7 4.4 %all-to-all-start = ((bf16[32,8,512]{2,1,0:T(8,128)(2,1)}), bf16[32,8,512]{2,1,0:T(8,128)(2,1)S(1)}, u32[]{:S(2)}, u32[]{:S(2)}) async-start(bf16[32,8,512]{2,1,0:T(8,128)(2,1)} %get-tuple-element.25), calls=%async_computation | async-start | bytes 524288 | tf_op jit(solution)/shard_map/all_to_all | solution.py:359
  61.1 1.4 %shard_map.77 = bf16[256,2048]{1,0:T(8,128)(2,1)} custom-call(bf16[128,256]{1,0:T(8,128)(2,1)S(1)} %get-tuple-element.24.weights, bf16[32,4224]{1,0:T(8,128)(2,1)S(1)} %shard_map.75.near, bf16[32,4224]{1,0:T(8,128)(2,1)S(1)} %collective-permute-done.17.far, bf16[32,2048]{1,0:T(8,128)(2,1)S(1)} %shard_map.69.near.table_near, ...), custom_call_target="tpu_custom_call" | custom-call | flops 10000000000 | bytes 4194304 | tf_op jit(solution)/shard_map/pallas_call | solution.py:40
  62.5 8.9 %all-to-all-done = bf16[32,8,512]{2,1,0:T(8,128)(2,1)S(1)} async-done(((bf16[32,8,512]{2,1,0:T(8,128)(2,1)}), bf16[32,8,512]{2,1,0:T(8,128)(2,1)S(1)}, u32[]{:S(2)}, u32[]{:S(2)}) %all-to-all-start) | async-done | bytes 262176 | tf_op jit(solution)/shard_map/all_to_all | solution.py:359
  71.5 0.7 convert_reduce_fusion
  (33 shorter events, 3.0 us)
Async XLA Ops:
  0.6 7.2 %collective-permute-start.2 = (bf16[8,2048]{1,0:T(8,128)(2,1)}, bf16[8,2048]{1,0:T(8,128)(2,1)S(1)}, u32[]{:S(2)}, u32[]{:S(2)}) collective-permute-start(bf16[8,2048]{1,0:T(8,128)(2,1)} %bitcast.6), channel_id=1, source_target_pairs={{0,6},{1,7},{2,4},{3,5},{4,2},{5,3},{6,0},{7,1},{8,14},{9,15},{10,... | collective-permute-start | bytes 98312 | tf_op jit(solution)/shard_map/ppermute | solution.py:18
  5.7 5.0 %collective-permute-start.1 = (bf16[8,2048]{1,0:T(8,128)(2,1)}, bf16[8,2048]{1,0:T(8,128)(2,1)S(1)}, u32[]{:S(2)}, u32[]{:S(2)}) collective-permute-start(bf16[8,2048]{1,0:T(8,128)(2,1)} %bitcast.7), channel_id=1, source_target_pairs={{0,4},{1,5},{2,6},{3,7},{4,0},{5,1},{6,2},{7,3},{8,12},{9,13},{10,... | collective-permute-start | bytes 98312 | tf_op jit(solution)/shard_map/ppermute | solution.py:18
  5.7 5.0 %collective-permute-start = (bf16[8,2048]{1,0:T(8,128)(2,1)}, bf16[8,2048]{1,0:T(8,128)(2,1)S(1)}, u32[]{:S(2)}, u32[]{:S(2)}) collective-permute-start(bf16[8,2048]{1,0:T(8,128)(2,1)} %bitcast.8), channel_id=1, source_target_pairs={{0,2},{1,3},{2,0},{3,1},{4,6},{5,7},{6,4},{7,5},{8,10},{9,11},{10,... | collective-permute-start | bytes 98312 | tf_op jit(solution)/shard_map/ppermute | solution.py:18
  6.4 0.8 %copy-start.2 = (bf16[2048,8]{0,1:T(8,128)(2,1)S(1)}, bf16[2048,8]{0,1:T(8,128)(2,1)}, u32[]{:S(2)}) copy-start(bf16[2048,8]{0,1:T(8,128)(2,1)} %param.6) | copy-start | bytes 98308
  7.2 5.0 %copy-start = (bf16[256,2048]{1,0:T(8,128)(2,1)S(1)}, bf16[256,2048]{1,0:T(8,128)(2,1)}, u32[]{:S(2)}) copy-start(bf16[256,2048]{1,0:T(8,128)(2,1)} %tokens.3) | copy-start | bytes 3145732
  7.2 5.0 %copy-start.1 = (bf16[256,2048]{1,0:T(8,128)(2,1)S(1)}, bf16[256,2048]{1,0:T(8,128)(2,1)}, u32[]{:S(2)}) copy-start(bf16[256,2048]{1,0:T(8,128)(2,1)} %out_grad.3) | copy-start | bytes 3145732
  10.8 1.4 %collective-permute-start.3 = (bf16[32,2048]{1,0:T(8,128)(2,1)S(1)}, bf16[32,2048]{1,0:T(8,128)(2,1)S(1)}, u32[]{:S(2)}, u32[]{:S(2)}) collective-permute-start(bf16[32,2048]{1,0:T(8,128)(2,1)S(1)} %shard_map.69.near.table_near), channel_id=1, source_target_pairs={{0,1},{1,0},{2,3},{3,2},{4,5},{5,4},{6,7},{7,6},{8,9},{9,8},{10,11... | collective-permute-start | bytes 393224 | tf_op jit(solution)/shard_map/ppermute | solution.py:18
  13.5 1.6 %collective-permute-start.4 = (bf16[32,4224]{1,0:T(8,128)(2,1)S(1)}, bf16[32,4224]{1,0:T(8,128)(2,1)S(1)}, u32[]{:S(2)}, u32[]{:S(2)}) collective-permute-start(bf16[32,4224]{1,0:T(8,128)(2,1)S(1)} %get-tuple-element.15), channel_id=1, source_target_pairs={{0,1},{1,0},{2,3},{3,2},{4,5},{5,4},{6,7},{7,6},{8,9},{9,8},{10,11... | collective-permute-start | bytes 811016 | tf_op jit(solution)/shard_map/ppermute | solution.py:18
  15.1 16.6 %slice-start = ((s8[8388608]{0:T(1024)(128)(4,1)}), s8[4194304]{0:T(1024)(128)(4,1)S(1)}, s32[]{:S(2)}) async-start(s8[8388608]{0:T(1024)(128)(4,1)} %bitcast.2), calls=%async_computation.1 | async-start | bytes 8388608
  15.1 16.6 %slice-start.2 = ((s8[8388608]{0:T(1024)(128)(4,1)}), s8[4194304]{0:T(1024)(128)(4,1)S(1)}, s32[]{:S(2)}) async-start(s8[8388608]{0:T(1024)(128)(4,1)} %bitcast.4), calls=%async_computation.3 | async-start | bytes 8388608
  15.2 6.8 %collective-permute-start.5 = (bf16[8,4224]{1,0:T(8,128)(2,1)S(1)}, bf16[8,4224]{1,0:T(8,128)(2,1)S(1)}, u32[]{:S(2)}, u32[]{:S(2)}) collective-permute-start(bf16[8,4224]{1,0:T(8,128)(2,1)S(1)} %get-tuple-element.17), channel_id=1, source_target_pairs={{0,6},{1,7},{2,4},{3,5},{4,2},{5,3},{6,0},{7,1},{8,14},{9,15},{10,... | collective-permute-start | bytes 202760 | tf_op jit(solution)/shard_map/ppermute | solution.py:18
  16.8 14.8 %slice-start.1 = ((s8[8388608]{0:T(1024)(128)(4,1)}), s8[4194304]{0:T(1024)(128)(4,1)S(1)}, s32[]{:S(2)}) async-start(s8[8388608]{0:T(1024)(128)(4,1)} %bitcast.2), calls=%async_computation.2 | async-start | bytes 8388608
  16.8 14.8 %slice-start.3 = ((s8[8388608]{0:T(1024)(128)(4,1)}), s8[4194304]{0:T(1024)(128)(4,1)S(1)}, s32[]{:S(2)}) async-start(s8[8388608]{0:T(1024)(128)(4,1)} %bitcast.4), calls=%async_computation.4 | async-start | bytes 8388608
  16.8 7.4 %collective-permute-start.6 = (bf16[8,4224]{1,0:T(8,128)(2,1)S(1)}, bf16[8,4224]{1,0:T(8,128)(2,1)S(1)}, u32[]{:S(2)}, u32[]{:S(2)}) collective-permute-start(bf16[8,4224]{1,0:T(8,128)(2,1)S(1)} %get-tuple-element.18), channel_id=1, source_target_pairs={{0,4},{1,5},{2,6},{3,7},{4,0},{5,1},{6,2},{7,3},{8,12},{9,13},{10,... | collective-permute-start | bytes 202760 | tf_op jit(solution)/shard_map/ppermute | solution.py:18
  17.4 6.8 %collective-permute-start.7 = (bf16[8,4224]{1,0:T(8,128)(2,1)S(1)}, bf16[8,4224]{1,0:T(8,128)(2,1)S(1)}, u32[]{:S(2)}, u32[]{:S(2)}) collective-permute-start(bf16[8,4224]{1,0:T(8,128)(2,1)S(1)} %get-tuple-element.19), channel_id=1, source_target_pairs={{0,2},{1,3},{2,0},{3,1},{4,6},{5,7},{6,4},{7,5},{8,10},{9,11},{10,... | collective-permute-start | bytes 202760 | tf_op jit(solution)/shard_map/ppermute | solution.py:18
  24.3 5.3 %collective-permute-start.10 = (bf16[8,4224]{1,0:T(8,128)(2,1)S(1)}, bf16[8,4224]{1,0:T(8,128)(2,1)S(1)}, u32[]{:S(2)}, u32[]{:S(2)}) collective-permute-start(bf16[8,4224]{1,0:T(8,128)(2,1)S(1)} %shard_map.72.refs_0_), channel_id=1, source_target_pairs={{0,24},{8,16},{16,8},{24,0},{1,25},{9,17},{17,9},{25,1},{2,26},{10... | collective-permute-start | bytes 202760 | tf_op jit(solution)/shard_map/ppermute | solution.py:18
  26.8 4.3 %collective-permute-start.9 = (bf16[8,4224]{1,0:T(8,128)(2,1)S(1)}, bf16[8,4224]{1,0:T(8,128)(2,1)S(1)}, u32[]{:S(2)}, u32[]{:S(2)}) collective-permute-start(bf16[8,4224]{1,0:T(8,128)(2,1)S(1)} %shard_map.72.refs_0_), channel_id=1, source_target_pairs={{0,16},{8,24},{16,0},{24,8},{1,17},{9,25},{17,1},{25,9},{2,18},{10... | collective-permute-start | bytes 202760 | tf_op jit(solution)/shard_map/ppermute | solution.py:18
  27.3 4.3 %collective-permute-start.8 = (bf16[8,4224]{1,0:T(8,128)(2,1)S(1)}, bf16[8,4224]{1,0:T(8,128)(2,1)S(1)}, u32[]{:S(2)}, u32[]{:S(2)}) collective-permute-start(bf16[8,4224]{1,0:T(8,128)(2,1)S(1)} %shard_map.72.refs_0_), channel_id=1, source_target_pairs={{0,8},{8,0},{16,24},{24,16},{1,9},{9,1},{17,25},{25,17},{2,10},{10... | collective-permute-start | bytes 202760 | tf_op jit(solution)/shard_map/ppermute | solution.py:18
  38.3 5.2 %collective-permute-start.13 = (bf16[8,4096]{1,0:T(8,128)(2,1)S(1)}, bf16[8,4096]{1,0:T(8,128)(2,1)S(1)}, u32[]{:S(2)}, u32[]{:S(2)}) collective-permute-start(bf16[8,4096]{1,0:T(8,128)(2,1)S(1)} %get-tuple-element.20.refs_0_), channel_id=1, source_target_pairs={{0,24},{8,16},{16,8},{24,0},{1,25},{9,17},{17,9},{25,1},{2,26},{10... | collective-permute-start | bytes 196616 | tf_op jit(solution)/shard_map/ppermute | solution.py:18
  39.8 4.4 %collective-permute-start.12 = (bf16[8,4096]{1,0:T(8,128)(2,1)S(1)}, bf16[8,4096]{1,0:T(8,128)(2,1)S(1)}, u32[]{:S(2)}, u32[]{:S(2)}) collective-permute-start(bf16[8,4096]{1,0:T(8,128)(2,1)S(1)} %get-tuple-element.20.refs_0_), channel_id=1, source_target_pairs={{0,16},{8,24},{16,0},{24,8},{1,17},{9,25},{17,1},{25,9},{2,18},{10... | collective-permute-start | bytes 196616 | tf_op jit(solution)/shard_map/ppermute | solution.py:18
  40.5 4.3 %collective-permute-start.11 = (bf16[8,4096]{1,0:T(8,128)(2,1)S(1)}, bf16[8,4096]{1,0:T(8,128)(2,1)S(1)}, u32[]{:S(2)}, u32[]{:S(2)}) collective-permute-start(bf16[8,4096]{1,0:T(8,128)(2,1)S(1)} %get-tuple-element.20.refs_0_), channel_id=1, source_target_pairs={{0,8},{8,0},{16,24},{24,16},{1,9},{9,1},{17,25},{25,17},{2,10},{10... | collective-permute-start | bytes 196616 | tf_op jit(solution)/shard_map/ppermute | solution.py:18
  44.9 6.3 %collective-permute-start.16 = (bf16[8,4224]{1,0:T(8,128)(2,1)S(1)}, bf16[8,4224]{1,0:T(8,128)(2,1)S(1)}, u32[]{:S(2)}, u32[]{:S(2)}) collective-permute-start(bf16[8,4224]{1,0:T(8,128)(2,1)S(1)} %shard_map.74.refs_0_), channel_id=1, source_target_pairs={{0,6},{1,7},{2,4},{3,5},{4,2},{5,3},{6,0},{7,1},{8,14},{9,15},{10,... | collective-permute-start | bytes 202760 | tf_op jit(solution)/shard_map/ppermute | solution.py:18
  47.4 5.4 %collective-permute-start.15 = (bf16[8,4224]{1,0:T(8,128)(2,1)S(1)}, bf16[8,4224]{1,0:T(8,128)(2,1)S(1)}, u32[]{:S(2)}, u32[]{:S(2)}) collective-permute-start(bf16[8,4224]{1,0:T(8,128)(2,1)S(1)} %shard_map.74.refs_0_), channel_id=1, source_target_pairs={{0,4},{1,5},{2,6},{3,7},{4,0},{5,1},{6,2},{7,3},{8,12},{9,13},{10,... | collective-permute-start | bytes 202760 | tf_op jit(solution)/shard_map/ppermute | solution.py:18
  47.4 5.4 %collective-permute-start.14 = (bf16[8,4224]{1,0:T(8,128)(2,1)S(1)}, bf16[8,4224]{1,0:T(8,128)(2,1)S(1)}, u32[]{:S(2)}, u32[]{:S(2)}) collective-permute-start(bf16[8,4224]{1,0:T(8,128)(2,1)S(1)} %shard_map.74.refs_0_), channel_id=1, source_target_pairs={{0,2},{1,3},{2,0},{3,1},{4,6},{5,7},{6,4},{7,5},{8,10},{9,11},{10,... | collective-permute-start | bytes 202760 | tf_op jit(solution)/shard_map/ppermute | solution.py:18
  52.8 1.6 %collective-permute-start.17 = (bf16[32,4224]{1,0:T(8,128)(2,1)S(1)}, bf16[32,4224]{1,0:T(8,128)(2,1)S(1)}, u32[]{:S(2)}, u32[]{:S(2)}) collective-permute-start(bf16[32,4224]{1,0:T(8,128)(2,1)S(1)} %shard_map.75.near), channel_id=1, source_target_pairs={{0,1},{1,0},{2,3},{3,2},{4,5},{5,4},{6,7},{7,6},{8,9},{9,8},{10,11... | collective-permute-start | bytes 811016 | tf_op jit(solution)/shard_map/ppermute | solution.py:18
  56.7 14.8 %all-to-all-start = ((bf16[32,8,512]{2,1,0:T(8,128)(2,1)}), bf16[32,8,512]{2,1,0:T(8,128)(2,1)S(1)}, u32[]{:S(2)}, u32[]{:S(2)}) async-start(bf16[32,8,512]{2,1,0:T(8,128)(2,1)} %get-tuple-element.25), calls=%async_computation | async-start | bytes 524288 | tf_op jit(solution)/shard_map/all_to_all | solution.py:359

commit v6 on v5

--- a/solution.py
+++ b/solution.py
@@ -36,7 +36,7 @@
     return pltpu.with_memory_space_constraint(x, pltpu.VMEM)
 
 
-def local_call(body, outs, *operands, limit=8, to_hbm=()):
+def local_call(body, outs, *operands, limit=8, to_hbm=(), loose=(), flops=10**10):
     return pl.pallas_call(
         body,
         out_shape=tuple(
@@ -46,7 +46,7 @@
         in_specs=[pl.BlockSpec(memory_space=pltpu.VMEM)] * len(operands),
         out_specs=tuple(pl.BlockSpec(memory_space=pltpu.VMEM) for _ in outs),
         compiler_params=pltpu.CompilerParams(vmem_limit_bytes=limit * MIB),
-        cost_estimate=pl.CostEstimate(flops=10**10, bytes_accessed=4 * MIB, transcendentals=0),
+        cost_estimate=pl.CostEstimate(flops=flops, bytes_accessed=4 * MIB, transcendentals=0),
     )(*[in_vmem(x) for x in operands])
 
 
@@ -169,6 +169,20 @@
     )
 
 
+def flip_kernel(index, weight, after, out):
+    out[...] = weight[index].T
+
+
+def flipped(weights, after):
+    experts, rows, columns = weights.shape
+    return [
+        local_call(
+            partial(flip_kernel, e), [((columns, rows), BF16)], weights, after, flops=10**9
+        )[0]
+        for e in range(experts)
+    ]
+
+
 def gelu_and_slope(v):
     root = math.sqrt(2.0 / math.pi)
     t = jnp.tanh(root * (v + 0.044715 * (v * v * v)))
@@ -178,13 +192,16 @@
 
 def expert_kernel(count, width, *refs):
     parts = refs[:count]
-    weight_in, weight_out, both, slot_sum, stats = refs[count:]
+    weight_in, weight_out = refs[count : count + 2]
+    experts, _, units = weight_in.shape
+    flips = refs[count + 2 : count + 2 + 2 * experts]
+    in_flipped, out_flipped = flips[:experts], flips[experts:]
+    both, slot_sum, stats = refs[count + 2 + 2 * experts :]
     sums, grads, top, total = merged(parts, width)
     stats[...] = packed([top, total], stats.shape[0])
     sums = sums / total
     slot_sum[...] = sums
     slot_in, grad_out = sums.astype(BF16), grads.astype(BF16)
-    experts, _, units = weight_in.shape
     rows = sums.shape[0]
     step = min(units, 512)
     row = lax.broadcasted_iota(jnp.int32, (rows, step), 0)
@@ -195,12 +212,12 @@
         for c in range(units // step):
             at = slice(c * step, (c + 1) * step)
             pre_act = product(slot_in, weight_in[e, :, at], 1, 0)
-            hid_grad = product(grad_out, weight_out[e, at, :], 1, 1)
+            hid_grad = product(grad_out, out_flipped[e][:, at], 1, 0)
             act, slope = gelu_and_slope(pre_act)
             hidden = jnp.where(own, act, 0.0).astype(BF16)
             act_grad = jnp.where(own, hid_grad * slope, 0.0).astype(BF16)
             out_part += product(hidden, weight_out[e, at, :], 1, 0)
-            in_part += product(act_grad, weight_in[e, :, at], 1, 1)
+            in_part += product(act_grad, in_flipped[e][at, :], 1, 0)
     both[:, :width] = out_part.astype(BF16)
     both[:, width:] = in_part.astype(BF16)
 
@@ -303,9 +320,11 @@
     for masks in chip_groups:
         pieces = merge(parts, width, len(masks) + 1)
         parts = [pieces[0]] + swaps(pieces[1:], "exp", masks[::-1])
+    own_piece = pieces[0]
     for masks in seq_groups:
         (x,) = merge(parts, width, 1)
         parts = [x] + swaps([x] * len(masks), "seq", masks)
+    own_sum = x
 
     both, slot_sum, stats = local_call(
         partial(expert_kernel, len(parts), width),
@@ -313,6 +332,8 @@
         *parts,
         expert_in,
         expert_out,
+        *flipped(expert_in, own_sum),
+        *flipped(expert_out, own_piece),
         limit=16,
     )
     parts = [both]

time: 72.4 us -> 70.2 us (0.970)
  waiting for transfers between devices: 31.3 us -> 27 us
  Pallas kernels: 12.1 us -> 14.9 us
    ppermute x18, waiting for transfers between devices: 22.4 us -> 18 us  [swap(): lax.ppermute(x, axis, [(k, k ^ mask) for k in range(lax.axis_size(axis))])]
    pallas_call x9 -> x13, Pallas kernels: 12.1 us -> 14.8 us  [local_call(): pl.pallas_call(body, out_shape=tuple((jax.ShapeDtypeStruct(s, d) if k in...]
  transfers between devices with their start and end apart: 19 -> 19, of which waited for: 16 -> 14; matrix products, arithmetic and copies ran while one was open for 0% -> 0% of each run, Pallas kernels for 2% -> 9%
where the time goes in v6:
time: 70.2 us; the launch traced here: 69.9 us
  waiting for transfers between devices  27 us (38%)
  starting transfers between devices  25.8 us (37%)
  Pallas kernels  14.9 us (21%)
  local copies, waits for them, and re-layouts  0.84 us (1%)
  between operations  0.81 us (1%)
    ppermute x18, starting transfers between devices, swap(): lax.ppermute(x, axis, [(k, k ^ mask) for k in range(lax.axis_size(axis))])  22.1 us
    ppermute x18, waiting for transfers between devices, swap(): lax.ppermute(x, axis, [(k, k ^ mask) for k in range(lax.axis_size(axis))])  18 us
    pallas_call x13, Pallas kernels, local_call(): pl.pallas_call(body, out_shape=tuple((jax.ShapeDtypeStruct(s, d) if k in...  14.8 us
    all_to_all x1, waiting for transfers between devices, shards(): part = lax.all_to_all(blocks, ('seq', 'exp'), 0, 0, tiled=True)  8.95 us
    all_to_all x1, starting transfers between devices, shards(): part = lax.all_to_all(blocks, ('seq', 'exp'), 0, 0, tiled=True)  3.71 us
  transfers between devices with their start and end apart: 19, of which 14 were waited for; matrix products, arithmetic and copies ran while one was open for 0% of the time, Pallas kernels for 9%

profile of v6, /device:TPU:0, one launch (start us, length us, event | category | flops | bytes accessed | tf_op | source)
XLA Modules:
  0.0 69.9 jit_solution(17951073051546530515)
XLA Ops:
  0.6 5.1 %collective-permute-start.2 = (bf16[8,2048]{1,0:T(8,128)(2,1)}, bf16[8,2048]{1,0:T(8,128)(2,1)S(1)}, u32[]{:S(2)}, u32[]{:S(2)}) collective-permute-start(bf16[8,2048]{1,0:T(8,128)(2,1)} %bitcast.8), channel_id=1, source_target_pairs={{0,6},{1,7},{2,4},{3,5},{4,2},{5,3},{6,0},{7,1},{8,14},{9,15},{10,... | collective-permute-start | bytes 98312 | tf_op jit(solution)/shard_map/ppermute | solution.py:18
  5.7 0.6 collective-permute-start
  6.4 0.8 %copy-done.2 = bf16[2048,8]{0,1:T(8,128)(2,1)S(1)} copy-done((bf16[2048,8]{0,1:T(8,128)(2,1)S(1)}, bf16[2048,8]{0,1:T(8,128)(2,1)}, u32[]{:S(2)}) %copy-start.2) | copy-done | bytes 32792
  7.2 0.6 collective-permute-done.2.refs_3_
  7.8 2.9 %collective-permute-done.1.refs_2_ = bf16[8,2048]{1,0:T(8,128)(2,1)S(1)} collective-permute-done((bf16[8,2048]{1,0:T(8,128)(2,1)}, bf16[8,2048]{1,0:T(8,128)(2,1)S(1)}, u32[]{:S(2)}, u32[]{:S(2)}) %collective-permute-start.1) | collective-permute-done | bytes 32800 | tf_op jit(solution)/shard_map/ppermute | solution.py:18
  10.9 1.3 %collective-permute-done.3.far.table_far = bf16[32,2048]{1,0:T(8,128)(2,1)S(1)} collective-permute-done((bf16[32,2048]{1,0:T(8,128)(2,1)S(1)}, bf16[32,2048]{1,0:T(8,128)(2,1)S(1)}, u32[]{:S(2)}, u32[]{:S(2)}) %collective-permute-start.3) | collective-permute-done | bytes 131104 | tf_op jit(solution)/shard_map/ppermute | solution.py:18
  12.2 1.2 %shard_map.70 = (f32[64,256]{1,0:T(8,128)S(1)}, bf16[32,4224]{1,0:T(8,128)(2,1)S(1)}, bf16[32,4224]{1,0:T(8,128)(2,1)S(1)}) custom-call(bf16[32,2048]{1,0:T(8,128)(2,1)S(1)} %shard_map.69.near.table_near, bf16[32,2048]{1,0:T(8,128)(2,1)S(1)} %collective-permute-done.3.far.table_far, bf16[256,2048]{1,0:T(8,128)(2,1)S(1)} %copy-done, ...), custom_call_target="tpu_custom_call" | custom-call | flops 10000000000 | bytes 4194304 | tf_op jit(solution)/shard_map/pallas_call | solution.py:40
  13.7 1.4 %collective-permute-done.4.refs_1_ = bf16[32,4224]{1,0:T(8,128)(2,1)S(1)} collective-permute-done((bf16[32,4224]{1,0:T(8,128)(2,1)S(1)}, bf16[32,4224]{1,0:T(8,128)(2,1)S(1)}, u32[]{:S(2)}, u32[]{:S(2)}) %collective-permute-start.4) | collective-permute-done | bytes 270368 | tf_op jit(solution)/shard_map/ppermute | solution.py:18
  15.2 1.6 %collective-permute-start.5 = (bf16[8,4224]{1,0:T(8,128)(2,1)S(1)}, bf16[8,4224]{1,0:T(8,128)(2,1)S(1)}, u32[]{:S(2)}, u32[]{:S(2)}) collective-permute-start(bf16[8,4224]{1,0:T(8,128)(2,1)S(1)} %get-tuple-element.17), channel_id=1, source_target_pairs={{0,6},{1,7},{2,4},{3,5},{4,2},{5,3},{6,0},{7,1},{8,14},{9,15},{10,... | collective-permute-start | bytes 202760 | tf_op jit(solution)/shard_map/ppermute | solution.py:18
  16.8 0.6 collective-permute-start.6
  17.4 2.3 %collective-permute-start.7 = (bf16[8,4224]{1,0:T(8,128)(2,1)S(1)}, bf16[8,4224]{1,0:T(8,128)(2,1)S(1)}, u32[]{:S(2)}, u32[]{:S(2)}) collective-permute-start(bf16[8,4224]{1,0:T(8,128)(2,1)S(1)} %get-tuple-element.19), channel_id=1, source_target_pairs={{0,2},{1,3},{2,0},{3,1},{4,6},{5,7},{6,4},{7,5},{8,10},{9,11},{10,... | collective-permute-start | bytes 202760 | tf_op jit(solution)/shard_map/ppermute | solution.py:18
  19.7 1.2 %shard_map.76.refs_9_ = bf16[2048,1024]{1,0:T(8,128)(2,1)S(1)} custom-call(bf16[2,1024,2048]{2,1,0:T(8,128)(2,1)S(1)} %bitcast.5, bf16[8,4224]{1,0:T(8,128)(2,1)S(1)} %get-tuple-element.16.refs_0_.after), custom_call_target="tpu_custom_call" | custom-call | flops 1000000000 | bytes 4194304 | tf_op jit(solution)/shard_map/pallas_call | solution.py:40
  20.9 1.2 %shard_map.75.refs_8_ = bf16[2048,1024]{1,0:T(8,128)(2,1)S(1)} custom-call(bf16[2,1024,2048]{2,1,0:T(8,128)(2,1)S(1)} %bitcast.5, bf16[8,4224]{1,0:T(8,128)(2,1)S(1)} %get-tuple-element.16.refs_0_.after), custom_call_target="tpu_custom_call" | custom-call | flops 1000000000 | bytes 4194304 | tf_op jit(solution)/shard_map/pallas_call | solution.py:40
  22.2 2.0 %collective-permute-done.6.refs_2_ = bf16[8,4224]{1,0:T(8,128)(2,1)S(1)} collective-permute-done((bf16[8,4224]{1,0:T(8,128)(2,1)S(1)}, bf16[8,4224]{1,0:T(8,128)(2,1)S(1)}, u32[]{:S(2)}, u32[]{:S(2)}) %collective-permute-start.6) | collective-permute-done | bytes 67616 | tf_op jit(solution)/shard_map/ppermute | solution.py:18
  24.3 2.5 %collective-permute-start.10 = (bf16[8,4224]{1,0:T(8,128)(2,1)S(1)}, bf16[8,4224]{1,0:T(8,128)(2,1)S(1)}, u32[]{:S(2)}, u32[]{:S(2)}) collective-permute-start(bf16[8,4224]{1,0:T(8,128)(2,1)S(1)} %shard_map.72.after.refs_0_), channel_id=1, source_target_pairs={{0,24},{8,16},{16,8},{24,0},{1,25},{9,17},{17,9},{25,1},{2,26},{10... | collective-permute-start | bytes 202760 | tf_op jit(solution)/shard_map/ppermute | solution.py:18
  27.9 1.2 %shard_map.74.refs_7_ = bf16[1024,2048]{1,0:T(8,128)(2,1)S(1)} custom-call(bf16[2,2048,1024]{2,1,0:T(8,128)(2,1)S(1)} %bitcast.3, bf16[8,4224]{1,0:T(8,128)(2,1)S(1)} %shard_map.72.after.refs_0_), custom_call_target="tpu_custom_call" | custom-call | flops 1000000000 | bytes 4194304 | tf_op jit(solution)/shard_map/pallas_call | solution.py:40
  29.1 1.2 %shard_map.73.refs_6_ = bf16[1024,2048]{1,0:T(8,128)(2,1)S(1)} custom-call(bf16[2,2048,1024]{2,1,0:T(8,128)(2,1)S(1)} %bitcast.3, bf16[8,4224]{1,0:T(8,128)(2,1)S(1)} %shard_map.72.after.refs_0_), custom_call_target="tpu_custom_call" | custom-call | flops 1000000000 | bytes 4194304 | tf_op jit(solution)/shard_map/pallas_call | solution.py:40
  30.4 0.7 %collective-permute-done.9.refs_2_ = bf16[8,4224]{1,0:T(8,128)(2,1)S(1)} collective-permute-done((bf16[8,4224]{1,0:T(8,128)(2,1)S(1)}, bf16[8,4224]{1,0:T(8,128)(2,1)S(1)}, u32[]{:S(2)}, u32[]{:S(2)}) %collective-permute-start.9) | collective-permute-done | bytes 67616 | tf_op jit(solution)/shard_map/ppermute | solution.py:18
  31.6 4.5 %shard_map.77 = (bf16[8,4096]{1,0:T(8,128)(2,1)S(1)}, f32[8,2048]{1,0:T(8,128)S(1)}, f32[8,128]{1,0:T(8,128)S(1)}) custom-call(bf16[8,4224]{1,0:T(8,128)(2,1)S(1)} %shard_map.72.after.refs_0_, bf16[8,4224]{1,0:T(8,128)(2,1)S(1)} %collective-permute-done.8.refs_1_, bf16[8,4224]{1,0:T(8,128)(2,1)S(1)} %collective-permute-done.9.refs_2_, ...), custom_call_target="tpu_custom_call" | custom-call | flops 10000000000 | bytes 4194304 | tf_op jit(solution)/shard_map/pallas_call | solution.py:40
  36.1 2.4 %collective-permute-start.13 = (bf16[8,4096]{1,0:T(8,128)(2,1)S(1)}, bf16[8,4096]{1,0:T(8,128)(2,1)S(1)}, u32[]{:S(2)}, u32[]{:S(2)}) collective-permute-start(bf16[8,4096]{1,0:T(8,128)(2,1)S(1)} %get-tuple-element.20.refs_0_), channel_id=1, source_target_pairs={{0,24},{8,16},{16,8},{24,0},{1,25},{9,17},{17,9},{25,1},{2,26},{10... | collective-permute-start | bytes 196616 | tf_op jit(solution)/shard_map/ppermute | solution.py:18
  39.6 1.8 %collective-permute-done.13.refs_3_ = bf16[8,4096]{1,0:T(8,128)(2,1)S(1)} collective-permute-done((bf16[8,4096]{1,0:T(8,128)(2,1)S(1)}, bf16[8,4096]{1,0:T(8,128)(2,1)S(1)}, u32[]{:S(2)}, u32[]{:S(2)}) %collective-permute-start.13) | collective-permute-done | bytes 65568 | tf_op jit(solution)/shard_map/ppermute | solution.py:18
  41.5 1.3 %collective-permute-done.12.refs_2_ = bf16[8,4096]{1,0:T(8,128)(2,1)S(1)} collective-permute-done((bf16[8,4096]{1,0:T(8,128)(2,1)S(1)}, bf16[8,4096]{1,0:T(8,128)(2,1)S(1)}, u32[]{:S(2)}, u32[]{:S(2)}) %collective-permute-start.12) | collective-permute-done | bytes 65568 | tf_op jit(solution)/shard_map/ppermute | solution.py:18
  43.4 2.6 %collective-permute-start.16 = (bf16[8,4224]{1,0:T(8,128)(2,1)S(1)}, bf16[8,4224]{1,0:T(8,128)(2,1)S(1)}, u32[]{:S(2)}, u32[]{:S(2)}) collective-permute-start(bf16[8,4224]{1,0:T(8,128)(2,1)S(1)} %shard_map.78.refs_0_), channel_id=1, source_target_pairs={{0,6},{1,7},{2,4},{3,5},{4,2},{5,3},{6,0},{7,1},{8,14},{9,15},{10,... | collective-permute-start | bytes 202760 | tf_op jit(solution)/shard_map/ppermute | solution.py:18
  46.0 1.8 %collective-permute-start.14 = (bf16[8,4224]{1,0:T(8,128)(2,1)S(1)}, bf16[8,4224]{1,0:T(8,128)(2,1)S(1)}, u32[]{:S(2)}, u32[]{:S(2)}) collective-permute-start(bf16[8,4224]{1,0:T(8,128)(2,1)S(1)} %shard_map.78.refs_0_), channel_id=1, source_target_pairs={{0,2},{1,3},{2,0},{3,1},{4,6},{5,7},{6,4},{7,5},{8,10},{9,11},{10,... | collective-permute-start | bytes 202760 | tf_op jit(solution)/shard_map/ppermute | solution.py:18
  47.9 1.8 %collective-permute-done.16.refs_3_ = bf16[8,4224]{1,0:T(8,128)(2,1)S(1)} collective-permute-done((bf16[8,4224]{1,0:T(8,128)(2,1)S(1)}, bf16[8,4224]{1,0:T(8,128)(2,1)S(1)}, u32[]{:S(2)}, u32[]{:S(2)}) %collective-permute-start.16) | collective-permute-done | bytes 67616 | tf_op jit(solution)/shard_map/ppermute | solution.py:18
  49.7 1.6 %collective-permute-done.15.refs_2_ = bf16[8,4224]{1,0:T(8,128)(2,1)S(1)} collective-permute-done((bf16[8,4224]{1,0:T(8,128)(2,1)S(1)}, bf16[8,4224]{1,0:T(8,128)(2,1)S(1)}, u32[]{:S(2)}, u32[]{:S(2)}) %collective-permute-start.15) | collective-permute-done | bytes 67616 | tf_op jit(solution)/shard_map/ppermute | solution.py:18
  51.3 1.5 %collective-permute-done.17.far = bf16[32,4224]{1,0:T(8,128)(2,1)S(1)} collective-permute-done((bf16[32,4224]{1,0:T(8,128)(2,1)S(1)}, bf16[32,4224]{1,0:T(8,128)(2,1)S(1)}, u32[]{:S(2)}, u32[]{:S(2)}) %collective-permute-start.17) | collective-permute-done | bytes 270368 | tf_op jit(solution)/shard_map/ppermute | solution.py:18
  52.9 2.3 %shard_map.80 = (bf16[128,256]{1,0:T(8,128)(2,1)S(1)}, bf16[32,8,512]{2,1,0:T(8,128)(2,1)}) custom-call(bf16[32,4224]{1,0:T(8,128)(2,1)S(1)} %shard_map.79.near, bf16[32,4224]{1,0:T(8,128)(2,1)S(1)} %collective-permute-done.17.far, f32[64,256]{1,0:T(8,128)S(1)} %get-tuple-element.23.logits, bf16[256,2048]{1,0:T(8,128)(2,1)S(1)} %copy-done, ...), custom_call_target="tpu_custom_call" | custom-call | flops 10000000000 | bytes 4194304 | tf_op jit(solution)/shard_map/pallas_call | solution.py:40
  55.2 3.7 %all-to-all-start = ((bf16[32,8,512]{2,1,0:T(8,128)(2,1)}), bf16[32,8,512]{2,1,0:T(8,128)(2,1)S(1)}, u32[]{:S(2)}, u32[]{:S(2)}) async-start(bf16[32,8,512]{2,1,0:T(8,128)(2,1)} %get-tuple-element.25), calls=%async_computation | async-start | bytes 524288 | tf_op jit(solution)/shard_map/all_to_all | solution.py:380
  58.9 1.4 %shard_map.81 = bf16[256,2048]{1,0:T(8,128)(2,1)} custom-call(bf16[128,256]{1,0:T(8,128)(2,1)S(1)} %get-tuple-element.24.weights, bf16[32,4224]{1,0:T(8,128)(2,1)S(1)} %shard_map.79.near, bf16[32,4224]{1,0:T(8,128)(2,1)S(1)} %collective-permute-done.17.far, bf16[32,2048]{1,0:T(8,128)(2,1)S(1)} %shard_map.69.near.table_near, ...), custom_call_target="tpu_custom_call" | custom-call | flops 10000000000 | bytes 4194304 | tf_op jit(solution)/shard_map/pallas_call | solution.py:40
  60.3 8.9 %all-to-all-done = bf16[32,8,512]{2,1,0:T(8,128)(2,1)S(1)} async-done(((bf16[32,8,512]{2,1,0:T(8,128)(2,1)}), bf16[32,8,512]{2,1,0:T(8,128)(2,1)S(1)}, u32[]{:S(2)}, u32[]{:S(2)}) %all-to-all-start) | async-done | bytes 262176 | tf_op jit(solution)/shard_map/all_to_all | solution.py:380
  69.3 0.7 convert_reduce_fusion
  (42 shorter events, 4.0 us)
Async XLA Ops:
  0.6 7.2 %collective-permute-start.2 = (bf16[8,2048]{1,0:T(8,128)(2,1)}, bf16[8,2048]{1,0:T(8,128)(2,1)S(1)}, u32[]{:S(2)}, u32[]{:S(2)}) collective-permute-start(bf16[8,2048]{1,0:T(8,128)(2,1)} %bitcast.8), channel_id=1, source_target_pairs={{0,6},{1,7},{2,4},{3,5},{4,2},{5,3},{6,0},{7,1},{8,14},{9,15},{10,... | collective-permute-start | bytes 98312 | tf_op jit(solution)/shard_map/ppermute | solution.py:18
  5.7 5.0 %collective-permute-start.1 = (bf16[8,2048]{1,0:T(8,128)(2,1)}, bf16[8,2048]{1,0:T(8,128)(2,1)S(1)}, u32[]{:S(2)}, u32[]{:S(2)}) collective-permute-start(bf16[8,2048]{1,0:T(8,128)(2,1)} %bitcast.9), channel_id=1, source_target_pairs={{0,4},{1,5},{2,6},{3,7},{4,0},{5,1},{6,2},{7,3},{8,12},{9,13},{10,... | collective-permute-start | bytes 98312 | tf_op jit(solution)/shard_map/ppermute | solution.py:18
  5.7 5.0 %collective-permute-start = (bf16[8,2048]{1,0:T(8,128)(2,1)}, bf16[8,2048]{1,0:T(8,128)(2,1)S(1)}, u32[]{:S(2)}, u32[]{:S(2)}) collective-permute-start(bf16[8,2048]{1,0:T(8,128)(2,1)} %bitcast.10), channel_id=1, source_target_pairs={{0,2},{1,3},{2,0},{3,1},{4,6},{5,7},{6,4},{7,5},{8,10},{9,11},{10,... | collective-permute-start | bytes 98312 | tf_op jit(solution)/shard_map/ppermute | solution.py:18
  6.4 0.8 %copy-start.2 = (bf16[2048,8]{0,1:T(8,128)(2,1)S(1)}, bf16[2048,8]{0,1:T(8,128)(2,1)}, u32[]{:S(2)}) copy-start(bf16[2048,8]{0,1:T(8,128)(2,1)} %param.6) | copy-start | bytes 98308
  7.2 5.0 %copy-start = (bf16[256,2048]{1,0:T(8,128)(2,1)S(1)}, bf16[256,2048]{1,0:T(8,128)(2,1)}, u32[]{:S(2)}) copy-start(bf16[256,2048]{1,0:T(8,128)(2,1)} %tokens.3) | copy-start | bytes 3145732
  7.2 5.0 %copy-start.1 = (bf16[256,2048]{1,0:T(8,128)(2,1)S(1)}, bf16[256,2048]{1,0:T(8,128)(2,1)}, u32[]{:S(2)}) copy-start(bf16[256,2048]{1,0:T(8,128)(2,1)} %out_grad.3) | copy-start | bytes 3145732
  10.8 1.4 %collective-permute-start.3 = (bf16[32,2048]{1,0:T(8,128)(2,1)S(1)}, bf16[32,2048]{1,0:T(8,128)(2,1)S(1)}, u32[]{:S(2)}, u32[]{:S(2)}) collective-permute-start(bf16[32,2048]{1,0:T(8,128)(2,1)S(1)} %shard_map.69.near.table_near), channel_id=1, source_target_pairs={{0,1},{1,0},{2,3},{3,2},{4,5},{5,4},{6,7},{7,6},{8,9},{9,8},{10,11... | collective-permute-start | bytes 393224 | tf_op jit(solution)/shard_map/ppermute | solution.py:18
  13.5 1.6 %collective-permute-start.4 = (bf16[32,4224]{1,0:T(8,128)(2,1)S(1)}, bf16[32,4224]{1,0:T(8,128)(2,1)S(1)}, u32[]{:S(2)}, u32[]{:S(2)}) collective-permute-start(bf16[32,4224]{1,0:T(8,128)(2,1)S(1)} %get-tuple-element.15), channel_id=1, source_target_pairs={{0,1},{1,0},{2,3},{3,2},{4,5},{5,4},{6,7},{7,6},{8,9},{9,8},{10,11... | collective-permute-start | bytes 811016 | tf_op jit(solution)/shard_map/ppermute | solution.py:18
  15.1 4.6 %slice-start.2 = ((s8[8388608]{0:T(1024)(128)(4,1)}), s8[4194304]{0:T(1024)(128)(4,1)S(1)}, s32[]{:S(2)}) async-start(s8[8388608]{0:T(1024)(128)(4,1)} %bitcast.4), calls=%async_computation.3 | async-start | bytes 8388608
  15.1 4.6 %slice-start.3 = ((s8[8388608]{0:T(1024)(128)(4,1)}), s8[4194304]{0:T(1024)(128)(4,1)S(1)}, s32[]{:S(2)}) async-start(s8[8388608]{0:T(1024)(128)(4,1)} %bitcast.4), calls=%async_computation.4 | async-start | bytes 8388608
  15.2 7.0 %collective-permute-start.5 = (bf16[8,4224]{1,0:T(8,128)(2,1)S(1)}, bf16[8,4224]{1,0:T(8,128)(2,1)S(1)}, u32[]{:S(2)}, u32[]{:S(2)}) collective-permute-start(bf16[8,4224]{1,0:T(8,128)(2,1)S(1)} %get-tuple-element.17), channel_id=1, source_target_pairs={{0,6},{1,7},{2,4},{3,5},{4,2},{5,3},{6,0},{7,1},{8,14},{9,15},{10,... | collective-permute-start | bytes 202760 | tf_op jit(solution)/shard_map/ppermute | solution.py:18
  16.8 7.4 %collective-permute-start.6 = (bf16[8,4224]{1,0:T(8,128)(2,1)S(1)}, bf16[8,4224]{1,0:T(8,128)(2,1)S(1)}, u32[]{:S(2)}, u32[]{:S(2)}) collective-permute-start(bf16[8,4224]{1,0:T(8,128)(2,1)S(1)} %get-tuple-element.18), channel_id=1, source_target_pairs={{0,4},{1,5},{2,6},{3,7},{4,0},{5,1},{6,2},{7,3},{8,12},{9,13},{10,... | collective-permute-start | bytes 202760 | tf_op jit(solution)/shard_map/ppermute | solution.py:18
  17.4 6.8 %collective-permute-start.7 = (bf16[8,4224]{1,0:T(8,128)(2,1)S(1)}, bf16[8,4224]{1,0:T(8,128)(2,1)S(1)}, u32[]{:S(2)}, u32[]{:S(2)}) collective-permute-start(bf16[8,4224]{1,0:T(8,128)(2,1)S(1)} %get-tuple-element.19), channel_id=1, source_target_pairs={{0,2},{1,3},{2,0},{3,1},{4,6},{5,7},{6,4},{7,5},{8,10},{9,11},{10,... | collective-permute-start | bytes 202760 | tf_op jit(solution)/shard_map/ppermute | solution.py:18
  20.9 6.9 %slice-start = ((s8[8388608]{0:T(1024)(128)(4,1)}), s8[4194304]{0:T(1024)(128)(4,1)S(1)}, s32[]{:S(2)}) async-start(s8[8388608]{0:T(1024)(128)(4,1)} %bitcast.2), calls=%async_computation.1 | async-start | bytes 8388608
  22.2 5.7 %slice-start.1 = ((s8[8388608]{0:T(1024)(128)(4,1)}), s8[4194304]{0:T(1024)(128)(4,1)S(1)}, s32[]{:S(2)}) async-start(s8[8388608]{0:T(1024)(128)(4,1)} %bitcast.2), calls=%async_computation.2 | async-start | bytes 8388608
  24.3 6.1 %collective-permute-start.10 = (bf16[8,4224]{1,0:T(8,128)(2,1)S(1)}, bf16[8,4224]{1,0:T(8,128)(2,1)S(1)}, u32[]{:S(2)}, u32[]{:S(2)}) collective-permute-start(bf16[8,4224]{1,0:T(8,128)(2,1)S(1)} %shard_map.72.after.refs_0_), channel_id=1, source_target_pairs={{0,24},{8,16},{16,8},{24,0},{1,25},{9,17},{17,9},{25,1},{2,26},{10... | collective-permute-start | bytes 202760 | tf_op jit(solution)/shard_map/ppermute | solution.py:18
  26.8 4.3 %collective-permute-start.9 = (bf16[8,4224]{1,0:T(8,128)(2,1)S(1)}, bf16[8,4224]{1,0:T(8,128)(2,1)S(1)}, u32[]{:S(2)}, u32[]{:S(2)}) collective-permute-start(bf16[8,4224]{1,0:T(8,128)(2,1)S(1)} %shard_map.72.after.refs_0_), channel_id=1, source_target_pairs={{0,16},{8,24},{16,0},{24,8},{1,17},{9,25},{17,1},{25,9},{2,18},{10... | collective-permute-start | bytes 202760 | tf_op jit(solution)/shard_map/ppermute | solution.py:18
  27.3 4.3 %collective-permute-start.8 = (bf16[8,4224]{1,0:T(8,128)(2,1)S(1)}, bf16[8,4224]{1,0:T(8,128)(2,1)S(1)}, u32[]{:S(2)}, u32[]{:S(2)}) collective-permute-start(bf16[8,4224]{1,0:T(8,128)(2,1)S(1)} %shard_map.72.after.refs_0_), channel_id=1, source_target_pairs={{0,8},{8,0},{16,24},{24,16},{1,9},{9,1},{17,25},{25,17},{2,10},{10... | collective-permute-start | bytes 202760 | tf_op jit(solution)/shard_map/ppermute | solution.py:18
  27.9 3.7 %slice-start.4 = ((s8[8388608]{0:T(1024)(128)(4,1)}), s8[4194304]{0:T(1024)(128)(4,1)S(1)}, s32[]{:S(2)}) async-start(s8[8388608]{0:T(1024)(128)(4,1)} %bitcast.6), calls=%async_computation.5 | async-start | bytes 8388608
  29.1 2.5 %slice-start.5 = ((s8[8388608]{0:T(1024)(128)(4,1)}), s8[4194304]{0:T(1024)(128)(4,1)S(1)}, s32[]{:S(2)}) async-start(s8[8388608]{0:T(1024)(128)(4,1)} %bitcast.6), calls=%async_computation.6 | async-start | bytes 8388608
  36.1 5.3 %collective-permute-start.13 = (bf16[8,4096]{1,0:T(8,128)(2,1)S(1)}, bf16[8,4096]{1,0:T(8,128)(2,1)S(1)}, u32[]{:S(2)}, u32[]{:S(2)}) collective-permute-start(bf16[8,4096]{1,0:T(8,128)(2,1)S(1)} %get-tuple-element.20.refs_0_), channel_id=1, source_target_pairs={{0,24},{8,16},{16,8},{24,0},{1,25},{9,17},{17,9},{25,1},{2,26},{10... | collective-permute-start | bytes 196616 | tf_op jit(solution)/shard_map/ppermute | solution.py:18
  38.5 4.3 %collective-permute-start.12 = (bf16[8,4096]{1,0:T(8,128)(2,1)S(1)}, bf16[8,4096]{1,0:T(8,128)(2,1)S(1)}, u32[]{:S(2)}, u32[]{:S(2)}) collective-permute-start(bf16[8,4096]{1,0:T(8,128)(2,1)S(1)} %get-tuple-element.20.refs_0_), channel_id=1, source_target_pairs={{0,16},{8,24},{16,0},{24,8},{1,17},{9,25},{17,1},{25,9},{2,18},{10... | collective-permute-start | bytes 196616 | tf_op jit(solution)/shard_map/ppermute | solution.py:18
  39.0 4.3 %collective-permute-start.11 = (bf16[8,4096]{1,0:T(8,128)(2,1)S(1)}, bf16[8,4096]{1,0:T(8,128)(2,1)S(1)}, u32[]{:S(2)}, u32[]{:S(2)}) collective-permute-start(bf16[8,4096]{1,0:T(8,128)(2,1)S(1)} %get-tuple-element.20.refs_0_), channel_id=1, source_target_pairs={{0,8},{8,0},{16,24},{24,16},{1,9},{9,1},{17,25},{25,17},{2,10},{10... | collective-permute-start | bytes 196616 | tf_op jit(solution)/shard_map/ppermute | solution.py:18
  43.4 6.2 %collective-permute-start.16 = (bf16[8,4224]{1,0:T(8,128)(2,1)S(1)}, bf16[8,4224]{1,0:T(8,128)(2,1)S(1)}, u32[]{:S(2)}, u32[]{:S(2)}) collective-permute-start(bf16[8,4224]{1,0:T(8,128)(2,1)S(1)} %shard_map.78.refs_0_), channel_id=1, source_target_pairs={{0,6},{1,7},{2,4},{3,5},{4,2},{5,3},{6,0},{7,1},{8,14},{9,15},{10,... | collective-permute-start | bytes 202760 | tf_op jit(solution)/shard_map/ppermute | solution.py:18
  46.0 5.2 %collective-permute-start.15 = (bf16[8,4224]{1,0:T(8,128)(2,1)S(1)}, bf16[8,4224]{1,0:T(8,128)(2,1)S(1)}, u32[]{:S(2)}, u32[]{:S(2)}) collective-permute-start(bf16[8,4224]{1,0:T(8,128)(2,1)S(1)} %shard_map.78.refs_0_), channel_id=1, source_target_pairs={{0,4},{1,5},{2,6},{3,7},{4,0},{5,1},{6,2},{7,3},{8,12},{9,13},{10,... | collective-permute-start | bytes 202760 | tf_op jit(solution)/shard_map/ppermute | solution.py:18
  46.0 5.2 %collective-permute-start.14 = (bf16[8,4224]{1,0:T(8,128)(2,1)S(1)}, bf16[8,4224]{1,0:T(8,128)(2,1)S(1)}, u32[]{:S(2)}, u32[]{:S(2)}) collective-permute-start(bf16[8,4224]{1,0:T(8,128)(2,1)S(1)} %shard_map.78.refs_0_), channel_id=1, source_target_pairs={{0,2},{1,3},{2,0},{3,1},{4,6},{5,7},{6,4},{7,5},{8,10},{9,11},{10,... | collective-permute-start | bytes 202760 | tf_op jit(solution)/shard_map/ppermute | solution.py:18
  51.3 1.6 %collective-permute-start.17 = (bf16[32,4224]{1,0:T(8,128)(2,1)S(1)}, bf16[32,4224]{1,0:T(8,128)(2,1)S(1)}, u32[]{:S(2)}, u32[]{:S(2)}) collective-permute-start(bf16[32,4224]{1,0:T(8,128)(2,1)S(1)} %shard_map.79.near), channel_id=1, source_target_pairs={{0,1},{1,0},{2,3},{3,2},{4,5},{5,4},{6,7},{7,6},{8,9},{9,8},{10,11... | collective-permute-start | bytes 811016 | tf_op jit(solution)/shard_map/ppermute | solution.py:18
  55.2 14.1 %all-to-all-start = ((bf16[32,8,512]{2,1,0:T(8,128)(2,1)}), bf16[32,8,512]{2,1,0:T(8,128)(2,1)S(1)}, u32[]{:S(2)}, u32[]{:S(2)}) async-start(bf16[32,8,512]{2,1,0:T(8,128)(2,1)} %get-tuple-element.25), calls=%async_computation | async-start | bytes 524288 | tf_op jit(solution)/shard_map/all_to_all | solution.py:380

commit v7 on v6

--- a/solution.py
+++ b/solution.py
@@ -22,10 +22,14 @@
     return [swap(x, axis, mask) for x, mask in zip(parts, masks)]
 
 
+def to_all(x, axis, masks):
+    return swaps([x] * len(masks), axis, masks)
+
+
 def groups(n, first):
     bits = [1 << k for k in range(n.bit_length() - 1) if 1 << k >= first]
     return [
-        [b for b in (pair[0], *pair[1:], sum(pair)) if b]
+        [sum(pair), pair[1], pair[0]]
         if len(pair) == 2
         else [pair[0]]
         for pair in (bits[k : k + 2] for k in range(0, len(bits), 2))
@@ -116,11 +120,11 @@
     return weight / jnp.sum(weight, axis=0, keepdims=True)
 
 
-def first_kernel(near, far, tokens, out_grad, logits_out, keep, send):
+def first_kernel(near, far, tokens_flipped, tokens, out_grad, logits_out, keep, send):
     width = tokens.shape[1]
     half = near.shape[0]
     logits = jnp.concatenate(
-        [product(near[...], tokens[...], 1, 1), product(far[...], tokens[...], 1, 1)], axis=0
+        [product(x[...], tokens_flipped[...], 1, 0) for x in (near, far)], axis=0
     )
     logits_out[...] = logits
     top = jnp.max(logits, axis=1, keepdims=True)
@@ -152,8 +156,7 @@
     outs = refs[count:]
     rows = outs[0].shape[0]
     stats = packed([top, total], sums.shape[0])
-    places = [0, *reversed(range(1, len(outs)))]
-    for k, out in zip(places, outs):
+    for k, out in enumerate(outs):
         part = slice(k * rows, (k + 1) * rows)
         out[:, :width] = sums[part].astype(BF16)
         out[:, width : 2 * width] = grads[part].astype(BF16)
@@ -171,6 +174,15 @@
 
 def flip_kernel(index, weight, after, out):
     out[...] = weight[index].T
+
+
+def flip_whole_kernel(x, out):
+    out[...] = x[...].T
+
+
+def flipped_whole(x):
+    shape = (x.shape[1], x.shape[0])
+    return local_call(flip_whole_kernel, [(shape, BF16)], x, flops=3 * 10**8)[0]
 
 
 def flipped(weights, after):
@@ -248,17 +260,18 @@
     out[:, 2 * width :] = packed([centre, top, denominator], stats.shape[0]).astype(BF16)
 
 
-def second_kernel(order, near, far, logits, tokens, out_grad, weights, blocks):
+def second_kernel(
+    order, near, far, logits, tokens_flipped, tokens, out_grad_flipped, weights, blocks
+):
     width = tokens.shape[1]
     half = near.shape[0]
 
     def against(columns, rows):
-        return jnp.concatenate(
-            [product(x[:, columns], rows[...], 1, 1) for x in (near, far)], axis=0
-        )
-
-    comb_grad = against(slice(0, width), out_grad)
-    disp_grad = against(slice(width, 2 * width), tokens)
+        both = jnp.concatenate([near[:, columns], far[:, columns]], axis=0)
+        return product(both, rows[...], 1, 0)
+
+    comb_grad = against(slice(0, width), out_grad_flipped)
+    disp_grad = against(slice(width, 2 * width), tokens_flipped)
     stats = jnp.concatenate([x[:, 2 * width :].astype(F32) for x in (near, far)], axis=0)
     centre, top, total = unpacked(stats, 3)
     scores = logits[...]
@@ -301,17 +314,19 @@
 
     def gathered_over_chips(x, here):
         for masks in reversed(chip_groups):
-            x = here = stack([here] + swaps([x] * len(masks), "exp", masks))
+            x = here = stack([here] + to_all(x, "exp", masks))
         return x
 
     table_near = gathered_over_chips(slot_embed.T, loaded(slot_embed.T))
     table_far = swap(table_near, "exp", 1)
 
+    tokens_flipped, out_grad_flipped = flipped_whole(tokens), flipped_whole(out_grad)
     logits, keep, send = local_call(
         first_kernel,
         [((slots, patches), F32), ((half, columns), BF16), ((half, columns), BF16)],
         table_near,
         table_far,
+        tokens_flipped,
         tokens,
         out_grad,
         limit=12,
@@ -319,11 +334,11 @@
     parts = [keep, swap(send, "exp", 1)]
     for masks in chip_groups:
         pieces = merge(parts, width, len(masks) + 1)
-        parts = [pieces[0]] + swaps(pieces[1:], "exp", masks[::-1])
+        parts = [pieces[0]] + swaps(pieces[1:], "exp", masks)
     own_piece = pieces[0]
     for masks in seq_groups:
         (x,) = merge(parts, width, 1)
-        parts = [x] + swaps([x] * len(masks), "seq", masks)
+        parts = [x] + to_all(x, "seq", masks)
     own_sum = x
 
     both, slot_sum, stats = local_call(
@@ -340,7 +355,7 @@
     for k, masks in enumerate(seq_groups):
         if k:
             parts = list(sum_of(parts, 1, BF16))
-        parts = parts + swaps(parts * len(masks), "seq", masks)
+        parts = parts + to_all(parts[0], "seq", masks)
     (packet,) = local_call(
         partial(centre_kernel, len(parts), width),
         [((own, columns), BF16)],
@@ -361,8 +376,9 @@
         near,
         far,
         logits,
+        tokens_flipped,
         tokens,
-        out_grad,
+        out_grad_flipped,
         limit=12,
     )
     (tok_grad,) = local_call(

time: 70.2 us -> 69.1 us (0.984)
    pallas_call x13 -> x15, Pallas kernels: 14.8 us -> 14.4 us  [local_call(): pl.pallas_call(body, out_shape=tuple((jax.ShapeDtypeStruct(s, d) if k in...]
  transfers between devices with their start and end apart: 19 -> 19, of which waited for: 14 -> 14; matrix products, arithmetic and copies ran while one was open for 0% -> 0% of each run, Pallas kernels for 9% -> 10%
where the time goes in v7:
time: 69.1 us; the launch traced here: 68.8 us
  waiting for transfers between devices  26.5 us (38%)
  starting transfers between devices  25.5 us (37%)
  Pallas kernels  14.5 us (21%)
  local copies, waits for them, and re-layouts  0.84 us (1%)
  between operations  0.82 us (1%)
    ppermute x18, starting transfers between devices, swap(): lax.ppermute(x, axis, [(k, k ^ mask) for k in range(lax.axis_size(axis))])  22.1 us
    ppermute x18, waiting for transfers between devices, swap(): lax.ppermute(x, axis, [(k, k ^ mask) for k in range(lax.axis_size(axis))])  17.6 us
    pallas_call x15, Pallas kernels, local_call(): pl.pallas_call(body, out_shape=tuple((jax.ShapeDtypeStruct(s, d) if k in...  14.4 us
    all_to_all x1, waiting for transfers between devices, shards(): part = lax.all_to_all(blocks, ('seq', 'exp'), 0, 0, tiled=True)  8.95 us
    all_to_all x1, starting transfers between devices, shards(): part = lax.all_to_all(blocks, ('seq', 'exp'), 0, 0, tiled=True)  3.45 us
  transfers between devices with their start and end apart: 19, of which 14 were waited for; matrix products, arithmetic and copies ran while one was open for 0% of the time, Pallas kernels for 10%

profile of v7, /device:TPU:0, one launch (start us, length us, event | category | flops | bytes accessed | tf_op | source)
XLA Modules:
  0.0 68.8 jit_solution(635747803681123908)
XLA Ops:
  0.6 5.1 %collective-permute-start = (bf16[8,2048]{1,0:T(8,128)(2,1)}, bf16[8,2048]{1,0:T(8,128)(2,1)S(1)}, u32[]{:S(2)}, u32[]{:S(2)}) collective-permute-start(bf16[8,2048]{1,0:T(8,128)(2,1)} %bitcast.8), channel_id=1, source_target_pairs={{0,6},{1,7},{2,4},{3,5},{4,2},{5,3},{6,0},{7,1},{8,14},{9,15},{10,... | collective-permute-start | bytes 98312 | tf_op jit(solution)/shard_map/ppermute | solution.py:18
  6.4 0.8 %copy-done.2 = bf16[2048,8]{0,1:T(8,128)(2,1)S(1)} copy-done((bf16[2048,8]{0,1:T(8,128)(2,1)S(1)}, bf16[2048,8]{0,1:T(8,128)(2,1)}, u32[]{:S(2)}) %copy-start.2) | copy-done | bytes 32792
  7.8 2.9 %collective-permute-done.1.refs_2_ = bf16[8,2048]{1,0:T(8,128)(2,1)S(1)} collective-permute-done((bf16[8,2048]{1,0:T(8,128)(2,1)}, bf16[8,2048]{1,0:T(8,128)(2,1)S(1)}, u32[]{:S(2)}, u32[]{:S(2)}) %collective-permute-start.1) | collective-permute-done | bytes 32800 | tf_op jit(solution)/shard_map/ppermute | solution.py:18
  11.2 1.0 %collective-permute-done.3.far.table_far = bf16[32,2048]{1,0:T(8,128)(2,1)S(1)} collective-permute-done((bf16[32,2048]{1,0:T(8,128)(2,1)S(1)}, bf16[32,2048]{1,0:T(8,128)(2,1)S(1)}, u32[]{:S(2)}, u32[]{:S(2)}) %collective-permute-start.3) | collective-permute-done | bytes 131104 | tf_op jit(solution)/shard_map/ppermute | solution.py:18
  12.2 1.0 %shard_map.71 = (f32[64,256]{1,0:T(8,128)S(1)}, bf16[32,4224]{1,0:T(8,128)(2,1)S(1)}, bf16[32,4224]{1,0:T(8,128)(2,1)S(1)}) custom-call(bf16[32,2048]{1,0:T(8,128)(2,1)S(1)} %shard_map.69.near.table_near, bf16[32,2048]{1,0:T(8,128)(2,1)S(1)} %collective-permute-done.3.far.table_far, bf16[2048,256]{1,0:T(8,128)(2,1)S(1)} %shard_map.70.tokens_flipped, ...), custom_call_target="tpu_custom_call" | custom-call | flops 10000000000 | bytes 4194304 | tf_op jit(solution)/shard_map/pallas_call | solution.py:44
  13.4 1.4 %collective-permute-done.4.refs_1_ = bf16[32,4224]{1,0:T(8,128)(2,1)S(1)} collective-permute-done((bf16[32,4224]{1,0:T(8,128)(2,1)S(1)}, bf16[32,4224]{1,0:T(8,128)(2,1)S(1)}, u32[]{:S(2)}, u32[]{:S(2)}) %collective-permute-start.4) | collective-permute-done | bytes 270368 | tf_op jit(solution)/shard_map/ppermute | solution.py:18
  15.0 1.6 %collective-permute-start.5 = (bf16[8,4224]{1,0:T(8,128)(2,1)S(1)}, bf16[8,4224]{1,0:T(8,128)(2,1)S(1)}, u32[]{:S(2)}, u32[]{:S(2)}) collective-permute-start(bf16[8,4224]{1,0:T(8,128)(2,1)S(1)} %get-tuple-element.17), channel_id=1, source_target_pairs={{0,6},{1,7},{2,4},{3,5},{4,2},{5,3},{6,0},{7,1},{8,14},{9,15},{10,... | collective-permute-start | bytes 202760 | tf_op jit(solution)/shard_map/ppermute | solution.py:18
  17.1 2.3 %collective-permute-start.7 = (bf16[8,4224]{1,0:T(8,128)(2,1)S(1)}, bf16[8,4224]{1,0:T(8,128)(2,1)S(1)}, u32[]{:S(2)}, u32[]{:S(2)}) collective-permute-start(bf16[8,4224]{1,0:T(8,128)(2,1)S(1)} %get-tuple-element.19), channel_id=1, source_target_pairs={{0,2},{1,3},{2,0},{3,1},{4,6},{5,7},{6,4},{7,5},{8,10},{9,11},{10,... | collective-permute-start | bytes 202760 | tf_op jit(solution)/shard_map/ppermute | solution.py:18
  19.4 1.2 %shard_map.76.refs_8_ = bf16[2048,1024]{1,0:T(8,128)(2,1)S(1)} custom-call(bf16[2,1024,2048]{2,1,0:T(8,128)(2,1)S(1)} %bitcast.5, bf16[8,4224]{1,0:T(8,128)(2,1)S(1)} %get-tuple-element.16.refs_0_.after), custom_call_target="tpu_custom_call" | custom-call | flops 1000000000 | bytes 4194304 | tf_op jit(solution)/shard_map/pallas_call | solution.py:44
  20.7 1.2 %shard_map.77.refs_9_ = bf16[2048,1024]{1,0:T(8,128)(2,1)S(1)} custom-call(bf16[2,1024,2048]{2,1,0:T(8,128)(2,1)S(1)} %bitcast.5, bf16[8,4224]{1,0:T(8,128)(2,1)S(1)} %get-tuple-element.16.refs_0_.after), custom_call_target="tpu_custom_call" | custom-call | flops 1000000000 | bytes 4194304 | tf_op jit(solution)/shard_map/pallas_call | solution.py:44
  22.0 2.0 %collective-permute-done.6.refs_2_ = bf16[8,4224]{1,0:T(8,128)(2,1)S(1)} collective-permute-done((bf16[8,4224]{1,0:T(8,128)(2,1)S(1)}, bf16[8,4224]{1,0:T(8,128)(2,1)S(1)}, u32[]{:S(2)}, u32[]{:S(2)}) %collective-permute-start.6) | collective-permute-done | bytes 67616 | tf_op jit(solution)/shard_map/ppermute | solution.py:18
  24.1 1.6 %collective-permute-start.10 = (bf16[8,4224]{1,0:T(8,128)(2,1)S(1)}, bf16[8,4224]{1,0:T(8,128)(2,1)S(1)}, u32[]{:S(2)}, u32[]{:S(2)}) collective-permute-start(bf16[8,4224]{1,0:T(8,128)(2,1)S(1)} %shard_map.73.after.refs_0_), channel_id=1, source_target_pairs={{0,8},{8,0},{16,24},{24,16},{1,9},{9,1},{17,25},{25,17},{2,10},{10... | collective-permute-start | bytes 202760 | tf_op jit(solution)/shard_map/ppermute | solution.py:18
  25.6 1.5 %collective-permute-start.8 = (bf16[8,4224]{1,0:T(8,128)(2,1)S(1)}, bf16[8,4224]{1,0:T(8,128)(2,1)S(1)}, u32[]{:S(2)}, u32[]{:S(2)}) collective-permute-start(bf16[8,4224]{1,0:T(8,128)(2,1)S(1)} %shard_map.73.after.refs_0_), channel_id=1, source_target_pairs={{0,24},{8,16},{16,8},{24,0},{1,25},{9,17},{17,9},{25,1},{2,26},{10... | collective-permute-start | bytes 202760 | tf_op jit(solution)/shard_map/ppermute | solution.py:18
  27.6 1.2 %shard_map.74.refs_6_ = bf16[1024,2048]{1,0:T(8,128)(2,1)S(1)} custom-call(bf16[2,2048,1024]{2,1,0:T(8,128)(2,1)S(1)} %bitcast.3, bf16[8,4224]{1,0:T(8,128)(2,1)S(1)} %shard_map.73.after.refs_0_), custom_call_target="tpu_custom_call" | custom-call | flops 1000000000 | bytes 4194304 | tf_op jit(solution)/shard_map/pallas_call | solution.py:44
  28.9 1.2 %shard_map.75.refs_7_ = bf16[1024,2048]{1,0:T(8,128)(2,1)S(1)} custom-call(bf16[2,2048,1024]{2,1,0:T(8,128)(2,1)S(1)} %bitcast.3, bf16[8,4224]{1,0:T(8,128)(2,1)S(1)} %shard_map.73.after.refs_0_), custom_call_target="tpu_custom_call" | custom-call | flops 1000000000 | bytes 4194304 | tf_op jit(solution)/shard_map/pallas_call | solution.py:44
  30.1 0.8 %collective-permute-done.8.refs_1_ = bf16[8,4224]{1,0:T(8,128)(2,1)S(1)} collective-permute-done((bf16[8,4224]{1,0:T(8,128)(2,1)S(1)}, bf16[8,4224]{1,0:T(8,128)(2,1)S(1)}, u32[]{:S(2)}, u32[]{:S(2)}) %collective-permute-start.8) | collective-permute-done | bytes 67616 | tf_op jit(solution)/shard_map/ppermute | solution.py:18
  30.9 1.0 %collective-permute-done.9.refs_2_ = bf16[8,4224]{1,0:T(8,128)(2,1)S(1)} collective-permute-done((bf16[8,4224]{1,0:T(8,128)(2,1)S(1)}, bf16[8,4224]{1,0:T(8,128)(2,1)S(1)}, u32[]{:S(2)}, u32[]{:S(2)}) %collective-permute-start.9) | collective-permute-done | bytes 67616 | tf_op jit(solution)/shard_map/ppermute | solution.py:18
  31.9 4.5 %shard_map.78 = (bf16[8,4096]{1,0:T(8,128)(2,1)S(1)}, f32[8,2048]{1,0:T(8,128)S(1)}, f32[8,128]{1,0:T(8,128)S(1)}) custom-call(bf16[8,4224]{1,0:T(8,128)(2,1)S(1)} %shard_map.73.after.refs_0_, bf16[8,4224]{1,0:T(8,128)(2,1)S(1)} %collective-permute-done.8.refs_1_, bf16[8,4224]{1,0:T(8,128)(2,1)S(1)} %collective-permute-done.9.refs_2_, ...), custom_call_target="tpu_custom_call" | custom-call | flops 10000000000 | bytes 4194304 | tf_op jit(solution)/shard_map/pallas_call | solution.py:44
  36.4 1.9 %collective-permute-start.11 = (bf16[8,4096]{1,0:T(8,128)(2,1)S(1)}, bf16[8,4096]{1,0:T(8,128)(2,1)S(1)}, u32[]{:S(2)}, u32[]{:S(2)}) collective-permute-start(bf16[8,4096]{1,0:T(8,128)(2,1)S(1)} %get-tuple-element.20.refs_0_), channel_id=1, source_target_pairs={{0,24},{8,16},{16,8},{24,0},{1,25},{9,17},{17,9},{25,1},{2,26},{10... | collective-permute-start | bytes 196616 | tf_op jit(solution)/shard_map/ppermute | solution.py:18
  38.3 0.8 %collective-permute-start.12 = (bf16[8,4096]{1,0:T(8,128)(2,1)S(1)}, bf16[8,4096]{1,0:T(8,128)(2,1)S(1)}, u32[]{:S(2)}, u32[]{:S(2)}) collective-permute-start(bf16[8,4096]{1,0:T(8,128)(2,1)S(1)} %get-tuple-element.20.refs_0_), channel_id=1, source_target_pairs={{0,16},{8,24},{16,0},{24,8},{1,17},{9,25},{17,1},{25,9},{2,18},{10... | collective-permute-start | bytes 196616 | tf_op jit(solution)/shard_map/ppermute | solution.py:18
  39.1 0.9 %collective-permute-start.13 = (bf16[8,4096]{1,0:T(8,128)(2,1)S(1)}, bf16[8,4096]{1,0:T(8,128)(2,1)S(1)}, u32[]{:S(2)}, u32[]{:S(2)}) collective-permute-start(bf16[8,4096]{1,0:T(8,128)(2,1)S(1)} %get-tuple-element.20.refs_0_), channel_id=1, source_target_pairs={{0,8},{8,0},{16,24},{24,16},{1,9},{9,1},{17,25},{25,17},{2,10},{10... | collective-permute-start | bytes 196616 | tf_op jit(solution)/shard_map/ppermute | solution.py:18
  39.9 2.3 %collective-permute-done.11.refs_1_ = bf16[8,4096]{1,0:T(8,128)(2,1)S(1)} collective-permute-done((bf16[8,4096]{1,0:T(8,128)(2,1)S(1)}, bf16[8,4096]{1,0:T(8,128)(2,1)S(1)}, u32[]{:S(2)}, u32[]{:S(2)}) %collective-permute-start.11) | collective-permute-done | bytes 65568 | tf_op jit(solution)/shard_map/ppermute | solution.py:18
  43.4 2.4 %collective-permute-start.14 = (bf16[8,4224]{1,0:T(8,128)(2,1)S(1)}, bf16[8,4224]{1,0:T(8,128)(2,1)S(1)}, u32[]{:S(2)}, u32[]{:S(2)}) collective-permute-start(bf16[8,4224]{1,0:T(8,128)(2,1)S(1)} %shard_map.79.refs_0_), channel_id=1, source_target_pairs={{0,6},{1,7},{2,4},{3,5},{4,2},{5,3},{6,0},{7,1},{8,14},{9,15},{10,... | collective-permute-start | bytes 202760 | tf_op jit(solution)/shard_map/ppermute | solution.py:18
  45.9 2.0 %collective-permute-start.16 = (bf16[8,4224]{1,0:T(8,128)(2,1)S(1)}, bf16[8,4224]{1,0:T(8,128)(2,1)S(1)}, u32[]{:S(2)}, u32[]{:S(2)}) collective-permute-start(bf16[8,4224]{1,0:T(8,128)(2,1)S(1)} %shard_map.79.refs_0_), channel_id=1, source_target_pairs={{0,2},{1,3},{2,0},{3,1},{4,6},{5,7},{6,4},{7,5},{8,10},{9,11},{10,... | collective-permute-start | bytes 202760 | tf_op jit(solution)/shard_map/ppermute | solution.py:18
  47.9 1.8 %collective-permute-done.14.refs_1_ = bf16[8,4224]{1,0:T(8,128)(2,1)S(1)} collective-permute-done((bf16[8,4224]{1,0:T(8,128)(2,1)S(1)}, bf16[8,4224]{1,0:T(8,128)(2,1)S(1)}, u32[]{:S(2)}, u32[]{:S(2)}) %collective-permute-start.14) | collective-permute-done | bytes 67616 | tf_op jit(solution)/shard_map/ppermute | solution.py:18
  49.7 1.5 %collective-permute-done.15.refs_2_ = bf16[8,4224]{1,0:T(8,128)(2,1)S(1)} collective-permute-done((bf16[8,4224]{1,0:T(8,128)(2,1)S(1)}, bf16[8,4224]{1,0:T(8,128)(2,1)S(1)}, u32[]{:S(2)}, u32[]{:S(2)}) %collective-permute-start.15) | collective-permute-done | bytes 67616 | tf_op jit(solution)/shard_map/ppermute | solution.py:18
  51.6 1.2 %collective-permute-done.17.far = bf16[32,4224]{1,0:T(8,128)(2,1)S(1)} collective-permute-done((bf16[32,4224]{1,0:T(8,128)(2,1)S(1)}, bf16[32,4224]{1,0:T(8,128)(2,1)S(1)}, u32[]{:S(2)}, u32[]{:S(2)}) %collective-permute-start.17) | collective-permute-done | bytes 270368 | tf_op jit(solution)/shard_map/ppermute | solution.py:18
  52.8 1.5 %shard_map.82 = (bf16[128,256]{1,0:T(8,128)(2,1)S(1)}, bf16[32,8,512]{2,1,0:T(8,128)(2,1)}) custom-call(bf16[32,4224]{1,0:T(8,128)(2,1)S(1)} %shard_map.80.near, bf16[32,4224]{1,0:T(8,128)(2,1)S(1)} %collective-permute-done.17.far, f32[64,256]{1,0:T(8,128)S(1)} %get-tuple-element.23.logits, bf16[2048,256]{1,0:T(8,128)(2,1)S(1)} %shard_map.70.tokens_flipped, ...), custom_call_target="tpu_custom_call" | custom-call | flops 10000000000 | bytes 4194304 | tf_op jit(solution)/shard_map/pallas_call | solution.py:44
  54.3 3.5 %all-to-all-start = ((bf16[32,8,512]{2,1,0:T(8,128)(2,1)}), bf16[32,8,512]{2,1,0:T(8,128)(2,1)S(1)}, u32[]{:S(2)}, u32[]{:S(2)}) async-start(bf16[32,8,512]{2,1,0:T(8,128)(2,1)} %get-tuple-element.25), calls=%async_computation | async-start | bytes 524288 | tf_op jit(solution)/shard_map/all_to_all | solution.py:396
  57.8 1.4 %shard_map.83 = bf16[256,2048]{1,0:T(8,128)(2,1)} custom-call(bf16[128,256]{1,0:T(8,128)(2,1)S(1)} %get-tuple-element.24.weights, bf16[32,4224]{1,0:T(8,128)(2,1)S(1)} %shard_map.80.near, bf16[32,4224]{1,0:T(8,128)(2,1)S(1)} %collective-permute-done.17.far, bf16[32,2048]{1,0:T(8,128)(2,1)S(1)} %shard_map.69.near.table_near, ...), custom_call_target="tpu_custom_call" | custom-call | flops 10000000000 | bytes 4194304 | tf_op jit(solution)/shard_map/pallas_call | solution.py:44
  59.2 8.9 %all-to-all-done = bf16[32,8,512]{2,1,0:T(8,128)(2,1)S(1)} async-done(((bf16[32,8,512]{2,1,0:T(8,128)(2,1)}), bf16[32,8,512]{2,1,0:T(8,128)(2,1)S(1)}, u32[]{:S(2)}, u32[]{:S(2)}) %all-to-all-start) | async-done | bytes 262176 | tf_op jit(solution)/shard_map/all_to_all | solution.py:396
  68.2 0.7 convert_reduce_fusion
  (44 shorter events, 5.0 us)
Async XLA Ops:
  0.6 7.2 %collective-permute-start = (bf16[8,2048]{1,0:T(8,128)(2,1)}, bf16[8,2048]{1,0:T(8,128)(2,1)S(1)}, u32[]{:S(2)}, u32[]{:S(2)}) collective-permute-start(bf16[8,2048]{1,0:T(8,128)(2,1)} %bitcast.8), channel_id=1, source_target_pairs={{0,6},{1,7},{2,4},{3,5},{4,2},{5,3},{6,0},{7,1},{8,14},{9,15},{10,... | collective-permute-start | bytes 98312 | tf_op jit(solution)/shard_map/ppermute | solution.py:18
  5.7 5.0 %collective-permute-start.1 = (bf16[8,2048]{1,0:T(8,128)(2,1)}, bf16[8,2048]{1,0:T(8,128)(2,1)S(1)}, u32[]{:S(2)}, u32[]{:S(2)}) collective-permute-start(bf16[8,2048]{1,0:T(8,128)(2,1)} %bitcast.9), channel_id=1, source_target_pairs={{0,4},{1,5},{2,6},{3,7},{4,0},{5,1},{6,2},{7,3},{8,12},{9,13},{10,... | collective-permute-start | bytes 98312 | tf_op jit(solution)/shard_map/ppermute | solution.py:18
  5.7 5.0 %collective-permute-start.2 = (bf16[8,2048]{1,0:T(8,128)(2,1)}, bf16[8,2048]{1,0:T(8,128)(2,1)S(1)}, u32[]{:S(2)}, u32[]{:S(2)}) collective-permute-start(bf16[8,2048]{1,0:T(8,128)(2,1)} %bitcast.10), channel_id=1, source_target_pairs={{0,2},{1,3},{2,0},{3,1},{4,6},{5,7},{6,4},{7,5},{8,10},{9,11},{10,... | collective-permute-start | bytes 98312 | tf_op jit(solution)/shard_map/ppermute | solution.py:18
  6.4 0.8 %copy-start.2 = (bf16[2048,8]{0,1:T(8,128)(2,1)S(1)}, bf16[2048,8]{0,1:T(8,128)(2,1)}, u32[]{:S(2)}) copy-start(bf16[2048,8]{0,1:T(8,128)(2,1)} %param.6) | copy-start | bytes 98308
  7.2 3.7 %copy-start.1 = (bf16[256,2048]{1,0:T(8,128)(2,1)S(1)}, bf16[256,2048]{1,0:T(8,128)(2,1)}, u32[]{:S(2)}) copy-start(bf16[256,2048]{1,0:T(8,128)(2,1)} %tokens.3) | copy-start | bytes 3145732
  7.2 5.0 %copy-start = (bf16[256,2048]{1,0:T(8,128)(2,1)S(1)}, bf16[256,2048]{1,0:T(8,128)(2,1)}, u32[]{:S(2)}) copy-start(bf16[256,2048]{1,0:T(8,128)(2,1)} %x.3) | copy-start | bytes 3145732
  10.8 1.4 %collective-permute-start.3 = (bf16[32,2048]{1,0:T(8,128)(2,1)S(1)}, bf16[32,2048]{1,0:T(8,128)(2,1)S(1)}, u32[]{:S(2)}, u32[]{:S(2)}) collective-permute-start(bf16[32,2048]{1,0:T(8,128)(2,1)S(1)} %shard_map.69.near.table_near), channel_id=1, source_target_pairs={{0,1},{1,0},{2,3},{3,2},{4,5},{5,4},{6,7},{7,6},{8,9},{9,8},{10,11... | collective-permute-start | bytes 393224 | tf_op jit(solution)/shard_map/ppermute | solution.py:18
  13.2 1.6 %collective-permute-start.4 = (bf16[32,4224]{1,0:T(8,128)(2,1)S(1)}, bf16[32,4224]{1,0:T(8,128)(2,1)S(1)}, u32[]{:S(2)}, u32[]{:S(2)}) collective-permute-start(bf16[32,4224]{1,0:T(8,128)(2,1)S(1)} %get-tuple-element.15), channel_id=1, source_target_pairs={{0,1},{1,0},{2,3},{3,2},{4,5},{5,4},{6,7},{7,6},{8,9},{9,8},{10,11... | collective-permute-start | bytes 811016 | tf_op jit(solution)/shard_map/ppermute | solution.py:18
  14.8 4.6 %slice-start.2 = ((s8[8388608]{0:T(1024)(128)(4,1)}), s8[4194304]{0:T(1024)(128)(4,1)S(1)}, s32[]{:S(2)}) async-start(s8[8388608]{0:T(1024)(128)(4,1)} %bitcast.4), calls=%async_computation.3 | async-start | bytes 8388608
  14.8 4.6 %slice-start.3 = ((s8[8388608]{0:T(1024)(128)(4,1)}), s8[4194304]{0:T(1024)(128)(4,1)S(1)}, s32[]{:S(2)}) async-start(s8[8388608]{0:T(1024)(128)(4,1)} %bitcast.4), calls=%async_computation.4 | async-start | bytes 8388608
  15.0 7.0 %collective-permute-start.5 = (bf16[8,4224]{1,0:T(8,128)(2,1)S(1)}, bf16[8,4224]{1,0:T(8,128)(2,1)S(1)}, u32[]{:S(2)}, u32[]{:S(2)}) collective-permute-start(bf16[8,4224]{1,0:T(8,128)(2,1)S(1)} %get-tuple-element.17), channel_id=1, source_target_pairs={{0,6},{1,7},{2,4},{3,5},{4,2},{5,3},{6,0},{7,1},{8,14},{9,15},{10,... | collective-permute-start | bytes 202760 | tf_op jit(solution)/shard_map/ppermute | solution.py:18
  16.5 7.4 %collective-permute-start.6 = (bf16[8,4224]{1,0:T(8,128)(2,1)S(1)}, bf16[8,4224]{1,0:T(8,128)(2,1)S(1)}, u32[]{:S(2)}, u32[]{:S(2)}) collective-permute-start(bf16[8,4224]{1,0:T(8,128)(2,1)S(1)} %get-tuple-element.18), channel_id=1, source_target_pairs={{0,4},{1,5},{2,6},{3,7},{4,0},{5,1},{6,2},{7,3},{8,12},{9,13},{10,... | collective-permute-start | bytes 202760 | tf_op jit(solution)/shard_map/ppermute | solution.py:18
  17.1 6.8 %collective-permute-start.7 = (bf16[8,4224]{1,0:T(8,128)(2,1)S(1)}, bf16[8,4224]{1,0:T(8,128)(2,1)S(1)}, u32[]{:S(2)}, u32[]{:S(2)}) collective-permute-start(bf16[8,4224]{1,0:T(8,128)(2,1)S(1)} %get-tuple-element.19), channel_id=1, source_target_pairs={{0,2},{1,3},{2,0},{3,1},{4,6},{5,7},{6,4},{7,5},{8,10},{9,11},{10,... | collective-permute-start | bytes 202760 | tf_op jit(solution)/shard_map/ppermute | solution.py:18
  20.7 6.9 %slice-start = ((s8[8388608]{0:T(1024)(128)(4,1)}), s8[4194304]{0:T(1024)(128)(4,1)S(1)}, s32[]{:S(2)}) async-start(s8[8388608]{0:T(1024)(128)(4,1)} %bitcast.2), calls=%async_computation.1 | async-start | bytes 8388608
  22.0 5.7 %slice-start.1 = ((s8[8388608]{0:T(1024)(128)(4,1)}), s8[4194304]{0:T(1024)(128)(4,1)S(1)}, s32[]{:S(2)}) async-start(s8[8388608]{0:T(1024)(128)(4,1)} %bitcast.2), calls=%async_computation.2 | async-start | bytes 8388608
  24.1 6.1 %collective-permute-start.10 = (bf16[8,4224]{1,0:T(8,128)(2,1)S(1)}, bf16[8,4224]{1,0:T(8,128)(2,1)S(1)}, u32[]{:S(2)}, u32[]{:S(2)}) collective-permute-start(bf16[8,4224]{1,0:T(8,128)(2,1)S(1)} %shard_map.73.after.refs_0_), channel_id=1, source_target_pairs={{0,8},{8,0},{16,24},{24,16},{1,9},{9,1},{17,25},{25,17},{2,10},{10... | collective-permute-start | bytes 202760 | tf_op jit(solution)/shard_map/ppermute | solution.py:18
  25.6 5.3 %collective-permute-start.8 = (bf16[8,4224]{1,0:T(8,128)(2,1)S(1)}, bf16[8,4224]{1,0:T(8,128)(2,1)S(1)}, u32[]{:S(2)}, u32[]{:S(2)}) collective-permute-start(bf16[8,4224]{1,0:T(8,128)(2,1)S(1)} %shard_map.73.after.refs_0_), channel_id=1, source_target_pairs={{0,24},{8,16},{16,8},{24,0},{1,25},{9,17},{17,9},{25,1},{2,26},{10... | collective-permute-start | bytes 202760 | tf_op jit(solution)/shard_map/ppermute | solution.py:18
  27.1 4.8 %collective-permute-start.9 = (bf16[8,4224]{1,0:T(8,128)(2,1)S(1)}, bf16[8,4224]{1,0:T(8,128)(2,1)S(1)}, u32[]{:S(2)}, u32[]{:S(2)}) collective-permute-start(bf16[8,4224]{1,0:T(8,128)(2,1)S(1)} %shard_map.73.after.refs_0_), channel_id=1, source_target_pairs={{0,16},{8,24},{16,0},{24,8},{1,17},{9,25},{17,1},{25,9},{2,18},{10... | collective-permute-start | bytes 202760 | tf_op jit(solution)/shard_map/ppermute | solution.py:18
  27.6 4.3 %slice-start.4 = ((s8[8388608]{0:T(1024)(128)(4,1)}), s8[4194304]{0:T(1024)(128)(4,1)S(1)}, s32[]{:S(2)}) async-start(s8[8388608]{0:T(1024)(128)(4,1)} %bitcast.6), calls=%async_computation.5 | async-start | bytes 8388608
  28.9 3.0 %slice-start.5 = ((s8[8388608]{0:T(1024)(128)(4,1)}), s8[4194304]{0:T(1024)(128)(4,1)S(1)}, s32[]{:S(2)}) async-start(s8[8388608]{0:T(1024)(128)(4,1)} %bitcast.6), calls=%async_computation.6 | async-start | bytes 8388608
  36.4 5.8 %collective-permute-start.11 = (bf16[8,4096]{1,0:T(8,128)(2,1)S(1)}, bf16[8,4096]{1,0:T(8,128)(2,1)S(1)}, u32[]{:S(2)}, u32[]{:S(2)}) collective-permute-start(bf16[8,4096]{1,0:T(8,128)(2,1)S(1)} %get-tuple-element.20.refs_0_), channel_id=1, source_target_pairs={{0,24},{8,16},{16,8},{24,0},{1,25},{9,17},{17,9},{25,1},{2,26},{10... | collective-permute-start | bytes 196616 | tf_op jit(solution)/shard_map/ppermute | solution.py:18
  38.3 4.4 %collective-permute-start.12 = (bf16[8,4096]{1,0:T(8,128)(2,1)S(1)}, bf16[8,4096]{1,0:T(8,128)(2,1)S(1)}, u32[]{:S(2)}, u32[]{:S(2)}) collective-permute-start(bf16[8,4096]{1,0:T(8,128)(2,1)S(1)} %get-tuple-element.20.refs_0_), channel_id=1, source_target_pairs={{0,16},{8,24},{16,0},{24,8},{1,17},{9,25},{17,1},{25,9},{2,18},{10... | collective-permute-start | bytes 196616 | tf_op jit(solution)/shard_map/ppermute | solution.py:18
  39.1 4.3 %collective-permute-start.13 = (bf16[8,4096]{1,0:T(8,128)(2,1)S(1)}, bf16[8,4096]{1,0:T(8,128)(2,1)S(1)}, u32[]{:S(2)}, u32[]{:S(2)}) collective-permute-start(bf16[8,4096]{1,0:T(8,128)(2,1)S(1)} %get-tuple-element.20.refs_0_), channel_id=1, source_target_pairs={{0,8},{8,0},{16,24},{24,16},{1,9},{9,1},{17,25},{25,17},{2,10},{10... | collective-permute-start | bytes 196616 | tf_op jit(solution)/shard_map/ppermute | solution.py:18
  43.4 6.3 %collective-permute-start.14 = (bf16[8,4224]{1,0:T(8,128)(2,1)S(1)}, bf16[8,4224]{1,0:T(8,128)(2,1)S(1)}, u32[]{:S(2)}, u32[]{:S(2)}) collective-permute-start(bf16[8,4224]{1,0:T(8,128)(2,1)S(1)} %shard_map.79.refs_0_), channel_id=1, source_target_pairs={{0,6},{1,7},{2,4},{3,5},{4,2},{5,3},{6,0},{7,1},{8,14},{9,15},{10,... | collective-permute-start | bytes 202760 | tf_op jit(solution)/shard_map/ppermute | solution.py:18
  45.9 5.3 %collective-permute-start.15 = (bf16[8,4224]{1,0:T(8,128)(2,1)S(1)}, bf16[8,4224]{1,0:T(8,128)(2,1)S(1)}, u32[]{:S(2)}, u32[]{:S(2)}) collective-permute-start(bf16[8,4224]{1,0:T(8,128)(2,1)S(1)} %shard_map.79.refs_0_), channel_id=1, source_target_pairs={{0,4},{1,5},{2,6},{3,7},{4,0},{5,1},{6,2},{7,3},{8,12},{9,13},{10,... | collective-permute-start | bytes 202760 | tf_op jit(solution)/shard_map/ppermute | solution.py:18
  45.9 5.3 %collective-permute-start.16 = (bf16[8,4224]{1,0:T(8,128)(2,1)S(1)}, bf16[8,4224]{1,0:T(8,128)(2,1)S(1)}, u32[]{:S(2)}, u32[]{:S(2)}) collective-permute-start(bf16[8,4224]{1,0:T(8,128)(2,1)S(1)} %shard_map.79.refs_0_), channel_id=1, source_target_pairs={{0,2},{1,3},{2,0},{3,1},{4,6},{5,7},{6,4},{7,5},{8,10},{9,11},{10,... | collective-permute-start | bytes 202760 | tf_op jit(solution)/shard_map/ppermute | solution.py:18
  51.2 1.6 %collective-permute-start.17 = (bf16[32,4224]{1,0:T(8,128)(2,1)S(1)}, bf16[32,4224]{1,0:T(8,128)(2,1)S(1)}, u32[]{:S(2)}, u32[]{:S(2)}) collective-permute-start(bf16[32,4224]{1,0:T(8,128)(2,1)S(1)} %shard_map.80.near), channel_id=1, source_target_pairs={{0,1},{1,0},{2,3},{3,2},{4,5},{5,4},{6,7},{7,6},{8,9},{9,8},{10,11... | collective-permute-start | bytes 811016 | tf_op jit(solution)/shard_map/ppermute | solution.py:18
  54.3 13.8 %all-to-all-start = ((bf16[32,8,512]{2,1,0:T(8,128)(2,1)}), bf16[32,8,512]{2,1,0:T(8,128)(2,1)S(1)}, u32[]{:S(2)}, u32[]{:S(2)}) async-start(bf16[32,8,512]{2,1,0:T(8,128)(2,1)} %get-tuple-element.25), calls=%async_computation | async-start | bytes 524288 | tf_op jit(solution)/shard_map/all_to_all | solution.py:396

commit v8 on v7

--- a/solution.py
+++ b/solution.py
@@ -120,23 +120,51 @@
     return weight / jnp.sum(weight, axis=0, keepdims=True)
 
 
-def first_kernel(near, far, tokens_flipped, tokens, out_grad, logits_out, keep, send):
-    width = tokens.shape[1]
-    half = near.shape[0]
+def logit_kernel(table, tokens_flipped, tokens_far, logits_out, stats):
     logits = jnp.concatenate(
-        [product(x[...], tokens_flipped[...], 1, 0) for x in (near, far)], axis=0
+        [
+            product(table[...], tokens_flipped[...], 1, 0),
+            product(table[...], tokens_far[...], 1, 1),
+        ],
+        axis=1,
     )
     logits_out[...] = logits
-    top = jnp.max(logits, axis=1, keepdims=True)
-    weight = jnp.exp(logits - top)
-    stats = packed([top, jnp.sum(weight, axis=1, keepdims=True)], 2 * half).astype(BF16)
-    sums = product(weight.astype(BF16), tokens[...], 1, 0).astype(BF16)
-    grads = product(softmax_columns(logits).astype(BF16), out_grad[...], 1, 0).astype(BF16)
-    for k, out in enumerate((keep, send)):
-        rows = slice(k * half, (k + 1) * half)
-        out[:, :width] = sums[rows]
-        out[:, width : 2 * width] = grads[rows]
-        out[:, 2 * width :] = stats[rows]
+    top = jnp.max(logits, axis=0, keepdims=True)
+    total = jnp.sum(jnp.exp(logits - top), axis=0, keepdims=True)
+    row = lax.broadcasted_iota(jnp.int32, stats.shape, 0)
+    stats[...] = jnp.where(row == 0, top, jnp.where(row == 1, total, 0.0))
+
+
+def far_logit_kernel(table, tokens_flipped, out):
+    out[...] = product(table[...], tokens_flipped[...], 1, 0)
+
+
+def dispatch_kernel(logits, tokens, tokens_far, table, sums, stats, table_out):
+    table_out[...] = table[...]
+    patches = tokens.shape[0]
+    top = jnp.max(logits[...], axis=1, keepdims=True)
+    weight = jnp.exp(logits[...] - top)
+    stats[...] = packed([top, jnp.sum(weight, axis=1, keepdims=True)], stats.shape[0]).astype(BF16)
+    weight = weight.astype(BF16)
+    both = product(weight[:, :patches], tokens[...], 1, 0)
+    both += product(weight[:, patches:], tokens_far[...], 1, 0)
+    sums[...] = both.astype(BF16)
+
+
+def combine_kernel(logits, rows, rows_far, out_grad, out_far, sums, stats, *outs):
+    patches, width = out_grad.shape
+    other = jnp.concatenate([rows_far[:, patches:], rows_far[:, :patches]], axis=1)
+    top = jnp.maximum(rows[:1], other[:1])
+    total = rows[1:2] * jnp.exp(rows[:1] - top) + other[1:2] * jnp.exp(other[:1] - top)
+    combine = (jnp.exp(logits[...] - top) / total).astype(BF16)
+    grads = product(combine[:, :patches], out_grad[...], 1, 0)
+    grads += product(combine[:, patches:], out_far[...], 1, 0)
+    count = outs[0].shape[0]
+    for k, out in enumerate(outs):
+        part = slice(k * count, (k + 1) * count)
+        out[:, :width] = sums[part].astype(BF16)
+        out[:, width : 2 * width] = grads[part].astype(BF16)
+        out[:, 2 * width :] = stats[part]
 
 
 def merged(refs, width):
@@ -151,9 +179,9 @@
     return sums, grads, top, total
 
 
-def merge_kernel(count, width, *refs):
+def merge_kernel(count, unread, width, *refs):
     sums, grads, top, total = merged(refs[:count], width)
-    outs = refs[count:]
+    outs = refs[count + unread :]
     rows = outs[0].shape[0]
     stats = packed([top, total], sums.shape[0])
     for k, out in enumerate(outs):
@@ -163,12 +191,13 @@
         out[:, 2 * width :] = stats[part].astype(BF16)
 
 
-def merge(parts, width, pieces):
+def merge(parts, width, pieces, *after):
     rows, columns = parts[0].shape
     return local_call(
-        partial(merge_kernel, len(parts), width),
+        partial(merge_kernel, len(parts), len(after), width),
         [((rows // pieces, columns), BF16)] * pieces,
         *parts,
+        *after,
     )
 
 
@@ -251,7 +280,7 @@
 
 def centre_kernel(count, width, *refs):
     parts = refs[:count]
-    slot_sum, stats, out = refs[count:]
+    slot_sum, stats, _, out = refs[count:]
     total = sum(r[...].astype(F32) for r in parts).astype(BF16)
     grad_in = total[:, width:].astype(F32)
     centre = jnp.sum(slot_sum[...] * grad_in, axis=1, keepdims=True)
@@ -261,7 +290,7 @@
 
 
 def second_kernel(
-    order, near, far, logits, tokens_flipped, tokens, out_grad_flipped, weights, blocks
+    order, near, far, logits_near, logits_far, tokens_flipped, tokens, out_grad_flipped, weights, blocks
 ):
     width = tokens.shape[1]
     half = near.shape[0]
@@ -274,7 +303,7 @@
     disp_grad = against(slice(width, 2 * width), tokens_flipped)
     stats = jnp.concatenate([x[:, 2 * width :].astype(F32) for x in (near, far)], axis=0)
     centre, top, total = unpacked(stats, 3)
-    scores = logits[...]
+    scores = jnp.concatenate([logits_near[:, : tokens.shape[0]], logits_far[...]], axis=0)
     dispatch = jnp.exp(scores - top) / total
     combine = softmax_columns(scores)
     comb_mean = jnp.sum(combine * comb_grad, axis=0, keepdims=True)
@@ -318,22 +347,45 @@
         return x
 
     table_near = gathered_over_chips(slot_embed.T, loaded(slot_embed.T))
-    table_far = swap(table_near, "exp", 1)
+    tokens_far, out_far = swap(tokens, "exp", 1), swap(out_grad, "exp", 1)
 
     tokens_flipped, out_grad_flipped = flipped_whole(tokens), flipped_whole(out_grad)
-    logits, keep, send = local_call(
-        first_kernel,
-        [((slots, patches), F32), ((half, columns), BF16), ((half, columns), BF16)],
+    logits, rows = local_call(
+        logit_kernel,
+        [((half, 2 * patches), F32), ((8, 2 * patches), F32)],
         table_near,
-        table_far,
         tokens_flipped,
+        tokens_far,
+    )
+    sums, stats, table_sent = local_call(
+        dispatch_kernel,
+        [((half, width), BF16), ((half, LANES), BF16), ((half, width), BF16)],
+        logits,
         tokens,
+        tokens_far,
+        table_near,
+        flops=10**9,
+    )
+    table_far = swap(table_sent, "exp", 1)
+    (logits_far,) = local_call(
+        far_logit_kernel, [((half, patches), F32)], table_far, tokens_flipped, flops=3 * 10**8
+    )
+    pieces_first = len(chip_groups[0]) + 1
+    pieces = local_call(
+        combine_kernel,
+        [((half // pieces_first, columns), BF16)] * pieces_first,
+        logits,
+        rows,
+        swap(rows, "exp", 1),
         out_grad,
+        out_far,
+        sums,
+        stats,
         limit=12,
     )
-    parts = [keep, swap(send, "exp", 1)]
-    for masks in chip_groups:
-        pieces = merge(parts, width, len(masks) + 1)
+    for k, masks in enumerate(chip_groups):
+        if k:
+            pieces = merge(parts, width, len(masks) + 1)
         parts = [pieces[0]] + swaps(pieces[1:], "exp", masks)
     own_piece = pieces[0]
     for masks in seq_groups:
@@ -362,6 +414,7 @@
         *parts,
         slot_sum,
         stats,
+        logits_far,
     )
     near = gathered_over_chips(packet, packet)
     far = swap(near, "exp", 1)
@@ -376,6 +429,7 @@
         near,
         far,
         logits,
+        logits_far,
         tokens_flipped,
         tokens,
         out_grad_flipped,

time: 69.1 us -> 67.4 us (0.975)
  waiting for transfers between devices: 26.5 us -> 23.1 us
  starting transfers between devices: 25.5 us -> 26.5 us
  Pallas kernels: 14.5 us -> 15.2 us
    ppermute x18 -> x20, waiting for transfers between devices: 17.6 us -> 14.1 us  [swap(): lax.ppermute(x, axis, [(k, k ^ mask) for k in range(lax.axis_size(axis))])]
    ppermute x18 -> x20, starting transfers between devices: 22.1 us -> 22.9 us  [swap(): lax.ppermute(x, axis, [(k, k ^ mask) for k in range(lax.axis_size(axis))])]
    pallas_call x15 -> x17, Pallas kernels: 14.4 us -> 15.2 us  [local_call(): pl.pallas_call(body, out_shape=tuple((jax.ShapeDtypeStruct(s, d) if k in...]
  transfers between devices with their start and end apart: 19 -> 21, of which waited for: 14 -> 12; matrix products, arithmetic and copies ran while one was open for 0% -> 0% of each run, Pallas kernels for 10% -> 20%
where the time goes in v8:
time: 67.4 us; the launch traced here: 67.1 us
  starting transfers between devices  26.5 us (39%)
  waiting for transfers between devices  23.1 us (34%)
  Pallas kernels  15.2 us (23%)
  between operations  0.83 us (1%)
  local copies, waits for them, and re-layouts  0.8 us (1%)
    ppermute x20, starting transfers between devices, swap(): lax.ppermute(x, axis, [(k, k ^ mask) for k in range(lax.axis_size(axis))])  22.9 us
    pallas_call x17, Pallas kernels, local_call(): pl.pallas_call(body, out_shape=tuple((jax.ShapeDtypeStruct(s, d) if k in...  15.2 us
    ppermute x20, waiting for transfers between devices, swap(): lax.ppermute(x, axis, [(k, k ^ mask) for k in range(lax.axis_size(axis))])  14.1 us
    all_to_all x1, waiting for transfers between devices, shards(): part = lax.all_to_all(blocks, ('seq', 'exp'), 0, 0, tiled=True)  8.95 us
    all_to_all x1, starting transfers between devices, shards(): part = lax.all_to_all(blocks, ('seq', 'exp'), 0, 0, tiled=True)  3.64 us
  transfers between devices with their start and end apart: 21, of which 12 were waited for; matrix products, arithmetic and copies ran while one was open for 0% of the time, Pallas kernels for 20%

profile of v8, /device:TPU:0, one launch (start us, length us, event | category | flops | bytes accessed | tf_op | source)
XLA Modules:
  0.0 67.1 jit_solution(16160824548111081824)
XLA Ops:
  0.6 5.1 %collective-permute-start = (bf16[8,2048]{1,0:T(8,128)(2,1)}, bf16[8,2048]{1,0:T(8,128)(2,1)S(1)}, u32[]{:S(2)}, u32[]{:S(2)}) collective-permute-start(bf16[8,2048]{1,0:T(8,128)(2,1)} %bitcast.8), channel_id=1, source_target_pairs={{0,6},{1,7},{2,4},{3,5},{4,2},{5,3},{6,0},{7,1},{8,14},{9,15},{10,... | collective-permute-start | bytes 98312 | tf_op jit(solution)/shard_map/ppermute | solution.py:18
  5.8 0.6 collective-permute-start.2
  6.9 0.8 %copy-done.2 = bf16[2048,8]{0,1:T(8,128)(2,1)S(1)} copy-done((bf16[2048,8]{0,1:T(8,128)(2,1)S(1)}, bf16[2048,8]{0,1:T(8,128)(2,1)}, u32[]{:S(2)}) %copy-start.2) | copy-done | bytes 32792
  8.0 2.7 %collective-permute-done.1.refs_2_ = bf16[8,2048]{1,0:T(8,128)(2,1)S(1)} collective-permute-done((bf16[8,2048]{1,0:T(8,128)(2,1)}, bf16[8,2048]{1,0:T(8,128)(2,1)S(1)}, u32[]{:S(2)}, u32[]{:S(2)}) %collective-permute-start.1) | collective-permute-done | bytes 32800 | tf_op jit(solution)/shard_map/ppermute | solution.py:18
  10.8 0.6 shard_map.71
  11.5 0.5 shard_map.72
  12.0 0.5 collective-permute-start.15
  13.1 2.2 %collective-permute-start.6 = (bf16[8,4224]{1,0:T(8,128)(2,1)S(1)}, bf16[8,4224]{1,0:T(8,128)(2,1)S(1)}, u32[]{:S(2)}, u32[]{:S(2)}) collective-permute-start(bf16[8,4224]{1,0:T(8,128)(2,1)S(1)} %get-tuple-element.21), channel_id=1, source_target_pairs={{0,6},{1,7},{2,4},{3,5},{4,2},{5,3},{6,0},{7,1},{8,14},{9,15},{10,... | collective-permute-start | bytes 202760 | tf_op jit(solution)/shard_map/ppermute | solution.py:18
  15.4 2.2 %collective-permute-start.8 = (bf16[8,4224]{1,0:T(8,128)(2,1)S(1)}, bf16[8,4224]{1,0:T(8,128)(2,1)S(1)}, u32[]{:S(2)}, u32[]{:S(2)}) collective-permute-start(bf16[8,4224]{1,0:T(8,128)(2,1)S(1)} %get-tuple-element.23), channel_id=1, source_target_pairs={{0,2},{1,3},{2,0},{3,1},{4,6},{5,7},{6,4},{7,5},{8,10},{9,11},{10,... | collective-permute-start | bytes 202760 | tf_op jit(solution)/shard_map/ppermute | solution.py:18
  17.6 1.2 %shard_map.77.refs_8_ = bf16[2048,1024]{1,0:T(8,128)(2,1)S(1)} custom-call(bf16[2,1024,2048]{2,1,0:T(8,128)(2,1)S(1)} %bitcast.5, bf16[8,4224]{1,0:T(8,128)(2,1)S(1)} %get-tuple-element.20.refs_0_.after), custom_call_target="tpu_custom_call" | custom-call | flops 1000000000 | bytes 4194304 | tf_op jit(solution)/shard_map/pallas_call | solution.py:44
  18.9 1.2 %shard_map.78.refs_9_ = bf16[2048,1024]{1,0:T(8,128)(2,1)S(1)} custom-call(bf16[2,1024,2048]{2,1,0:T(8,128)(2,1)S(1)} %bitcast.5, bf16[8,4224]{1,0:T(8,128)(2,1)S(1)} %get-tuple-element.20.refs_0_.after), custom_call_target="tpu_custom_call" | custom-call | flops 1000000000 | bytes 4194304 | tf_op jit(solution)/shard_map/pallas_call | solution.py:44
  20.1 2.0 %collective-permute-done.7.refs_2_ = bf16[8,4224]{1,0:T(8,128)(2,1)S(1)} collective-permute-done((bf16[8,4224]{1,0:T(8,128)(2,1)S(1)}, bf16[8,4224]{1,0:T(8,128)(2,1)S(1)}, u32[]{:S(2)}, u32[]{:S(2)}) %collective-permute-start.7) | collective-permute-done | bytes 67616 | tf_op jit(solution)/shard_map/ppermute | solution.py:18
  22.3 1.6 %collective-permute-start.10 = (bf16[8,4224]{1,0:T(8,128)(2,1)S(1)}, bf16[8,4224]{1,0:T(8,128)(2,1)S(1)}, u32[]{:S(2)}, u32[]{:S(2)}) collective-permute-start(bf16[8,4224]{1,0:T(8,128)(2,1)S(1)} %shard_map.74.after.refs_0_), channel_id=1, source_target_pairs={{0,16},{8,24},{16,0},{24,8},{1,17},{9,25},{17,1},{25,9},{2,18},{10... | collective-permute-start | bytes 202760 | tf_op jit(solution)/shard_map/ppermute | solution.py:18
  23.9 1.5 %collective-permute-start.11 = (bf16[8,4224]{1,0:T(8,128)(2,1)S(1)}, bf16[8,4224]{1,0:T(8,128)(2,1)S(1)}, u32[]{:S(2)}, u32[]{:S(2)}) collective-permute-start(bf16[8,4224]{1,0:T(8,128)(2,1)S(1)} %shard_map.74.after.refs_0_), channel_id=1, source_target_pairs={{0,8},{8,0},{16,24},{24,16},{1,9},{9,1},{17,25},{25,17},{2,10},{10... | collective-permute-start | bytes 202760 | tf_op jit(solution)/shard_map/ppermute | solution.py:18
  25.9 1.2 %shard_map.75.refs_6_ = bf16[1024,2048]{1,0:T(8,128)(2,1)S(1)} custom-call(bf16[2,2048,1024]{2,1,0:T(8,128)(2,1)S(1)} %bitcast.3, bf16[8,4224]{1,0:T(8,128)(2,1)S(1)} %shard_map.74.after.refs_0_), custom_call_target="tpu_custom_call" | custom-call | flops 1000000000 | bytes 4194304 | tf_op jit(solution)/shard_map/pallas_call | solution.py:44
  27.1 1.2 %shard_map.76.refs_7_ = bf16[1024,2048]{1,0:T(8,128)(2,1)S(1)} custom-call(bf16[2,2048,1024]{2,1,0:T(8,128)(2,1)S(1)} %bitcast.3, bf16[8,4224]{1,0:T(8,128)(2,1)S(1)} %shard_map.74.after.refs_0_), custom_call_target="tpu_custom_call" | custom-call | flops 1000000000 | bytes 4194304 | tf_op jit(solution)/shard_map/pallas_call | solution.py:44
  28.8 1.7 %collective-permute-done.9.refs_1_ = bf16[8,4224]{1,0:T(8,128)(2,1)S(1)} collective-permute-done((bf16[8,4224]{1,0:T(8,128)(2,1)S(1)}, bf16[8,4224]{1,0:T(8,128)(2,1)S(1)}, u32[]{:S(2)}, u32[]{:S(2)}) %collective-permute-start.9) | collective-permute-done | bytes 67616 | tf_op jit(solution)/shard_map/ppermute | solution.py:18
  30.6 4.5 %shard_map.79 = (bf16[8,4096]{1,0:T(8,128)(2,1)S(1)}, f32[8,2048]{1,0:T(8,128)S(1)}, f32[8,128]{1,0:T(8,128)S(1)}) custom-call(bf16[8,4224]{1,0:T(8,128)(2,1)S(1)} %shard_map.74.after.refs_0_, bf16[8,4224]{1,0:T(8,128)(2,1)S(1)} %collective-permute-done.9.refs_1_, bf16[8,4224]{1,0:T(8,128)(2,1)S(1)} %collective-permute-done.10.refs_2_, ...), custom_call_target="tpu_custom_call" | custom-call | flops 10000000000 | bytes 4194304 | tf_op jit(solution)/shard_map/pallas_call | solution.py:44
  35.1 1.4 %collective-permute-start.12 = (bf16[8,4096]{1,0:T(8,128)(2,1)S(1)}, bf16[8,4096]{1,0:T(8,128)(2,1)S(1)}, u32[]{:S(2)}, u32[]{:S(2)}) collective-permute-start(bf16[8,4096]{1,0:T(8,128)(2,1)S(1)} %get-tuple-element.24.refs_0_), channel_id=1, source_target_pairs={{0,24},{8,16},{16,8},{24,0},{1,25},{9,17},{17,9},{25,1},{2,26},{10... | collective-permute-start | bytes 196616 | tf_op jit(solution)/shard_map/ppermute | solution.py:18
  36.5 0.6 collective-permute-start.13
  37.1 1.5 %collective-permute-start.14 = (bf16[8,4096]{1,0:T(8,128)(2,1)S(1)}, bf16[8,4096]{1,0:T(8,128)(2,1)S(1)}, u32[]{:S(2)}, u32[]{:S(2)}) collective-permute-start(bf16[8,4096]{1,0:T(8,128)(2,1)S(1)} %get-tuple-element.24.refs_0_), channel_id=1, source_target_pairs={{0,8},{8,0},{16,24},{24,16},{1,9},{9,1},{17,25},{25,17},{2,10},{10... | collective-permute-start | bytes 196616 | tf_op jit(solution)/shard_map/ppermute | solution.py:18
  38.9 1.8 %collective-permute-done.12.refs_1_ = bf16[8,4096]{1,0:T(8,128)(2,1)S(1)} collective-permute-done((bf16[8,4096]{1,0:T(8,128)(2,1)S(1)}, bf16[8,4096]{1,0:T(8,128)(2,1)S(1)}, u32[]{:S(2)}, u32[]{:S(2)}) %collective-permute-start.12) | collective-permute-done | bytes 65568 | tf_op jit(solution)/shard_map/ppermute | solution.py:18
  41.5 2.6 %collective-permute-start.16 = (bf16[8,4224]{1,0:T(8,128)(2,1)S(1)}, bf16[8,4224]{1,0:T(8,128)(2,1)S(1)}, u32[]{:S(2)}, u32[]{:S(2)}) collective-permute-start(bf16[8,4224]{1,0:T(8,128)(2,1)S(1)} %shard_map.81.refs_0_), channel_id=1, source_target_pairs={{0,6},{1,7},{2,4},{3,5},{4,2},{5,3},{6,0},{7,1},{8,14},{9,15},{10,... | collective-permute-start | bytes 202760 | tf_op jit(solution)/shard_map/ppermute | solution.py:18
  44.1 1.8 %collective-permute-start.18 = (bf16[8,4224]{1,0:T(8,128)(2,1)S(1)}, bf16[8,4224]{1,0:T(8,128)(2,1)S(1)}, u32[]{:S(2)}, u32[]{:S(2)}) collective-permute-start(bf16[8,4224]{1,0:T(8,128)(2,1)S(1)} %shard_map.81.refs_0_), channel_id=1, source_target_pairs={{0,2},{1,3},{2,0},{3,1},{4,6},{5,7},{6,4},{7,5},{8,10},{9,11},{10,... | collective-permute-start | bytes 202760 | tf_op jit(solution)/shard_map/ppermute | solution.py:18
  45.9 1.7 %collective-permute-done.16.refs_1_ = bf16[8,4224]{1,0:T(8,128)(2,1)S(1)} collective-permute-done((bf16[8,4224]{1,0:T(8,128)(2,1)S(1)}, bf16[8,4224]{1,0:T(8,128)(2,1)S(1)}, u32[]{:S(2)}, u32[]{:S(2)}) %collective-permute-start.16) | collective-permute-done | bytes 67616 | tf_op jit(solution)/shard_map/ppermute | solution.py:18
  47.6 1.7 %collective-permute-done.17.refs_2_ = bf16[8,4224]{1,0:T(8,128)(2,1)S(1)} collective-permute-done((bf16[8,4224]{1,0:T(8,128)(2,1)S(1)}, bf16[8,4224]{1,0:T(8,128)(2,1)S(1)}, u32[]{:S(2)}, u32[]{:S(2)}) %collective-permute-start.17) | collective-permute-done | bytes 67616 | tf_op jit(solution)/shard_map/ppermute | solution.py:18
  49.7 1.2 %collective-permute-done.19.far = bf16[32,4224]{1,0:T(8,128)(2,1)S(1)} collective-permute-done((bf16[32,4224]{1,0:T(8,128)(2,1)S(1)}, bf16[32,4224]{1,0:T(8,128)(2,1)S(1)}, u32[]{:S(2)}, u32[]{:S(2)}) %collective-permute-start.19) | collective-permute-done | bytes 270368 | tf_op jit(solution)/shard_map/ppermute | solution.py:18
  50.9 1.5 %shard_map.84 = (bf16[128,256]{1,0:T(8,128)(2,1)S(1)}, bf16[32,8,512]{2,1,0:T(8,128)(2,1)}) custom-call(bf16[32,4224]{1,0:T(8,128)(2,1)S(1)} %shard_map.82.near, bf16[32,4224]{1,0:T(8,128)(2,1)S(1)} %collective-permute-done.19.far, f32[32,512]{1,0:T(8,128)S(1)} %get-tuple-element.16.logits.logits_near, f32[32,256]{1,0:T(8,128)S(1)} %shard_map.80.refs_6_.logits_far, ...), custom_call_target="tpu_custom_call" | custom-call | flops 10000000000 | bytes 4194304 | tf_op jit(solution)/shard_map/pallas_call | solution.py:44
  52.4 3.6 %all-to-all-start = ((bf16[32,8,512]{2,1,0:T(8,128)(2,1)}), bf16[32,8,512]{2,1,0:T(8,128)(2,1)S(1)}, u32[]{:S(2)}, u32[]{:S(2)}) async-start(bf16[32,8,512]{2,1,0:T(8,128)(2,1)} %get-tuple-element.29), calls=%async_computation | async-start | bytes 524288 | tf_op jit(solution)/shard_map/all_to_all | solution.py:450
  56.1 1.4 %shard_map.85 = bf16[256,2048]{1,0:T(8,128)(2,1)} custom-call(bf16[128,256]{1,0:T(8,128)(2,1)S(1)} %get-tuple-element.28.weights, bf16[32,4224]{1,0:T(8,128)(2,1)S(1)} %shard_map.82.near, bf16[32,4224]{1,0:T(8,128)(2,1)S(1)} %collective-permute-done.19.far, bf16[32,2048]{1,0:T(8,128)(2,1)S(1)} %shard_map.69.table.table_near, ...), custom_call_target="tpu_custom_call" | custom-call | flops 10000000000 | bytes 4194304 | tf_op jit(solution)/shard_map/pallas_call | solution.py:44
  57.5 9.0 %all-to-all-done = bf16[32,8,512]{2,1,0:T(8,128)(2,1)S(1)} async-done(((bf16[32,8,512]{2,1,0:T(8,128)(2,1)}), bf16[32,8,512]{2,1,0:T(8,128)(2,1)S(1)}, u32[]{:S(2)}, u32[]{:S(2)}) %all-to-all-start) | async-done | bytes 262176 | tf_op jit(solution)/shard_map/all_to_all | solution.py:450
  66.5 0.7 convert_reduce_fusion
  (50 shorter events, 4.1 us)
Async XLA Ops:
  0.6 7.1 %copy-start.1 = (bf16[256,2048]{1,0:T(8,128)(2,1)S(1)}, bf16[256,2048]{1,0:T(8,128)(2,1)}, u32[]{:S(2)}) copy-start(bf16[256,2048]{1,0:T(8,128)(2,1)} %tokens.3) | copy-start | bytes 3145732
  0.6 7.4 %collective-permute-start = (bf16[8,2048]{1,0:T(8,128)(2,1)}, bf16[8,2048]{1,0:T(8,128)(2,1)S(1)}, u32[]{:S(2)}, u32[]{:S(2)}) collective-permute-start(bf16[8,2048]{1,0:T(8,128)(2,1)} %bitcast.8), channel_id=1, source_target_pairs={{0,6},{1,7},{2,4},{3,5},{4,2},{5,3},{6,0},{7,1},{8,14},{9,15},{10,... | collective-permute-start | bytes 98312 | tf_op jit(solution)/shard_map/ppermute | solution.py:18
  5.8 5.0 %collective-permute-start.1 = (bf16[8,2048]{1,0:T(8,128)(2,1)}, bf16[8,2048]{1,0:T(8,128)(2,1)S(1)}, u32[]{:S(2)}, u32[]{:S(2)}) collective-permute-start(bf16[8,2048]{1,0:T(8,128)(2,1)} %bitcast.9), channel_id=1, source_target_pairs={{0,4},{1,5},{2,6},{3,7},{4,0},{5,1},{6,2},{7,3},{8,12},{9,13},{10,... | collective-permute-start | bytes 98312 | tf_op jit(solution)/shard_map/ppermute | solution.py:18
  5.8 5.0 %collective-permute-start.2 = (bf16[8,2048]{1,0:T(8,128)(2,1)}, bf16[8,2048]{1,0:T(8,128)(2,1)S(1)}, u32[]{:S(2)}, u32[]{:S(2)}) collective-permute-start(bf16[8,2048]{1,0:T(8,128)(2,1)} %bitcast.10), channel_id=1, source_target_pairs={{0,2},{1,3},{2,0},{3,1},{4,6},{5,7},{6,4},{7,5},{8,10},{9,11},{10,... | collective-permute-start | bytes 98312 | tf_op jit(solution)/shard_map/ppermute | solution.py:18
  6.4 4.4 %collective-permute-start.3 = (bf16[256,2048]{1,0:T(8,128)(2,1)}, bf16[256,2048]{1,0:T(8,128)(2,1)S(1)}, u32[]{:S(2)}, u32[]{:S(2)}) collective-permute-start(bf16[256,2048]{1,0:T(8,128)(2,1)} %tokens.3), channel_id=1, source_target_pairs={{0,1},{1,0},{2,3},{3,2},{4,5},{5,4},{6,7},{7,6},{8,9},{9,8},{10,11... | collective-permute-start | bytes 3145736 | tf_op jit(solution)/shard_map/ppermute | solution.py:18
  6.4 6.2 %collective-permute-start.5 = (bf16[256,2048]{1,0:T(8,128)(2,1)}, bf16[256,2048]{1,0:T(8,128)(2,1)S(1)}, u32[]{:S(2)}, u32[]{:S(2)}) collective-permute-start(bf16[256,2048]{1,0:T(8,128)(2,1)} %x.3), channel_id=1, source_target_pairs={{0,1},{1,0},{2,3},{3,2},{4,5},{5,4},{6,7},{7,6},{8,9},{9,8},{10,11... | collective-permute-start | bytes 3145736 | tf_op jit(solution)/shard_map/ppermute | solution.py:18
  6.9 0.8 %copy-start.2 = (bf16[2048,8]{0,1:T(8,128)(2,1)S(1)}, bf16[2048,8]{0,1:T(8,128)(2,1)}, u32[]{:S(2)}) copy-start(bf16[2048,8]{0,1:T(8,128)(2,1)} %param.6) | copy-start | bytes 98308
  10.8 1.9 %copy-start = (bf16[256,2048]{1,0:T(8,128)(2,1)S(1)}, bf16[256,2048]{1,0:T(8,128)(2,1)}, u32[]{:S(2)}) copy-start(bf16[256,2048]{1,0:T(8,128)(2,1)} %x.3) | copy-start | bytes 3145732
  11.4 1.2 %collective-permute-start.4 = (f32[8,512]{1,0:T(8,128)S(1)}, f32[8,512]{1,0:T(8,128)S(1)}, u32[]{:S(2)}, u32[]{:S(2)}) collective-permute-start(f32[8,512]{1,0:T(8,128)S(1)} %get-tuple-element.17.rows), channel_id=1, source_target_pairs={{0,1},{1,0},{2,3},{3,2},{4,5},{5,4},{6,7},{7,6},{8,9},{9,8},{10,11... | collective-permute-start | bytes 49160 | tf_op jit(solution)/shard_map/ppermute | solution.py:18
  12.0 26.6 %collective-permute-start.15 = (bf16[32,2048]{1,0:T(8,128)(2,1)S(1)}, bf16[32,2048]{1,0:T(8,128)(2,1)S(1)}, u32[]{:S(2)}, u32[]{:S(2)}) collective-permute-start(bf16[32,2048]{1,0:T(8,128)(2,1)S(1)} %get-tuple-element.27), channel_id=1, source_target_pairs={{0,1},{1,0},{2,3},{3,2},{4,5},{5,4},{6,7},{7,6},{8,9},{9,8},{10,11... | collective-permute-start | bytes 393224 | tf_op jit(solution)/shard_map/ppermute | solution.py:18
  12.7 4.9 %slice-start.2 = ((s8[8388608]{0:T(1024)(128)(4,1)}), s8[4194304]{0:T(1024)(128)(4,1)S(1)}, s32[]{:S(2)}) async-start(s8[8388608]{0:T(1024)(128)(4,1)} %bitcast.4), calls=%async_computation.3 | async-start | bytes 8388608
  12.7 4.9 %slice-start.3 = ((s8[8388608]{0:T(1024)(128)(4,1)}), s8[4194304]{0:T(1024)(128)(4,1)S(1)}, s32[]{:S(2)}) async-start(s8[8388608]{0:T(1024)(128)(4,1)} %bitcast.4), calls=%async_computation.4 | async-start | bytes 8388608
  13.1 7.0 %collective-permute-start.6 = (bf16[8,4224]{1,0:T(8,128)(2,1)S(1)}, bf16[8,4224]{1,0:T(8,128)(2,1)S(1)}, u32[]{:S(2)}, u32[]{:S(2)}) collective-permute-start(bf16[8,4224]{1,0:T(8,128)(2,1)S(1)} %get-tuple-element.21), channel_id=1, source_target_pairs={{0,6},{1,7},{2,4},{3,5},{4,2},{5,3},{6,0},{7,1},{8,14},{9,15},{10,... | collective-permute-start | bytes 202760 | tf_op jit(solution)/shard_map/ppermute | solution.py:18
  15.4 6.8 %collective-permute-start.7 = (bf16[8,4224]{1,0:T(8,128)(2,1)S(1)}, bf16[8,4224]{1,0:T(8,128)(2,1)S(1)}, u32[]{:S(2)}, u32[]{:S(2)}) collective-permute-start(bf16[8,4224]{1,0:T(8,128)(2,1)S(1)} %get-tuple-element.22), channel_id=1, source_target_pairs={{0,4},{1,5},{2,6},{3,7},{4,0},{5,1},{6,2},{7,3},{8,12},{9,13},{10,... | collective-permute-start | bytes 202760 | tf_op jit(solution)/shard_map/ppermute | solution.py:18
  15.4 6.8 %collective-permute-start.8 = (bf16[8,4224]{1,0:T(8,128)(2,1)S(1)}, bf16[8,4224]{1,0:T(8,128)(2,1)S(1)}, u32[]{:S(2)}, u32[]{:S(2)}) collective-permute-start(bf16[8,4224]{1,0:T(8,128)(2,1)S(1)} %get-tuple-element.23), channel_id=1, source_target_pairs={{0,2},{1,3},{2,0},{3,1},{4,6},{5,7},{6,4},{7,5},{8,10},{9,11},{10,... | collective-permute-start | bytes 202760 | tf_op jit(solution)/shard_map/ppermute | solution.py:18
  18.8 7.0 %slice-start = ((s8[8388608]{0:T(1024)(128)(4,1)}), s8[4194304]{0:T(1024)(128)(4,1)S(1)}, s32[]{:S(2)}) async-start(s8[8388608]{0:T(1024)(128)(4,1)} %bitcast.2), calls=%async_computation.1 | async-start | bytes 8388608
  20.1 5.8 %slice-start.1 = ((s8[8388608]{0:T(1024)(128)(4,1)}), s8[4194304]{0:T(1024)(128)(4,1)S(1)}, s32[]{:S(2)}) async-start(s8[8388608]{0:T(1024)(128)(4,1)} %bitcast.2), calls=%async_computation.2 | async-start | bytes 8388608
  22.3 6.1 %collective-permute-start.10 = (bf16[8,4224]{1,0:T(8,128)(2,1)S(1)}, bf16[8,4224]{1,0:T(8,128)(2,1)S(1)}, u32[]{:S(2)}, u32[]{:S(2)}) collective-permute-start(bf16[8,4224]{1,0:T(8,128)(2,1)S(1)} %shard_map.74.after.refs_0_), channel_id=1, source_target_pairs={{0,16},{8,24},{16,0},{24,8},{1,17},{9,25},{17,1},{25,9},{2,18},{10... | collective-permute-start | bytes 202760 | tf_op jit(solution)/shard_map/ppermute | solution.py:18
  23.9 4.9 %collective-permute-start.11 = (bf16[8,4224]{1,0:T(8,128)(2,1)S(1)}, bf16[8,4224]{1,0:T(8,128)(2,1)S(1)}, u32[]{:S(2)}, u32[]{:S(2)}) collective-permute-start(bf16[8,4224]{1,0:T(8,128)(2,1)S(1)} %shard_map.74.after.refs_0_), channel_id=1, source_target_pairs={{0,8},{8,0},{16,24},{24,16},{1,9},{9,1},{17,25},{25,17},{2,10},{10... | collective-permute-start | bytes 202760 | tf_op jit(solution)/shard_map/ppermute | solution.py:18
  25.4 5.2 %collective-permute-start.9 = (bf16[8,4224]{1,0:T(8,128)(2,1)S(1)}, bf16[8,4224]{1,0:T(8,128)(2,1)S(1)}, u32[]{:S(2)}, u32[]{:S(2)}) collective-permute-start(bf16[8,4224]{1,0:T(8,128)(2,1)S(1)} %shard_map.74.after.refs_0_), channel_id=1, source_target_pairs={{0,24},{8,16},{16,8},{24,0},{1,25},{9,17},{17,9},{25,1},{2,26},{10... | collective-permute-start | bytes 202760 | tf_op jit(solution)/shard_map/ppermute | solution.py:18
  25.9 4.7 %slice-start.4 = ((s8[8388608]{0:T(1024)(128)(4,1)}), s8[4194304]{0:T(1024)(128)(4,1)S(1)}, s32[]{:S(2)}) async-start(s8[8388608]{0:T(1024)(128)(4,1)} %bitcast.6), calls=%async_computation.5 | async-start | bytes 8388608
  27.1 3.5 %slice-start.5 = ((s8[8388608]{0:T(1024)(128)(4,1)}), s8[4194304]{0:T(1024)(128)(4,1)S(1)}, s32[]{:S(2)}) async-start(s8[8388608]{0:T(1024)(128)(4,1)} %bitcast.6), calls=%async_computation.6 | async-start | bytes 8388608
  35.1 5.6 %collective-permute-start.12 = (bf16[8,4096]{1,0:T(8,128)(2,1)S(1)}, bf16[8,4096]{1,0:T(8,128)(2,1)S(1)}, u32[]{:S(2)}, u32[]{:S(2)}) collective-permute-start(bf16[8,4096]{1,0:T(8,128)(2,1)S(1)} %get-tuple-element.24.refs_0_), channel_id=1, source_target_pairs={{0,24},{8,16},{16,8},{24,0},{1,25},{9,17},{17,9},{25,1},{2,26},{10... | collective-permute-start | bytes 196616 | tf_op jit(solution)/shard_map/ppermute | solution.py:18
  36.5 4.7 %collective-permute-start.13 = (bf16[8,4096]{1,0:T(8,128)(2,1)S(1)}, bf16[8,4096]{1,0:T(8,128)(2,1)S(1)}, u32[]{:S(2)}, u32[]{:S(2)}) collective-permute-start(bf16[8,4096]{1,0:T(8,128)(2,1)S(1)} %get-tuple-element.24.refs_0_), channel_id=1, source_target_pairs={{0,16},{8,24},{16,0},{24,8},{1,17},{9,25},{17,1},{25,9},{2,18},{10... | collective-permute-start | bytes 196616 | tf_op jit(solution)/shard_map/ppermute | solution.py:18
  37.1 4.3 %collective-permute-start.14 = (bf16[8,4096]{1,0:T(8,128)(2,1)S(1)}, bf16[8,4096]{1,0:T(8,128)(2,1)S(1)}, u32[]{:S(2)}, u32[]{:S(2)}) collective-permute-start(bf16[8,4096]{1,0:T(8,128)(2,1)S(1)} %get-tuple-element.24.refs_0_), channel_id=1, source_target_pairs={{0,8},{8,0},{16,24},{24,16},{1,9},{9,1},{17,25},{25,17},{2,10},{10... | collective-permute-start | bytes 196616 | tf_op jit(solution)/shard_map/ppermute | solution.py:18
  41.5 6.1 %collective-permute-start.16 = (bf16[8,4224]{1,0:T(8,128)(2,1)S(1)}, bf16[8,4224]{1,0:T(8,128)(2,1)S(1)}, u32[]{:S(2)}, u32[]{:S(2)}) collective-permute-start(bf16[8,4224]{1,0:T(8,128)(2,1)S(1)} %shard_map.81.refs_0_), channel_id=1, source_target_pairs={{0,6},{1,7},{2,4},{3,5},{4,2},{5,3},{6,0},{7,1},{8,14},{9,15},{10,... | collective-permute-start | bytes 202760 | tf_op jit(solution)/shard_map/ppermute | solution.py:18
  44.1 5.2 %collective-permute-start.17 = (bf16[8,4224]{1,0:T(8,128)(2,1)S(1)}, bf16[8,4224]{1,0:T(8,128)(2,1)S(1)}, u32[]{:S(2)}, u32[]{:S(2)}) collective-permute-start(bf16[8,4224]{1,0:T(8,128)(2,1)S(1)} %shard_map.81.refs_0_), channel_id=1, source_target_pairs={{0,4},{1,5},{2,6},{3,7},{4,0},{5,1},{6,2},{7,3},{8,12},{9,13},{10,... | collective-permute-start | bytes 202760 | tf_op jit(solution)/shard_map/ppermute | solution.py:18
  44.1 5.2 %collective-permute-start.18 = (bf16[8,4224]{1,0:T(8,128)(2,1)S(1)}, bf16[8,4224]{1,0:T(8,128)(2,1)S(1)}, u32[]{:S(2)}, u32[]{:S(2)}) collective-permute-start(bf16[8,4224]{1,0:T(8,128)(2,1)S(1)} %shard_map.81.refs_0_), channel_id=1, source_target_pairs={{0,2},{1,3},{2,0},{3,1},{4,6},{5,7},{6,4},{7,5},{8,10},{9,11},{10,... | collective-permute-start | bytes 202760 | tf_op jit(solution)/shard_map/ppermute | solution.py:18
  49.3 1.6 %collective-permute-start.19 = (bf16[32,4224]{1,0:T(8,128)(2,1)S(1)}, bf16[32,4224]{1,0:T(8,128)(2,1)S(1)}, u32[]{:S(2)}, u32[]{:S(2)}) collective-permute-start(bf16[32,4224]{1,0:T(8,128)(2,1)S(1)} %shard_map.82.near), channel_id=1, source_target_pairs={{0,1},{1,0},{2,3},{3,2},{4,5},{5,4},{6,7},{7,6},{8,9},{9,8},{10,11... | collective-permute-start | bytes 811016 | tf_op jit(solution)/shard_map/ppermute | solution.py:18
  52.4 14.0 %all-to-all-start = ((bf16[32,8,512]{2,1,0:T(8,128)(2,1)}), bf16[32,8,512]{2,1,0:T(8,128)(2,1)S(1)}, u32[]{:S(2)}, u32[]{:S(2)}) async-start(bf16[32,8,512]{2,1,0:T(8,128)(2,1)} %get-tuple-element.29), calls=%async_computation | async-start | bytes 524288 | tf_op jit(solution)/shard_map/all_to_all | solution.py:450

commit v9 on v8

--- a/solution.py
+++ b/solution.py
@@ -135,10 +135,6 @@
     stats[...] = jnp.where(row == 0, top, jnp.where(row == 1, total, 0.0))
 
 
-def far_logit_kernel(table, tokens_flipped, out):
-    out[...] = product(table[...], tokens_flipped[...], 1, 0)
-
-
 def dispatch_kernel(logits, tokens, tokens_far, table, sums, stats, table_out):
     table_out[...] = table[...]
     patches = tokens.shape[0]
@@ -151,12 +147,21 @@
     sums[...] = both.astype(BF16)
 
 
+def as_here(rows_far):
+    half = rows_far.shape[1] // 2
+    return jnp.concatenate([rows_far[:, half:], rows_far[:, :half]], axis=1)
+
+
+def combine_weights(logits, rows, rows_far):
+    other = as_here(rows_far)
+    top = jnp.maximum(rows[:1], other[:1])
+    total = rows[1:2] * jnp.exp(rows[:1] - top) + other[1:2] * jnp.exp(other[:1] - top)
+    return jnp.exp(logits[...] - top) / total
+
+
 def combine_kernel(logits, rows, rows_far, out_grad, out_far, sums, stats, *outs):
     patches, width = out_grad.shape
-    other = jnp.concatenate([rows_far[:, patches:], rows_far[:, :patches]], axis=1)
-    top = jnp.maximum(rows[:1], other[:1])
-    total = rows[1:2] * jnp.exp(rows[:1] - top) + other[1:2] * jnp.exp(other[:1] - top)
-    combine = (jnp.exp(logits[...] - top) / total).astype(BF16)
+    combine = combine_weights(logits, rows, rows_far).astype(BF16)
     grads = product(combine[:, :patches], out_grad[...], 1, 0)
     grads += product(combine[:, patches:], out_far[...], 1, 0)
     count = outs[0].shape[0]
@@ -289,45 +294,87 @@
     out[:, 2 * width :] = packed([centre, top, denominator], stats.shape[0]).astype(BF16)
 
 
-def second_kernel(
-    order, near, far, logits_near, logits_far, tokens_flipped, tokens, out_grad_flipped, weights, blocks
+def grad_kernel(
+    near,
+    logits,
+    rows,
+    rows_far,
+    tokens_flipped,
+    tokens_far,
+    out_grad_flipped,
+    out_far,
+    direct,
+    combine_out,
+    dispatch_out,
+    mean,
 ):
-    width = tokens.shape[1]
-    half = near.shape[0]
-
-    def against(columns, rows):
-        both = jnp.concatenate([near[:, columns], far[:, columns]], axis=0)
-        return product(both, rows[...], 1, 0)
-
-    comb_grad = against(slice(0, width), out_grad_flipped)
-    disp_grad = against(slice(width, 2 * width), tokens_flipped)
-    stats = jnp.concatenate([x[:, 2 * width :].astype(F32) for x in (near, far)], axis=0)
-    centre, top, total = unpacked(stats, 3)
-    scores = jnp.concatenate([logits_near[:, : tokens.shape[0]], logits_far[...]], axis=0)
-    dispatch = jnp.exp(scores - top) / total
-    combine = softmax_columns(scores)
-    comb_mean = jnp.sum(combine * comb_grad, axis=0, keepdims=True)
-    logit_grad = dispatch * (disp_grad - centre) + combine * (comb_grad - comb_mean)
+    width = tokens_flipped.shape[0]
+
+    def against(columns, flipped_here, far):
+        left = near[:, columns]
+        return jnp.concatenate(
+            [product(left, flipped_here[...], 1, 0), product(left, far[...], 1, 1)], axis=1
+        )
+
+    comb_grad = against(slice(0, width), out_grad_flipped, out_far)
+    disp_grad = against(slice(width, 2 * width), tokens_flipped, tokens_far)
+    centre, top, total = unpacked(near[:, 2 * width :].astype(F32), 3)
+    dispatch = jnp.exp(logits[...] - top) / total
+    combine = combine_weights(logits, rows, rows_far)
+    weighted = combine * comb_grad
+    direct[...] = dispatch * (disp_grad - centre) + weighted
+    combine_out[...] = combine
+    dispatch_out[...] = dispatch
+    row = lax.broadcasted_iota(jnp.int32, mean.shape, 0)
+    mean[...] = jnp.where(row == 0, jnp.sum(weighted, axis=0, keepdims=True), 0.0)
+
+
+def block_kernel(
+    order,
+    direct,
+    combine,
+    dispatch,
+    mean,
+    mean_far,
+    tokens,
+    tokens_far,
+    weights,
+    weights_sent,
+    blocks,
+):
+    patches, width = tokens.shape
+    half = direct.shape[0]
+    comb_mean = mean[:1] + as_here(mean_far)[:1]
+    logit_grad = direct[...] - combine[...] * comb_mean
     logit_b = logit_grad.astype(BF16)
-    weights[: 2 * half] = dispatch.astype(BF16)
-    weights[2 * half :] = logit_b
-    part = product(logit_b, tokens[...], 1, 0).astype(BF16)
-    me = lax.axis_index("exp")
-    n_seq, n_exp = lax.axis_size("seq"), lax.axis_size("exp")
+    part = product(logit_b[:, :patches], tokens[...], 1, 0)
+    part += product(logit_b[:, patches:], tokens_far[...], 1, 0)
+    part = part.astype(BF16)
+    for out, at in ((weights, slice(0, patches)), (weights_sent, slice(patches, 2 * patches))):
+        out[:half] = dispatch[:, at].astype(BF16)
+        out[half:] = logit_b[:, at]
+    chip = lax.axis_index("exp") // 2
+    n_seq, n_chips = lax.axis_size("seq"), lax.axis_size("exp") // 2
     _, rows, share = blocks.shape
     for k, mask in enumerate(order):
         for s in range(n_seq):
-            blocks[s * n_exp + (me ^ mask)] = part[
+            blocks[s * n_chips + (chip ^ mask)] = part[
                 k * rows : (k + 1) * rows, s * share : (s + 1) * share
             ]
 
 
-def patch_kernel(weights, near, far, table_near, table_far, out):
+def grad_part_kernel(near, after, out):
     width = out.shape[1]
+    out[...] = near[:, width : 2 * width]
+
+
+def patch_kernel(weights, weights_far, near, table, grad_far, table_far, out):
+    width = out.shape[1]
+    left = jnp.concatenate([weights[...], weights_far[...]], axis=0)
     rows = jnp.concatenate(
-        [x[:, width : 2 * width] for x in (near, far)] + [table_near[...], table_far[...]], axis=0
-    )
-    out[...] = product(weights[...], rows, 0, 0).astype(BF16)
+        [near[:, width : 2 * width], table[...], grad_far[...], table_far[...]], axis=0
+    )
+    out[...] = product(left, rows, 0, 0).astype(BF16)
 
 
 def shards(tokens, slot_embed, expert_in, expert_out, out_grad):
@@ -367,16 +414,14 @@
         flops=10**9,
     )
     table_far = swap(table_sent, "exp", 1)
-    (logits_far,) = local_call(
-        far_logit_kernel, [((half, patches), F32)], table_far, tokens_flipped, flops=3 * 10**8
-    )
     pieces_first = len(chip_groups[0]) + 1
+    rows_far = swap(rows, "exp", 1)
     pieces = local_call(
         combine_kernel,
         [((half // pieces_first, columns), BF16)] * pieces_first,
         logits,
         rows,
-        swap(rows, "exp", 1),
+        rows_far,
         out_grad,
         out_far,
         sums,
@@ -414,40 +459,60 @@
         *parts,
         slot_sum,
         stats,
-        logits_far,
+        table_far,
     )
     near = gathered_over_chips(packet, packet)
-    far = swap(near, "exp", 1)
-
+    direct, combine, dispatch, mean = local_call(
+        grad_kernel,
+        [((half, 2 * patches), F32)] * 3 + [((8, 2 * patches), F32)],
+        near,
+        logits,
+        rows,
+        rows_far,
+        tokens_flipped,
+        tokens_far,
+        out_grad_flipped,
+        out_far,
+        limit=12,
+    )
     order = [0]
     for masks in reversed(chip_groups):
-        order = [r ^ mask for mask in (0, *masks) for r in order]
-    order = order + [r ^ 1 for r in order]
-    weights, blocks = local_call(
-        partial(second_kernel, order),
-        [((2 * slots, patches), BF16), ((n_seq * n_exp, own, width // n_seq), BF16)],
-        near,
-        far,
-        logits,
-        logits_far,
-        tokens_flipped,
+        order = [r ^ (mask // 2) for mask in (0, *masks) for r in order]
+    (grad_sent,) = local_call(
+        grad_part_kernel, [((half, width), BF16)], near, mean, flops=10**8
+    )
+    weights, weights_sent, blocks = local_call(
+        partial(block_kernel, order),
+        [((2 * half, patches), BF16)] * 2
+        + [((n_seq * n_exp // 2, own, width // n_seq), BF16)],
+        direct,
+        combine,
+        dispatch,
+        mean,
+        swap(mean, "exp", 1),
         tokens,
-        out_grad_flipped,
+        tokens_far,
         limit=12,
     )
     (tok_grad,) = local_call(
         patch_kernel,
         [((patches, width), BF16)],
         weights,
+        swap(weights_sent, "exp", 1),
         near,
-        far,
         table_near,
+        swap(grad_sent, "exp", 1),
         table_far,
         limit=12,
         to_hbm=(0,),
     )
-
-    part = lax.all_to_all(blocks, ("seq", "exp"), 0, 0, tiled=True)
+    same_core = [
+        [s * n_exp + 2 * chip + core for s in range(n_seq) for chip in range(n_exp // 2)]
+        for core in range(2)
+    ]
+    part = lax.all_to_all(
+        blocks, ("seq", "exp"), 0, 0, tiled=True, axis_index_groups=same_core
+    )
     part = jnp.sum(part.astype(F32), axis=0)
     return (tok_grad, part.T)
 

time: 67.4 us -> 66.9 us (level)
  waiting for transfers between devices: 23.1 us -> 20.4 us
  starting transfers between devices: 26.5 us -> 28.3 us
    all_to_all x1, waiting for transfers between devices: 8.95 us -> 6.93 us  [shards(): lax.all_to_all(blocks, ('seq', 'exp'), 0, 0, tiled=True, axis_index_group...]
    all_to_all x1, starting transfers between devices: 3.64 us -> 4.65 us  [shards(): lax.all_to_all(blocks, ('seq', 'exp'), 0, 0, tiled=True, axis_index_group...]
    ppermute x20 -> x22, starting transfers between devices: 22.9 us -> 23.6 us  [swap(): lax.ppermute(x, axis, [(k, k ^ mask) for k in range(lax.axis_size(axis))])]
    ppermute x20 -> x22, waiting for transfers between devices: 14.1 us -> 13.5 us  [swap(): lax.ppermute(x, axis, [(k, k ^ mask) for k in range(lax.axis_size(axis))])]
    pallas_call x17 -> x18, Pallas kernels: 15.2 us -> 15.6 us  [local_call(): pl.pallas_call(body, out_shape=tuple((jax.ShapeDtypeStruct(s, d) if k in...]
  transfers between devices with their start and end apart: 21 -> 23, of which waited for: 12 -> 12; matrix products, arithmetic and copies ran while one was open for 0% -> 0% of each run, Pallas kernels for 20% -> 22%
where the time goes in v9:
time: 66.9 us; the launch traced here: 66.6 us
  starting transfers between devices  28.3 us (42%)
  waiting for transfers between devices  20.4 us (30%)
  Pallas kernels  15.6 us (23%)
  between operations  0.87 us (1%)
  local copies, waits for them, and re-layouts  0.8 us (1%)
    ppermute x22, starting transfers between devices, swap(): lax.ppermute(x, axis, [(k, k ^ mask) for k in range(lax.axis_size(axis))])  23.6 us
    pallas_call x18, Pallas kernels, local_call(): pl.pallas_call(body, out_shape=tuple((jax.ShapeDtypeStruct(s, d) if k in...  15.6 us
    ppermute x22, waiting for transfers between devices, swap(): lax.ppermute(x, axis, [(k, k ^ mask) for k in range(lax.axis_size(axis))])  13.5 us
    all_to_all x1, waiting for transfers between devices, shards(): lax.all_to_all(blocks, ('seq', 'exp'), 0, 0, tiled=True, axis_index_group...  6.93 us
    all_to_all x1, starting transfers between devices, shards(): lax.all_to_all(blocks, ('seq', 'exp'), 0, 0, tiled=True, axis_index_group...  4.65 us
  transfers between devices with their start and end apart: 23, of which 12 were waited for; matrix products, arithmetic and copies ran while one was open for 0% of the time, Pallas kernels for 22%

profile of v9, /device:TPU:0, one launch (start us, length us, event | category | flops | bytes accessed | tf_op | source)
XLA Modules:
  0.0 66.6 jit_solution(319736126987748976)
XLA Ops:
  0.6 5.1 %collective-permute-start = (bf16[8,2048]{1,0:T(8,128)(2,1)}, bf16[8,2048]{1,0:T(8,128)(2,1)S(1)}, u32[]{:S(2)}, u32[]{:S(2)}) collective-permute-start(bf16[8,2048]{1,0:T(8,128)(2,1)} %bitcast.8), channel_id=1, source_target_pairs={{0,6},{1,7},{2,4},{3,5},{4,2},{5,3},{6,0},{7,1},{8,14},{9,15},{10,... | collective-permute-start | bytes 98312 | tf_op jit(solution)/shard_map/ppermute | solution.py:18
  5.8 0.6 collective-permute-start.2
  6.9 0.8 %copy-done.2 = bf16[2048,8]{0,1:T(8,128)(2,1)S(1)} copy-done((bf16[2048,8]{0,1:T(8,128)(2,1)S(1)}, bf16[2048,8]{0,1:T(8,128)(2,1)}, u32[]{:S(2)}) %copy-start.2) | copy-done | bytes 32792
  8.0 2.7 %collective-permute-done.1.refs_2_ = bf16[8,2048]{1,0:T(8,128)(2,1)S(1)} collective-permute-done((bf16[8,2048]{1,0:T(8,128)(2,1)}, bf16[8,2048]{1,0:T(8,128)(2,1)S(1)}, u32[]{:S(2)}, u32[]{:S(2)}) %collective-permute-start.1) | collective-permute-done | bytes 32800 | tf_op jit(solution)/shard_map/ppermute | solution.py:18
  10.8 0.6 shard_map.71
  13.1 2.2 %collective-permute-start.6 = (bf16[8,4224]{1,0:T(8,128)(2,1)S(1)}, bf16[8,4224]{1,0:T(8,128)(2,1)S(1)}, u32[]{:S(2)}, u32[]{:S(2)}) collective-permute-start(bf16[8,4224]{1,0:T(8,128)(2,1)S(1)} %get-tuple-element.26), channel_id=1, source_target_pairs={{0,6},{1,7},{2,4},{3,5},{4,2},{5,3},{6,0},{7,1},{8,14},{9,15},{10,... | collective-permute-start | bytes 202760 | tf_op jit(solution)/shard_map/ppermute | solution.py:18
  15.4 2.2 %collective-permute-start.8 = (bf16[8,4224]{1,0:T(8,128)(2,1)S(1)}, bf16[8,4224]{1,0:T(8,128)(2,1)S(1)}, u32[]{:S(2)}, u32[]{:S(2)}) collective-permute-start(bf16[8,4224]{1,0:T(8,128)(2,1)S(1)} %get-tuple-element.28), channel_id=1, source_target_pairs={{0,2},{1,3},{2,0},{3,1},{4,6},{5,7},{6,4},{7,5},{8,10},{9,11},{10,... | collective-permute-start | bytes 202760 | tf_op jit(solution)/shard_map/ppermute | solution.py:18
  17.6 1.2 %shard_map.77.refs_8_ = bf16[2048,1024]{1,0:T(8,128)(2,1)S(1)} custom-call(bf16[2,1024,2048]{2,1,0:T(8,128)(2,1)S(1)} %bitcast.5, bf16[8,4224]{1,0:T(8,128)(2,1)S(1)} %get-tuple-element.25.refs_0_.after), custom_call_target="tpu_custom_call" | custom-call | flops 1000000000 | bytes 4194304 | tf_op jit(solution)/shard_map/pallas_call | solution.py:44
  18.9 1.2 %shard_map.78.refs_9_ = bf16[2048,1024]{1,0:T(8,128)(2,1)S(1)} custom-call(bf16[2,1024,2048]{2,1,0:T(8,128)(2,1)S(1)} %bitcast.5, bf16[8,4224]{1,0:T(8,128)(2,1)S(1)} %get-tuple-element.25.refs_0_.after), custom_call_target="tpu_custom_call" | custom-call | flops 1000000000 | bytes 4194304 | tf_op jit(solution)/shard_map/pallas_call | solution.py:44
  20.1 2.0 %collective-permute-done.7.refs_2_ = bf16[8,4224]{1,0:T(8,128)(2,1)S(1)} collective-permute-done((bf16[8,4224]{1,0:T(8,128)(2,1)S(1)}, bf16[8,4224]{1,0:T(8,128)(2,1)S(1)}, u32[]{:S(2)}, u32[]{:S(2)}) %collective-permute-start.7) | collective-permute-done | bytes 67616 | tf_op jit(solution)/shard_map/ppermute | solution.py:18
  22.3 1.6 %collective-permute-start.10 = (bf16[8,4224]{1,0:T(8,128)(2,1)S(1)}, bf16[8,4224]{1,0:T(8,128)(2,1)S(1)}, u32[]{:S(2)}, u32[]{:S(2)}) collective-permute-start(bf16[8,4224]{1,0:T(8,128)(2,1)S(1)} %shard_map.74.after.refs_0_), channel_id=1, source_target_pairs={{0,16},{8,24},{16,0},{24,8},{1,17},{9,25},{17,1},{25,9},{2,18},{10... | collective-permute-start | bytes 202760 | tf_op jit(solution)/shard_map/ppermute | solution.py:18
  23.9 1.5 %collective-permute-start.11 = (bf16[8,4224]{1,0:T(8,128)(2,1)S(1)}, bf16[8,4224]{1,0:T(8,128)(2,1)S(1)}, u32[]{:S(2)}, u32[]{:S(2)}) collective-permute-start(bf16[8,4224]{1,0:T(8,128)(2,1)S(1)} %shard_map.74.after.refs_0_), channel_id=1, source_target_pairs={{0,8},{8,0},{16,24},{24,16},{1,9},{9,1},{17,25},{25,17},{2,10},{10... | collective-permute-start | bytes 202760 | tf_op jit(solution)/shard_map/ppermute | solution.py:18
  25.9 1.2 %shard_map.75.refs_6_ = bf16[1024,2048]{1,0:T(8,128)(2,1)S(1)} custom-call(bf16[2,2048,1024]{2,1,0:T(8,128)(2,1)S(1)} %bitcast.3, bf16[8,4224]{1,0:T(8,128)(2,1)S(1)} %shard_map.74.after.refs_0_), custom_call_target="tpu_custom_call" | custom-call | flops 1000000000 | bytes 4194304 | tf_op jit(solution)/shard_map/pallas_call | solution.py:44
  27.1 1.2 %shard_map.76.refs_7_ = bf16[1024,2048]{1,0:T(8,128)(2,1)S(1)} custom-call(bf16[2,2048,1024]{2,1,0:T(8,128)(2,1)S(1)} %bitcast.3, bf16[8,4224]{1,0:T(8,128)(2,1)S(1)} %shard_map.74.after.refs_0_), custom_call_target="tpu_custom_call" | custom-call | flops 1000000000 | bytes 4194304 | tf_op jit(solution)/shard_map/pallas_call | solution.py:44
  28.8 1.7 %collective-permute-done.9.refs_1_ = bf16[8,4224]{1,0:T(8,128)(2,1)S(1)} collective-permute-done((bf16[8,4224]{1,0:T(8,128)(2,1)S(1)}, bf16[8,4224]{1,0:T(8,128)(2,1)S(1)}, u32[]{:S(2)}, u32[]{:S(2)}) %collective-permute-start.9) | collective-permute-done | bytes 67616 | tf_op jit(solution)/shard_map/ppermute | solution.py:18
  30.6 4.5 %shard_map.79 = (bf16[8,4096]{1,0:T(8,128)(2,1)S(1)}, f32[8,2048]{1,0:T(8,128)S(1)}, f32[8,128]{1,0:T(8,128)S(1)}) custom-call(bf16[8,4224]{1,0:T(8,128)(2,1)S(1)} %shard_map.74.after.refs_0_, bf16[8,4224]{1,0:T(8,128)(2,1)S(1)} %collective-permute-done.9.refs_1_, bf16[8,4224]{1,0:T(8,128)(2,1)S(1)} %collective-permute-done.10.refs_2_, ...), custom_call_target="tpu_custom_call" | custom-call | flops 10000000000 | bytes 4194304 | tf_op jit(solution)/shard_map/pallas_call | solution.py:44
  35.1 1.4 %collective-permute-start.12 = (bf16[8,4096]{1,0:T(8,128)(2,1)S(1)}, bf16[8,4096]{1,0:T(8,128)(2,1)S(1)}, u32[]{:S(2)}, u32[]{:S(2)}) collective-permute-start(bf16[8,4096]{1,0:T(8,128)(2,1)S(1)} %get-tuple-element.29.refs_0_), channel_id=1, source_target_pairs={{0,24},{8,16},{16,8},{24,0},{1,25},{9,17},{17,9},{25,1},{2,26},{10... | collective-permute-start | bytes 196616 | tf_op jit(solution)/shard_map/ppermute | solution.py:18
  36.5 0.6 collective-permute-start.13
  37.1 1.5 %collective-permute-start.14 = (bf16[8,4096]{1,0:T(8,128)(2,1)S(1)}, bf16[8,4096]{1,0:T(8,128)(2,1)S(1)}, u32[]{:S(2)}, u32[]{:S(2)}) collective-permute-start(bf16[8,4096]{1,0:T(8,128)(2,1)S(1)} %get-tuple-element.29.refs_0_), channel_id=1, source_target_pairs={{0,8},{8,0},{16,24},{24,16},{1,9},{9,1},{17,25},{25,17},{2,10},{10... | collective-permute-start | bytes 196616 | tf_op jit(solution)/shard_map/ppermute | solution.py:18
  38.6 2.1 %collective-permute-done.12.refs_1_ = bf16[8,4096]{1,0:T(8,128)(2,1)S(1)} collective-permute-done((bf16[8,4096]{1,0:T(8,128)(2,1)S(1)}, bf16[8,4096]{1,0:T(8,128)(2,1)S(1)}, u32[]{:S(2)}, u32[]{:S(2)}) %collective-permute-start.12) | collective-permute-done | bytes 65568 | tf_op jit(solution)/shard_map/ppermute | solution.py:18
  41.5 2.6 %collective-permute-start.16 = (bf16[8,4224]{1,0:T(8,128)(2,1)S(1)}, bf16[8,4224]{1,0:T(8,128)(2,1)S(1)}, u32[]{:S(2)}, u32[]{:S(2)}) collective-permute-start(bf16[8,4224]{1,0:T(8,128)(2,1)S(1)} %shard_map.80.refs_0_), channel_id=1, source_target_pairs={{0,6},{1,7},{2,4},{3,5},{4,2},{5,3},{6,0},{7,1},{8,14},{9,15},{10,... | collective-permute-start | bytes 202760 | tf_op jit(solution)/shard_map/ppermute | solution.py:18
  44.1 1.8 %collective-permute-start.18 = (bf16[8,4224]{1,0:T(8,128)(2,1)S(1)}, bf16[8,4224]{1,0:T(8,128)(2,1)S(1)}, u32[]{:S(2)}, u32[]{:S(2)}) collective-permute-start(bf16[8,4224]{1,0:T(8,128)(2,1)S(1)} %shard_map.80.refs_0_), channel_id=1, source_target_pairs={{0,2},{1,3},{2,0},{3,1},{4,6},{5,7},{6,4},{7,5},{8,10},{9,11},{10,... | collective-permute-start | bytes 202760 | tf_op jit(solution)/shard_map/ppermute | solution.py:18
  46.3 1.4 %collective-permute-done.16.refs_1_ = bf16[8,4224]{1,0:T(8,128)(2,1)S(1)} collective-permute-done((bf16[8,4224]{1,0:T(8,128)(2,1)S(1)}, bf16[8,4224]{1,0:T(8,128)(2,1)S(1)}, u32[]{:S(2)}, u32[]{:S(2)}) %collective-permute-start.16) | collective-permute-done | bytes 67616 | tf_op jit(solution)/shard_map/ppermute | solution.py:18
  47.6 1.7 %collective-permute-done.17.refs_2_ = bf16[8,4224]{1,0:T(8,128)(2,1)S(1)} collective-permute-done((bf16[8,4224]{1,0:T(8,128)(2,1)S(1)}, bf16[8,4224]{1,0:T(8,128)(2,1)S(1)}, u32[]{:S(2)}, u32[]{:S(2)}) %collective-permute-start.17) | collective-permute-done | bytes 67616 | tf_op jit(solution)/shard_map/ppermute | solution.py:18
  49.3 1.0 %shard_map.83 = (f32[32,512]{1,0:T(8,128)S(1)}, f32[32,512]{1,0:T(8,128)S(1)}, f32[32,512]{1,0:T(8,128)S(1)}, f32[8,512]{1,0:T(8,128)S(1)}) custom-call(bf16[32,4224]{1,0:T(8,128)(2,1)S(1)} %shard_map.81.near, f32[32,512]{1,0:T(8,128)S(1)} %get-tuple-element.21.logits, f32[8,512]{1,0:T(8,128)S(1)} %get-tuple-element.22.rows, ...), custom_call_target="tpu_custom_call" | custom-call | flops 10000000000 | bytes 4194304 | tf_op jit(solution)/shard_map/pallas_call | solution.py:44
  50.5 0.6 collective-permute-start.21
  51.0 0.6 collective-permute-done.19.mean_far
  51.6 1.1 %shard_map.84 = (bf16[64,256]{1,0:T(8,128)(2,1)S(1)}, bf16[64,256]{1,0:T(8,128)(2,1)S(1)}, bf16[16,8,512]{2,1,0:T(8,128)(2,1)}) custom-call(f32[32,512]{1,0:T(8,128)S(1)} %get-tuple-element.33.direct, f32[32,512]{1,0:T(8,128)S(1)} %get-tuple-element.34.combine, f32[32,512]{1,0:T(8,128)S(1)} %get-tuple-element.35.dispatch, ...), custom_call_target="tpu_custom_call" | custom-call | flops 10000000000 | bytes 4194304 | tf_op jit(solution)/shard_map/pallas_call | solution.py:44
  52.9 4.7 %all-to-all-start = ((bf16[16,8,512]{2,1,0:T(8,128)(2,1)}), bf16[16,8,512]{2,1,0:T(8,128)(2,1)S(1)}, u32[]{:S(2)}, u32[]{:S(2)}) async-start(bf16[16,8,512]{2,1,0:T(8,128)(2,1)} %get-tuple-element.39), calls=%async_computation | async-start | bytes 262144 | tf_op jit(solution)/shard_map/all_to_all | solution.py:513
  57.6 1.4 %shard_map.86 = bf16[256,2048]{1,0:T(8,128)(2,1)} custom-call(bf16[64,256]{1,0:T(8,128)(2,1)S(1)} %get-tuple-element.37.weights, bf16[64,256]{1,0:T(8,128)(2,1)S(1)} %collective-permute-done.20.weights_far, bf16[32,4224]{1,0:T(8,128)(2,1)S(1)} %shard_map.81.near, bf16[32,2048]{1,0:T(8,128)(2,1)S(1)} %shard_map.69.table, ...), custom_call_target="tpu_custom_call" | custom-call | flops 10000000000 | bytes 4194304 | tf_op jit(solution)/shard_map/pallas_call | solution.py:44
  59.0 6.9 %all-to-all-done = bf16[16,8,512]{2,1,0:T(8,128)(2,1)S(1)} async-done(((bf16[16,8,512]{2,1,0:T(8,128)(2,1)}), bf16[16,8,512]{2,1,0:T(8,128)(2,1)S(1)}, u32[]{:S(2)}, u32[]{:S(2)}) %all-to-all-start) | async-done | bytes 131104 | tf_op jit(solution)/shard_map/all_to_all | solution.py:513
  66.0 0.6 convert_reduce_fusion
  (55 shorter events, 5.1 us)
Async XLA Ops:
  0.6 7.1 %copy-start.1 = (bf16[256,2048]{1,0:T(8,128)(2,1)S(1)}, bf16[256,2048]{1,0:T(8,128)(2,1)}, u32[]{:S(2)}) copy-start(bf16[256,2048]{1,0:T(8,128)(2,1)} %tokens.3) | copy-start | bytes 3145732
  0.6 7.4 %collective-permute-start = (bf16[8,2048]{1,0:T(8,128)(2,1)}, bf16[8,2048]{1,0:T(8,128)(2,1)S(1)}, u32[]{:S(2)}, u32[]{:S(2)}) collective-permute-start(bf16[8,2048]{1,0:T(8,128)(2,1)} %bitcast.8), channel_id=1, source_target_pairs={{0,6},{1,7},{2,4},{3,5},{4,2},{5,3},{6,0},{7,1},{8,14},{9,15},{10,... | collective-permute-start | bytes 98312 | tf_op jit(solution)/shard_map/ppermute | solution.py:18
  5.8 5.0 %collective-permute-start.1 = (bf16[8,2048]{1,0:T(8,128)(2,1)}, bf16[8,2048]{1,0:T(8,128)(2,1)S(1)}, u32[]{:S(2)}, u32[]{:S(2)}) collective-permute-start(bf16[8,2048]{1,0:T(8,128)(2,1)} %bitcast.9), channel_id=1, source_target_pairs={{0,4},{1,5},{2,6},{3,7},{4,0},{5,1},{6,2},{7,3},{8,12},{9,13},{10,... | collective-permute-start | bytes 98312 | tf_op jit(solution)/shard_map/ppermute | solution.py:18
  5.8 5.0 %collective-permute-start.2 = (bf16[8,2048]{1,0:T(8,128)(2,1)}, bf16[8,2048]{1,0:T(8,128)(2,1)S(1)}, u32[]{:S(2)}, u32[]{:S(2)}) collective-permute-start(bf16[8,2048]{1,0:T(8,128)(2,1)} %bitcast.10), channel_id=1, source_target_pairs={{0,2},{1,3},{2,0},{3,1},{4,6},{5,7},{6,4},{7,5},{8,10},{9,11},{10,... | collective-permute-start | bytes 98312 | tf_op jit(solution)/shard_map/ppermute | solution.py:18
  6.4 4.4 %collective-permute-start.3 = (bf16[256,2048]{1,0:T(8,128)(2,1)}, bf16[256,2048]{1,0:T(8,128)(2,1)S(1)}, u32[]{:S(2)}, u32[]{:S(2)}) collective-permute-start(bf16[256,2048]{1,0:T(8,128)(2,1)} %tokens.3), channel_id=1, source_target_pairs={{0,1},{1,0},{2,3},{3,2},{4,5},{5,4},{6,7},{7,6},{8,9},{9,8},{10,11... | collective-permute-start | bytes 3145736 | tf_op jit(solution)/shard_map/ppermute | solution.py:18
  6.4 6.2 %collective-permute-start.5 = (bf16[256,2048]{1,0:T(8,128)(2,1)}, bf16[256,2048]{1,0:T(8,128)(2,1)S(1)}, u32[]{:S(2)}, u32[]{:S(2)}) collective-permute-start(bf16[256,2048]{1,0:T(8,128)(2,1)} %x.3), channel_id=1, source_target_pairs={{0,1},{1,0},{2,3},{3,2},{4,5},{5,4},{6,7},{7,6},{8,9},{9,8},{10,11... | collective-permute-start | bytes 3145736 | tf_op jit(solution)/shard_map/ppermute | solution.py:18
  6.9 0.8 %copy-start.2 = (bf16[2048,8]{0,1:T(8,128)(2,1)S(1)}, bf16[2048,8]{0,1:T(8,128)(2,1)}, u32[]{:S(2)}) copy-start(bf16[2048,8]{0,1:T(8,128)(2,1)} %param.6) | copy-start | bytes 98308
  10.8 1.9 %copy-start = (bf16[256,2048]{1,0:T(8,128)(2,1)S(1)}, bf16[256,2048]{1,0:T(8,128)(2,1)}, u32[]{:S(2)}) copy-start(bf16[256,2048]{1,0:T(8,128)(2,1)} %x.3) | copy-start | bytes 3145732
  11.4 1.2 %collective-permute-start.4 = (f32[8,512]{1,0:T(8,128)S(1)}, f32[8,512]{1,0:T(8,128)S(1)}, u32[]{:S(2)}, u32[]{:S(2)}) collective-permute-start(f32[8,512]{1,0:T(8,128)S(1)} %get-tuple-element.22.rows), channel_id=1, source_target_pairs={{0,1},{1,0},{2,3},{3,2},{4,5},{5,4},{6,7},{7,6},{8,9},{9,8},{10,11... | collective-permute-start | bytes 49160 | tf_op jit(solution)/shard_map/ppermute | solution.py:18
  12.0 26.6 %collective-permute-start.15 = (bf16[32,2048]{1,0:T(8,128)(2,1)S(1)}, bf16[32,2048]{1,0:T(8,128)(2,1)S(1)}, u32[]{:S(2)}, u32[]{:S(2)}) collective-permute-start(bf16[32,2048]{1,0:T(8,128)(2,1)S(1)} %get-tuple-element.32), channel_id=1, source_target_pairs={{0,1},{1,0},{2,3},{3,2},{4,5},{5,4},{6,7},{7,6},{8,9},{9,8},{10,11... | collective-permute-start | bytes 393224 | tf_op jit(solution)/shard_map/ppermute | solution.py:18
  12.7 4.9 %slice-start.2 = ((s8[8388608]{0:T(1024)(128)(4,1)}), s8[4194304]{0:T(1024)(128)(4,1)S(1)}, s32[]{:S(2)}) async-start(s8[8388608]{0:T(1024)(128)(4,1)} %bitcast.4), calls=%async_computation.3 | async-start | bytes 8388608
  12.7 4.9 %slice-start.3 = ((s8[8388608]{0:T(1024)(128)(4,1)}), s8[4194304]{0:T(1024)(128)(4,1)S(1)}, s32[]{:S(2)}) async-start(s8[8388608]{0:T(1024)(128)(4,1)} %bitcast.4), calls=%async_computation.4 | async-start | bytes 8388608
  13.1 7.0 %collective-permute-start.6 = (bf16[8,4224]{1,0:T(8,128)(2,1)S(1)}, bf16[8,4224]{1,0:T(8,128)(2,1)S(1)}, u32[]{:S(2)}, u32[]{:S(2)}) collective-permute-start(bf16[8,4224]{1,0:T(8,128)(2,1)S(1)} %get-tuple-element.26), channel_id=1, source_target_pairs={{0,6},{1,7},{2,4},{3,5},{4,2},{5,3},{6,0},{7,1},{8,14},{9,15},{10,... | collective-permute-start | bytes 202760 | tf_op jit(solution)/shard_map/ppermute | solution.py:18
  15.4 6.8 %collective-permute-start.7 = (bf16[8,4224]{1,0:T(8,128)(2,1)S(1)}, bf16[8,4224]{1,0:T(8,128)(2,1)S(1)}, u32[]{:S(2)}, u32[]{:S(2)}) collective-permute-start(bf16[8,4224]{1,0:T(8,128)(2,1)S(1)} %get-tuple-element.27), channel_id=1, source_target_pairs={{0,4},{1,5},{2,6},{3,7},{4,0},{5,1},{6,2},{7,3},{8,12},{9,13},{10,... | collective-permute-start | bytes 202760 | tf_op jit(solution)/shard_map/ppermute | solution.py:18
  15.4 6.8 %collective-permute-start.8 = (bf16[8,4224]{1,0:T(8,128)(2,1)S(1)}, bf16[8,4224]{1,0:T(8,128)(2,1)S(1)}, u32[]{:S(2)}, u32[]{:S(2)}) collective-permute-start(bf16[8,4224]{1,0:T(8,128)(2,1)S(1)} %get-tuple-element.28), channel_id=1, source_target_pairs={{0,2},{1,3},{2,0},{3,1},{4,6},{5,7},{6,4},{7,5},{8,10},{9,11},{10,... | collective-permute-start | bytes 202760 | tf_op jit(solution)/shard_map/ppermute | solution.py:18
  18.8 7.0 %slice-start = ((s8[8388608]{0:T(1024)(128)(4,1)}), s8[4194304]{0:T(1024)(128)(4,1)S(1)}, s32[]{:S(2)}) async-start(s8[8388608]{0:T(1024)(128)(4,1)} %bitcast.2), calls=%async_computation.1 | async-start | bytes 8388608
  20.1 5.8 %slice-start.1 = ((s8[8388608]{0:T(1024)(128)(4,1)}), s8[4194304]{0:T(1024)(128)(4,1)S(1)}, s32[]{:S(2)}) async-start(s8[8388608]{0:T(1024)(128)(4,1)} %bitcast.2), calls=%async_computation.2 | async-start | bytes 8388608
  22.3 6.1 %collective-permute-start.10 = (bf16[8,4224]{1,0:T(8,128)(2,1)S(1)}, bf16[8,4224]{1,0:T(8,128)(2,1)S(1)}, u32[]{:S(2)}, u32[]{:S(2)}) collective-permute-start(bf16[8,4224]{1,0:T(8,128)(2,1)S(1)} %shard_map.74.after.refs_0_), channel_id=1, source_target_pairs={{0,16},{8,24},{16,0},{24,8},{1,17},{9,25},{17,1},{25,9},{2,18},{10... | collective-permute-start | bytes 202760 | tf_op jit(solution)/shard_map/ppermute | solution.py:18
  23.9 4.9 %collective-permute-start.11 = (bf16[8,4224]{1,0:T(8,128)(2,1)S(1)}, bf16[8,4224]{1,0:T(8,128)(2,1)S(1)}, u32[]{:S(2)}, u32[]{:S(2)}) collective-permute-start(bf16[8,4224]{1,0:T(8,128)(2,1)S(1)} %shard_map.74.after.refs_0_), channel_id=1, source_target_pairs={{0,8},{8,0},{16,24},{24,16},{1,9},{9,1},{17,25},{25,17},{2,10},{10... | collective-permute-start | bytes 202760 | tf_op jit(solution)/shard_map/ppermute | solution.py:18
  25.4 5.2 %collective-permute-start.9 = (bf16[8,4224]{1,0:T(8,128)(2,1)S(1)}, bf16[8,4224]{1,0:T(8,128)(2,1)S(1)}, u32[]{:S(2)}, u32[]{:S(2)}) collective-permute-start(bf16[8,4224]{1,0:T(8,128)(2,1)S(1)} %shard_map.74.after.refs_0_), channel_id=1, source_target_pairs={{0,24},{8,16},{16,8},{24,0},{1,25},{9,17},{17,9},{25,1},{2,26},{10... | collective-permute-start | bytes 202760 | tf_op jit(solution)/shard_map/ppermute | solution.py:18
  25.9 4.7 %slice-start.4 = ((s8[8388608]{0:T(1024)(128)(4,1)}), s8[4194304]{0:T(1024)(128)(4,1)S(1)}, s32[]{:S(2)}) async-start(s8[8388608]{0:T(1024)(128)(4,1)} %bitcast.6), calls=%async_computation.5 | async-start | bytes 8388608
  27.1 3.5 %slice-start.5 = ((s8[8388608]{0:T(1024)(128)(4,1)}), s8[4194304]{0:T(1024)(128)(4,1)S(1)}, s32[]{:S(2)}) async-start(s8[8388608]{0:T(1024)(128)(4,1)} %bitcast.6), calls=%async_computation.6 | async-start | bytes 8388608
  35.1 5.6 %collective-permute-start.12 = (bf16[8,4096]{1,0:T(8,128)(2,1)S(1)}, bf16[8,4096]{1,0:T(8,128)(2,1)S(1)}, u32[]{:S(2)}, u32[]{:S(2)}) collective-permute-start(bf16[8,4096]{1,0:T(8,128)(2,1)S(1)} %get-tuple-element.29.refs_0_), channel_id=1, source_target_pairs={{0,24},{8,16},{16,8},{24,0},{1,25},{9,17},{17,9},{25,1},{2,26},{10... | collective-permute-start | bytes 196616 | tf_op jit(solution)/shard_map/ppermute | solution.py:18
  36.5 4.7 %collective-permute-start.13 = (bf16[8,4096]{1,0:T(8,128)(2,1)S(1)}, bf16[8,4096]{1,0:T(8,128)(2,1)S(1)}, u32[]{:S(2)}, u32[]{:S(2)}) collective-permute-start(bf16[8,4096]{1,0:T(8,128)(2,1)S(1)} %get-tuple-element.29.refs_0_), channel_id=1, source_target_pairs={{0,16},{8,24},{16,0},{24,8},{1,17},{9,25},{17,1},{25,9},{2,18},{10... | collective-permute-start | bytes 196616 | tf_op jit(solution)/shard_map/ppermute | solution.py:18
  37.1 4.3 %collective-permute-start.14 = (bf16[8,4096]{1,0:T(8,128)(2,1)S(1)}, bf16[8,4096]{1,0:T(8,128)(2,1)S(1)}, u32[]{:S(2)}, u32[]{:S(2)}) collective-permute-start(bf16[8,4096]{1,0:T(8,128)(2,1)S(1)} %get-tuple-element.29.refs_0_), channel_id=1, source_target_pairs={{0,8},{8,0},{16,24},{24,16},{1,9},{9,1},{17,25},{25,17},{2,10},{10... | collective-permute-start | bytes 196616 | tf_op jit(solution)/shard_map/ppermute | solution.py:18
  41.5 6.1 %collective-permute-start.16 = (bf16[8,4224]{1,0:T(8,128)(2,1)S(1)}, bf16[8,4224]{1,0:T(8,128)(2,1)S(1)}, u32[]{:S(2)}, u32[]{:S(2)}) collective-permute-start(bf16[8,4224]{1,0:T(8,128)(2,1)S(1)} %shard_map.80.refs_0_), channel_id=1, source_target_pairs={{0,6},{1,7},{2,4},{3,5},{4,2},{5,3},{6,0},{7,1},{8,14},{9,15},{10,... | collective-permute-start | bytes 202760 | tf_op jit(solution)/shard_map/ppermute | solution.py:18
  44.1 5.2 %collective-permute-start.17 = (bf16[8,4224]{1,0:T(8,128)(2,1)S(1)}, bf16[8,4224]{1,0:T(8,128)(2,1)S(1)}, u32[]{:S(2)}, u32[]{:S(2)}) collective-permute-start(bf16[8,4224]{1,0:T(8,128)(2,1)S(1)} %shard_map.80.refs_0_), channel_id=1, source_target_pairs={{0,4},{1,5},{2,6},{3,7},{4,0},{5,1},{6,2},{7,3},{8,12},{9,13},{10,... | collective-permute-start | bytes 202760 | tf_op jit(solution)/shard_map/ppermute | solution.py:18
  44.1 5.2 %collective-permute-start.18 = (bf16[8,4224]{1,0:T(8,128)(2,1)S(1)}, bf16[8,4224]{1,0:T(8,128)(2,1)S(1)}, u32[]{:S(2)}, u32[]{:S(2)}) collective-permute-start(bf16[8,4224]{1,0:T(8,128)(2,1)S(1)} %shard_map.80.refs_0_), channel_id=1, source_target_pairs={{0,2},{1,3},{2,0},{3,1},{4,6},{5,7},{6,4},{7,5},{8,10},{9,11},{10,... | collective-permute-start | bytes 202760 | tf_op jit(solution)/shard_map/ppermute | solution.py:18
  50.4 1.2 %collective-permute-start.19 = (f32[8,512]{1,0:T(8,128)S(1)}, f32[8,512]{1,0:T(8,128)S(1)}, u32[]{:S(2)}, u32[]{:S(2)}) collective-permute-start(f32[8,512]{1,0:T(8,128)S(1)} %get-tuple-element.36.mean.after), channel_id=1, source_target_pairs={{0,1},{1,0},{2,3},{3,2},{4,5},{5,4},{6,7},{7,6},{8,9},{9,8},{10,11... | collective-permute-start | bytes 49160 | tf_op jit(solution)/shard_map/ppermute | solution.py:18
  50.5 7.1 %collective-permute-start.21 = (bf16[32,2048]{1,0:T(8,128)(2,1)S(1)}, bf16[32,2048]{1,0:T(8,128)(2,1)S(1)}, u32[]{:S(2)}, u32[]{:S(2)}) collective-permute-start(bf16[32,2048]{1,0:T(8,128)(2,1)S(1)} %shard_map.85), channel_id=1, source_target_pairs={{0,1},{1,0},{2,3},{3,2},{4,5},{5,4},{6,7},{7,6},{8,9},{9,8},{10,11... | collective-permute-start | bytes 393224 | tf_op jit(solution)/shard_map/ppermute | solution.py:18
  52.8 4.8 %collective-permute-start.20 = (bf16[64,256]{1,0:T(8,128)(2,1)S(1)}, bf16[64,256]{1,0:T(8,128)(2,1)S(1)}, u32[]{:S(2)}, u32[]{:S(2)}) collective-permute-start(bf16[64,256]{1,0:T(8,128)(2,1)S(1)} %get-tuple-element.38), channel_id=1, source_target_pairs={{0,1},{1,0},{2,3},{3,2},{4,5},{5,4},{6,7},{7,6},{8,9},{9,8},{10,11... | collective-permute-start | bytes 98312 | tf_op jit(solution)/shard_map/ppermute | solution.py:18
  52.9 13.0 %all-to-all-start = ((bf16[16,8,512]{2,1,0:T(8,128)(2,1)}), bf16[16,8,512]{2,1,0:T(8,128)(2,1)S(1)}, u32[]{:S(2)}, u32[]{:S(2)}) async-start(bf16[16,8,512]{2,1,0:T(8,128)(2,1)} %get-tuple-element.39), calls=%async_computation | async-start | bytes 262144 | tf_op jit(solution)/shard_map/all_to_all | solution.py:513

commit v10 on v9

--- a/solution.py
+++ b/solution.py
@@ -29,7 +29,7 @@
 def groups(n, first):
     bits = [1 << k for k in range(n.bit_length() - 1) if 1 << k >= first]
     return [
-        [sum(pair), pair[1], pair[0]]
+        [pair[1], sum(pair), pair[0]] if first > 1 else [sum(pair), pair[1], pair[0]]
         if len(pair) == 2
         else [pair[0]]
         for pair in (bits[k : k + 2] for k in range(0, len(bits), 2))
@@ -85,22 +85,12 @@
     ]
 
 
-def load_kernel(source, out, semaphore):
-    copy = pltpu.make_async_copy(source, out, semaphore)
-    copy.start()
-    copy.wait()
+def plain_copy_kernel(x, out):
+    out[...] = x[...]
 
 
 def loaded(x):
-    return pl.pallas_call(
-        load_kernel,
-        out_shape=pltpu.VMEM(x.shape, x.dtype),
-        in_specs=[pl.BlockSpec(memory_space=pl.ANY)],
-        out_specs=pl.BlockSpec(memory_space=pltpu.VMEM),
-        scratch_shapes=[pltpu.SemaphoreType.DMA],
-        compiler_params=pltpu.CompilerParams(vmem_limit_bytes=2 * MIB),
-        cost_estimate=pl.CostEstimate(flops=10**9, bytes_accessed=2 * x.size, transcendentals=0),
-    )(x)
+    return local_call(plain_copy_kernel, [(x.shape, x.dtype)], x, limit=2, flops=10**9)[0]
 
 
 def concat_kernel(*refs):
@@ -135,8 +125,7 @@
     stats[...] = jnp.where(row == 0, top, jnp.where(row == 1, total, 0.0))
 
 
-def dispatch_kernel(logits, tokens, tokens_far, table, sums, stats, table_out):
-    table_out[...] = table[...]
+def dispatch_kernel(logits, tokens, tokens_far, sums, stats):
     patches = tokens.shape[0]
     top = jnp.max(logits[...], axis=1, keepdims=True)
     weight = jnp.exp(logits[...] - top)
@@ -285,7 +274,7 @@
 
 def centre_kernel(count, width, *refs):
     parts = refs[:count]
-    slot_sum, stats, _, out = refs[count:]
+    slot_sum, stats, out = refs[count:]
     total = sum(r[...].astype(F32) for r in parts).astype(BF16)
     grad_in = total[:, width:].astype(F32)
     centre = jnp.sum(slot_sum[...] * grad_in, axis=1, keepdims=True)
@@ -368,6 +357,10 @@
     out[...] = near[:, width : 2 * width]
 
 
+def copy_kernel(x, after, out):
+    out[...] = x[...]
+
+
 def patch_kernel(weights, weights_far, near, table, grad_far, table_far, out):
     width = out.shape[1]
     left = jnp.concatenate([weights[...], weights_far[...]], axis=0)
@@ -404,16 +397,14 @@
         tokens_flipped,
         tokens_far,
     )
-    sums, stats, table_sent = local_call(
+    sums, stats = local_call(
         dispatch_kernel,
-        [((half, width), BF16), ((half, LANES), BF16), ((half, width), BF16)],
+        [((half, width), BF16), ((half, LANES), BF16)],
         logits,
         tokens,
         tokens_far,
-        table_near,
         flops=10**9,
     )
-    table_far = swap(table_sent, "exp", 1)
     pieces_first = len(chip_groups[0]) + 1
     rows_far = swap(rows, "exp", 1)
     pieces = local_call(
@@ -459,8 +450,11 @@
         *parts,
         slot_sum,
         stats,
-        table_far,
-    )
+    )
+    (table_sent,) = local_call(
+        copy_kernel, [((half, width), BF16)], table_near, packet, flops=10**8
+    )
+    table_far = swap(table_sent, "exp", 1)
     near = gathered_over_chips(packet, packet)
     direct, combine, dispatch, mean = local_call(
         grad_kernel,

time: 66.9 us -> 66.7 us (level)
  starting transfers between devices: 28.3 us -> 25.5 us
  waiting for transfers between devices: 20.4 us -> 23.1 us
    ppermute x22, waiting for transfers between devices: 13.5 us -> 16.2 us  [swap(): lax.ppermute(x, axis, [(k, k ^ mask) for k in range(lax.axis_size(axis))])]
    ppermute x22, starting transfers between devices: 23.6 us -> 21.3 us  [swap(): lax.ppermute(x, axis, [(k, k ^ mask) for k in range(lax.axis_size(axis))])]
    pallas_call x18 -> x20, Pallas kernels: 15.6 us -> 15.6 us  [local_call(): pl.pallas_call(body, out_shape=tuple((jax.ShapeDtypeStruct(s, d) if k in...]
  transfers between devices with their start and end apart: 23 -> 23, of which waited for: 12 -> 14; matrix products, arithmetic and copies ran while one was open for 0% -> 0% of each run, Pallas kernels for 22% -> 14%
where the time goes in v10:
time: 66.7 us; the launch traced here: 66.4 us
  starting transfers between devices  25.5 us (38%)
  waiting for transfers between devices  23.1 us (35%)
  Pallas kernels  15.6 us (23%)
  between operations  0.86 us (1%)
  local copies, waits for them, and re-layouts  0.8 us (1%)
    ppermute x22, starting transfers between devices, swap(): lax.ppermute(x, axis, [(k, k ^ mask) for k in range(lax.axis_size(axis))])  21.3 us
    ppermute x22, waiting for transfers between devices, swap(): lax.ppermute(x, axis, [(k, k ^ mask) for k in range(lax.axis_size(axis))])  16.2 us
    pallas_call x20, Pallas kernels, local_call(): pl.pallas_call(body, out_shape=tuple((jax.ShapeDtypeStruct(s, d) if k in...  15.6 us
    all_to_all x1, waiting for transfers between devices, shards(): lax.all_to_all(blocks, ('seq', 'exp'), 0, 0, tiled=True, axis_index_group...  6.92 us
    all_to_all x1, starting transfers between devices, shards(): lax.all_to_all(blocks, ('seq', 'exp'), 0, 0, tiled=True, axis_index_group...  4.21 us
  transfers between devices with their start and end apart: 23, of which 14 were waited for; matrix products, arithmetic and copies ran while one was open for 0% of the time, Pallas kernels for 14%

profile of v10, /device:TPU:0, one launch (start us, length us, event | category | flops | bytes accessed | tf_op | source)
XLA Modules:
  0.0 66.4 jit_solution(14032971572661464110)
XLA Ops:
  0.6 4.1 %collective-permute-start = (bf16[8,2048]{1,0:T(8,128)(2,1)}, bf16[8,2048]{1,0:T(8,128)(2,1)S(1)}, u32[]{:S(2)}, u32[]{:S(2)}) collective-permute-start(bf16[8,2048]{1,0:T(8,128)(2,1)} %bitcast.8), channel_id=1, source_target_pairs={{0,4},{1,5},{2,6},{3,7},{4,0},{5,1},{6,2},{7,3},{8,12},{9,13},{10,... | collective-permute-start | bytes 98312 | tf_op jit(solution)/shard_map/ppermute | solution.py:18
  4.7 1.3 %collective-permute-start.1 = (bf16[8,2048]{1,0:T(8,128)(2,1)}, bf16[8,2048]{1,0:T(8,128)(2,1)S(1)}, u32[]{:S(2)}, u32[]{:S(2)}) collective-permute-start(bf16[8,2048]{1,0:T(8,128)(2,1)} %bitcast.9), channel_id=1, source_target_pairs={{0,6},{1,7},{2,4},{3,5},{4,2},{5,3},{6,0},{7,1},{8,14},{9,15},{10,... | collective-permute-start | bytes 98312 | tf_op jit(solution)/shard_map/ppermute | solution.py:18
  6.8 0.8 %copy-done.2 = bf16[2048,8]{0,1:T(8,128)(2,1)S(1)} copy-done((bf16[2048,8]{0,1:T(8,128)(2,1)S(1)}, bf16[2048,8]{0,1:T(8,128)(2,1)}, u32[]{:S(2)}) %copy-start.2) | copy-done | bytes 32792
  7.9 2.7 %collective-permute-done.1.refs_2_ = bf16[8,2048]{1,0:T(8,128)(2,1)S(1)} collective-permute-done((bf16[8,2048]{1,0:T(8,128)(2,1)}, bf16[8,2048]{1,0:T(8,128)(2,1)S(1)}, u32[]{:S(2)}, u32[]{:S(2)}) %collective-permute-start.1) | collective-permute-done | bytes 32800 | tf_op jit(solution)/shard_map/ppermute | solution.py:18
  10.7 0.6 shard_map.71
  11.9 0.6 collective-permute-done.4.rows_far
  13.0 1.3 %collective-permute-start.6 = (bf16[8,4224]{1,0:T(8,128)(2,1)S(1)}, bf16[8,4224]{1,0:T(8,128)(2,1)S(1)}, u32[]{:S(2)}, u32[]{:S(2)}) collective-permute-start(bf16[8,4224]{1,0:T(8,128)(2,1)S(1)} %get-tuple-element.25), channel_id=1, source_target_pairs={{0,4},{1,5},{2,6},{3,7},{4,0},{5,1},{6,2},{7,3},{8,12},{9,13},{10,... | collective-permute-start | bytes 202760 | tf_op jit(solution)/shard_map/ppermute | solution.py:18
  14.4 1.3 %collective-permute-start.7 = (bf16[8,4224]{1,0:T(8,128)(2,1)S(1)}, bf16[8,4224]{1,0:T(8,128)(2,1)S(1)}, u32[]{:S(2)}, u32[]{:S(2)}) collective-permute-start(bf16[8,4224]{1,0:T(8,128)(2,1)S(1)} %get-tuple-element.26), channel_id=1, source_target_pairs={{0,6},{1,7},{2,4},{3,5},{4,2},{5,3},{6,0},{7,1},{8,14},{9,15},{10,... | collective-permute-start | bytes 202760 | tf_op jit(solution)/shard_map/ppermute | solution.py:18
  15.7 0.8 %collective-permute-start.8 = (bf16[8,4224]{1,0:T(8,128)(2,1)S(1)}, bf16[8,4224]{1,0:T(8,128)(2,1)S(1)}, u32[]{:S(2)}, u32[]{:S(2)}) collective-permute-start(bf16[8,4224]{1,0:T(8,128)(2,1)S(1)} %get-tuple-element.27), channel_id=1, source_target_pairs={{0,2},{1,3},{2,0},{3,1},{4,6},{5,7},{6,4},{7,5},{8,10},{9,11},{10,... | collective-permute-start | bytes 202760 | tf_op jit(solution)/shard_map/ppermute | solution.py:18
  16.6 1.2 %shard_map.77.refs_8_ = bf16[2048,1024]{1,0:T(8,128)(2,1)S(1)} custom-call(bf16[2,1024,2048]{2,1,0:T(8,128)(2,1)S(1)} %bitcast.5, bf16[8,4224]{1,0:T(8,128)(2,1)S(1)} %get-tuple-element.24.refs_0_.after), custom_call_target="tpu_custom_call" | custom-call | flops 1000000000 | bytes 4194304 | tf_op jit(solution)/shard_map/pallas_call | solution.py:44
  17.8 1.2 %shard_map.78.refs_9_ = bf16[2048,1024]{1,0:T(8,128)(2,1)S(1)} custom-call(bf16[2,1024,2048]{2,1,0:T(8,128)(2,1)S(1)} %bitcast.5, bf16[8,4224]{1,0:T(8,128)(2,1)S(1)} %get-tuple-element.24.refs_0_.after), custom_call_target="tpu_custom_call" | custom-call | flops 1000000000 | bytes 4194304 | tf_op jit(solution)/shard_map/pallas_call | solution.py:44
  19.1 1.8 %collective-permute-done.6.refs_1_ = bf16[8,4224]{1,0:T(8,128)(2,1)S(1)} collective-permute-done((bf16[8,4224]{1,0:T(8,128)(2,1)S(1)}, bf16[8,4224]{1,0:T(8,128)(2,1)S(1)}, u32[]{:S(2)}, u32[]{:S(2)}) %collective-permute-start.6) | collective-permute-done | bytes 67616 | tf_op jit(solution)/shard_map/ppermute | solution.py:18
  21.0 1.2 %collective-permute-done.8.refs_3_ = bf16[8,4224]{1,0:T(8,128)(2,1)S(1)} collective-permute-done((bf16[8,4224]{1,0:T(8,128)(2,1)S(1)}, bf16[8,4224]{1,0:T(8,128)(2,1)S(1)}, u32[]{:S(2)}, u32[]{:S(2)}) %collective-permute-start.8) | collective-permute-done | bytes 67616 | tf_op jit(solution)/shard_map/ppermute | solution.py:18
  22.3 1.6 %collective-permute-start.10 = (bf16[8,4224]{1,0:T(8,128)(2,1)S(1)}, bf16[8,4224]{1,0:T(8,128)(2,1)S(1)}, u32[]{:S(2)}, u32[]{:S(2)}) collective-permute-start(bf16[8,4224]{1,0:T(8,128)(2,1)S(1)} %shard_map.74.after.refs_0_), channel_id=1, source_target_pairs={{0,16},{8,24},{16,0},{24,8},{1,17},{9,25},{17,1},{25,9},{2,18},{10... | collective-permute-start | bytes 202760 | tf_op jit(solution)/shard_map/ppermute | solution.py:18
  23.9 1.5 %collective-permute-start.11 = (bf16[8,4224]{1,0:T(8,128)(2,1)S(1)}, bf16[8,4224]{1,0:T(8,128)(2,1)S(1)}, u32[]{:S(2)}, u32[]{:S(2)}) collective-permute-start(bf16[8,4224]{1,0:T(8,128)(2,1)S(1)} %shard_map.74.after.refs_0_), channel_id=1, source_target_pairs={{0,8},{8,0},{16,24},{24,16},{1,9},{9,1},{17,25},{25,17},{2,10},{10... | collective-permute-start | bytes 202760 | tf_op jit(solution)/shard_map/ppermute | solution.py:18
  25.9 1.2 %shard_map.75.refs_6_ = bf16[1024,2048]{1,0:T(8,128)(2,1)S(1)} custom-call(bf16[2,2048,1024]{2,1,0:T(8,128)(2,1)S(1)} %bitcast.3, bf16[8,4224]{1,0:T(8,128)(2,1)S(1)} %shard_map.74.after.refs_0_), custom_call_target="tpu_custom_call" | custom-call | flops 1000000000 | bytes 4194304 | tf_op jit(solution)/shard_map/pallas_call | solution.py:44
  27.1 1.2 %shard_map.76.refs_7_ = bf16[1024,2048]{1,0:T(8,128)(2,1)S(1)} custom-call(bf16[2,2048,1024]{2,1,0:T(8,128)(2,1)S(1)} %bitcast.3, bf16[8,4224]{1,0:T(8,128)(2,1)S(1)} %shard_map.74.after.refs_0_), custom_call_target="tpu_custom_call" | custom-call | flops 1000000000 | bytes 4194304 | tf_op jit(solution)/shard_map/pallas_call | solution.py:44
  28.7 1.8 %collective-permute-done.9.refs_1_ = bf16[8,4224]{1,0:T(8,128)(2,1)S(1)} collective-permute-done((bf16[8,4224]{1,0:T(8,128)(2,1)S(1)}, bf16[8,4224]{1,0:T(8,128)(2,1)S(1)}, u32[]{:S(2)}, u32[]{:S(2)}) %collective-permute-start.9) | collective-permute-done | bytes 67616 | tf_op jit(solution)/shard_map/ppermute | solution.py:18
  30.6 4.5 %shard_map.79 = (bf16[8,4096]{1,0:T(8,128)(2,1)S(1)}, f32[8,2048]{1,0:T(8,128)S(1)}, f32[8,128]{1,0:T(8,128)S(1)}) custom-call(bf16[8,4224]{1,0:T(8,128)(2,1)S(1)} %shard_map.74.after.refs_0_, bf16[8,4224]{1,0:T(8,128)(2,1)S(1)} %collective-permute-done.9.refs_1_, bf16[8,4224]{1,0:T(8,128)(2,1)S(1)} %collective-permute-done.10.refs_2_, ...), custom_call_target="tpu_custom_call" | custom-call | flops 10000000000 | bytes 4194304 | tf_op jit(solution)/shard_map/pallas_call | solution.py:44
  35.1 1.4 %collective-permute-start.12 = (bf16[8,4096]{1,0:T(8,128)(2,1)S(1)}, bf16[8,4096]{1,0:T(8,128)(2,1)S(1)}, u32[]{:S(2)}, u32[]{:S(2)}) collective-permute-start(bf16[8,4096]{1,0:T(8,128)(2,1)S(1)} %get-tuple-element.28.refs_0_), channel_id=1, source_target_pairs={{0,24},{8,16},{16,8},{24,0},{1,25},{9,17},{17,9},{25,1},{2,26},{10... | collective-permute-start | bytes 196616 | tf_op jit(solution)/shard_map/ppermute | solution.py:18
  37.1 1.5 %collective-permute-start.14 = (bf16[8,4096]{1,0:T(8,128)(2,1)S(1)}, bf16[8,4096]{1,0:T(8,128)(2,1)S(1)}, u32[]{:S(2)}, u32[]{:S(2)}) collective-permute-start(bf16[8,4096]{1,0:T(8,128)(2,1)S(1)} %get-tuple-element.28.refs_0_), channel_id=1, source_target_pairs={{0,8},{8,0},{16,24},{24,16},{1,9},{9,1},{17,25},{25,17},{2,10},{10... | collective-permute-start | bytes 196616 | tf_op jit(solution)/shard_map/ppermute | solution.py:18
  38.6 2.0 %collective-permute-done.12.refs_1_ = bf16[8,4096]{1,0:T(8,128)(2,1)S(1)} collective-permute-done((bf16[8,4096]{1,0:T(8,128)(2,1)S(1)}, bf16[8,4096]{1,0:T(8,128)(2,1)S(1)}, u32[]{:S(2)}, u32[]{:S(2)}) %collective-permute-start.12) | collective-permute-done | bytes 65568 | tf_op jit(solution)/shard_map/ppermute | solution.py:18
  41.5 1.6 %collective-permute-start.15 = (bf16[8,4224]{1,0:T(8,128)(2,1)S(1)}, bf16[8,4224]{1,0:T(8,128)(2,1)S(1)}, u32[]{:S(2)}, u32[]{:S(2)}) collective-permute-start(bf16[8,4224]{1,0:T(8,128)(2,1)S(1)} %shard_map.80.refs_0_.after), channel_id=1, source_target_pairs={{0,4},{1,5},{2,6},{3,7},{4,0},{5,1},{6,2},{7,3},{8,12},{9,13},{10,... | collective-permute-start | bytes 202760 | tf_op jit(solution)/shard_map/ppermute | solution.py:18
  43.1 1.5 %collective-permute-start.16 = (bf16[8,4224]{1,0:T(8,128)(2,1)S(1)}, bf16[8,4224]{1,0:T(8,128)(2,1)S(1)}, u32[]{:S(2)}, u32[]{:S(2)}) collective-permute-start(bf16[8,4224]{1,0:T(8,128)(2,1)S(1)} %shard_map.80.refs_0_.after), channel_id=1, source_target_pairs={{0,6},{1,7},{2,4},{3,5},{4,2},{5,3},{6,0},{7,1},{8,14},{9,15},{10,... | collective-permute-start | bytes 202760 | tf_op jit(solution)/shard_map/ppermute | solution.py:18
  45.4 2.1 %collective-permute-done.15.refs_1_ = bf16[8,4224]{1,0:T(8,128)(2,1)S(1)} collective-permute-done((bf16[8,4224]{1,0:T(8,128)(2,1)S(1)}, bf16[8,4224]{1,0:T(8,128)(2,1)S(1)}, u32[]{:S(2)}, u32[]{:S(2)}) %collective-permute-start.15) | collective-permute-done | bytes 67616 | tf_op jit(solution)/shard_map/ppermute | solution.py:18
  47.4 1.8 %collective-permute-done.16.refs_2_ = bf16[8,4224]{1,0:T(8,128)(2,1)S(1)} collective-permute-done((bf16[8,4224]{1,0:T(8,128)(2,1)S(1)}, bf16[8,4224]{1,0:T(8,128)(2,1)S(1)}, u32[]{:S(2)}, u32[]{:S(2)}) %collective-permute-start.16) | collective-permute-done | bytes 67616 | tf_op jit(solution)/shard_map/ppermute | solution.py:18
  49.6 1.1 %shard_map.83 = (f32[32,512]{1,0:T(8,128)S(1)}, f32[32,512]{1,0:T(8,128)S(1)}, f32[32,512]{1,0:T(8,128)S(1)}, f32[8,512]{1,0:T(8,128)S(1)}) custom-call(bf16[32,4224]{1,0:T(8,128)(2,1)S(1)} %shard_map.81.near, f32[32,512]{1,0:T(8,128)S(1)} %get-tuple-element.20.logits, f32[8,512]{1,0:T(8,128)S(1)} %get-tuple-element.21.rows, ...), custom_call_target="tpu_custom_call" | custom-call | flops 10000000000 | bytes 4194304 | tf_op jit(solution)/shard_map/pallas_call | solution.py:44
  51.9 1.1 %shard_map.84 = (bf16[64,256]{1,0:T(8,128)(2,1)S(1)}, bf16[64,256]{1,0:T(8,128)(2,1)S(1)}, bf16[16,8,512]{2,1,0:T(8,128)(2,1)}) custom-call(f32[32,512]{1,0:T(8,128)S(1)} %get-tuple-element.31.direct, f32[32,512]{1,0:T(8,128)S(1)} %get-tuple-element.32.combine, f32[32,512]{1,0:T(8,128)S(1)} %get-tuple-element.33.dispatch, ...), custom_call_target="tpu_custom_call" | custom-call | flops 10000000000 | bytes 4194304 | tf_op jit(solution)/shard_map/pallas_call | solution.py:44
  53.2 4.2 %all-to-all-start = ((bf16[16,8,512]{2,1,0:T(8,128)(2,1)}), bf16[16,8,512]{2,1,0:T(8,128)(2,1)S(1)}, u32[]{:S(2)}, u32[]{:S(2)}) async-start(bf16[16,8,512]{2,1,0:T(8,128)(2,1)} %get-tuple-element.37), calls=%async_computation | async-start | bytes 262144 | tf_op jit(solution)/shard_map/all_to_all | solution.py:507
  57.5 1.4 %shard_map.87 = bf16[256,2048]{1,0:T(8,128)(2,1)} custom-call(bf16[64,256]{1,0:T(8,128)(2,1)S(1)} %get-tuple-element.35.weights, bf16[64,256]{1,0:T(8,128)(2,1)S(1)} %collective-permute-done.19.weights_far, bf16[32,4224]{1,0:T(8,128)(2,1)S(1)} %shard_map.81.near, bf16[32,2048]{1,0:T(8,128)(2,1)S(1)} %shard_map.69.table.x, ...), custom_call_target="tpu_custom_call" | custom-call | flops 10000000000 | bytes 4194304 | tf_op jit(solution)/shard_map/pallas_call | solution.py:44
  58.9 6.9 %all-to-all-done = bf16[16,8,512]{2,1,0:T(8,128)(2,1)S(1)} async-done(((bf16[16,8,512]{2,1,0:T(8,128)(2,1)}), bf16[16,8,512]{2,1,0:T(8,128)(2,1)S(1)}, u32[]{:S(2)}, u32[]{:S(2)}) %all-to-all-start) | async-done | bytes 131104 | tf_op jit(solution)/shard_map/all_to_all | solution.py:507
  65.8 0.6 convert_reduce_fusion
  (56 shorter events, 7.1 us)
Async XLA Ops:
  0.6 7.0 %copy-start.1 = (bf16[256,2048]{1,0:T(8,128)(2,1)S(1)}, bf16[256,2048]{1,0:T(8,128)(2,1)}, u32[]{:S(2)}) copy-start(bf16[256,2048]{1,0:T(8,128)(2,1)} %tokens.3) | copy-start | bytes 3145732
  0.6 7.3 %collective-permute-start = (bf16[8,2048]{1,0:T(8,128)(2,1)}, bf16[8,2048]{1,0:T(8,128)(2,1)S(1)}, u32[]{:S(2)}, u32[]{:S(2)}) collective-permute-start(bf16[8,2048]{1,0:T(8,128)(2,1)} %bitcast.8), channel_id=1, source_target_pairs={{0,4},{1,5},{2,6},{3,7},{4,0},{5,1},{6,2},{7,3},{8,12},{9,13},{10,... | collective-permute-start | bytes 98312 | tf_op jit(solution)/shard_map/ppermute | solution.py:18
  4.7 5.9 %collective-permute-start.1 = (bf16[8,2048]{1,0:T(8,128)(2,1)}, bf16[8,2048]{1,0:T(8,128)(2,1)S(1)}, u32[]{:S(2)}, u32[]{:S(2)}) collective-permute-start(bf16[8,2048]{1,0:T(8,128)(2,1)} %bitcast.9), channel_id=1, source_target_pairs={{0,6},{1,7},{2,4},{3,5},{4,2},{5,3},{6,0},{7,1},{8,14},{9,15},{10,... | collective-permute-start | bytes 98312 | tf_op jit(solution)/shard_map/ppermute | solution.py:18
  6.1 4.6 %collective-permute-start.2 = (bf16[8,2048]{1,0:T(8,128)(2,1)}, bf16[8,2048]{1,0:T(8,128)(2,1)S(1)}, u32[]{:S(2)}, u32[]{:S(2)}) collective-permute-start(bf16[8,2048]{1,0:T(8,128)(2,1)} %bitcast.10), channel_id=1, source_target_pairs={{0,2},{1,3},{2,0},{3,1},{4,6},{5,7},{6,4},{7,5},{8,10},{9,11},{10,... | collective-permute-start | bytes 98312 | tf_op jit(solution)/shard_map/ppermute | solution.py:18
  6.3 4.4 %collective-permute-start.3 = (bf16[256,2048]{1,0:T(8,128)(2,1)}, bf16[256,2048]{1,0:T(8,128)(2,1)S(1)}, u32[]{:S(2)}, u32[]{:S(2)}) collective-permute-start(bf16[256,2048]{1,0:T(8,128)(2,1)} %tokens.3), channel_id=1, source_target_pairs={{0,1},{1,0},{2,3},{3,2},{4,5},{5,4},{6,7},{7,6},{8,9},{9,8},{10,11... | collective-permute-start | bytes 3145736 | tf_op jit(solution)/shard_map/ppermute | solution.py:18
  6.3 5.6 %collective-permute-start.5 = (bf16[256,2048]{1,0:T(8,128)(2,1)}, bf16[256,2048]{1,0:T(8,128)(2,1)S(1)}, u32[]{:S(2)}, u32[]{:S(2)}) collective-permute-start(bf16[256,2048]{1,0:T(8,128)(2,1)} %x.3), channel_id=1, source_target_pairs={{0,1},{1,0},{2,3},{3,2},{4,5},{5,4},{6,7},{7,6},{8,9},{9,8},{10,11... | collective-permute-start | bytes 3145736 | tf_op jit(solution)/shard_map/ppermute | solution.py:18
  6.8 0.8 %copy-start.2 = (bf16[2048,8]{0,1:T(8,128)(2,1)S(1)}, bf16[2048,8]{0,1:T(8,128)(2,1)}, u32[]{:S(2)}) copy-start(bf16[2048,8]{0,1:T(8,128)(2,1)} %param.6) | copy-start | bytes 98308
  10.7 1.9 %copy-start = (bf16[256,2048]{1,0:T(8,128)(2,1)S(1)}, bf16[256,2048]{1,0:T(8,128)(2,1)}, u32[]{:S(2)}) copy-start(bf16[256,2048]{1,0:T(8,128)(2,1)} %x.3) | copy-start | bytes 3145732
  11.3 1.2 %collective-permute-start.4 = (f32[8,512]{1,0:T(8,128)S(1)}, f32[8,512]{1,0:T(8,128)S(1)}, u32[]{:S(2)}, u32[]{:S(2)}) collective-permute-start(f32[8,512]{1,0:T(8,128)S(1)} %get-tuple-element.21.rows), channel_id=1, source_target_pairs={{0,1},{1,0},{2,3},{3,2},{4,5},{5,4},{6,7},{7,6},{8,9},{9,8},{10,11... | collective-permute-start | bytes 49160 | tf_op jit(solution)/shard_map/ppermute | solution.py:18
  12.6 4.0 %slice-start.2 = ((s8[8388608]{0:T(1024)(128)(4,1)}), s8[4194304]{0:T(1024)(128)(4,1)S(1)}, s32[]{:S(2)}) async-start(s8[8388608]{0:T(1024)(128)(4,1)} %bitcast.4), calls=%async_computation.3 | async-start | bytes 8388608
  12.6 4.0 %slice-start.3 = ((s8[8388608]{0:T(1024)(128)(4,1)}), s8[4194304]{0:T(1024)(128)(4,1)S(1)}, s32[]{:S(2)}) async-start(s8[8388608]{0:T(1024)(128)(4,1)} %bitcast.4), calls=%async_computation.4 | async-start | bytes 8388608
  13.0 7.9 %collective-permute-start.6 = (bf16[8,4224]{1,0:T(8,128)(2,1)S(1)}, bf16[8,4224]{1,0:T(8,128)(2,1)S(1)}, u32[]{:S(2)}, u32[]{:S(2)}) collective-permute-start(bf16[8,4224]{1,0:T(8,128)(2,1)S(1)} %get-tuple-element.25), channel_id=1, source_target_pairs={{0,4},{1,5},{2,6},{3,7},{4,0},{5,1},{6,2},{7,3},{8,12},{9,13},{10,... | collective-permute-start | bytes 202760 | tf_op jit(solution)/shard_map/ppermute | solution.py:18
  14.4 6.6 %collective-permute-start.7 = (bf16[8,4224]{1,0:T(8,128)(2,1)S(1)}, bf16[8,4224]{1,0:T(8,128)(2,1)S(1)}, u32[]{:S(2)}, u32[]{:S(2)}) collective-permute-start(bf16[8,4224]{1,0:T(8,128)(2,1)S(1)} %get-tuple-element.26), channel_id=1, source_target_pairs={{0,6},{1,7},{2,4},{3,5},{4,2},{5,3},{6,0},{7,1},{8,14},{9,15},{10,... | collective-permute-start | bytes 202760 | tf_op jit(solution)/shard_map/ppermute | solution.py:18
  15.7 6.4 %collective-permute-start.8 = (bf16[8,4224]{1,0:T(8,128)(2,1)S(1)}, bf16[8,4224]{1,0:T(8,128)(2,1)S(1)}, u32[]{:S(2)}, u32[]{:S(2)}) collective-permute-start(bf16[8,4224]{1,0:T(8,128)(2,1)S(1)} %get-tuple-element.27), channel_id=1, source_target_pairs={{0,2},{1,3},{2,0},{3,1},{4,6},{5,7},{6,4},{7,5},{8,10},{9,11},{10,... | collective-permute-start | bytes 202760 | tf_op jit(solution)/shard_map/ppermute | solution.py:18
  17.8 8.0 %slice-start = ((s8[8388608]{0:T(1024)(128)(4,1)}), s8[4194304]{0:T(1024)(128)(4,1)S(1)}, s32[]{:S(2)}) async-start(s8[8388608]{0:T(1024)(128)(4,1)} %bitcast.2), calls=%async_computation.1 | async-start | bytes 8388608
  19.1 6.8 %slice-start.1 = ((s8[8388608]{0:T(1024)(128)(4,1)}), s8[4194304]{0:T(1024)(128)(4,1)S(1)}, s32[]{:S(2)}) async-start(s8[8388608]{0:T(1024)(128)(4,1)} %bitcast.2), calls=%async_computation.2 | async-start | bytes 8388608
  22.3 6.1 %collective-permute-start.10 = (bf16[8,4224]{1,0:T(8,128)(2,1)S(1)}, bf16[8,4224]{1,0:T(8,128)(2,1)S(1)}, u32[]{:S(2)}, u32[]{:S(2)}) collective-permute-start(bf16[8,4224]{1,0:T(8,128)(2,1)S(1)} %shard_map.74.after.refs_0_), channel_id=1, source_target_pairs={{0,16},{8,24},{16,0},{24,8},{1,17},{9,25},{17,1},{25,9},{2,18},{10... | collective-permute-start | bytes 202760 | tf_op jit(solution)/shard_map/ppermute | solution.py:18
  23.9 4.8 %collective-permute-start.11 = (bf16[8,4224]{1,0:T(8,128)(2,1)S(1)}, bf16[8,4224]{1,0:T(8,128)(2,1)S(1)}, u32[]{:S(2)}, u32[]{:S(2)}) collective-permute-start(bf16[8,4224]{1,0:T(8,128)(2,1)S(1)} %shard_map.74.after.refs_0_), channel_id=1, source_target_pairs={{0,8},{8,0},{16,24},{24,16},{1,9},{9,1},{17,25},{25,17},{2,10},{10... | collective-permute-start | bytes 202760 | tf_op jit(solution)/shard_map/ppermute | solution.py:18
  25.4 5.2 %collective-permute-start.9 = (bf16[8,4224]{1,0:T(8,128)(2,1)S(1)}, bf16[8,4224]{1,0:T(8,128)(2,1)S(1)}, u32[]{:S(2)}, u32[]{:S(2)}) collective-permute-start(bf16[8,4224]{1,0:T(8,128)(2,1)S(1)} %shard_map.74.after.refs_0_), channel_id=1, source_target_pairs={{0,24},{8,16},{16,8},{24,0},{1,25},{9,17},{17,9},{25,1},{2,26},{10... | collective-permute-start | bytes 202760 | tf_op jit(solution)/shard_map/ppermute | solution.py:18
  25.9 4.7 %slice-start.4 = ((s8[8388608]{0:T(1024)(128)(4,1)}), s8[4194304]{0:T(1024)(128)(4,1)S(1)}, s32[]{:S(2)}) async-start(s8[8388608]{0:T(1024)(128)(4,1)} %bitcast.6), calls=%async_computation.5 | async-start | bytes 8388608
  27.1 3.5 %slice-start.5 = ((s8[8388608]{0:T(1024)(128)(4,1)}), s8[4194304]{0:T(1024)(128)(4,1)S(1)}, s32[]{:S(2)}) async-start(s8[8388608]{0:T(1024)(128)(4,1)} %bitcast.6), calls=%async_computation.6 | async-start | bytes 8388608
  35.1 5.5 %collective-permute-start.12 = (bf16[8,4096]{1,0:T(8,128)(2,1)S(1)}, bf16[8,4096]{1,0:T(8,128)(2,1)S(1)}, u32[]{:S(2)}, u32[]{:S(2)}) collective-permute-start(bf16[8,4096]{1,0:T(8,128)(2,1)S(1)} %get-tuple-element.28.refs_0_), channel_id=1, source_target_pairs={{0,24},{8,16},{16,8},{24,0},{1,25},{9,17},{17,9},{25,1},{2,26},{10... | collective-permute-start | bytes 196616 | tf_op jit(solution)/shard_map/ppermute | solution.py:18
  36.5 4.7 %collective-permute-start.13 = (bf16[8,4096]{1,0:T(8,128)(2,1)S(1)}, bf16[8,4096]{1,0:T(8,128)(2,1)S(1)}, u32[]{:S(2)}, u32[]{:S(2)}) collective-permute-start(bf16[8,4096]{1,0:T(8,128)(2,1)S(1)} %get-tuple-element.28.refs_0_), channel_id=1, source_target_pairs={{0,16},{8,24},{16,0},{24,8},{1,17},{9,25},{17,1},{25,9},{2,18},{10... | collective-permute-start | bytes 196616 | tf_op jit(solution)/shard_map/ppermute | solution.py:18
  37.1 4.3 %collective-permute-start.14 = (bf16[8,4096]{1,0:T(8,128)(2,1)S(1)}, bf16[8,4096]{1,0:T(8,128)(2,1)S(1)}, u32[]{:S(2)}, u32[]{:S(2)}) collective-permute-start(bf16[8,4096]{1,0:T(8,128)(2,1)S(1)} %get-tuple-element.28.refs_0_), channel_id=1, source_target_pairs={{0,8},{8,0},{16,24},{24,16},{1,9},{9,1},{17,25},{25,17},{2,10},{10... | collective-permute-start | bytes 196616 | tf_op jit(solution)/shard_map/ppermute | solution.py:18
  41.5 6.0 %collective-permute-start.15 = (bf16[8,4224]{1,0:T(8,128)(2,1)S(1)}, bf16[8,4224]{1,0:T(8,128)(2,1)S(1)}, u32[]{:S(2)}, u32[]{:S(2)}) collective-permute-start(bf16[8,4224]{1,0:T(8,128)(2,1)S(1)} %shard_map.80.refs_0_.after), channel_id=1, source_target_pairs={{0,4},{1,5},{2,6},{3,7},{4,0},{5,1},{6,2},{7,3},{8,12},{9,13},{10,... | collective-permute-start | bytes 202760 | tf_op jit(solution)/shard_map/ppermute | solution.py:18
  43.1 6.2 %collective-permute-start.16 = (bf16[8,4224]{1,0:T(8,128)(2,1)S(1)}, bf16[8,4224]{1,0:T(8,128)(2,1)S(1)}, u32[]{:S(2)}, u32[]{:S(2)}) collective-permute-start(bf16[8,4224]{1,0:T(8,128)(2,1)S(1)} %shard_map.80.refs_0_.after), channel_id=1, source_target_pairs={{0,6},{1,7},{2,4},{3,5},{4,2},{5,3},{6,0},{7,1},{8,14},{9,15},{10,... | collective-permute-start | bytes 202760 | tf_op jit(solution)/shard_map/ppermute | solution.py:18
  44.6 5.0 %collective-permute-start.17 = (bf16[8,4224]{1,0:T(8,128)(2,1)S(1)}, bf16[8,4224]{1,0:T(8,128)(2,1)S(1)}, u32[]{:S(2)}, u32[]{:S(2)}) collective-permute-start(bf16[8,4224]{1,0:T(8,128)(2,1)S(1)} %shard_map.80.refs_0_.after), channel_id=1, source_target_pairs={{0,2},{1,3},{2,0},{3,1},{4,6},{5,7},{6,4},{7,5},{8,10},{9,11},{10,... | collective-permute-start | bytes 202760 | tf_op jit(solution)/shard_map/ppermute | solution.py:18
  50.7 1.2 %collective-permute-start.18 = (f32[8,512]{1,0:T(8,128)S(1)}, f32[8,512]{1,0:T(8,128)S(1)}, u32[]{:S(2)}, u32[]{:S(2)}) collective-permute-start(f32[8,512]{1,0:T(8,128)S(1)} %get-tuple-element.34.mean.after), channel_id=1, source_target_pairs={{0,1},{1,0},{2,3},{3,2},{4,5},{5,4},{6,7},{7,6},{8,9},{9,8},{10,11... | collective-permute-start | bytes 49160 | tf_op jit(solution)/shard_map/ppermute | solution.py:18
  50.8 6.7 %collective-permute-start.21 = (bf16[32,2048]{1,0:T(8,128)(2,1)S(1)}, bf16[32,2048]{1,0:T(8,128)(2,1)S(1)}, u32[]{:S(2)}, u32[]{:S(2)}) collective-permute-start(bf16[32,2048]{1,0:T(8,128)(2,1)S(1)} %shard_map.86), channel_id=1, source_target_pairs={{0,1},{1,0},{2,3},{3,2},{4,5},{5,4},{6,7},{7,6},{8,9},{9,8},{10,11... | collective-permute-start | bytes 393224 | tf_op jit(solution)/shard_map/ppermute | solution.py:18
  51.4 6.1 %collective-permute-start.20 = (bf16[32,2048]{1,0:T(8,128)(2,1)S(1)}, bf16[32,2048]{1,0:T(8,128)(2,1)S(1)}, u32[]{:S(2)}, u32[]{:S(2)}) collective-permute-start(bf16[32,2048]{1,0:T(8,128)(2,1)S(1)} %shard_map.85), channel_id=1, source_target_pairs={{0,1},{1,0},{2,3},{3,2},{4,5},{5,4},{6,7},{7,6},{8,9},{9,8},{10,11... | collective-permute-start | bytes 393224 | tf_op jit(solution)/shard_map/ppermute | solution.py:18
  53.1 4.4 %collective-permute-start.19 = (bf16[64,256]{1,0:T(8,128)(2,1)S(1)}, bf16[64,256]{1,0:T(8,128)(2,1)S(1)}, u32[]{:S(2)}, u32[]{:S(2)}) collective-permute-start(bf16[64,256]{1,0:T(8,128)(2,1)S(1)} %get-tuple-element.36), channel_id=1, source_target_pairs={{0,1},{1,0},{2,3},{3,2},{4,5},{5,4},{6,7},{7,6},{8,9},{9,8},{10,11... | collective-permute-start | bytes 98312 | tf_op jit(solution)/shard_map/ppermute | solution.py:18
  53.2 12.6 %all-to-all-start = ((bf16[16,8,512]{2,1,0:T(8,128)(2,1)}), bf16[16,8,512]{2,1,0:T(8,128)(2,1)S(1)}, u32[]{:S(2)}, u32[]{:S(2)}) async-start(bf16[16,8,512]{2,1,0:T(8,128)(2,1)} %get-tuple-element.37), calls=%async_computation | async-start | bytes 262144 | tf_op jit(solution)/shard_map/all_to_all | solution.py:507

commit v11 on v10

--- a/solution.py
+++ b/solution.py
@@ -110,10 +110,10 @@
     return weight / jnp.sum(weight, axis=0, keepdims=True)
 
 
-def logit_kernel(table, tokens_flipped, tokens_far, logits_out, stats):
+def logit_kernel(table, tokens, tokens_far, logits_out, stats):
     logits = jnp.concatenate(
         [
-            product(table[...], tokens_flipped[...], 1, 0),
+            product(table[...], tokens[...], 1, 1),
             product(table[...], tokens_far[...], 1, 1),
         ],
         axis=1,
@@ -302,7 +302,7 @@
     def against(columns, flipped_here, far):
         left = near[:, columns]
         return jnp.concatenate(
-            [product(left, flipped_here[...], 1, 0), product(left, far[...], 1, 1)], axis=1
+            [product(left, flipped_here[...], 1, 0), product(left, far[...], 1, 0)], axis=1
         )
 
     comb_grad = against(slice(0, width), out_grad_flipped, out_far)
@@ -394,7 +394,7 @@
         logit_kernel,
         [((half, 2 * patches), F32), ((8, 2 * patches), F32)],
         table_near,
-        tokens_flipped,
+        tokens,
         tokens_far,
     )
     sums, stats = local_call(
@@ -464,9 +464,9 @@
         rows,
         rows_far,
         tokens_flipped,
-        tokens_far,
+        flipped_whole(tokens_far),
         out_grad_flipped,
-        out_far,
+        flipped_whole(out_far),
         limit=12,
     )
     order = [0]

time: 66.7 us -> 66.6 us (level)
    pallas_call x20 -> x22, Pallas kernels: 15.6 us -> 16.2 us  [local_call(): pl.pallas_call(body, out_shape=tuple((jax.ShapeDtypeStruct(s, d) if k in...]
  transfers between devices with their start and end apart: 23 -> 23, of which waited for: 14 -> 15; matrix products, arithmetic and copies ran while one was open for 0% -> 0% of each run, Pallas kernels for 14% -> 15%
where the time goes in v11:
time: 66.6 us; the launch traced here: 66.3 us
  starting transfers between devices  25 us (38%)
  waiting for transfers between devices  22.7 us (34%)
  Pallas kernels  16.2 us (24%)
  between operations  0.86 us (1%)
  local copies, waits for them, and re-layouts  0.83 us (1%)
    ppermute x22, starting transfers between devices, swap(): lax.ppermute(x, axis, [(k, k ^ mask) for k in range(lax.axis_size(axis))])  20.8 us
    pallas_call x22, Pallas kernels, local_call(): pl.pallas_call(body, out_shape=tuple((jax.ShapeDtypeStruct(s, d) if k in...  16.2 us
    ppermute x22, waiting for transfers between devices, swap(): lax.ppermute(x, axis, [(k, k ^ mask) for k in range(lax.axis_size(axis))])  15.8 us
    all_to_all x1, waiting for transfers between devices, shards(): lax.all_to_all(blocks, ('seq', 'exp'), 0, 0, tiled=True, axis_index_group...  6.92 us
    all_to_all x1, starting transfers between devices, shards(): lax.all_to_all(blocks, ('seq', 'exp'), 0, 0, tiled=True, axis_index_group...  4.21 us
  transfers between devices with their start and end apart: 23, of which 15 were waited for; matrix products, arithmetic and copies ran while one was open for 0% of the time, Pallas kernels for 15%

profile of v11, /device:TPU:0, one launch (start us, length us, event | category | flops | bytes accessed | tf_op | source)
XLA Modules:
  0.0 66.3 jit_solution(17415468287385389851)
XLA Ops:
  1.1 3.7 %collective-permute-start = (bf16[8,2048]{1,0:T(8,128)(2,1)}, bf16[8,2048]{1,0:T(8,128)(2,1)S(1)}, u32[]{:S(2)}, u32[]{:S(2)}) collective-permute-start(bf16[8,2048]{1,0:T(8,128)(2,1)} %bitcast.8), channel_id=1, source_target_pairs={{0,4},{1,5},{2,6},{3,7},{4,0},{5,1},{6,2},{7,3},{8,12},{9,13},{10,... | collective-permute-start | bytes 98312 | tf_op jit(solution)/shard_map/ppermute | solution.py:18
  4.8 1.3 %collective-permute-start.1 = (bf16[8,2048]{1,0:T(8,128)(2,1)}, bf16[8,2048]{1,0:T(8,128)(2,1)S(1)}, u32[]{:S(2)}, u32[]{:S(2)}) collective-permute-start(bf16[8,2048]{1,0:T(8,128)(2,1)} %bitcast.9), channel_id=1, source_target_pairs={{0,6},{1,7},{2,4},{3,5},{4,2},{5,3},{6,0},{7,1},{8,14},{9,15},{10,... | collective-permute-start | bytes 98312 | tf_op jit(solution)/shard_map/ppermute | solution.py:18
  6.4 0.8 %copy-done.2 = bf16[2048,8]{0,1:T(8,128)(2,1)S(1)} copy-done((bf16[2048,8]{0,1:T(8,128)(2,1)S(1)}, bf16[2048,8]{0,1:T(8,128)(2,1)}, u32[]{:S(2)}) %copy-start.2) | copy-done | bytes 32792
  7.2 3.5 %collective-permute-done.1.refs_2_ = bf16[8,2048]{1,0:T(8,128)(2,1)S(1)} collective-permute-done((bf16[8,2048]{1,0:T(8,128)(2,1)}, bf16[8,2048]{1,0:T(8,128)(2,1)S(1)}, u32[]{:S(2)}, u32[]{:S(2)}) %collective-permute-start.1) | collective-permute-done | bytes 32800 | tf_op jit(solution)/shard_map/ppermute | solution.py:18
  10.8 0.8 %shard_map.70 = (f32[32,512]{1,0:T(8,128)S(1)}, f32[8,512]{1,0:T(8,128)S(1)}) custom-call(bf16[32,2048]{1,0:T(8,128)(2,1)S(1)} %shard_map.69.table.x, bf16[256,2048]{1,0:T(8,128)(2,1)S(1)} %copy-done.1, bf16[256,2048]{1,0:T(8,128)(2,1)S(1)} %collective-permute-done.3.tokens_far.x), custom_call_target="tpu_custom_call" | custom-call | flops 10000000000 | bytes 4194304 | tf_op jit(solution)/shard_map/pallas_call | solution.py:44
  12.2 0.6 collective-permute-done.4.rows_far
  13.3 1.3 %collective-permute-start.6 = (bf16[8,4224]{1,0:T(8,128)(2,1)S(1)}, bf16[8,4224]{1,0:T(8,128)(2,1)S(1)}, u32[]{:S(2)}, u32[]{:S(2)}) collective-permute-start(bf16[8,4224]{1,0:T(8,128)(2,1)S(1)} %get-tuple-element.25), channel_id=1, source_target_pairs={{0,4},{1,5},{2,6},{3,7},{4,0},{5,1},{6,2},{7,3},{8,12},{9,13},{10,... | collective-permute-start | bytes 202760 | tf_op jit(solution)/shard_map/ppermute | solution.py:18
  14.6 1.2 %collective-permute-start.7 = (bf16[8,4224]{1,0:T(8,128)(2,1)S(1)}, bf16[8,4224]{1,0:T(8,128)(2,1)S(1)}, u32[]{:S(2)}, u32[]{:S(2)}) collective-permute-start(bf16[8,4224]{1,0:T(8,128)(2,1)S(1)} %get-tuple-element.26), channel_id=1, source_target_pairs={{0,6},{1,7},{2,4},{3,5},{4,2},{5,3},{6,0},{7,1},{8,14},{9,15},{10,... | collective-permute-start | bytes 202760 | tf_op jit(solution)/shard_map/ppermute | solution.py:18
  15.8 1.0 %collective-permute-start.8 = (bf16[8,4224]{1,0:T(8,128)(2,1)S(1)}, bf16[8,4224]{1,0:T(8,128)(2,1)S(1)}, u32[]{:S(2)}, u32[]{:S(2)}) collective-permute-start(bf16[8,4224]{1,0:T(8,128)(2,1)S(1)} %get-tuple-element.27), channel_id=1, source_target_pairs={{0,2},{1,3},{2,0},{3,1},{4,6},{5,7},{6,4},{7,5},{8,10},{9,11},{10,... | collective-permute-start | bytes 202760 | tf_op jit(solution)/shard_map/ppermute | solution.py:18
  16.8 1.2 %shard_map.76.refs_8_ = bf16[2048,1024]{1,0:T(8,128)(2,1)S(1)} custom-call(bf16[2,1024,2048]{2,1,0:T(8,128)(2,1)S(1)} %bitcast.5, bf16[8,4224]{1,0:T(8,128)(2,1)S(1)} %get-tuple-element.24.refs_0_.after), custom_call_target="tpu_custom_call" | custom-call | flops 1000000000 | bytes 4194304 | tf_op jit(solution)/shard_map/pallas_call | solution.py:44
  18.1 1.2 %shard_map.77.refs_9_ = bf16[2048,1024]{1,0:T(8,128)(2,1)S(1)} custom-call(bf16[2,1024,2048]{2,1,0:T(8,128)(2,1)S(1)} %bitcast.5, bf16[8,4224]{1,0:T(8,128)(2,1)S(1)} %get-tuple-element.24.refs_0_.after), custom_call_target="tpu_custom_call" | custom-call | flops 1000000000 | bytes 4194304 | tf_op jit(solution)/shard_map/pallas_call | solution.py:44
  19.3 1.3 %collective-permute-done.6.refs_1_ = bf16[8,4224]{1,0:T(8,128)(2,1)S(1)} collective-permute-done((bf16[8,4224]{1,0:T(8,128)(2,1)S(1)}, bf16[8,4224]{1,0:T(8,128)(2,1)S(1)}, u32[]{:S(2)}, u32[]{:S(2)}) %collective-permute-start.6) | collective-permute-done | bytes 67616 | tf_op jit(solution)/shard_map/ppermute | solution.py:18
  21.1 1.2 %collective-permute-done.8.refs_3_ = bf16[8,4224]{1,0:T(8,128)(2,1)S(1)} collective-permute-done((bf16[8,4224]{1,0:T(8,128)(2,1)S(1)}, bf16[8,4224]{1,0:T(8,128)(2,1)S(1)}, u32[]{:S(2)}, u32[]{:S(2)}) %collective-permute-start.8) | collective-permute-done | bytes 67616 | tf_op jit(solution)/shard_map/ppermute | solution.py:18
  22.4 1.6 %collective-permute-start.10 = (bf16[8,4224]{1,0:T(8,128)(2,1)S(1)}, bf16[8,4224]{1,0:T(8,128)(2,1)S(1)}, u32[]{:S(2)}, u32[]{:S(2)}) collective-permute-start(bf16[8,4224]{1,0:T(8,128)(2,1)S(1)} %shard_map.73.after.refs_0_), channel_id=1, source_target_pairs={{0,16},{8,24},{16,0},{24,8},{1,17},{9,25},{17,1},{25,9},{2,18},{10... | collective-permute-start | bytes 202760 | tf_op jit(solution)/shard_map/ppermute | solution.py:18
  24.0 1.5 %collective-permute-start.11 = (bf16[8,4224]{1,0:T(8,128)(2,1)S(1)}, bf16[8,4224]{1,0:T(8,128)(2,1)S(1)}, u32[]{:S(2)}, u32[]{:S(2)}) collective-permute-start(bf16[8,4224]{1,0:T(8,128)(2,1)S(1)} %shard_map.73.after.refs_0_), channel_id=1, source_target_pairs={{0,8},{8,0},{16,24},{24,16},{1,9},{9,1},{17,25},{25,17},{2,10},{10... | collective-permute-start | bytes 202760 | tf_op jit(solution)/shard_map/ppermute | solution.py:18
  25.9 1.2 %shard_map.74.refs_6_ = bf16[1024,2048]{1,0:T(8,128)(2,1)S(1)} custom-call(bf16[2,2048,1024]{2,1,0:T(8,128)(2,1)S(1)} %bitcast.3, bf16[8,4224]{1,0:T(8,128)(2,1)S(1)} %shard_map.73.after.refs_0_), custom_call_target="tpu_custom_call" | custom-call | flops 1000000000 | bytes 4194304 | tf_op jit(solution)/shard_map/pallas_call | solution.py:44
  27.2 1.2 %shard_map.75.refs_7_ = bf16[1024,2048]{1,0:T(8,128)(2,1)S(1)} custom-call(bf16[2,2048,1024]{2,1,0:T(8,128)(2,1)S(1)} %bitcast.3, bf16[8,4224]{1,0:T(8,128)(2,1)S(1)} %shard_map.73.after.refs_0_), custom_call_target="tpu_custom_call" | custom-call | flops 1000000000 | bytes 4194304 | tf_op jit(solution)/shard_map/pallas_call | solution.py:44
  28.8 1.8 %collective-permute-done.9.refs_1_ = bf16[8,4224]{1,0:T(8,128)(2,1)S(1)} collective-permute-done((bf16[8,4224]{1,0:T(8,128)(2,1)S(1)}, bf16[8,4224]{1,0:T(8,128)(2,1)S(1)}, u32[]{:S(2)}, u32[]{:S(2)}) %collective-permute-start.9) | collective-permute-done | bytes 67616 | tf_op jit(solution)/shard_map/ppermute | solution.py:18
  30.6 4.5 %shard_map.78 = (bf16[8,4096]{1,0:T(8,128)(2,1)S(1)}, f32[8,2048]{1,0:T(8,128)S(1)}, f32[8,128]{1,0:T(8,128)S(1)}) custom-call(bf16[8,4224]{1,0:T(8,128)(2,1)S(1)} %shard_map.73.after.refs_0_, bf16[8,4224]{1,0:T(8,128)(2,1)S(1)} %collective-permute-done.9.refs_1_, bf16[8,4224]{1,0:T(8,128)(2,1)S(1)} %collective-permute-done.10.refs_2_, ...), custom_call_target="tpu_custom_call" | custom-call | flops 10000000000 | bytes 4194304 | tf_op jit(solution)/shard_map/pallas_call | solution.py:44
  35.2 1.4 %collective-permute-start.12 = (bf16[8,4096]{1,0:T(8,128)(2,1)S(1)}, bf16[8,4096]{1,0:T(8,128)(2,1)S(1)}, u32[]{:S(2)}, u32[]{:S(2)}) collective-permute-start(bf16[8,4096]{1,0:T(8,128)(2,1)S(1)} %get-tuple-element.28.refs_0_), channel_id=1, source_target_pairs={{0,24},{8,16},{16,8},{24,0},{1,25},{9,17},{17,9},{25,1},{2,26},{10... | collective-permute-start | bytes 196616 | tf_op jit(solution)/shard_map/ppermute | solution.py:18
  37.2 1.5 %collective-permute-start.14 = (bf16[8,4096]{1,0:T(8,128)(2,1)S(1)}, bf16[8,4096]{1,0:T(8,128)(2,1)S(1)}, u32[]{:S(2)}, u32[]{:S(2)}) collective-permute-start(bf16[8,4096]{1,0:T(8,128)(2,1)S(1)} %get-tuple-element.28.refs_0_), channel_id=1, source_target_pairs={{0,8},{8,0},{16,24},{24,16},{1,9},{9,1},{17,25},{25,17},{2,10},{10... | collective-permute-start | bytes 196616 | tf_op jit(solution)/shard_map/ppermute | solution.py:18
  39.0 1.7 %collective-permute-done.12.refs_1_ = bf16[8,4096]{1,0:T(8,128)(2,1)S(1)} collective-permute-done((bf16[8,4096]{1,0:T(8,128)(2,1)S(1)}, bf16[8,4096]{1,0:T(8,128)(2,1)S(1)}, u32[]{:S(2)}, u32[]{:S(2)}) %collective-permute-start.12) | collective-permute-done | bytes 65568 | tf_op jit(solution)/shard_map/ppermute | solution.py:18
  41.5 1.8 %collective-permute-start.15 = (bf16[8,4224]{1,0:T(8,128)(2,1)S(1)}, bf16[8,4224]{1,0:T(8,128)(2,1)S(1)}, u32[]{:S(2)}, u32[]{:S(2)}) collective-permute-start(bf16[8,4224]{1,0:T(8,128)(2,1)S(1)} %shard_map.79.refs_0_.after), channel_id=1, source_target_pairs={{0,4},{1,5},{2,6},{3,7},{4,0},{5,1},{6,2},{7,3},{8,12},{9,13},{10,... | collective-permute-start | bytes 202760 | tf_op jit(solution)/shard_map/ppermute | solution.py:18
  43.3 1.3 %collective-permute-start.16 = (bf16[8,4224]{1,0:T(8,128)(2,1)S(1)}, bf16[8,4224]{1,0:T(8,128)(2,1)S(1)}, u32[]{:S(2)}, u32[]{:S(2)}) collective-permute-start(bf16[8,4224]{1,0:T(8,128)(2,1)S(1)} %shard_map.79.refs_0_.after), channel_id=1, source_target_pairs={{0,6},{1,7},{2,4},{3,5},{4,2},{5,3},{6,0},{7,1},{8,14},{9,15},{10,... | collective-permute-start | bytes 202760 | tf_op jit(solution)/shard_map/ppermute | solution.py:18
  46.1 1.4 %collective-permute-done.15.refs_1_ = bf16[8,4224]{1,0:T(8,128)(2,1)S(1)} collective-permute-done((bf16[8,4224]{1,0:T(8,128)(2,1)S(1)}, bf16[8,4224]{1,0:T(8,128)(2,1)S(1)}, u32[]{:S(2)}, u32[]{:S(2)}) %collective-permute-start.15) | collective-permute-done | bytes 67616 | tf_op jit(solution)/shard_map/ppermute | solution.py:18
  47.5 2.0 %collective-permute-done.16.refs_2_ = bf16[8,4224]{1,0:T(8,128)(2,1)S(1)} collective-permute-done((bf16[8,4224]{1,0:T(8,128)(2,1)S(1)}, bf16[8,4224]{1,0:T(8,128)(2,1)S(1)}, u32[]{:S(2)}, u32[]{:S(2)}) %collective-permute-start.16) | collective-permute-done | bytes 67616 | tf_op jit(solution)/shard_map/ppermute | solution.py:18
  49.7 0.8 %shard_map.85 = (f32[32,512]{1,0:T(8,128)S(1)}, f32[32,512]{1,0:T(8,128)S(1)}, f32[32,512]{1,0:T(8,128)S(1)}, f32[8,512]{1,0:T(8,128)S(1)}) custom-call(bf16[32,4224]{1,0:T(8,128)(2,1)S(1)} %shard_map.80.near, f32[32,512]{1,0:T(8,128)S(1)} %get-tuple-element.20.logits, f32[8,512]{1,0:T(8,128)S(1)} %get-tuple-element.21.rows, ...), custom_call_target="tpu_custom_call" | custom-call | flops 10000000000 | bytes 4194304 | tf_op jit(solution)/shard_map/pallas_call | solution.py:44
  51.8 1.1 %shard_map.86 = (bf16[64,256]{1,0:T(8,128)(2,1)S(1)}, bf16[64,256]{1,0:T(8,128)(2,1)S(1)}, bf16[16,8,512]{2,1,0:T(8,128)(2,1)}) custom-call(f32[32,512]{1,0:T(8,128)S(1)} %get-tuple-element.31.direct, f32[32,512]{1,0:T(8,128)S(1)} %get-tuple-element.32.combine, f32[32,512]{1,0:T(8,128)S(1)} %get-tuple-element.33.dispatch, ...), custom_call_target="tpu_custom_call" | custom-call | flops 10000000000 | bytes 4194304 | tf_op jit(solution)/shard_map/pallas_call | solution.py:44
  53.1 4.2 %all-to-all-start = ((bf16[16,8,512]{2,1,0:T(8,128)(2,1)}), bf16[16,8,512]{2,1,0:T(8,128)(2,1)S(1)}, u32[]{:S(2)}, u32[]{:S(2)}) async-start(bf16[16,8,512]{2,1,0:T(8,128)(2,1)} %get-tuple-element.37), calls=%async_computation | async-start | bytes 262144 | tf_op jit(solution)/shard_map/all_to_all | solution.py:507
  57.3 1.4 %shard_map.89 = bf16[256,2048]{1,0:T(8,128)(2,1)} custom-call(bf16[64,256]{1,0:T(8,128)(2,1)S(1)} %get-tuple-element.35.weights, bf16[64,256]{1,0:T(8,128)(2,1)S(1)} %collective-permute-done.19.weights_far, bf16[32,4224]{1,0:T(8,128)(2,1)S(1)} %shard_map.80.near, bf16[32,2048]{1,0:T(8,128)(2,1)S(1)} %shard_map.69.table.x, ...), custom_call_target="tpu_custom_call" | custom-call | flops 10000000000 | bytes 4194304 | tf_op jit(solution)/shard_map/pallas_call | solution.py:44
  58.7 6.9 %all-to-all-done = bf16[16,8,512]{2,1,0:T(8,128)(2,1)S(1)} async-done(((bf16[16,8,512]{2,1,0:T(8,128)(2,1)}), bf16[16,8,512]{2,1,0:T(8,128)(2,1)S(1)}, u32[]{:S(2)}, u32[]{:S(2)}) %all-to-all-start) | async-done | bytes 131104 | tf_op jit(solution)/shard_map/all_to_all | solution.py:507
  65.7 0.6 convert_reduce_fusion
  (58 shorter events, 8.0 us)
Async XLA Ops:
  0.6 10.1 %collective-permute-start.3 = (bf16[256,2048]{1,0:T(8,128)(2,1)}, bf16[256,2048]{1,0:T(8,128)(2,1)S(1)}, u32[]{:S(2)}, u32[]{:S(2)}) collective-permute-start(bf16[256,2048]{1,0:T(8,128)(2,1)} %tokens.5), channel_id=1, source_target_pairs={{0,1},{1,0},{2,3},{3,2},{4,5},{5,4},{6,7},{7,6},{8,9},{9,8},{10,11... | collective-permute-start | bytes 3145736 | tf_op jit(solution)/shard_map/ppermute | solution.py:18
  1.1 6.0 %collective-permute-start = (bf16[8,2048]{1,0:T(8,128)(2,1)}, bf16[8,2048]{1,0:T(8,128)(2,1)S(1)}, u32[]{:S(2)}, u32[]{:S(2)}) collective-permute-start(bf16[8,2048]{1,0:T(8,128)(2,1)} %bitcast.8), channel_id=1, source_target_pairs={{0,4},{1,5},{2,6},{3,7},{4,0},{5,1},{6,2},{7,3},{8,12},{9,13},{10,... | collective-permute-start | bytes 98312 | tf_op jit(solution)/shard_map/ppermute | solution.py:18
  4.8 5.9 %collective-permute-start.1 = (bf16[8,2048]{1,0:T(8,128)(2,1)}, bf16[8,2048]{1,0:T(8,128)(2,1)S(1)}, u32[]{:S(2)}, u32[]{:S(2)}) collective-permute-start(bf16[8,2048]{1,0:T(8,128)(2,1)} %bitcast.9), channel_id=1, source_target_pairs={{0,6},{1,7},{2,4},{3,5},{4,2},{5,3},{6,0},{7,1},{8,14},{9,15},{10,... | collective-permute-start | bytes 98312 | tf_op jit(solution)/shard_map/ppermute | solution.py:18
  6.2 4.6 %collective-permute-start.2 = (bf16[8,2048]{1,0:T(8,128)(2,1)}, bf16[8,2048]{1,0:T(8,128)(2,1)S(1)}, u32[]{:S(2)}, u32[]{:S(2)}) collective-permute-start(bf16[8,2048]{1,0:T(8,128)(2,1)} %bitcast.10), channel_id=1, source_target_pairs={{0,2},{1,3},{2,0},{3,1},{4,6},{5,7},{6,4},{7,5},{8,10},{9,11},{10,... | collective-permute-start | bytes 98312 | tf_op jit(solution)/shard_map/ppermute | solution.py:18
  6.4 5.8 %collective-permute-start.5 = (bf16[256,2048]{1,0:T(8,128)(2,1)}, bf16[256,2048]{1,0:T(8,128)(2,1)S(1)}, u32[]{:S(2)}, u32[]{:S(2)}) collective-permute-start(bf16[256,2048]{1,0:T(8,128)(2,1)} %x.3), channel_id=1, source_target_pairs={{0,1},{1,0},{2,3},{3,2},{4,5},{5,4},{6,7},{7,6},{8,9},{9,8},{10,11... | collective-permute-start | bytes 3145736 | tf_op jit(solution)/shard_map/ppermute | solution.py:18
  6.4 0.8 %copy-start.2 = (bf16[2048,8]{0,1:T(8,128)(2,1)S(1)}, bf16[2048,8]{0,1:T(8,128)(2,1)}, u32[]{:S(2)}) copy-start(bf16[2048,8]{0,1:T(8,128)(2,1)} %param.6) | copy-start | bytes 98308
  7.2 3.6 %copy-start.1 = (bf16[256,2048]{1,0:T(8,128)(2,1)S(1)}, bf16[256,2048]{1,0:T(8,128)(2,1)}, u32[]{:S(2)}) copy-start(bf16[256,2048]{1,0:T(8,128)(2,1)} %tokens.5) | copy-start | bytes 3145732
  10.8 2.1 %copy-start = (bf16[256,2048]{1,0:T(8,128)(2,1)S(1)}, bf16[256,2048]{1,0:T(8,128)(2,1)}, u32[]{:S(2)}) copy-start(bf16[256,2048]{1,0:T(8,128)(2,1)} %x.3) | copy-start | bytes 3145732
  11.6 1.2 %collective-permute-start.4 = (f32[8,512]{1,0:T(8,128)S(1)}, f32[8,512]{1,0:T(8,128)S(1)}, u32[]{:S(2)}, u32[]{:S(2)}) collective-permute-start(f32[8,512]{1,0:T(8,128)S(1)} %get-tuple-element.21.rows), channel_id=1, source_target_pairs={{0,1},{1,0},{2,3},{3,2},{4,5},{5,4},{6,7},{7,6},{8,9},{9,8},{10,11... | collective-permute-start | bytes 49160 | tf_op jit(solution)/shard_map/ppermute | solution.py:18
  12.8 4.0 %slice-start.2 = ((s8[8388608]{0:T(1024)(128)(4,1)}), s8[4194304]{0:T(1024)(128)(4,1)S(1)}, s32[]{:S(2)}) async-start(s8[8388608]{0:T(1024)(128)(4,1)} %bitcast.4), calls=%async_computation.3 | async-start | bytes 8388608
  12.8 4.0 %slice-start.3 = ((s8[8388608]{0:T(1024)(128)(4,1)}), s8[4194304]{0:T(1024)(128)(4,1)S(1)}, s32[]{:S(2)}) async-start(s8[8388608]{0:T(1024)(128)(4,1)} %bitcast.4), calls=%async_computation.4 | async-start | bytes 8388608
  13.3 7.4 %collective-permute-start.6 = (bf16[8,4224]{1,0:T(8,128)(2,1)S(1)}, bf16[8,4224]{1,0:T(8,128)(2,1)S(1)}, u32[]{:S(2)}, u32[]{:S(2)}) collective-permute-start(bf16[8,4224]{1,0:T(8,128)(2,1)S(1)} %get-tuple-element.25), channel_id=1, source_target_pairs={{0,4},{1,5},{2,6},{3,7},{4,0},{5,1},{6,2},{7,3},{8,12},{9,13},{10,... | collective-permute-start | bytes 202760 | tf_op jit(solution)/shard_map/ppermute | solution.py:18
  14.6 6.5 %collective-permute-start.7 = (bf16[8,4224]{1,0:T(8,128)(2,1)S(1)}, bf16[8,4224]{1,0:T(8,128)(2,1)S(1)}, u32[]{:S(2)}, u32[]{:S(2)}) collective-permute-start(bf16[8,4224]{1,0:T(8,128)(2,1)S(1)} %get-tuple-element.26), channel_id=1, source_target_pairs={{0,6},{1,7},{2,4},{3,5},{4,2},{5,3},{6,0},{7,1},{8,14},{9,15},{10,... | collective-permute-start | bytes 202760 | tf_op jit(solution)/shard_map/ppermute | solution.py:18
  15.8 6.4 %collective-permute-start.8 = (bf16[8,4224]{1,0:T(8,128)(2,1)S(1)}, bf16[8,4224]{1,0:T(8,128)(2,1)S(1)}, u32[]{:S(2)}, u32[]{:S(2)}) collective-permute-start(bf16[8,4224]{1,0:T(8,128)(2,1)S(1)} %get-tuple-element.27), channel_id=1, source_target_pairs={{0,2},{1,3},{2,0},{3,1},{4,6},{5,7},{6,4},{7,5},{8,10},{9,11},{10,... | collective-permute-start | bytes 202760 | tf_op jit(solution)/shard_map/ppermute | solution.py:18
  18.1 7.9 %slice-start = ((s8[8388608]{0:T(1024)(128)(4,1)}), s8[4194304]{0:T(1024)(128)(4,1)S(1)}, s32[]{:S(2)}) async-start(s8[8388608]{0:T(1024)(128)(4,1)} %bitcast.2), calls=%async_computation.1 | async-start | bytes 8388608
  19.3 6.6 %slice-start.1 = ((s8[8388608]{0:T(1024)(128)(4,1)}), s8[4194304]{0:T(1024)(128)(4,1)S(1)}, s32[]{:S(2)}) async-start(s8[8388608]{0:T(1024)(128)(4,1)} %bitcast.2), calls=%async_computation.2 | async-start | bytes 8388608
  22.4 6.1 %collective-permute-start.10 = (bf16[8,4224]{1,0:T(8,128)(2,1)S(1)}, bf16[8,4224]{1,0:T(8,128)(2,1)S(1)}, u32[]{:S(2)}, u32[]{:S(2)}) collective-permute-start(bf16[8,4224]{1,0:T(8,128)(2,1)S(1)} %shard_map.73.after.refs_0_), channel_id=1, source_target_pairs={{0,16},{8,24},{16,0},{24,8},{1,17},{9,25},{17,1},{25,9},{2,18},{10... | collective-permute-start | bytes 202760 | tf_op jit(solution)/shard_map/ppermute | solution.py:18
  24.0 4.8 %collective-permute-start.11 = (bf16[8,4224]{1,0:T(8,128)(2,1)S(1)}, bf16[8,4224]{1,0:T(8,128)(2,1)S(1)}, u32[]{:S(2)}, u32[]{:S(2)}) collective-permute-start(bf16[8,4224]{1,0:T(8,128)(2,1)S(1)} %shard_map.73.after.refs_0_), channel_id=1, source_target_pairs={{0,8},{8,0},{16,24},{24,16},{1,9},{9,1},{17,25},{25,17},{2,10},{10... | collective-permute-start | bytes 202760 | tf_op jit(solution)/shard_map/ppermute | solution.py:18
  25.4 5.2 %collective-permute-start.9 = (bf16[8,4224]{1,0:T(8,128)(2,1)S(1)}, bf16[8,4224]{1,0:T(8,128)(2,1)S(1)}, u32[]{:S(2)}, u32[]{:S(2)}) collective-permute-start(bf16[8,4224]{1,0:T(8,128)(2,1)S(1)} %shard_map.73.after.refs_0_), channel_id=1, source_target_pairs={{0,24},{8,16},{16,8},{24,0},{1,25},{9,17},{17,9},{25,1},{2,26},{10... | collective-permute-start | bytes 202760 | tf_op jit(solution)/shard_map/ppermute | solution.py:18
  25.9 4.7 %slice-start.4 = ((s8[8388608]{0:T(1024)(128)(4,1)}), s8[4194304]{0:T(1024)(128)(4,1)S(1)}, s32[]{:S(2)}) async-start(s8[8388608]{0:T(1024)(128)(4,1)} %bitcast.6), calls=%async_computation.5 | async-start | bytes 8388608
  27.2 3.5 %slice-start.5 = ((s8[8388608]{0:T(1024)(128)(4,1)}), s8[4194304]{0:T(1024)(128)(4,1)S(1)}, s32[]{:S(2)}) async-start(s8[8388608]{0:T(1024)(128)(4,1)} %bitcast.6), calls=%async_computation.6 | async-start | bytes 8388608
  35.2 5.5 %collective-permute-start.12 = (bf16[8,4096]{1,0:T(8,128)(2,1)S(1)}, bf16[8,4096]{1,0:T(8,128)(2,1)S(1)}, u32[]{:S(2)}, u32[]{:S(2)}) collective-permute-start(bf16[8,4096]{1,0:T(8,128)(2,1)S(1)} %get-tuple-element.28.refs_0_), channel_id=1, source_target_pairs={{0,24},{8,16},{16,8},{24,0},{1,25},{9,17},{17,9},{25,1},{2,26},{10... | collective-permute-start | bytes 196616 | tf_op jit(solution)/shard_map/ppermute | solution.py:18
  36.6 4.7 %collective-permute-start.13 = (bf16[8,4096]{1,0:T(8,128)(2,1)S(1)}, bf16[8,4096]{1,0:T(8,128)(2,1)S(1)}, u32[]{:S(2)}, u32[]{:S(2)}) collective-permute-start(bf16[8,4096]{1,0:T(8,128)(2,1)S(1)} %get-tuple-element.28.refs_0_), channel_id=1, source_target_pairs={{0,16},{8,24},{16,0},{24,8},{1,17},{9,25},{17,1},{25,9},{2,18},{10... | collective-permute-start | bytes 196616 | tf_op jit(solution)/shard_map/ppermute | solution.py:18
  37.2 4.3 %collective-permute-start.14 = (bf16[8,4096]{1,0:T(8,128)(2,1)S(1)}, bf16[8,4096]{1,0:T(8,128)(2,1)S(1)}, u32[]{:S(2)}, u32[]{:S(2)}) collective-permute-start(bf16[8,4096]{1,0:T(8,128)(2,1)S(1)} %get-tuple-element.28.refs_0_), channel_id=1, source_target_pairs={{0,8},{8,0},{16,24},{24,16},{1,9},{9,1},{17,25},{25,17},{2,10},{10... | collective-permute-start | bytes 196616 | tf_op jit(solution)/shard_map/ppermute | solution.py:18
  41.5 6.0 %collective-permute-start.15 = (bf16[8,4224]{1,0:T(8,128)(2,1)S(1)}, bf16[8,4224]{1,0:T(8,128)(2,1)S(1)}, u32[]{:S(2)}, u32[]{:S(2)}) collective-permute-start(bf16[8,4224]{1,0:T(8,128)(2,1)S(1)} %shard_map.79.refs_0_.after), channel_id=1, source_target_pairs={{0,4},{1,5},{2,6},{3,7},{4,0},{5,1},{6,2},{7,3},{8,12},{9,13},{10,... | collective-permute-start | bytes 202760 | tf_op jit(solution)/shard_map/ppermute | solution.py:18
  43.3 6.2 %collective-permute-start.16 = (bf16[8,4224]{1,0:T(8,128)(2,1)S(1)}, bf16[8,4224]{1,0:T(8,128)(2,1)S(1)}, u32[]{:S(2)}, u32[]{:S(2)}) collective-permute-start(bf16[8,4224]{1,0:T(8,128)(2,1)S(1)} %shard_map.79.refs_0_.after), channel_id=1, source_target_pairs={{0,6},{1,7},{2,4},{3,5},{4,2},{5,3},{6,0},{7,1},{8,14},{9,15},{10,... | collective-permute-start | bytes 202760 | tf_op jit(solution)/shard_map/ppermute | solution.py:18
  44.7 5.0 %collective-permute-start.17 = (bf16[8,4224]{1,0:T(8,128)(2,1)S(1)}, bf16[8,4224]{1,0:T(8,128)(2,1)S(1)}, u32[]{:S(2)}, u32[]{:S(2)}) collective-permute-start(bf16[8,4224]{1,0:T(8,128)(2,1)S(1)} %shard_map.79.refs_0_.after), channel_id=1, source_target_pairs={{0,2},{1,3},{2,0},{3,1},{4,6},{5,7},{6,4},{7,5},{8,10},{9,11},{10,... | collective-permute-start | bytes 202760 | tf_op jit(solution)/shard_map/ppermute | solution.py:18
  50.5 1.2 %collective-permute-start.18 = (f32[8,512]{1,0:T(8,128)S(1)}, f32[8,512]{1,0:T(8,128)S(1)}, u32[]{:S(2)}, u32[]{:S(2)}) collective-permute-start(f32[8,512]{1,0:T(8,128)S(1)} %get-tuple-element.34.mean.after), channel_id=1, source_target_pairs={{0,1},{1,0},{2,3},{3,2},{4,5},{5,4},{6,7},{7,6},{8,9},{9,8},{10,11... | collective-permute-start | bytes 49160 | tf_op jit(solution)/shard_map/ppermute | solution.py:18
  50.6 6.7 %collective-permute-start.21 = (bf16[32,2048]{1,0:T(8,128)(2,1)S(1)}, bf16[32,2048]{1,0:T(8,128)(2,1)S(1)}, u32[]{:S(2)}, u32[]{:S(2)}) collective-permute-start(bf16[32,2048]{1,0:T(8,128)(2,1)S(1)} %shard_map.88), channel_id=1, source_target_pairs={{0,1},{1,0},{2,3},{3,2},{4,5},{5,4},{6,7},{7,6},{8,9},{9,8},{10,11... | collective-permute-start | bytes 393224 | tf_op jit(solution)/shard_map/ppermute | solution.py:18
  51.2 6.1 %collective-permute-start.20 = (bf16[32,2048]{1,0:T(8,128)(2,1)S(1)}, bf16[32,2048]{1,0:T(8,128)(2,1)S(1)}, u32[]{:S(2)}, u32[]{:S(2)}) collective-permute-start(bf16[32,2048]{1,0:T(8,128)(2,1)S(1)} %shard_map.87), channel_id=1, source_target_pairs={{0,1},{1,0},{2,3},{3,2},{4,5},{5,4},{6,7},{7,6},{8,9},{9,8},{10,11... | collective-permute-start | bytes 393224 | tf_op jit(solution)/shard_map/ppermute | solution.py:18
  52.9 4.4 %collective-permute-start.19 = (bf16[64,256]{1,0:T(8,128)(2,1)S(1)}, bf16[64,256]{1,0:T(8,128)(2,1)S(1)}, u32[]{:S(2)}, u32[]{:S(2)}) collective-permute-start(bf16[64,256]{1,0:T(8,128)(2,1)S(1)} %get-tuple-element.36), channel_id=1, source_target_pairs={{0,1},{1,0},{2,3},{3,2},{4,5},{5,4},{6,7},{7,6},{8,9},{9,8},{10,11... | collective-permute-start | bytes 98312 | tf_op jit(solution)/shard_map/ppermute | solution.py:18
  53.1 12.6 %all-to-all-start = ((bf16[16,8,512]{2,1,0:T(8,128)(2,1)}), bf16[16,8,512]{2,1,0:T(8,128)(2,1)S(1)}, u32[]{:S(2)}, u32[]{:S(2)}) async-start(bf16[16,8,512]{2,1,0:T(8,128)(2,1)} %get-tuple-element.37), calls=%async_computation | async-start | bytes 262144 | tf_op jit(solution)/shard_map/all_to_all | solution.py:507

commit v12 on v11

--- a/solution.py
+++ b/solution.py
@@ -357,6 +357,10 @@
     out[...] = near[:, width : 2 * width]
 
 
+def block_sum_kernel(blocks, out):
+    out[...] = sum(blocks[k].astype(F32) for k in range(blocks.shape[0]))
+
+
 def copy_kernel(x, after, out):
     out[...] = x[...]
 
@@ -507,7 +511,9 @@
     part = lax.all_to_all(
         blocks, ("seq", "exp"), 0, 0, tiled=True, axis_index_groups=same_core
     )
-    part = jnp.sum(part.astype(F32), axis=0)
+    (part,) = local_call(
+        block_sum_kernel, [(part.shape[1:], F32)], part, limit=4, to_hbm=(0,)
+    )
     return (tok_grad, part.T)
 
 

time: 66.6 us -> 66.6 us (level)
    pallas_call x22 -> x23, Pallas kernels: 16.2 us -> 16.8 us  [local_call(): pl.pallas_call(body, out_shape=tuple((jax.ShapeDtypeStruct(s, d) if k in...]
where the time goes in v12:
time: 66.6 us; the launch traced here: 66.3 us
  starting transfers between devices  25 us (38%)
  waiting for transfers between devices  22.7 us (34%)
  Pallas kernels  16.8 us (25%)
  between operations  0.86 us (1%)
  local copies, waits for them, and re-layouts  0.83 us (1%)
    ppermute x22, starting transfers between devices, swap(): lax.ppermute(x, axis, [(k, k ^ mask) for k in range(lax.axis_size(axis))])  20.8 us
    pallas_call x23, Pallas kernels, local_call(): pl.pallas_call(body, out_shape=tuple((jax.ShapeDtypeStruct(s, d) if k in...  16.8 us
    ppermute x22, waiting for transfers between devices, swap(): lax.ppermute(x, axis, [(k, k ^ mask) for k in range(lax.axis_size(axis))])  15.8 us
    all_to_all x1, waiting for transfers between devices, shards(): lax.all_to_all(blocks, ('seq', 'exp'), 0, 0, tiled=True, axis_index_group...  6.92 us
    all_to_all x1, starting transfers between devices, shards(): lax.all_to_all(blocks, ('seq', 'exp'), 0, 0, tiled=True, axis_index_group...  4.21 us
  transfers between devices with their start and end apart: 23, of which 15 were waited for; matrix products, arithmetic and copies ran while one was open for 0% of the time, Pallas kernels for 15%

profile of v12, /device:TPU:0, one launch (start us, length us, event | category | flops | bytes accessed | tf_op | source)
XLA Modules:
  0.0 66.3 jit_solution(5869644464960358079)
XLA Ops:
  1.1 3.7 %collective-permute-start = (bf16[8,2048]{1,0:T(8,128)(2,1)}, bf16[8,2048]{1,0:T(8,128)(2,1)S(1)}, u32[]{:S(2)}, u32[]{:S(2)}) collective-permute-start(bf16[8,2048]{1,0:T(8,128)(2,1)} %bitcast.8), channel_id=1, source_target_pairs={{0,4},{1,5},{2,6},{3,7},{4,0},{5,1},{6,2},{7,3},{8,12},{9,13},{10,... | collective-permute-start | bytes 98312 | tf_op jit(solution)/shard_map/ppermute | solution.py:18
  4.8 1.3 %collective-permute-start.1 = (bf16[8,2048]{1,0:T(8,128)(2,1)}, bf16[8,2048]{1,0:T(8,128)(2,1)S(1)}, u32[]{:S(2)}, u32[]{:S(2)}) collective-permute-start(bf16[8,2048]{1,0:T(8,128)(2,1)} %bitcast.9), channel_id=1, source_target_pairs={{0,6},{1,7},{2,4},{3,5},{4,2},{5,3},{6,0},{7,1},{8,14},{9,15},{10,... | collective-permute-start | bytes 98312 | tf_op jit(solution)/shard_map/ppermute | solution.py:18
  6.4 0.8 %copy-done.2 = bf16[2048,8]{0,1:T(8,128)(2,1)S(1)} copy-done((bf16[2048,8]{0,1:T(8,128)(2,1)S(1)}, bf16[2048,8]{0,1:T(8,128)(2,1)}, u32[]{:S(2)}) %copy-start.2) | copy-done | bytes 32792
  7.2 3.5 %collective-permute-done.1.refs_2_ = bf16[8,2048]{1,0:T(8,128)(2,1)S(1)} collective-permute-done((bf16[8,2048]{1,0:T(8,128)(2,1)}, bf16[8,2048]{1,0:T(8,128)(2,1)S(1)}, u32[]{:S(2)}, u32[]{:S(2)}) %collective-permute-start.1) | collective-permute-done | bytes 32800 | tf_op jit(solution)/shard_map/ppermute | solution.py:18
  10.8 0.8 %shard_map.70 = (f32[32,512]{1,0:T(8,128)S(1)}, f32[8,512]{1,0:T(8,128)S(1)}) custom-call(bf16[32,2048]{1,0:T(8,128)(2,1)S(1)} %shard_map.69.table.x, bf16[256,2048]{1,0:T(8,128)(2,1)S(1)} %copy-done.1, bf16[256,2048]{1,0:T(8,128)(2,1)S(1)} %collective-permute-done.3.tokens_far.x), custom_call_target="tpu_custom_call" | custom-call | flops 10000000000 | bytes 4194304 | tf_op jit(solution)/shard_map/pallas_call | solution.py:44
  12.2 0.6 collective-permute-done.4.rows_far
  13.3 1.3 %collective-permute-start.6 = (bf16[8,4224]{1,0:T(8,128)(2,1)S(1)}, bf16[8,4224]{1,0:T(8,128)(2,1)S(1)}, u32[]{:S(2)}, u32[]{:S(2)}) collective-permute-start(bf16[8,4224]{1,0:T(8,128)(2,1)S(1)} %get-tuple-element.25), channel_id=1, source_target_pairs={{0,4},{1,5},{2,6},{3,7},{4,0},{5,1},{6,2},{7,3},{8,12},{9,13},{10,... | collective-permute-start | bytes 202760 | tf_op jit(solution)/shard_map/ppermute | solution.py:18
  14.6 1.2 %collective-permute-start.7 = (bf16[8,4224]{1,0:T(8,128)(2,1)S(1)}, bf16[8,4224]{1,0:T(8,128)(2,1)S(1)}, u32[]{:S(2)}, u32[]{:S(2)}) collective-permute-start(bf16[8,4224]{1,0:T(8,128)(2,1)S(1)} %get-tuple-element.26), channel_id=1, source_target_pairs={{0,6},{1,7},{2,4},{3,5},{4,2},{5,3},{6,0},{7,1},{8,14},{9,15},{10,... | collective-permute-start | bytes 202760 | tf_op jit(solution)/shard_map/ppermute | solution.py:18
  15.8 1.0 %collective-permute-start.8 = (bf16[8,4224]{1,0:T(8,128)(2,1)S(1)}, bf16[8,4224]{1,0:T(8,128)(2,1)S(1)}, u32[]{:S(2)}, u32[]{:S(2)}) collective-permute-start(bf16[8,4224]{1,0:T(8,128)(2,1)S(1)} %get-tuple-element.27), channel_id=1, source_target_pairs={{0,2},{1,3},{2,0},{3,1},{4,6},{5,7},{6,4},{7,5},{8,10},{9,11},{10,... | collective-permute-start | bytes 202760 | tf_op jit(solution)/shard_map/ppermute | solution.py:18
  16.8 1.2 %shard_map.76.refs_8_ = bf16[2048,1024]{1,0:T(8,128)(2,1)S(1)} custom-call(bf16[2,1024,2048]{2,1,0:T(8,128)(2,1)S(1)} %bitcast.5, bf16[8,4224]{1,0:T(8,128)(2,1)S(1)} %get-tuple-element.24.refs_0_.after), custom_call_target="tpu_custom_call" | custom-call | flops 1000000000 | bytes 4194304 | tf_op jit(solution)/shard_map/pallas_call | solution.py:44
  18.1 1.2 %shard_map.77.refs_9_ = bf16[2048,1024]{1,0:T(8,128)(2,1)S(1)} custom-call(bf16[2,1024,2048]{2,1,0:T(8,128)(2,1)S(1)} %bitcast.5, bf16[8,4224]{1,0:T(8,128)(2,1)S(1)} %get-tuple-element.24.refs_0_.after), custom_call_target="tpu_custom_call" | custom-call | flops 1000000000 | bytes 4194304 | tf_op jit(solution)/shard_map/pallas_call | solution.py:44
  19.3 1.3 %collective-permute-done.6.refs_1_ = bf16[8,4224]{1,0:T(8,128)(2,1)S(1)} collective-permute-done((bf16[8,4224]{1,0:T(8,128)(2,1)S(1)}, bf16[8,4224]{1,0:T(8,128)(2,1)S(1)}, u32[]{:S(2)}, u32[]{:S(2)}) %collective-permute-start.6) | collective-permute-done | bytes 67616 | tf_op jit(solution)/shard_map/ppermute | solution.py:18
  21.1 1.2 %collective-permute-done.8.refs_3_ = bf16[8,4224]{1,0:T(8,128)(2,1)S(1)} collective-permute-done((bf16[8,4224]{1,0:T(8,128)(2,1)S(1)}, bf16[8,4224]{1,0:T(8,128)(2,1)S(1)}, u32[]{:S(2)}, u32[]{:S(2)}) %collective-permute-start.8) | collective-permute-done | bytes 67616 | tf_op jit(solution)/shard_map/ppermute | solution.py:18
  22.4 1.6 %collective-permute-start.10 = (bf16[8,4224]{1,0:T(8,128)(2,1)S(1)}, bf16[8,4224]{1,0:T(8,128)(2,1)S(1)}, u32[]{:S(2)}, u32[]{:S(2)}) collective-permute-start(bf16[8,4224]{1,0:T(8,128)(2,1)S(1)} %shard_map.73.after.refs_0_), channel_id=1, source_target_pairs={{0,16},{8,24},{16,0},{24,8},{1,17},{9,25},{17,1},{25,9},{2,18},{10... | collective-permute-start | bytes 202760 | tf_op jit(solution)/shard_map/ppermute | solution.py:18
  24.0 1.5 %collective-permute-start.11 = (bf16[8,4224]{1,0:T(8,128)(2,1)S(1)}, bf16[8,4224]{1,0:T(8,128)(2,1)S(1)}, u32[]{:S(2)}, u32[]{:S(2)}) collective-permute-start(bf16[8,4224]{1,0:T(8,128)(2,1)S(1)} %shard_map.73.after.refs_0_), channel_id=1, source_target_pairs={{0,8},{8,0},{16,24},{24,16},{1,9},{9,1},{17,25},{25,17},{2,10},{10... | collective-permute-start | bytes 202760 | tf_op jit(solution)/shard_map/ppermute | solution.py:18
  25.9 1.2 %shard_map.74.refs_6_ = bf16[1024,2048]{1,0:T(8,128)(2,1)S(1)} custom-call(bf16[2,2048,1024]{2,1,0:T(8,128)(2,1)S(1)} %bitcast.3, bf16[8,4224]{1,0:T(8,128)(2,1)S(1)} %shard_map.73.after.refs_0_), custom_call_target="tpu_custom_call" | custom-call | flops 1000000000 | bytes 4194304 | tf_op jit(solution)/shard_map/pallas_call | solution.py:44
  27.2 1.2 %shard_map.75.refs_7_ = bf16[1024,2048]{1,0:T(8,128)(2,1)S(1)} custom-call(bf16[2,2048,1024]{2,1,0:T(8,128)(2,1)S(1)} %bitcast.3, bf16[8,4224]{1,0:T(8,128)(2,1)S(1)} %shard_map.73.after.refs_0_), custom_call_target="tpu_custom_call" | custom-call | flops 1000000000 | bytes 4194304 | tf_op jit(solution)/shard_map/pallas_call | solution.py:44
  28.8 1.8 %collective-permute-done.9.refs_1_ = bf16[8,4224]{1,0:T(8,128)(2,1)S(1)} collective-permute-done((bf16[8,4224]{1,0:T(8,128)(2,1)S(1)}, bf16[8,4224]{1,0:T(8,128)(2,1)S(1)}, u32[]{:S(2)}, u32[]{:S(2)}) %collective-permute-start.9) | collective-permute-done | bytes 67616 | tf_op jit(solution)/shard_map/ppermute | solution.py:18
  30.6 4.5 %shard_map.78 = (bf16[8,4096]{1,0:T(8,128)(2,1)S(1)}, f32[8,2048]{1,0:T(8,128)S(1)}, f32[8,128]{1,0:T(8,128)S(1)}) custom-call(bf16[8,4224]{1,0:T(8,128)(2,1)S(1)} %shard_map.73.after.refs_0_, bf16[8,4224]{1,0:T(8,128)(2,1)S(1)} %collective-permute-done.9.refs_1_, bf16[8,4224]{1,0:T(8,128)(2,1)S(1)} %collective-permute-done.10.refs_2_, ...), custom_call_target="tpu_custom_call" | custom-call | flops 10000000000 | bytes 4194304 | tf_op jit(solution)/shard_map/pallas_call | solution.py:44
  35.2 1.4 %collective-permute-start.12 = (bf16[8,4096]{1,0:T(8,128)(2,1)S(1)}, bf16[8,4096]{1,0:T(8,128)(2,1)S(1)}, u32[]{:S(2)}, u32[]{:S(2)}) collective-permute-start(bf16[8,4096]{1,0:T(8,128)(2,1)S(1)} %get-tuple-element.28.refs_0_), channel_id=1, source_target_pairs={{0,24},{8,16},{16,8},{24,0},{1,25},{9,17},{17,9},{25,1},{2,26},{10... | collective-permute-start | bytes 196616 | tf_op jit(solution)/shard_map/ppermute | solution.py:18
  37.2 1.5 %collective-permute-start.14 = (bf16[8,4096]{1,0:T(8,128)(2,1)S(1)}, bf16[8,4096]{1,0:T(8,128)(2,1)S(1)}, u32[]{:S(2)}, u32[]{:S(2)}) collective-permute-start(bf16[8,4096]{1,0:T(8,128)(2,1)S(1)} %get-tuple-element.28.refs_0_), channel_id=1, source_target_pairs={{0,8},{8,0},{16,24},{24,16},{1,9},{9,1},{17,25},{25,17},{2,10},{10... | collective-permute-start | bytes 196616 | tf_op jit(solution)/shard_map/ppermute | solution.py:18
  39.0 1.7 %collective-permute-done.12.refs_1_ = bf16[8,4096]{1,0:T(8,128)(2,1)S(1)} collective-permute-done((bf16[8,4096]{1,0:T(8,128)(2,1)S(1)}, bf16[8,4096]{1,0:T(8,128)(2,1)S(1)}, u32[]{:S(2)}, u32[]{:S(2)}) %collective-permute-start.12) | collective-permute-done | bytes 65568 | tf_op jit(solution)/shard_map/ppermute | solution.py:18
  41.5 1.8 %collective-permute-start.15 = (bf16[8,4224]{1,0:T(8,128)(2,1)S(1)}, bf16[8,4224]{1,0:T(8,128)(2,1)S(1)}, u32[]{:S(2)}, u32[]{:S(2)}) collective-permute-start(bf16[8,4224]{1,0:T(8,128)(2,1)S(1)} %shard_map.79.refs_0_.after), channel_id=1, source_target_pairs={{0,4},{1,5},{2,6},{3,7},{4,0},{5,1},{6,2},{7,3},{8,12},{9,13},{10,... | collective-permute-start | bytes 202760 | tf_op jit(solution)/shard_map/ppermute | solution.py:18
  43.3 1.3 %collective-permute-start.16 = (bf16[8,4224]{1,0:T(8,128)(2,1)S(1)}, bf16[8,4224]{1,0:T(8,128)(2,1)S(1)}, u32[]{:S(2)}, u32[]{:S(2)}) collective-permute-start(bf16[8,4224]{1,0:T(8,128)(2,1)S(1)} %shard_map.79.refs_0_.after), channel_id=1, source_target_pairs={{0,6},{1,7},{2,4},{3,5},{4,2},{5,3},{6,0},{7,1},{8,14},{9,15},{10,... | collective-permute-start | bytes 202760 | tf_op jit(solution)/shard_map/ppermute | solution.py:18
  46.1 1.4 %collective-permute-done.15.refs_1_ = bf16[8,4224]{1,0:T(8,128)(2,1)S(1)} collective-permute-done((bf16[8,4224]{1,0:T(8,128)(2,1)S(1)}, bf16[8,4224]{1,0:T(8,128)(2,1)S(1)}, u32[]{:S(2)}, u32[]{:S(2)}) %collective-permute-start.15) | collective-permute-done | bytes 67616 | tf_op jit(solution)/shard_map/ppermute | solution.py:18
  47.5 2.0 %collective-permute-done.16.refs_2_ = bf16[8,4224]{1,0:T(8,128)(2,1)S(1)} collective-permute-done((bf16[8,4224]{1,0:T(8,128)(2,1)S(1)}, bf16[8,4224]{1,0:T(8,128)(2,1)S(1)}, u32[]{:S(2)}, u32[]{:S(2)}) %collective-permute-start.16) | collective-permute-done | bytes 67616 | tf_op jit(solution)/shard_map/ppermute | solution.py:18
  49.7 0.8 %shard_map.85 = (f32[32,512]{1,0:T(8,128)S(1)}, f32[32,512]{1,0:T(8,128)S(1)}, f32[32,512]{1,0:T(8,128)S(1)}, f32[8,512]{1,0:T(8,128)S(1)}) custom-call(bf16[32,4224]{1,0:T(8,128)(2,1)S(1)} %shard_map.80.near, f32[32,512]{1,0:T(8,128)S(1)} %get-tuple-element.20.logits, f32[8,512]{1,0:T(8,128)S(1)} %get-tuple-element.21.rows, ...), custom_call_target="tpu_custom_call" | custom-call | flops 10000000000 | bytes 4194304 | tf_op jit(solution)/shard_map/pallas_call | solution.py:44
  51.8 1.1 %shard_map.86 = (bf16[64,256]{1,0:T(8,128)(2,1)S(1)}, bf16[64,256]{1,0:T(8,128)(2,1)S(1)}, bf16[16,8,512]{2,1,0:T(8,128)(2,1)}) custom-call(f32[32,512]{1,0:T(8,128)S(1)} %get-tuple-element.31.direct, f32[32,512]{1,0:T(8,128)S(1)} %get-tuple-element.32.combine, f32[32,512]{1,0:T(8,128)S(1)} %get-tuple-element.33.dispatch, ...), custom_call_target="tpu_custom_call" | custom-call | flops 10000000000 | bytes 4194304 | tf_op jit(solution)/shard_map/pallas_call | solution.py:44
  53.1 4.2 %all-to-all-start = ((bf16[16,8,512]{2,1,0:T(8,128)(2,1)}), bf16[16,8,512]{2,1,0:T(8,128)(2,1)S(1)}, u32[]{:S(2)}, u32[]{:S(2)}) async-start(bf16[16,8,512]{2,1,0:T(8,128)(2,1)} %get-tuple-element.37), calls=%async_computation | async-start | bytes 262144 | tf_op jit(solution)/shard_map/all_to_all | solution.py:511
  57.3 1.4 %shard_map.89 = bf16[256,2048]{1,0:T(8,128)(2,1)} custom-call(bf16[64,256]{1,0:T(8,128)(2,1)S(1)} %get-tuple-element.35.weights, bf16[64,256]{1,0:T(8,128)(2,1)S(1)} %collective-permute-done.19.weights_far, bf16[32,4224]{1,0:T(8,128)(2,1)S(1)} %shard_map.80.near, bf16[32,2048]{1,0:T(8,128)(2,1)S(1)} %shard_map.69.table.x, ...), custom_call_target="tpu_custom_call" | custom-call | flops 10000000000 | bytes 4194304 | tf_op jit(solution)/shard_map/pallas_call | solution.py:44
  58.8 6.9 %all-to-all-done.blocks = bf16[16,8,512]{2,1,0:T(8,128)(2,1)S(1)} async-done(((bf16[16,8,512]{2,1,0:T(8,128)(2,1)}), bf16[16,8,512]{2,1,0:T(8,128)(2,1)S(1)}, u32[]{:S(2)}, u32[]{:S(2)}) %all-to-all-start) | async-done | bytes 131104 | tf_op jit(solution)/shard_map/all_to_all | solution.py:511
  65.7 0.6 shard_map.90
  (58 shorter events, 8.0 us)
Async XLA Ops:
  0.6 10.1 %collective-permute-start.3 = (bf16[256,2048]{1,0:T(8,128)(2,1)}, bf16[256,2048]{1,0:T(8,128)(2,1)S(1)}, u32[]{:S(2)}, u32[]{:S(2)}) collective-permute-start(bf16[256,2048]{1,0:T(8,128)(2,1)} %tokens.5), channel_id=1, source_target_pairs={{0,1},{1,0},{2,3},{3,2},{4,5},{5,4},{6,7},{7,6},{8,9},{9,8},{10,11... | collective-permute-start | bytes 3145736 | tf_op jit(solution)/shard_map/ppermute | solution.py:18
  1.1 6.0 %collective-permute-start = (bf16[8,2048]{1,0:T(8,128)(2,1)}, bf16[8,2048]{1,0:T(8,128)(2,1)S(1)}, u32[]{:S(2)}, u32[]{:S(2)}) collective-permute-start(bf16[8,2048]{1,0:T(8,128)(2,1)} %bitcast.8), channel_id=1, source_target_pairs={{0,4},{1,5},{2,6},{3,7},{4,0},{5,1},{6,2},{7,3},{8,12},{9,13},{10,... | collective-permute-start | bytes 98312 | tf_op jit(solution)/shard_map/ppermute | solution.py:18
  4.8 5.9 %collective-permute-start.1 = (bf16[8,2048]{1,0:T(8,128)(2,1)}, bf16[8,2048]{1,0:T(8,128)(2,1)S(1)}, u32[]{:S(2)}, u32[]{:S(2)}) collective-permute-start(bf16[8,2048]{1,0:T(8,128)(2,1)} %bitcast.9), channel_id=1, source_target_pairs={{0,6},{1,7},{2,4},{3,5},{4,2},{5,3},{6,0},{7,1},{8,14},{9,15},{10,... | collective-permute-start | bytes 98312 | tf_op jit(solution)/shard_map/ppermute | solution.py:18
  6.2 4.6 %collective-permute-start.2 = (bf16[8,2048]{1,0:T(8,128)(2,1)}, bf16[8,2048]{1,0:T(8,128)(2,1)S(1)}, u32[]{:S(2)}, u32[]{:S(2)}) collective-permute-start(bf16[8,2048]{1,0:T(8,128)(2,1)} %bitcast.10), channel_id=1, source_target_pairs={{0,2},{1,3},{2,0},{3,1},{4,6},{5,7},{6,4},{7,5},{8,10},{9,11},{10,... | collective-permute-start | bytes 98312 | tf_op jit(solution)/shard_map/ppermute | solution.py:18
  6.4 5.8 %collective-permute-start.5 = (bf16[256,2048]{1,0:T(8,128)(2,1)}, bf16[256,2048]{1,0:T(8,128)(2,1)S(1)}, u32[]{:S(2)}, u32[]{:S(2)}) collective-permute-start(bf16[256,2048]{1,0:T(8,128)(2,1)} %x.3), channel_id=1, source_target_pairs={{0,1},{1,0},{2,3},{3,2},{4,5},{5,4},{6,7},{7,6},{8,9},{9,8},{10,11... | collective-permute-start | bytes 3145736 | tf_op jit(solution)/shard_map/ppermute | solution.py:18
  6.4 0.8 %copy-start.2 = (bf16[2048,8]{0,1:T(8,128)(2,1)S(1)}, bf16[2048,8]{0,1:T(8,128)(2,1)}, u32[]{:S(2)}) copy-start(bf16[2048,8]{0,1:T(8,128)(2,1)} %param.6) | copy-start | bytes 98308
  7.2 3.6 %copy-start.1 = (bf16[256,2048]{1,0:T(8,128)(2,1)S(1)}, bf16[256,2048]{1,0:T(8,128)(2,1)}, u32[]{:S(2)}) copy-start(bf16[256,2048]{1,0:T(8,128)(2,1)} %tokens.5) | copy-start | bytes 3145732
  10.8 2.1 %copy-start = (bf16[256,2048]{1,0:T(8,128)(2,1)S(1)}, bf16[256,2048]{1,0:T(8,128)(2,1)}, u32[]{:S(2)}) copy-start(bf16[256,2048]{1,0:T(8,128)(2,1)} %x.3) | copy-start | bytes 3145732
  11.6 1.2 %collective-permute-start.4 = (f32[8,512]{1,0:T(8,128)S(1)}, f32[8,512]{1,0:T(8,128)S(1)}, u32[]{:S(2)}, u32[]{:S(2)}) collective-permute-start(f32[8,512]{1,0:T(8,128)S(1)} %get-tuple-element.21.rows), channel_id=1, source_target_pairs={{0,1},{1,0},{2,3},{3,2},{4,5},{5,4},{6,7},{7,6},{8,9},{9,8},{10,11... | collective-permute-start | bytes 49160 | tf_op jit(solution)/shard_map/ppermute | solution.py:18
  12.8 4.0 %slice-start.2 = ((s8[8388608]{0:T(1024)(128)(4,1)}), s8[4194304]{0:T(1024)(128)(4,1)S(1)}, s32[]{:S(2)}) async-start(s8[8388608]{0:T(1024)(128)(4,1)} %bitcast.4), calls=%async_computation.3 | async-start | bytes 8388608
  12.8 4.0 %slice-start.3 = ((s8[8388608]{0:T(1024)(128)(4,1)}), s8[4194304]{0:T(1024)(128)(4,1)S(1)}, s32[]{:S(2)}) async-start(s8[8388608]{0:T(1024)(128)(4,1)} %bitcast.4), calls=%async_computation.4 | async-start | bytes 8388608
  13.3 7.4 %collective-permute-start.6 = (bf16[8,4224]{1,0:T(8,128)(2,1)S(1)}, bf16[8,4224]{1,0:T(8,128)(2,1)S(1)}, u32[]{:S(2)}, u32[]{:S(2)}) collective-permute-start(bf16[8,4224]{1,0:T(8,128)(2,1)S(1)} %get-tuple-element.25), channel_id=1, source_target_pairs={{0,4},{1,5},{2,6},{3,7},{4,0},{5,1},{6,2},{7,3},{8,12},{9,13},{10,... | collective-permute-start | bytes 202760 | tf_op jit(solution)/shard_map/ppermute | solution.py:18
  14.6 6.5 %collective-permute-start.7 = (bf16[8,4224]{1,0:T(8,128)(2,1)S(1)}, bf16[8,4224]{1,0:T(8,128)(2,1)S(1)}, u32[]{:S(2)}, u32[]{:S(2)}) collective-permute-start(bf16[8,4224]{1,0:T(8,128)(2,1)S(1)} %get-tuple-element.26), channel_id=1, source_target_pairs={{0,6},{1,7},{2,4},{3,5},{4,2},{5,3},{6,0},{7,1},{8,14},{9,15},{10,... | collective-permute-start | bytes 202760 | tf_op jit(solution)/shard_map/ppermute | solution.py:18
  15.8 6.4 %collective-permute-start.8 = (bf16[8,4224]{1,0:T(8,128)(2,1)S(1)}, bf16[8,4224]{1,0:T(8,128)(2,1)S(1)}, u32[]{:S(2)}, u32[]{:S(2)}) collective-permute-start(bf16[8,4224]{1,0:T(8,128)(2,1)S(1)} %get-tuple-element.27), channel_id=1, source_target_pairs={{0,2},{1,3},{2,0},{3,1},{4,6},{5,7},{6,4},{7,5},{8,10},{9,11},{10,... | collective-permute-start | bytes 202760 | tf_op jit(solution)/shard_map/ppermute | solution.py:18
  18.1 7.9 %slice-start = ((s8[8388608]{0:T(1024)(128)(4,1)}), s8[4194304]{0:T(1024)(128)(4,1)S(1)}, s32[]{:S(2)}) async-start(s8[8388608]{0:T(1024)(128)(4,1)} %bitcast.2), calls=%async_computation.1 | async-start | bytes 8388608
  19.3 6.6 %slice-start.1 = ((s8[8388608]{0:T(1024)(128)(4,1)}), s8[4194304]{0:T(1024)(128)(4,1)S(1)}, s32[]{:S(2)}) async-start(s8[8388608]{0:T(1024)(128)(4,1)} %bitcast.2), calls=%async_computation.2 | async-start | bytes 8388608
  22.4 6.1 %collective-permute-start.10 = (bf16[8,4224]{1,0:T(8,128)(2,1)S(1)}, bf16[8,4224]{1,0:T(8,128)(2,1)S(1)}, u32[]{:S(2)}, u32[]{:S(2)}) collective-permute-start(bf16[8,4224]{1,0:T(8,128)(2,1)S(1)} %shard_map.73.after.refs_0_), channel_id=1, source_target_pairs={{0,16},{8,24},{16,0},{24,8},{1,17},{9,25},{17,1},{25,9},{2,18},{10... | collective-permute-start | bytes 202760 | tf_op jit(solution)/shard_map/ppermute | solution.py:18
  24.0 4.8 %collective-permute-start.11 = (bf16[8,4224]{1,0:T(8,128)(2,1)S(1)}, bf16[8,4224]{1,0:T(8,128)(2,1)S(1)}, u32[]{:S(2)}, u32[]{:S(2)}) collective-permute-start(bf16[8,4224]{1,0:T(8,128)(2,1)S(1)} %shard_map.73.after.refs_0_), channel_id=1, source_target_pairs={{0,8},{8,0},{16,24},{24,16},{1,9},{9,1},{17,25},{25,17},{2,10},{10... | collective-permute-start | bytes 202760 | tf_op jit(solution)/shard_map/ppermute | solution.py:18
  25.4 5.2 %collective-permute-start.9 = (bf16[8,4224]{1,0:T(8,128)(2,1)S(1)}, bf16[8,4224]{1,0:T(8,128)(2,1)S(1)}, u32[]{:S(2)}, u32[]{:S(2)}) collective-permute-start(bf16[8,4224]{1,0:T(8,128)(2,1)S(1)} %shard_map.73.after.refs_0_), channel_id=1, source_target_pairs={{0,24},{8,16},{16,8},{24,0},{1,25},{9,17},{17,9},{25,1},{2,26},{10... | collective-permute-start | bytes 202760 | tf_op jit(solution)/shard_map/ppermute | solution.py:18
  25.9 4.7 %slice-start.4 = ((s8[8388608]{0:T(1024)(128)(4,1)}), s8[4194304]{0:T(1024)(128)(4,1)S(1)}, s32[]{:S(2)}) async-start(s8[8388608]{0:T(1024)(128)(4,1)} %bitcast.6), calls=%async_computation.5 | async-start | bytes 8388608
  27.2 3.5 %slice-start.5 = ((s8[8388608]{0:T(1024)(128)(4,1)}), s8[4194304]{0:T(1024)(128)(4,1)S(1)}, s32[]{:S(2)}) async-start(s8[8388608]{0:T(1024)(128)(4,1)} %bitcast.6), calls=%async_computation.6 | async-start | bytes 8388608
  35.2 5.5 %collective-permute-start.12 = (bf16[8,4096]{1,0:T(8,128)(2,1)S(1)}, bf16[8,4096]{1,0:T(8,128)(2,1)S(1)}, u32[]{:S(2)}, u32[]{:S(2)}) collective-permute-start(bf16[8,4096]{1,0:T(8,128)(2,1)S(1)} %get-tuple-element.28.refs_0_), channel_id=1, source_target_pairs={{0,24},{8,16},{16,8},{24,0},{1,25},{9,17},{17,9},{25,1},{2,26},{10... | collective-permute-start | bytes 196616 | tf_op jit(solution)/shard_map/ppermute | solution.py:18
  36.6 4.7 %collective-permute-start.13 = (bf16[8,4096]{1,0:T(8,128)(2,1)S(1)}, bf16[8,4096]{1,0:T(8,128)(2,1)S(1)}, u32[]{:S(2)}, u32[]{:S(2)}) collective-permute-start(bf16[8,4096]{1,0:T(8,128)(2,1)S(1)} %get-tuple-element.28.refs_0_), channel_id=1, source_target_pairs={{0,16},{8,24},{16,0},{24,8},{1,17},{9,25},{17,1},{25,9},{2,18},{10... | collective-permute-start | bytes 196616 | tf_op jit(solution)/shard_map/ppermute | solution.py:18
  37.2 4.3 %collective-permute-start.14 = (bf16[8,4096]{1,0:T(8,128)(2,1)S(1)}, bf16[8,4096]{1,0:T(8,128)(2,1)S(1)}, u32[]{:S(2)}, u32[]{:S(2)}) collective-permute-start(bf16[8,4096]{1,0:T(8,128)(2,1)S(1)} %get-tuple-element.28.refs_0_), channel_id=1, source_target_pairs={{0,8},{8,0},{16,24},{24,16},{1,9},{9,1},{17,25},{25,17},{2,10},{10... | collective-permute-start | bytes 196616 | tf_op jit(solution)/shard_map/ppermute | solution.py:18
  41.5 6.0 %collective-permute-start.15 = (bf16[8,4224]{1,0:T(8,128)(2,1)S(1)}, bf16[8,4224]{1,0:T(8,128)(2,1)S(1)}, u32[]{:S(2)}, u32[]{:S(2)}) collective-permute-start(bf16[8,4224]{1,0:T(8,128)(2,1)S(1)} %shard_map.79.refs_0_.after), channel_id=1, source_target_pairs={{0,4},{1,5},{2,6},{3,7},{4,0},{5,1},{6,2},{7,3},{8,12},{9,13},{10,... | collective-permute-start | bytes 202760 | tf_op jit(solution)/shard_map/ppermute | solution.py:18
  43.3 6.2 %collective-permute-start.16 = (bf16[8,4224]{1,0:T(8,128)(2,1)S(1)}, bf16[8,4224]{1,0:T(8,128)(2,1)S(1)}, u32[]{:S(2)}, u32[]{:S(2)}) collective-permute-start(bf16[8,4224]{1,0:T(8,128)(2,1)S(1)} %shard_map.79.refs_0_.after), channel_id=1, source_target_pairs={{0,6},{1,7},{2,4},{3,5},{4,2},{5,3},{6,0},{7,1},{8,14},{9,15},{10,... | collective-permute-start | bytes 202760 | tf_op jit(solution)/shard_map/ppermute | solution.py:18
  44.7 5.0 %collective-permute-start.17 = (bf16[8,4224]{1,0:T(8,128)(2,1)S(1)}, bf16[8,4224]{1,0:T(8,128)(2,1)S(1)}, u32[]{:S(2)}, u32[]{:S(2)}) collective-permute-start(bf16[8,4224]{1,0:T(8,128)(2,1)S(1)} %shard_map.79.refs_0_.after), channel_id=1, source_target_pairs={{0,2},{1,3},{2,0},{3,1},{4,6},{5,7},{6,4},{7,5},{8,10},{9,11},{10,... | collective-permute-start | bytes 202760 | tf_op jit(solution)/shard_map/ppermute | solution.py:18
  50.5 1.2 %collective-permute-start.18 = (f32[8,512]{1,0:T(8,128)S(1)}, f32[8,512]{1,0:T(8,128)S(1)}, u32[]{:S(2)}, u32[]{:S(2)}) collective-permute-start(f32[8,512]{1,0:T(8,128)S(1)} %get-tuple-element.34.mean.after), channel_id=1, source_target_pairs={{0,1},{1,0},{2,3},{3,2},{4,5},{5,4},{6,7},{7,6},{8,9},{9,8},{10,11... | collective-permute-start | bytes 49160 | tf_op jit(solution)/shard_map/ppermute | solution.py:18
  50.6 6.7 %collective-permute-start.21 = (bf16[32,2048]{1,0:T(8,128)(2,1)S(1)}, bf16[32,2048]{1,0:T(8,128)(2,1)S(1)}, u32[]{:S(2)}, u32[]{:S(2)}) collective-permute-start(bf16[32,2048]{1,0:T(8,128)(2,1)S(1)} %shard_map.88), channel_id=1, source_target_pairs={{0,1},{1,0},{2,3},{3,2},{4,5},{5,4},{6,7},{7,6},{8,9},{9,8},{10,11... | collective-permute-start | bytes 393224 | tf_op jit(solution)/shard_map/ppermute | solution.py:18
  51.2 6.1 %collective-permute-start.20 = (bf16[32,2048]{1,0:T(8,128)(2,1)S(1)}, bf16[32,2048]{1,0:T(8,128)(2,1)S(1)}, u32[]{:S(2)}, u32[]{:S(2)}) collective-permute-start(bf16[32,2048]{1,0:T(8,128)(2,1)S(1)} %shard_map.87), channel_id=1, source_target_pairs={{0,1},{1,0},{2,3},{3,2},{4,5},{5,4},{6,7},{7,6},{8,9},{9,8},{10,11... | collective-permute-start | bytes 393224 | tf_op jit(solution)/shard_map/ppermute | solution.py:18
  52.9 4.4 %collective-permute-start.19 = (bf16[64,256]{1,0:T(8,128)(2,1)S(1)}, bf16[64,256]{1,0:T(8,128)(2,1)S(1)}, u32[]{:S(2)}, u32[]{:S(2)}) collective-permute-start(bf16[64,256]{1,0:T(8,128)(2,1)S(1)} %get-tuple-element.36), channel_id=1, source_target_pairs={{0,1},{1,0},{2,3},{3,2},{4,5},{5,4},{6,7},{7,6},{8,9},{9,8},{10,11... | collective-permute-start | bytes 98312 | tf_op jit(solution)/shard_map/ppermute | solution.py:18
  53.1 12.6 %all-to-all-start = ((bf16[16,8,512]{2,1,0:T(8,128)(2,1)}), bf16[16,8,512]{2,1,0:T(8,128)(2,1)S(1)}, u32[]{:S(2)}, u32[]{:S(2)}) async-start(bf16[16,8,512]{2,1,0:T(8,128)(2,1)} %get-tuple-element.37), calls=%async_computation | async-start | bytes 262144 | tf_op jit(solution)/shard_map/all_to_all | solution.py:511
